TPU v7x, 512 devices: a whole 4x8x8 slice. The times are simulated.
512 devices in a mesh: sec: 8 (over z_lo, core), ctx: 64 (over z_hi, x, y).
Axes of the slice: x: 4, y: 8, z: 8 (z_hi: 2, z_lo: 4; z = z_hi * 4 + z_lo), core: 2. Of those that a mesh axis runs over, the one named last changes fastest.
Arguments:
- offsets: int32 [64], replicated, may hold values from 0 to 112, as said below
- queries: bfloat16 [8, 1024, 2560], P('sec', 'ctx'), may hold values from -150 to 150
- output_grad: bfloat16 [8, 1024, 2560], P('sec', 'ctx'), may hold values from -6 to 6
- attention_out: bfloat16 [8, 1024, 2560], P('sec', 'ctx'), may hold values from -6 to 6
- cache_keys: bfloat16 [8192, 128], P('ctx'), may hold values from -7 to 7
- cache_values: bfloat16 [8192, 128], P('ctx'), may hold values from -6 to 6
- key_projection: bfloat16 [5120, 128], P('sec'), may hold values from -0.5 to 0.5
- value_projection: bfloat16 [5120, 128], P('sec'), may hold values from -0.5 to 0.5
- retention_query: bfloat16 [8192, 5120], P('ctx', 'sec'), may hold values from -0.046875 to 0.046875
- retention_key: bfloat16 [8192, 5120], P('ctx', 'sec'), may hold values from -0.046875 to 0.046875
- retention_value: bfloat16 [8192, 5120], P('ctx', 'sec'), may hold values from -6 to 6
- retention_decay: float32 [40, 8192], P('sec', 'ctx'), may hold values from -1 to 0, as said below
Outputs:
- cross_query_grad: bfloat16 [8, 1024, 2560], P('sec', 'ctx')
- cache_key_grad: bfloat16 [8192, 128], P('ctx')
- cache_value_grad: bfloat16 [8192, 128], P('ctx')
- retention_query_grad: float32 [8192, 5120], P('ctx', 'sec')
- retention_key_grad: float32 [8192, 5120], P('ctx', 'sec')
- retention_value_grad: float32 [8192, 5120], P('ctx', 'sec')
Inputs may be any that keep to these rules, and one draw needn't show every extreme that they name: Query row r of context shard c stands at sequence position c * 128 + offsets[c] + r; some shard has offset 128 - 16 and some shard has offset 0. `retention_decay`: every entry is negative.
All inputs are finite; a program needn't handle non-finite values.
Results may differ from a plain program's by a relative error of at most 0.015.
Values may be sent and summed in bfloat16 or wider, within the bound.
No kernel may reach another device: no remote copies, remote signals or barrier semaphores. Data moves between devices by JAX's collectives and lax.ppermute only.
A program may use at most 128 MiB of HBM per device.

v0:
```python
import math

import jax
import jax.numpy as jnp
from jax import lax
from jax.sharding import PartitionSpec as P


def entering(part, axis, combine, identity, reverse):
    count = lax.axis_size(axis)
    place = lax.axis_index(axis)
    ahead = count - 1 - place if reverse else place
    gathered = jax.tree.map(lambda a: lax.all_gather(a, axis), part)
    state = jax.tree.map(lambda a, e: jnp.zeros_like(a) + jnp.asarray(e, a.dtype), part, identity)

    def one(lap, state):
        source = count - 1 - lap if reverse else lap
        return combine(
            state, jax.tree.map(lambda a: lax.dynamic_index_in_dim(a, source, 0, False), gathered)
        )

    return lax.fori_loop(0, ahead, one, state)


def head_scores(query_flat, key_block, factor):
    return (
        jnp.einsum("md,nd->mn", query_flat, key_block, preferred_element_type=jnp.float32) * factor
    )


def stats_update(running, key_block, begin_row, query_flat, row_position, factor):
    row_max, row_sum = running
    scores = head_scores(query_flat, key_block, factor)
    key_count = key_block.shape[0]
    visible = (begin_row + jnp.arange(key_count, dtype=jnp.int32))[None, :] <= row_position[:, None]
    new_max = jnp.maximum(row_max, jnp.max(jnp.where(visible, scores, -1e30), axis=1))
    shifted = jnp.where(visible, jnp.exp(scores - new_max[:, None]), 0.0)
    new_sum = row_sum * jnp.exp(row_max - new_max) + jnp.sum(shifted, axis=1)
    return (new_max, new_sum)


def grad_update(
    running,
    key_block,
    value_block,
    begin_row,
    query_flat,
    grad_flat,
    row_position,
    log_total,
    row_delta,
    factor,
):
    scores = head_scores(query_flat, key_block, factor)
    key_count = key_block.shape[0]
    visible = (begin_row + jnp.arange(key_count, dtype=jnp.int32))[None, :] <= row_position[:, None]
    soft_probs = jnp.where(visible, jnp.exp(scores - log_total[:, None]), 0.0)
    grad_probs = jnp.einsum("md,nd->mn", grad_flat, value_block, preferred_element_type=jnp.float32)
    grad_scores = (soft_probs * (grad_probs - row_delta[:, None])).astype(jnp.bfloat16)
    query_total = running[0] + jnp.dot(grad_scores, key_block, preferred_element_type=jnp.float32)
    key_terms = jnp.einsum("mn,md->nd", grad_scores, query_flat, preferred_element_type=jnp.float32)
    value_terms = jnp.einsum(
        "mn,md->nd", soft_probs.astype(jnp.bfloat16), grad_flat, preferred_element_type=jnp.float32
    )
    key_buffer = lax.dynamic_update_slice_in_dim(running[1], key_terms, begin_row, 0)
    value_buffer = lax.dynamic_update_slice_in_dim(running[2], value_terms, begin_row, 0)
    return (query_total, key_buffer, value_buffer)


def compose(first_pair, second_pair):
    return (
        first_pair[0] * second_pair[0],
        second_pair[0][:, None, None] * first_pair[1] + second_pair[1],
    )


def body(
    offsets,
    queries,
    output_grad,
    attention_out,
    cache_keys,
    cache_values,
    key_projection,
    value_projection,
    retention_query,
    retention_key,
    retention_value,
    retention_decay,
):
    shard_count = lax.axis_size("ctx")
    shard_index = lax.axis_index("ctx")
    shard_rows, head_size = cache_keys.shape
    layer_count, query_rows, query_width = queries.shape
    head_count = query_width // head_size
    total_rows = shard_rows * shard_count
    factor = 1.0 / math.sqrt(head_size)
    shard_ids = jnp.arange(shard_count, dtype=jnp.int32)
    own_offset = jnp.sum(jnp.where(shard_ids == shard_index, offsets, 0))
    query_position = shard_index * shard_rows + own_offset + jnp.arange(query_rows, dtype=jnp.int32)
    last_position = shard_index * shard_rows + own_offset + query_rows - 1
    row_position = jnp.broadcast_to(
        query_position[None, :, None], (layer_count, query_rows, head_count)
    ).reshape(-1)
    query_flat = queries.reshape(-1, head_size)
    grad_flat = output_grad.reshape(-1, head_size)
    row_delta = jnp.sum(
        grad_flat.astype(jnp.float32) * attention_out.reshape(-1, head_size).astype(jnp.float32),
        axis=1,
    )
    row_count = query_flat.shape[0]
    stats_start = (jnp.full((row_count,), -1e30, jnp.float32), jnp.zeros((row_count,), jnp.float32))
    grad_start = (jnp.zeros((row_count, head_size), jnp.float32),)
    grad_start = grad_start + (
        jnp.zeros((total_rows, head_size), jnp.float32),
        jnp.zeros((total_rows, head_size), jnp.float32),
    )
    block_rows = math.gcd(total_rows, 512)
    block_needed = last_position // block_rows + 1
    key_whole, value_whole = (
        lax.all_gather(cache_keys, "ctx", axis=0, tiled=True),
        lax.all_gather(cache_values, "ctx", axis=0, tiled=True),
    )

    def stats_loop(block_index, running):
        begin_row = block_index * block_rows
        key_block = lax.dynamic_slice_in_dim(key_whole, begin_row, block_rows, 0)
        return stats_update(running, key_block, begin_row, query_flat, row_position, factor)

    row_max, row_sum = lax.fori_loop(0, block_needed, stats_loop, stats_start)
    log_total = row_max + jnp.log(row_sum)

    def grad_loop(block_index, running):
        begin_row = block_index * block_rows
        key_block = lax.dynamic_slice_in_dim(key_whole, begin_row, block_rows, 0)
        value_block = lax.dynamic_slice_in_dim(value_whole, begin_row, block_rows, 0)
        return grad_update(
            running,
            key_block,
            value_block,
            begin_row,
            query_flat,
            grad_flat,
            row_position,
            log_total,
            row_delta,
            factor,
        )

    grad_result = lax.fori_loop(0, block_needed, grad_loop, grad_start)
    cross_query_grad = (
        (grad_result[0] * factor).astype(jnp.bfloat16).reshape(layer_count, query_rows, query_width)
    )
    key_terms = grad_result[1].reshape(shard_count, shard_rows, head_size)
    value_terms = grad_result[2].reshape(shard_count, shard_rows, head_size)
    key_received, value_received = (
        lax.all_to_all(key_terms, "ctx", split_axis=0, concat_axis=0, tiled=True),
        lax.all_to_all(value_terms, "ctx", split_axis=0, concat_axis=0, tiled=True),
    )
    key_part = jnp.sum(key_received, axis=0)
    value_part = jnp.sum(value_received, axis=0)
    key_sum, value_sum = lax.psum((key_part, value_part), "sec")
    cache_key_grad = (key_sum * factor).astype(jnp.bfloat16)
    cache_value_grad = value_sum.astype(jnp.bfloat16)
    retention_out_grad = (
        jnp.einsum("jd,ed->je", cache_key_grad, key_projection, preferred_element_type=jnp.float32)
        + jnp.einsum(
            "jd,ed->je", cache_value_grad, value_projection, preferred_element_type=jnp.float32
        )
    ).astype(jnp.bfloat16)
    local_heads = retention_decay.shape[0]

    def head_view(array):
        return array.reshape(shard_rows, local_heads, head_size)

    query_heads = head_view(retention_query)
    key_heads = head_view(retention_key)
    value_heads = head_view(retention_value)
    grad_heads = head_view(retention_out_grad)
    running_decay = jnp.cumsum(retention_decay, axis=1)
    block_decay = jnp.exp(running_decay[:, -1])
    decay_to_end = jnp.exp(running_decay[:, -1:] - running_decay).T[:, :, None]
    decay_from_start = jnp.exp(running_decay).T[:, :, None]
    key_weighted = (key_heads.astype(jnp.float32) * decay_to_end).astype(jnp.bfloat16)
    query_weighted = (query_heads.astype(jnp.float32) * decay_from_start).astype(jnp.bfloat16)
    block_state = jnp.einsum(
        "thd,the->hde", key_weighted, value_heads, preferred_element_type=jnp.float32
    )
    block_grad = jnp.einsum(
        "thd,the->hde", query_weighted, grad_heads, preferred_element_type=jnp.float32
    )
    identity = (
        jnp.ones((local_heads,), jnp.float32),
        jnp.zeros((local_heads, head_size, head_size), jnp.float32),
    )
    state_enter = entering((block_decay, block_state), "ctx", compose, identity, False)[1]
    grad_enter = entering((block_decay, block_grad), "ctx", compose, identity, True)[1]
    state_rounded = state_enter.astype(jnp.bfloat16)
    grad_rounded = grad_enter.astype(jnp.bfloat16)
    row_index = jnp.arange(shard_rows, dtype=jnp.int32)
    causal = (row_index[:, None] >= row_index[None, :])[None]
    decay_gap = running_decay[:, :, None] - running_decay[:, None, :]
    decay_matrix = jnp.where(causal, jnp.exp(jnp.where(causal, decay_gap, 0.0)), 0.0)
    decay_back = jnp.transpose(decay_matrix, (0, 2, 1))
    grad_value_dot = jnp.einsum(
        "thd,uhd->htu", grad_heads, value_heads, preferred_element_type=jnp.float32
    )
    weight_one = (decay_matrix * grad_value_dot).astype(jnp.bfloat16)
    query_result = jnp.einsum(
        "htu,uhd->thd", weight_one, key_heads, preferred_element_type=jnp.float32
    ) + decay_from_start * jnp.einsum(
        "thd,hed->the", grad_heads, state_rounded, preferred_element_type=jnp.float32
    )
    value_grad_dot = jnp.einsum(
        "thd,shd->hts", value_heads, grad_heads, preferred_element_type=jnp.float32
    )
    weight_two = (decay_back * value_grad_dot).astype(jnp.bfloat16)
    key_result = jnp.einsum(
        "hts,shd->thd", weight_two, query_heads, preferred_element_type=jnp.float32
    ) + decay_to_end * jnp.einsum(
        "thd,hed->the", value_heads, grad_rounded, preferred_element_type=jnp.float32
    )
    key_query_dot = jnp.einsum(
        "thd,shd->hts", key_heads, query_heads, preferred_element_type=jnp.float32
    )
    weight_three = (decay_back * key_query_dot).astype(jnp.bfloat16)
    value_result = jnp.einsum(
        "hts,shd->thd", weight_three, grad_heads, preferred_element_type=jnp.float32
    ) + decay_to_end * jnp.einsum(
        "the,hed->thd", key_heads, grad_rounded, preferred_element_type=jnp.float32
    )
    flat_width = local_heads * head_size
    return (
        cross_query_grad,
        cache_key_grad,
        cache_value_grad,
        query_result.reshape(shard_rows, flat_width),
        key_result.reshape(shard_rows, flat_width),
        value_result.reshape(shard_rows, flat_width),
    )


def solution(mesh):
    in_specs = (
        P(),
        P("sec", "ctx", None),
        P("sec", "ctx", None),
        P("sec", "ctx", None),
        P("ctx", None),
        P("ctx", None),
        P("sec", None),
        P("sec", None),
        P("ctx", "sec"),
        P("ctx", "sec"),
        P("ctx", "sec"),
        P("sec", "ctx"),
    )
    out_specs = (
        P("sec", "ctx", None),
        P("ctx", None),
        P("ctx", None),
        P("ctx", "sec"),
        P("ctx", "sec"),
        P("ctx", "sec"),
    )
    return jax.shard_map(body, mesh=mesh, in_specs=in_specs, out_specs=out_specs, check_vma=False)
```

profile of v0, /device:TPU:1, one launch (start us, length us, event | category | flops | bytes accessed | tf_op | source)
XLA Modules:
  0.0 1433.2 jit_solution(2262105112509300691)
XLA Ops:
  8.7 1.3 fusion.52
  13.8 139.7 %all-gather.8.cloned.1.call-done = bf16[8192,128]{1,0:T(8,128)(2,1)} async-done(((bf16[128,128]{1,0:T(8,128)(2,1)}), bf16[8192,128]{1,0:T(8,128)(2,1)}) %all-gather.8.cloned.1.call-update) | async-done | bytes 2097168 | tf_op jit(solution)/shard_map/all_gather | solution.py:121
  153.5 1.8 while.56
  153.7 1.3 fusion.97
  155.3 135.1 %all-gather.10.cloned.1.call-done = bf16[8192,128]{1,0:T(8,128)(2,1)} async-done(((bf16[128,128]{1,0:T(8,128)(2,1)}), bf16[8192,128]{1,0:T(8,128)(2,1)}) %all-gather.10.cloned.1.call-update) | async-done | bytes 2097168 | tf_op jit(solution)/shard_map/all_gather | solution.py:122
  290.4 2.2 broadcast.48
  292.6 2.2 broadcast.48.clone
  294.8 5.7 while.57
  295.0 1.2 fusion.109
  296.2 1.2 fusion.110
  297.4 1.2 convolution_add_fusion.3
  300.5 86.7 %all-to-all-start = ((f32[64,128,128]{2,1,0:T(8,128)}), f32[64,128,128]{2,1,0:T(8,128)}, u32[]{:S(2)}, u32[]{:S(2)}) async-start(f32[64,128,128]{2,1,0:T(8,128)} %bitcast.114), calls=%async_computation | async-start | bytes 8388608 | tf_op jit(solution)/shard_map/all_to_all | solution.py:157
  388.2 94.8 %all-to-all-done = f32[64,128,128]{2,1,0:T(8,128)} async-done(((f32[64,128,128]{2,1,0:T(8,128)}), f32[64,128,128]{2,1,0:T(8,128)}, u32[]{:S(2)}, u32[]{:S(2)}) %all-to-all-start) | async-done | bytes 4194336 | tf_op jit(solution)/shard_map/all_to_all | solution.py:157
  482.9 3.0 reduce_sum.47
  487.0 17.9 %all-to-all-start.1 = ((f32[64,128,128]{2,1,0:T(8,128)}), f32[64,128,128]{2,1,0:T(8,128)}, u32[]{:S(2)}, u32[]{:S(2)}) async-start(f32[64,128,128]{2,1,0:T(8,128)} %bitcast.115), calls=%async_computation.1 | async-start | bytes 8388608 | tf_op jit(solution)/shard_map/all_to_all | solution.py:158
  505.2 102.5 %all-to-all-done.1 = f32[64,128,128]{2,1,0:T(8,128)} async-done(((f32[64,128,128]{2,1,0:T(8,128)}), f32[64,128,128]{2,1,0:T(8,128)}, u32[]{:S(2)}, u32[]{:S(2)}) %all-to-all-start.1) | async-done | bytes 4194336 | tf_op jit(solution)/shard_map/all_to_all | solution.py:158
  607.6 2.4 reduce_sum.48
  610.1 25.5 %psum.15 = bf16[128,128]{1,0:T(8,128)(2,1)S(1)} all-reduce(f32[128,128]{1,0:T(8,128)S(1)} %reduce_sum.48), channel_id=1, replica_groups=mesh['sec'=8,'ctx'=64] {'sec'}, use_global_device_ids=true, to_apply=%region_11.12 | all-reduce | flops 16384 | bytes 98304 | tf_op jit(solution)/shard_map/psum | solution.py:162
  635.5 8.3 all-reduce.3.cloned.1.call-done
  646.3 1.3 dynamic-slice
  648.4 199.3 %all-reduce = f32[320]{0:T(512)S(1)} all-reduce(f32[320]{0:T(512)S(1)} %dynamic-update-slice), channel_id=2, replica_groups=mesh['sec'=8,'ctx'=64] {'ctx'}, use_global_device_ids=true, to_apply=%add | all-reduce | flops 320 | bytes 2560
  849.5 153.4 %all-gather.12.cloned.1.call-done = f32[320,128,128]{2,1,0:T(8,128)} async-done(((f32[5,128,128]{2,1,0:T(8,128)}), f32[320,128,128]{2,1,0:T(8,128)}) %all-gather.12.cloned.1.call-update) | async-done | bytes 20971536 | tf_op jit(solution)/shard_map/all_gather | solution.py:13
  1004.4 348.0 %all-gather.14.cloned.1.call-done = f32[320,128,128]{2,1,0:T(8,128)} async-done(((f32[5,128,128]{2,1,0:T(8,128)}), f32[320,128,128]{2,1,0:T(8,128)}) %all-gather.14.cloned.1.call-update) | async-done | bytes 20971536 | tf_op jit(solution)/shard_map/all_gather | solution.py:13
  1352.5 71.6 %while.55 = (s32[]{:T(128)}, f32[5,128,128]{2,1,0:T(8,128)S(1)}, s32[]{:T(128)}, f32[64,5]{1,0:T(8,128)S(1)}, f32[64,5,128,128]{3,2,1,0:T(8,128)}, /*index=5*/s32[]{:T(128)}, s32[]{:T(128)}, s32[]{:T(128)}, s32[]{:T(128)}) while((s32[]{:T(128)}, f32[5,128,128]{2,1,0:T(8,128)S(1)}, s32[]{:T(128)}, f32[64,5]{1,0:T(8,128)S(1)}, ...), condition=%wide.region_16.17_spmd, body=%wide.region_15.16_spmd.sunk | while | flops 163846 | bytes 983255 | solution.py:22
  1354.8 1.1 bitcast_add_fusion.5
  1355.9 1.1 bitcast_add_fusion.5
  1359.4 1.1 bitcast_add_fusion.5
  1360.5 1.1 bitcast_add_fusion.5
  1361.6 1.1 bitcast_add_fusion.5
  1365.0 1.1 bitcast_add_fusion.5
  1366.2 1.1 bitcast_add_fusion.5
  1367.3 1.1 bitcast_add_fusion.5
  (198 shorter events, 78.8 us)
Async XLA Ops:
  7.2 637.5 %copy-start = (bf16[640,128]{1,0:T(8,128)(2,1)S(1)}, bf16[640,128]{1,0:T(8,128)(2,1)}, u32[]{:S(2)}) copy-start(bf16[640,128]{1,0:T(8,128)(2,1)} %param.26) | copy-start | bytes 491524
  7.2 146.3 %all-gather.8.cloned.1.call-start = ((), (), s32[]{:S(2)}) async-start(), calls=%async_computation.2 | async-start | bytes 2129920 | tf_op jit(solution)/shard_map/all_gather | solution.py:121
  7.9 282.4 %all-gather.10.cloned.1.call-start = ((), (), s32[]{:S(2)}) async-start(), calls=%async_computation.3 | async-start | bytes 2129920 | tf_op jit(solution)/shard_map/all_gather | solution.py:122
  300.5 86.8 %copy-start.1 = (bf16[128,640]{1,0:T(8,128)(2,1)S(1)}, bf16[128,640]{1,0:T(8,128)(2,1)}, u32[]{:S(2)}) copy-start(bf16[128,640]{1,0:T(8,128)(2,1)} %param.30) | copy-start | bytes 491524
  300.5 86.9 %copy-start.2 = (bf16[128,640]{1,0:T(8,128)(2,1)S(1)}, bf16[128,640]{1,0:T(8,128)(2,1)}, u32[]{:S(2)}) copy-start(bf16[128,640]{1,0:T(8,128)(2,1)} %param.29) | copy-start | bytes 491524
  300.5 87.1 %copy-start.7 = (f32[5,128]{1,0:T(8,128)S(1)}, f32[5,128]{1,0:T(8,128)}, u32[]{:S(2)}) copy-start(f32[5,128]{1,0:T(8,128)} %param.31) | copy-start | bytes 7684
  300.5 182.4 %all-to-all-start = ((f32[64,128,128]{2,1,0:T(8,128)}), f32[64,128,128]{2,1,0:T(8,128)}, u32[]{:S(2)}, u32[]{:S(2)}) async-start(f32[64,128,128]{2,1,0:T(8,128)} %bitcast.114), calls=%async_computation | async-start | bytes 8388608 | tf_op jit(solution)/shard_map/all_to_all | solution.py:157
  387.2 256.6 %all-reduce.3.cloned.1.call-start = ((), (), s32[]{:S(2)}) async-start(), calls=%async_computation.4 | async-start | bytes 131072 | tf_op jit(solution)/shard_map/psum | solution.py:162
  486.0 517.0 %all-gather.12.cloned.1.call-start = ((), (), s32[]{:S(2)}) async-start(), calls=%async_computation.5 | async-start | bytes 21299200 | tf_op jit(solution)/shard_map/all_gather | solution.py:13
  487.0 18.0 %copy-start.3 = (bf16[128,640]{1,0:T(8,128)(2,1)S(1)}, bf16[128,640]{1,0:T(8,128)(2,1)}, u32[]{:S(2)}) copy-start(bf16[128,640]{1,0:T(8,128)(2,1)} %param.28) | copy-start | bytes 491524
  487.0 120.6 %all-to-all-start.1 = ((f32[64,128,128]{2,1,0:T(8,128)}), f32[64,128,128]{2,1,0:T(8,128)}, u32[]{:S(2)}, u32[]{:S(2)}) async-start(f32[64,128,128]{2,1,0:T(8,128)} %bitcast.115), calls=%async_computation.1 | async-start | bytes 8388608 | tf_op jit(solution)/shard_map/all_to_all | solution.py:158
  504.9 140.0 %copy-start.4 = (bf16[640,128]{1,0:T(8,128)(2,1)S(1)}, bf16[640,128]{1,0:T(8,128)(2,1)}, u32[]{:S(2)}) copy-start(bf16[640,128]{1,0:T(8,128)(2,1)} %param.27) | copy-start | bytes 491524
  504.9 847.5 %all-gather.14.cloned.1.call-start = ((), (), s32[]{:S(2)}) async-start(), calls=%async_computation.6 | async-start | bytes 21299200 | tf_op jit(solution)/shard_map/all_gather | solution.py:13
  635.5 367.5 %copy-start.6 = (bf16[128,128]{1,0:T(8,128)(2,1)}, bf16[128,128]{1,0:T(8,128)(2,1)S(1)}, u32[]{:S(2)}) copy-start(bf16[128,128]{1,0:T(8,128)(2,1)S(1)} %psum.15) | copy-start | bytes 98308
  644.7 358.3 %copy-start.5 = (bf16[128,128]{1,0:T(8,128)(2,1)}, bf16[128,128]{1,0:T(8,128)(2,1)S(1)}, u32[]{:S(2)}) copy-start(bf16[128,128]{1,0:T(8,128)(2,1)S(1)} %multiply_convert_fusion.7) | copy-start | bytes 98308
Sparse Core Ops, SparseCore 0:
  12.5 140.9 all-gather.7
  158.0 132.3 all-gather.9
  486.1 157.6 all-reduce.2
  649.6 353.3 all-gather.11
  1008.7 343.7 all-gather.13
where the time goes:
time: 1440 us; the launch traced here: 1430 us
  waiting for transfers between devices  983 us (68%)
  blocking collectives  225 us (16%)
  starting transfers between devices  105 us (7%)
  other arithmetic  77.4 us (5%)
  between operations  15.4 us (1%)
  local copies, waits for them, and re-layouts  14.6 us (1%)
    all_gather x2, waiting for transfers between devices, entering(): gathered = jax.tree.map(lambda a: lax.all_gather(a, axis), part)  501 us
    unnamed x1, blocking collectives  199 us
    all_gather x1, waiting for transfers between devices, body(): lax.all_gather(cache_keys, 'ctx', axis=0, tiled=True)  140 us
    all_gather x1, waiting for transfers between devices, body(): lax.all_gather(cache_values, 'ctx', axis=0, tiled=True)  135 us
    all_to_all x1, waiting for transfers between devices, body(): lax.all_to_all(value_terms, 'ctx', split_axis=0, concat_axis=0, tiled=True)  102 us
    all_to_all x1, waiting for transfers between devices, body(): lax.all_to_all(key_terms, 'ctx', split_axis=0, concat_axis=0, tiled=True)  94.8 us
    all_to_all x1, starting transfers between devices, body(): lax.all_to_all(key_terms, 'ctx', split_axis=0, concat_axis=0, tiled=True)  86.7 us
    add x63, other arithmetic, compose(): second_pair[0][:, None, None] * first_pair[1] + second_pair[1]  68.9 us
  transfers between devices with their start and end apart: 7, of which 7 were waited for; matrix products, arithmetic and copies ran while one was open for 1% of the time, Pallas kernels for 0%

commit v1 on v0

v1 whole, which is shorter than its diff:
```python
import functools
import math

import jax
import jax.numpy as jnp
from jax import lax
from jax.experimental import pallas as pl
from jax.experimental.pallas import tpu as pltpu
from jax.sharding import PartitionSpec as P

BF = jnp.bfloat16
F32 = jnp.float32
LOW = -1e30
LOG2E = math.log2(math.e)
CHIPS = 4
CORES = 2
WIRE = 24
SCOPED = 32 * 1024 * 1024


def dot_nt(a, b):
    return lax.dot_general(a, b, (((1,), (1,)), ((), ())), preferred_element_type=F32)


def dot_nn(a, b):
    return lax.dot_general(a, b, (((1,), (0,)), ((), ())), preferred_element_type=F32)


def dot_tn(a, b):
    return lax.dot_general(a, b, (((0,), (0,)), ((), ())), preferred_element_type=F32)


def call(kernel, outs, in_smem, ins, scratch=(), flops=0):
    vmem = pl.BlockSpec(memory_space=pltpu.VMEM)
    smem = pl.BlockSpec(memory_space=pltpu.SMEM)
    return pl.pallas_call(
        kernel,
        out_shape=outs,
        in_specs=[smem] * len(in_smem) + [vmem] * len(ins),
        out_specs=jax.tree.map(lambda _: vmem, outs),
        scratch_shapes=list(scratch),
        compiler_params=pltpu.CompilerParams(vmem_limit_bytes=SCOPED),
        cost_estimate=pl.CostEstimate(flops=flops, bytes_accessed=4 << 20, transcendentals=0),
    )(*in_smem, *ins)


def key_positions(place, chunk, blocks, rows, width, block_rows):
    at = lax.broadcasted_iota(jnp.int32, (blocks * rows, width), 0)
    return (chunk * blocks + at // rows) * block_rows + place * rows + at % rows


def stats_kernel(blocks, block_rows, factor, where_ref, q_ref, kv_ref, pos_ref, lse_ref):
    shard, chip, place = where_ref[0], where_ref[1], where_ref[2]
    rows = kv_ref.shape[1] // 2
    width = q_ref.shape[1]
    full = shard // blocks
    pos = pos_ref[...]
    scale = factor * LOG2E
    for k in range(CHIPS):
        q = q_ref[k]

        def chunk(j, carry, masked=False):
            top, total = carry
            keys = kv_ref[pl.ds(j * blocks, blocks), 0:rows, :].reshape(blocks * rows, -1)
            s = dot_nt(keys, q)
            if masked:
                seen = key_positions(place, j, blocks, rows, width, block_rows) <= pos
                s = jnp.where(seen, s, LOW)
            new = jnp.maximum(top, jnp.max(s, axis=0, keepdims=True))
            p = jnp.exp2((s - new) * scale)
            if masked:
                p = jnp.where(seen, p, 0.0)
            total = total * jnp.exp2((top - new) * scale) + jnp.sum(p, axis=0, keepdims=True)
            return new, total

        start = (jnp.full((1, width), LOW, F32), jnp.zeros((1, width), F32))
        top, total = chunk(full, lax.fori_loop(0, full, chunk, start), masked=True)
        lse = jnp.where(total > 0.0, top * factor + jnp.log(total), LOW)
        lse_ref[lax.rem(chip + k, CHIPS)] = lse


def grads_kernel(
    blocks, block_rows, factor, where_ref, q_ref, g_ref, kv_ref, pos_ref, log_ref, delta_ref,
    dkv_ref, dq_ref, dk_total, dv_total,
):
    shard, chip, place = where_ref[0], where_ref[1], where_ref[2]
    rows = kv_ref.shape[1] // 2
    width = q_ref.shape[1]
    size = blocks * rows
    full = shard // blocks
    pos = pos_ref[...]
    scale = factor * LOG2E
    dk_total[...] = jnp.zeros_like(dk_total)
    dv_total[...] = jnp.zeros_like(dv_total)
    for k in range(CHIPS):
        layer = lax.rem(chip + k, CHIPS)
        q = q_ref[k]
        g = g_ref[k]
        log_total = log_ref[layer] * LOG2E
        delta = delta_ref[layer]

        def chunk(j, dq, masked=False):
            keys = kv_ref[pl.ds(j * blocks, blocks), 0:rows, :].reshape(size, -1)
            values = kv_ref[pl.ds(j * blocks, blocks), rows : 2 * rows, :].reshape(size, -1)
            p = jnp.exp2(dot_nt(keys, q) * scale - log_total)
            if masked:
                seen = key_positions(place, j, blocks, rows, width, block_rows) <= pos
                p = jnp.where(seen, p, 0.0)
            ds = (p * (dot_nt(values, g) - delta)).astype(BF)
            at = pl.ds(pl.multiple_of(j * size, size), size)
            dk_total[at, :] += dot_nn(ds, q)
            dv_total[at, :] += dot_nn(p.astype(BF), g)
            return dq + dot_tn(keys, ds)

        dq = lax.fori_loop(0, full, chunk, jnp.zeros((keys_width(kv_ref), width), F32))
        dq_ref[layer] = chunk(full, dq, masked=True).T
    for j in range(kv_ref.shape[0] // blocks):
        at = slice(j * size, (j + 1) * size)
        to = slice(j * blocks, (j + 1) * blocks)
        dkv_ref[to, 0:rows, :] = dk_total[at, :].astype(BF).reshape(blocks, rows, -1)
        dkv_ref[to, rows : 2 * rows, :] = dv_total[at, :].astype(BF).reshape(blocks, rows, -1)


def keys_width(ref):
    return ref.shape[-1]


def states_kernel(
    heads, ck_ref, cv_ref, kp_ref, vp_ref, rq_ref, rk_ref, rv_ref, from_ref, to_ref, extra_ref,
    gr_ref, send_ref, wire,
):
    half = send_ref.shape[0]
    wire[:, 4 * heads :, :] = jnp.broadcast_to(
        extra_ref[...][None], (half,) + extra_ref.shape
    )
    for i in range(heads):
        at = slice(i * 128, (i + 1) * 128)
        gr = (dot_nt(ck_ref[...], kp_ref[at, :]) + dot_nt(cv_ref[...], vp_ref[at, :])).astype(BF)
        gr_ref[:, at] = gr
        query_w = (rq_ref[:, at].astype(F32) * from_ref[:, i : i + 1]).astype(BF)
        key_w = (rk_ref[:, at].astype(F32) * to_ref[:, i : i + 1]).astype(BF)
        grad = dot_tn(query_w, gr)
        state = dot_tn(key_w, rv_ref[:, at])
        for k in range(2):
            wire[:, 2 * i + k, :] = grad[k * half : (k + 1) * half]
            wire[:, 2 * heads + 2 * i + k, :] = state[k * half : (k + 1) * half]
    send_ref[...] = wire[...].astype(BF)


def scan_kernel(heads, part_ref, decay_ref, out_ref, ahead, behind):
    count = part_ref.shape[0]
    zero = jnp.zeros(part_ref.shape[1:], F32)

    def step(b, carry):
        fore, back = carry
        ahead[b] = fore
        fore = decay_ref[b] * fore + part_ref[b].astype(F32)
        r = count - 1 - b
        behind[r] = back
        back = decay_ref[r] * back + part_ref[r].astype(F32)
        return fore, back

    lax.fori_loop(0, count, step, (zero, zero), unroll=4)
    row = lax.broadcasted_iota(jnp.int32, part_ref.shape, 1)
    out_ref[...] = jnp.where(row < 2 * heads, behind[...], ahead[...]).astype(BF)


def final_kernel(
    heads, rq_ref, rk_ref, rv_ref, gr_ref, cum_ref, cum_t_ref, from_ref, to_ref, wire_ref,
    q_ref, k_ref, v_ref, wire,
):
    wire[...] = wire_ref[...].astype(F32)

    def matrix(r):
        return jnp.concatenate([wire[:, r, :], wire[:, r + 1, :]], axis=0).astype(BF)

    size = rq_ref.shape[0]
    t = lax.broadcasted_iota(jnp.int32, (size, size), 0)
    u = lax.broadcasted_iota(jnp.int32, (size, size), 1)
    causal = t >= u
    for i in range(heads):
        at = slice(i * 128, (i + 1) * 128)
        qr, kr, vr, gr = rq_ref[:, at], rk_ref[:, at], rv_ref[:, at], gr_ref[:, at]
        grad_b, state_b = matrix(2 * i), matrix(2 * heads + 2 * i)
        gap = cum_t_ref[:, i : i + 1] - cum_ref[i : i + 1, :]
        decay = jnp.where(causal, jnp.exp(jnp.where(causal, gap, 0.0)), 0.0)
        from_start, to_end = from_ref[:, i : i + 1], to_ref[:, i : i + 1]
        one = (decay * dot_nt(gr, vr)).astype(BF)
        three = (decay * dot_nt(qr, kr)).astype(BF)
        q_ref[:, at] = dot_nn(one, kr) + from_start * dot_nt(gr, state_b)
        k_ref[:, at] = dot_tn(one, qr) + to_end * dot_nt(vr, grad_b)
        v_ref[:, at] = dot_tn(three, gr) + to_end * dot_nn(kr, grad_b)


def body(
    offsets,
    queries,
    output_grad,
    attention_out,
    cache_keys,
    cache_values,
    key_projection,
    value_projection,
    retention_query,
    retention_key,
    retention_value,
    retention_decay,
):
    shards = lax.axis_size("ctx")
    shard = lax.axis_index("ctx")
    secs = lax.axis_size("sec")
    place = lax.axis_index("sec")
    chip, core = place // CORES, lax.rem(place, CORES)
    block_rows, head = cache_keys.shape
    layers, query_rows, query_width = queries.shape
    heads = query_width // head
    flat = layers * query_rows * heads
    rows = block_rows // secs
    factor = 1.0 / math.sqrt(head)
    blocks = math.gcd(shards, 16)
    chips = secs // CORES

    q_own = queries.reshape(flat, head)
    g_own = output_grad.reshape(flat, head)
    own = jnp.concatenate([q_own, g_own], axis=0)
    parts = [own] + [
        lax.ppermute(own, "sec", [(i, (i - CORES * k) % secs) for i in range(secs)])
        for k in range(1, chips)
    ]
    kv_own = jnp.concatenate(
        [lax.dynamic_slice_in_dim(a, place * rows, rows, 0) for a in (cache_keys, cache_values)]
    )
    kv = lax.all_to_all(
        jnp.broadcast_to(kv_own[None], (shards,) + kv_own.shape), "ctx", 0, 0, tiled=True
    )
    mine = jnp.stack(parts)
    other = lax.ppermute(mine, "sec", [(i, i ^ 1) for i in range(secs)])
    first = jnp.where(core == 0, mine, other)
    second = jnp.where(core == 0, other, mine)
    q_all = jnp.concatenate([first[:, :flat], second[:, :flat]], axis=1)
    g_all = jnp.concatenate([first[:, flat:], second[:, flat:]], axis=1)

    own_offset = jnp.sum(
        jnp.where(jnp.arange(shards, dtype=jnp.int32) == shard, offsets, 0)
    )
    row_of = (jnp.arange(CORES * flat, dtype=jnp.int32) % (query_rows * heads)) // heads
    pos = (shard * block_rows + own_offset + row_of)[None]
    where = jnp.stack([shard, chip, place]).astype(jnp.int32)
    delta = jnp.sum(
        g_own.astype(F32) * attention_out.reshape(flat, head).astype(F32), axis=1
    )

    lse = call(
        functools.partial(stats_kernel, blocks, block_rows, factor),
        jax.ShapeDtypeStruct((chips, 1, CORES * flat), F32),
        (where,),
        (q_all, kv, pos),
        flops=1 << 30,
    )
    both = jnp.concatenate([lse.reshape(-1), delta])
    lines = -(-both.shape[0] // 1024) * 8
    both = jnp.pad(both, (0, lines * 128 - both.shape[0])).reshape(lines, 128)
    both = lax.all_to_all(
        jnp.broadcast_to(both[None], (secs,) + both.shape), "sec", 0, 0, tiled=True
    ).reshape(secs, -1)
    logs = both[:, : secs * flat]
    top = jnp.max(logs, axis=0)
    log_total = top + jnp.log(jnp.sum(jnp.exp(logs - top), axis=0))
    log_total = log_total.reshape(chips, 1, CORES * flat)
    deltas = both[:, secs * flat : (secs + 1) * flat].reshape(chips, 1, CORES * flat)

    dkv, dq = call(
        functools.partial(grads_kernel, blocks, block_rows, factor),
        (
            jax.ShapeDtypeStruct(kv.shape, BF),
            jax.ShapeDtypeStruct((chips, CORES * flat, head), F32),
        ),
        (where,),
        (q_all, g_all, kv, pos, log_total, deltas),
        scratch=[pltpu.VMEM((shards * rows, head), F32)] * 2,
        flops=4 << 30,
    )
    dq = lax.psum_scatter(
        dq.reshape(secs * flat, head), "sec", scatter_dimension=0, tiled=True
    )
    cross_query_grad = (dq * factor).astype(BF).reshape(layers, query_rows, query_width)

    terms = lax.all_to_all(dkv, "ctx", 0, 0, tiled=True)
    total = jnp.sum(terms.astype(F32), axis=0)
    scale = jnp.where(jnp.arange(2 * rows) < rows, factor, 1.0)[:, None]
    total = (total * scale).astype(BF)
    whole = lax.all_to_all(
        jnp.broadcast_to(total[None], (secs,) + total.shape), "sec", 0, 0, tiled=True
    )
    cache_key_grad = whole[:, :rows].reshape(block_rows, head)
    cache_value_grad = whole[:, rows:].reshape(block_rows, head)

    local = retention_decay.shape[0]
    cum = jnp.cumsum(retention_decay, axis=1)
    cum_t = cum.T
    last = cum[:, -1]
    from_start = jnp.exp(cum_t)
    to_end = jnp.exp(last[None] - cum_t)
    high = last.astype(BF)
    rest = last - high.astype(F32)
    middle = rest.astype(BF)
    low = (rest - middle.astype(F32)).astype(BF)
    extra = jnp.concatenate([high, middle, low]).astype(F32)
    extra = jnp.pad(
        extra[None], ((0, WIRE - 4 * local - 1), (0, head - extra.shape[0]))
    )
    out_grad, send = call(
        functools.partial(states_kernel, local),
        (
            jax.ShapeDtypeStruct(retention_query.shape, BF),
            jax.ShapeDtypeStruct((shards, WIRE, head), BF),
        ),
        (),
        (
            cache_key_grad, cache_value_grad, key_projection, value_projection,
            retention_query, retention_key, retention_value, from_start, to_end, extra,
        ),
        scratch=[pltpu.VMEM((shards, WIRE, head), F32)],
        flops=1 << 27,
    )
    part = lax.all_to_all(send, "ctx", 0, 0, tiled=True)
    lasts = part[:, 4 * local, : 3 * local].astype(F32).reshape(shards, 3, local)
    decays = jnp.exp(lasts[:, 0] + lasts[:, 1] + lasts[:, 2])
    decays = jnp.concatenate([decays, decays], axis=1)
    decays = jnp.broadcast_to(decays[:, :, None], (shards, 2 * local, 2))
    decays = decays.reshape(shards, 4 * local, 1)
    decays = jnp.pad(decays, ((0, 0), (0, WIRE - 4 * local), (0, 0)))
    decays = jnp.broadcast_to(decays, (shards, WIRE, head))
    enter = call(
        functools.partial(scan_kernel, local),
        jax.ShapeDtypeStruct(part.shape, BF),
        (),
        (part, decays),
        scratch=[pltpu.VMEM(part.shape, F32)] * 2,
    )
    enter = lax.all_to_all(enter, "ctx", 0, 0, tiled=True)
    grads = call(
        functools.partial(final_kernel, local),
        (jax.ShapeDtypeStruct(retention_query.shape, F32),) * 3,
        (),
        (
            retention_query, retention_key, retention_value, out_grad, cum, cum_t,
            from_start, to_end, enter,
        ),
        scratch=[pltpu.VMEM(enter.shape, F32)],
        flops=1 << 28,
    )
    return (cross_query_grad, cache_key_grad, cache_value_grad) + tuple(grads)


def solution(mesh):
    in_specs = (
        P(),
        P("sec", "ctx", None),
        P("sec", "ctx", None),
        P("sec", "ctx", None),
        P("ctx", None),
        P("ctx", None),
        P("sec", None),
        P("sec", None),
        P("ctx", "sec"),
        P("ctx", "sec"),
        P("ctx", "sec"),
        P("sec", "ctx"),
    )
    out_specs = (
        P("sec", "ctx", None),
        P("ctx", None),
        P("ctx", None),
        P("ctx", "sec"),
        P("ctx", "sec"),
        P("ctx", "sec"),
    )
    return jax.shard_map(body, mesh=mesh, in_specs=in_specs, out_specs=out_specs, check_vma=False)
```

time: 1440 us -> 206 us (0.14)
  the two profiles are of different devices: /device:TPU:1 before, /device:TPU:8 now
where the time goes in v1:
time: 206 us; the launch traced here: 205 us
  waiting for transfers between devices  82.6 us (40%)
  starting transfers between devices  61.1 us (30%)
  blocking collectives  24.4 us (12%)
  between operations  15.1 us (7%)
  Pallas kernels  11.9 us (6%)
  local copies, waits for them, and re-layouts  6.83 us (3%)
  other arithmetic  2.87 us (1%)
    all_to_all x1, blocking collectives, body(): part = lax.all_to_all(send, 'ctx', 0, 0, tiled=True)  24.4 us
    all_to_all x1, waiting for transfers between devices, body(): terms = lax.all_to_all(dkv, 'ctx', 0, 0, tiled=True)  21.3 us
    all_to_all x1, waiting for transfers between devices, body(): lax.all_to_all(jnp.broadcast_to(kv_own[None], (shards,) + kv_own.shape),...  20.9 us
    all_to_all x1, starting transfers between devices, body(): terms = lax.all_to_all(dkv, 'ctx', 0, 0, tiled=True)  17.9 us
    all_to_all x1, waiting for transfers between devices, body(): enter = lax.all_to_all(enter, 'ctx', 0, 0, tiled=True)  17.1 us
    all_to_all x1, starting transfers between devices, body(): lax.all_to_all(jnp.broadcast_to(kv_own[None], (shards,) + kv_own.shape),...  16.3 us
    ppermute x3, starting transfers between devices, body(): lax.ppermute(own, 'sec', [(i, (i - CORES * k) % secs) for i in range(secs)])  12.3 us
    pallas_call x5, Pallas kernels, call(): pl.pallas_call(kernel, out_shape=outs, in_specs=[smem] * len(in_smem) + [...  11.9 us
  transfers between devices with their start and end apart: 10, of which 7 were waited for; matrix products, arithmetic and copies ran while one was open for 3% of the time, Pallas kernels for 1%

profile of v1, /device:TPU:8, one launch (start us, length us, event | category | flops | bytes accessed | tf_op | source)
XLA Modules:
  0.0 204.8 jit_solution(17359933620242996063)
XLA Ops:
  7.2 1.0 reshape.193
  8.2 1.0 reshape.192
  9.2 7.9 %collective-permute-start = (bf16[640,128]{1,0:T(8,128)(2,1)S(1)}, bf16[640,128]{1,0:T(8,128)(2,1)S(1)}, u32[]{:S(2)}, u32[]{:S(2)}) collective-permute-start(bf16[640,128]{1,0:T(8,128)(2,1)S(1)} %constant_dynamic-update-slice_fusion), channel_id=1, source_target_pairs={{0,384},{64,448},{128,0},{192,64},{256,128},{320,192},{384,256},{4... | collective-permute-start | bytes 491528 | tf_op jit(solution)/shard_map/ppermute | solution.py:227
  17.1 1.9 collective-permute-start.1
  19.1 2.5 %collective-permute-start.2 = (bf16[640,128]{1,0:T(8,128)(2,1)S(1)}, bf16[640,128]{1,0:T(8,128)(2,1)S(1)}, u32[]{:S(2)}, u32[]{:S(2)}) collective-permute-start(bf16[640,128]{1,0:T(8,128)(2,1)S(1)} %constant_dynamic-update-slice_fusion), channel_id=1, source_target_pairs={{0,128},{64,192},{128,256},{192,320},{256,384},{320,448},{384,0},{... | collective-permute-start | bytes 491528 | tf_op jit(solution)/shard_map/ppermute | solution.py:227
  21.8 10.1 %collective-permute-done.1 = bf16[640,128]{1,0:T(8,128)(2,1)S(1)} collective-permute-done((bf16[640,128]{1,0:T(8,128)(2,1)S(1)}, bf16[640,128]{1,0:T(8,128)(2,1)S(1)}, u32[]{:S(2)}, u32[]{:S(2)}) %collective-permute-start.1) | collective-permute-done | bytes 163872 | tf_op jit(solution)/shard_map/ppermute | solution.py:227
  31.9 1.9 collective-permute-start.3
  33.9 0.7 constant_dynamic-slice_fusion
  34.6 0.9 broadcast_in_dim.26
  35.4 16.3 %all-to-all-start = ((bf16[64,32,128]{2,1,0:T(8,128)(2,1)}), bf16[64,32,128]{2,1,0:T(8,128)(2,1)S(1)}, u32[]{:S(2)}, u32[]{:S(2)}) async-start(bf16[64,32,128]{2,1,0:T(8,128)(2,1)} %broadcast_in_dim.26), calls=%async_computation | async-start | bytes 1048576 | tf_op jit(solution)/shard_map/all_to_all | solution.py:233
  51.7 0.6 fusion.14
  53.7 20.9 %all-to-all-done.kv_ref = bf16[64,32,128]{2,1,0:T(8,128)(2,1)S(1)} async-done(((bf16[64,32,128]{2,1,0:T(8,128)(2,1)}), bf16[64,32,128]{2,1,0:T(8,128)(2,1)S(1)}, u32[]{:S(2)}, u32[]{:S(2)}) %all-to-all-start) | async-done | bytes 524320 | tf_op jit(solution)/shard_map/all_to_all | solution.py:233
  74.6 2.3 %shard_map.163 = f32[4,1,640]{2,1,0:T(1,128)S(1)} custom-call(s32[3]{0:T(128)S(1)} %pad_add_fusion.where_ref, bf16[4,640,128]{2,1,0:T(8,128)(2,1)S(1)} %pad_maximum_fusion.1.q_ref, bf16[64,32,128]{2,1,0:T(8,128)(2,1)S(1)} %all-to-all-done.kv_ref, s32[1,640]{1,0:T(1,128)S(1)} %fusion.3.pos_ref), custom_call_target="tpu_custom_call" | custom-call | flops 1073741824 | bytes 4194304 | tf_op jit(solution)/shard_map/pallas_call | solution.py:36
  77.1 0.6 broadcast_in_dim.51
  77.7 4.0 %all-to-all-start.1 = ((f32[8,24,128]{2,1,0:T(8,128)}), f32[8,24,128]{2,1,0:T(8,128)S(1)}, u32[]{:S(2)}, u32[]{:S(2)}) async-start(f32[8,24,128]{2,1,0:T(8,128)} %broadcast_in_dim.51), calls=%async_computation.1 | async-start | bytes 196608 | tf_op jit(solution)/shard_map/all_to_all | solution.py:263
  81.8 6.3 %all-to-all-done.1 = f32[8,24,128]{2,1,0:T(8,128)S(1)} async-done(((f32[8,24,128]{2,1,0:T(8,128)}), f32[8,24,128]{2,1,0:T(8,128)S(1)}, u32[]{:S(2)}, u32[]{:S(2)}) %all-to-all-start.1) | async-done | bytes 98336 | tf_op jit(solution)/shard_map/all_to_all | solution.py:263
  88.3 5.0 %shard_map.164 = (bf16[64,32,128]{2,1,0:T(8,128)(2,1)}, f32[4,640,128]{2,1,0:T(8,128)}) custom-call(s32[3]{0:T(128)S(1)} %pad_add_fusion.where_ref, bf16[4,640,128]{2,1,0:T(8,128)(2,1)S(1)} %pad_maximum_fusion.1.q_ref, bf16[4,640,128]{2,1,0:T(8,128)(2,1)S(1)} %pad_maximum_fusion.2.g_ref, bf16[64,32,128]{2,1,0:T(8,128)(2,1)S(1)} %all-to-all-done.kv_ref, ...), custom_call_target="tpu_custom_call" | custom-call | flops 4294967296 | bytes 4194304 | tf_op jit(solution)/shard_map/pallas_call | solution.py:36
  93.3 17.9 %all-to-all-start.2 = ((bf16[64,32,128]{2,1,0:T(8,128)(2,1)}), bf16[64,32,128]{2,1,0:T(8,128)(2,1)S(1)}, u32[]{:S(2)}, u32[]{:S(2)}) async-start(bf16[64,32,128]{2,1,0:T(8,128)(2,1)} %get-tuple-element.14), calls=%async_computation.3 | async-start | bytes 1048576 | tf_op jit(solution)/shard_map/all_to_all | solution.py:288
  111.4 0.3 reduce_window_sum.11.cum_ref
  112.0 21.3 %all-to-all-done.2 = bf16[64,32,128]{2,1,0:T(8,128)(2,1)S(1)} async-done(((bf16[64,32,128]{2,1,0:T(8,128)(2,1)}), bf16[64,32,128]{2,1,0:T(8,128)(2,1)S(1)}, u32[]{:S(2)}, u32[]{:S(2)}) %all-to-all-start.2) | async-done | bytes 524320 | tf_op jit(solution)/shard_map/all_to_all | solution.py:288
  133.5 0.6 broadcast_in_dim.54
  134.1 3.4 %all-to-all-start.3 = ((bf16[8,32,128]{2,1,0:T(8,128)(2,1)}), bf16[8,32,128]{2,1,0:T(8,128)(2,1)S(1)}, u32[]{:S(2)}, u32[]{:S(2)}) async-start(bf16[8,32,128]{2,1,0:T(8,128)(2,1)} %broadcast_in_dim.54), calls=%async_computation.4 | async-start | bytes 131072 | tf_op jit(solution)/shard_map/all_to_all | solution.py:292
  137.6 6.7 %all-to-all-done.3 = bf16[8,32,128]{2,1,0:T(8,128)(2,1)S(1)} async-done(((bf16[8,32,128]{2,1,0:T(8,128)(2,1)}), bf16[8,32,128]{2,1,0:T(8,128)(2,1)S(1)}, u32[]{:S(2)}, u32[]{:S(2)}) %all-to-all-start.3) | async-done | bytes 65568 | tf_op jit(solution)/shard_map/all_to_all | solution.py:292
  144.3 1.2 shard_map.165
  145.5 24.4 %all_to_all.30.part_ref = bf16[64,24,128]{2,1,0:T(8,128)(2,1)S(1)} all-to-all(bf16[64,24,128]{2,1,0:T(8,128)(2,1)S(1)} %get-tuple-element.16), channel_id=1, replica_groups=mesh['sec'=8,'ctx'=64] {'ctx'}, dimensions={0} | all-to-all | bytes 786432 | tf_op jit(solution)/shard_map/all_to_all | solution.py:326
  170.2 0.3 broadcast_in_dim.57.decay_ref
  170.5 1.1 shard_map.166
  171.5 5.3 %all-to-all-start.5 = ((bf16[64,24,128]{2,1,0:T(8,128)(2,1)}), bf16[64,24,128]{2,1,0:T(8,128)(2,1)S(1)}, u32[]{:S(2)}, u32[]{:S(2)}) async-start(bf16[64,24,128]{2,1,0:T(8,128)(2,1)} %shard_map.166), calls=%async_computation.6 | async-start | bytes 786432 | tf_op jit(solution)/shard_map/all_to_all | solution.py:341
  176.9 0.9 multiply_convert_fusion
  177.8 0.8 reshape.198
  178.5 17.1 %all-to-all-done.5.wire_ref = bf16[64,24,128]{2,1,0:T(8,128)(2,1)S(1)} async-done(((bf16[64,24,128]{2,1,0:T(8,128)(2,1)}), bf16[64,24,128]{2,1,0:T(8,128)(2,1)S(1)}, u32[]{:S(2)}, u32[]{:S(2)}) %all-to-all-start.5) | async-done | bytes 393248 | tf_op jit(solution)/shard_map/all_to_all | solution.py:341
  195.6 2.3 %shard_map.167 = (f32[128,640]{1,0:T(8,128)}, f32[128,640]{1,0:T(8,128)}, f32[128,640]{1,0:T(8,128)}) custom-call(bf16[128,640]{1,0:T(8,128)(2,1)S(1)} %copy-done, bf16[128,640]{1,0:T(8,128)(2,1)S(1)} %copy-done.1, bf16[128,640]{1,0:T(8,128)(2,1)S(1)} %copy-done.2, bf16[128,640]{1,0:T(8,128)(2,1)S(1)} %get-tuple-element.15.gr_ref, ...), custom_call_target="tpu_custom_call" | custom-call | flops 268435456 | bytes 4194304 | tf_op jit(solution)/shard_map/pallas_call | solution.py:36
  (66 shorter events, 2.3 us)
Async XLA Ops:
  9.2 12.5 %collective-permute-start = (bf16[640,128]{1,0:T(8,128)(2,1)S(1)}, bf16[640,128]{1,0:T(8,128)(2,1)S(1)}, u32[]{:S(2)}, u32[]{:S(2)}) collective-permute-start(bf16[640,128]{1,0:T(8,128)(2,1)S(1)} %constant_dynamic-update-slice_fusion), channel_id=1, source_target_pairs={{0,384},{64,448},{128,0},{192,64},{256,128},{320,192},{384,256},{4... | collective-permute-start | bytes 491528 | tf_op jit(solution)/shard_map/ppermute | solution.py:227
  17.1 14.7 %collective-permute-start.1 = (bf16[640,128]{1,0:T(8,128)(2,1)S(1)}, bf16[640,128]{1,0:T(8,128)(2,1)S(1)}, u32[]{:S(2)}, u32[]{:S(2)}) collective-permute-start(bf16[640,128]{1,0:T(8,128)(2,1)S(1)} %constant_dynamic-update-slice_fusion), channel_id=1, source_target_pairs={{0,256},{64,320},{128,384},{192,448},{256,0},{320,64},{384,128},{4... | collective-permute-start | bytes 491528 | tf_op jit(solution)/shard_map/ppermute | solution.py:227
  19.1 12.8 %collective-permute-start.2 = (bf16[640,128]{1,0:T(8,128)(2,1)S(1)}, bf16[640,128]{1,0:T(8,128)(2,1)S(1)}, u32[]{:S(2)}, u32[]{:S(2)}) collective-permute-start(bf16[640,128]{1,0:T(8,128)(2,1)S(1)} %constant_dynamic-update-slice_fusion), channel_id=1, source_target_pairs={{0,128},{64,192},{128,256},{192,320},{256,384},{320,448},{384,0},{... | collective-permute-start | bytes 491528 | tf_op jit(solution)/shard_map/ppermute | solution.py:227
  31.8 19.9 %copy-start.9 = (s32[64]{0:T(128)S(1)}, s32[64]{0:T(128)}, u32[]{:S(2)}) copy-start(s32[64]{0:T(128)} %param.12) | copy-start | bytes 772
  31.8 20.6 %copy-start.7 = (bf16[1,16,2560]{2,1,0:T(8,128)(2,1)S(1)}, bf16[1,16,2560]{2,1,0:T(8,128)(2,1)}, u32[]{:S(2)}) copy-start(bf16[1,16,2560]{2,1,0:T(8,128)(2,1)} %param.15) | copy-start | bytes 245764
  31.9 21.5 %collective-permute-start.3 = (bf16[4,640,128]{2,1,0:T(8,128)(2,1)S(1)}, bf16[4,640,128]{2,1,0:T(8,128)(2,1)S(1)}, u32[]{:S(2)}, u32[]{:S(2)}) collective-permute-start(bf16[4,640,128]{2,1,0:T(8,128)(2,1)S(1)} %pad_maximum_fusion), channel_id=1, source_target_pairs={{0,64},{64,0},{128,192},{192,128},{256,320},{320,256},{384,448},{4... | collective-permute-start | bytes 1966088 | tf_op jit(solution)/shard_map/ppermute | solution.py:237
  35.4 39.2 %all-to-all-start = ((bf16[64,32,128]{2,1,0:T(8,128)(2,1)}), bf16[64,32,128]{2,1,0:T(8,128)(2,1)S(1)}, u32[]{:S(2)}, u32[]{:S(2)}) async-start(bf16[64,32,128]{2,1,0:T(8,128)(2,1)} %broadcast_in_dim.26), calls=%async_computation | async-start | bytes 1048576 | tf_op jit(solution)/shard_map/all_to_all | solution.py:233
  77.7 10.4 %all-to-all-start.1 = ((f32[8,24,128]{2,1,0:T(8,128)}), f32[8,24,128]{2,1,0:T(8,128)S(1)}, u32[]{:S(2)}, u32[]{:S(2)}) async-start(f32[8,24,128]{2,1,0:T(8,128)} %broadcast_in_dim.51), calls=%async_computation.1 | async-start | bytes 196608 | tf_op jit(solution)/shard_map/all_to_all | solution.py:263
  88.3 23.1 %copy-start.8 = (f32[5,128]{1,0:T(8,128)S(1)}, f32[5,128]{1,0:T(8,128)}, u32[]{:S(2)}) copy-start(f32[5,128]{1,0:T(8,128)} %param.23) | copy-start | bytes 7684
  93.3 40.0 %all-to-all-start.2 = ((bf16[64,32,128]{2,1,0:T(8,128)(2,1)}), bf16[64,32,128]{2,1,0:T(8,128)(2,1)S(1)}, u32[]{:S(2)}, u32[]{:S(2)}) async-start(bf16[64,32,128]{2,1,0:T(8,128)(2,1)} %get-tuple-element.14), calls=%async_computation.3 | async-start | bytes 1048576 | tf_op jit(solution)/shard_map/all_to_all | solution.py:288
  111.2 33.0 %copy-start = (bf16[128,640]{1,0:T(8,128)(2,1)S(1)}, bf16[128,640]{1,0:T(8,128)(2,1)}, u32[]{:S(2)}) copy-start(bf16[128,640]{1,0:T(8,128)(2,1)} %rq_ref.3) | copy-start | bytes 491524
  111.3 33.0 %copy-start.1 = (bf16[128,640]{1,0:T(8,128)(2,1)S(1)}, bf16[128,640]{1,0:T(8,128)(2,1)}, u32[]{:S(2)}) copy-start(bf16[128,640]{1,0:T(8,128)(2,1)} %rk_ref.3) | copy-start | bytes 491524
  111.3 33.0 %copy-start.2 = (bf16[128,640]{1,0:T(8,128)(2,1)S(1)}, bf16[128,640]{1,0:T(8,128)(2,1)}, u32[]{:S(2)}) copy-start(bf16[128,640]{1,0:T(8,128)(2,1)} %rv_ref.3) | copy-start | bytes 491524
  111.3 33.0 %copy-start.3 = (bf16[640,128]{1,0:T(8,128)(2,1)S(1)}, bf16[640,128]{1,0:T(8,128)(2,1)}, u32[]{:S(2)}) copy-start(bf16[640,128]{1,0:T(8,128)(2,1)} %kp_ref.1) | copy-start | bytes 491524
  111.3 33.0 %copy-start.4 = (bf16[640,128]{1,0:T(8,128)(2,1)S(1)}, bf16[640,128]{1,0:T(8,128)(2,1)}, u32[]{:S(2)}) copy-start(bf16[640,128]{1,0:T(8,128)(2,1)} %vp_ref.1) | copy-start | bytes 491524
  111.3 65.5 %reduce-scatter.2.cloned.1.call-start = ((), (), s32[]{:S(2)}) async-start(), calls=%async_computation.7 | async-start | bytes 1474560 | tf_op jit(solution)/shard_map/reduce_scatter | solution.py:283
  134.1 10.1 %all-to-all-start.3 = ((bf16[8,32,128]{2,1,0:T(8,128)(2,1)}), bf16[8,32,128]{2,1,0:T(8,128)(2,1)S(1)}, u32[]{:S(2)}, u32[]{:S(2)}) async-start(bf16[8,32,128]{2,1,0:T(8,128)(2,1)} %broadcast_in_dim.54), calls=%async_computation.4 | async-start | bytes 131072 | tf_op jit(solution)/shard_map/all_to_all | solution.py:292
  144.3 26.2 %copy-start.5 = (bf16[8,16,128]{2,1,0:T(8,128)(2,1)}, bf16[8,16,128]{2,1,0:T(8,128)(2,1)S(1)}, u32[]{:S(2)}) copy-start(bf16[8,16,128]{2,1,0:T(8,128)(2,1)S(1)} %get-tuple-element.28) | copy-start | bytes 98308
  144.3 26.2 %copy-start.6 = (bf16[8,16,128]{2,1,0:T(8,128)(2,1)}, bf16[8,16,128]{2,1,0:T(8,128)(2,1)S(1)}, u32[]{:S(2)}) copy-start(bf16[8,16,128]{2,1,0:T(8,128)(2,1)S(1)} %get-tuple-element.29) | copy-start | bytes 98308
  171.5 24.1 %all-to-all-start.5 = ((bf16[64,24,128]{2,1,0:T(8,128)(2,1)}), bf16[64,24,128]{2,1,0:T(8,128)(2,1)S(1)}, u32[]{:S(2)}, u32[]{:S(2)}) async-start(bf16[64,24,128]{2,1,0:T(8,128)(2,1)} %shard_map.166), calls=%async_computation.6 | async-start | bytes 786432 | tf_op jit(solution)/shard_map/all_to_all | solution.py:341
Sparse Core Ops, SparseCore 0:
  115.0 43.6 reduce-scatter.1

commit v2 on v1

v2 whole, which is shorter than its diff:
```python
import functools
import math

import jax
import jax.numpy as jnp
from jax import lax
from jax.experimental import pallas as pl
from jax.experimental.pallas import tpu as pltpu
from jax.sharding import Mesh
from jax.sharding import PartitionSpec as P

BF = jnp.bfloat16
F32 = jnp.float32
LOW = -1e30
LOG2E = math.log2(math.e)
CHIPS, CORES = 4, 2
HALVES, PLANE = 2, 32
PLANE_AXES = ("x", "y")
SLICE = 4
WIRE = 48
SCOPED = 32 * 1024 * 1024


def dot_nt(a, b):
    return lax.dot_general(a, b, (((1,), (1,)), ((), ())), preferred_element_type=F32)


def dot_nn(a, b):
    return lax.dot_general(a, b, (((1,), (0,)), ((), ())), preferred_element_type=F32)


def dot_tn(a, b):
    return lax.dot_general(a, b, (((0,), (0,)), ((), ())), preferred_element_type=F32)


def call(kernel, outs, in_smem, ins, scratch=(), flops=0):
    vmem = pl.BlockSpec(memory_space=pltpu.VMEM)
    smem = pl.BlockSpec(memory_space=pltpu.SMEM)
    return pl.pallas_call(
        kernel,
        out_shape=outs,
        in_specs=[smem] * len(in_smem) + [vmem] * len(ins),
        out_specs=jax.tree.map(lambda _: vmem, outs),
        scratch_shapes=list(scratch),
        compiler_params=pltpu.CompilerParams(vmem_limit_bytes=SCOPED),
        cost_estimate=pl.CostEstimate(flops=flops, bytes_accessed=1 << 20, transcendentals=0),
    )(*in_smem, *ins)


def shape(dims, dtype):
    return jax.ShapeDtypeStruct(dims, dtype)


def pinned_exchange(array, axes, later):
    array, later = lax.optimization_barrier((array, later))
    array = lax.all_to_all(array, axes, 0, 0, tiled=True)
    return lax.optimization_barrier((array, later))


def pack_kernel(heads, q_ref, g_ref, out_ref):
    rows = q_ref.shape[1]
    for h in range(heads):
        at = slice(h * 128, (h + 1) * 128)
        out_ref[h * rows : (h + 1) * rows, :] = q_ref[0, :, at]
        out_ref[(heads + h) * rows : (heads + h + 1) * rows, :] = g_ref[0, :, at]


def delta_kernel(heads, where_ref, g_ref, o_ref, out_ref, product):
    rows = g_ref.shape[1]
    base = where_ref[3] * (heads * rows)
    product[...] = jnp.zeros_like(product)
    for h in range(heads):
        at = slice(h * 128, (h + 1) * 128)
        to = pl.ds(pl.multiple_of(base + h * rows, rows), rows)
        product[to, :] = g_ref[0, :, at].astype(F32) * o_ref[0, :, at].astype(F32)
    sums = jnp.sum(product[...].T, axis=0, keepdims=True)
    out_ref[...] = jnp.zeros_like(out_ref)
    for n in range(sums.shape[1] // 128):
        out_ref[n : n + 1, :] = sums[:, n * 128 : (n + 1) * 128]


def key_positions(place, chunk, blocks, rows, block_rows):
    at = lax.broadcasted_iota(jnp.int32, (blocks * rows, 1), 0)
    return (chunk * blocks + at // rows) * block_rows + place * rows + at % rows


def cache_slice(kv_ref, chunk, blocks, rows, values):
    per = kv_ref.shape[0] // blocks
    line = pl.multiple_of((chunk // per) * (2 * rows) + values * rows, rows)
    at = pl.ds(lax.rem(chunk, per) * blocks, blocks)
    return kv_ref[at, pl.ds(line, rows), :].reshape(blocks * rows, -1)


def stats_kernel(blocks, rows, block_rows, factor, where_ref, q_ref, kv_ref, pos_ref, delta_ref, out_ref):
    shard, chip, place = where_ref[0], where_ref[1], where_ref[2]
    width = q_ref.shape[1]
    lines = width // 128
    full = shard // blocks
    pos = pos_ref[...]
    scale = factor * LOG2E
    out_ref[:, CHIPS * lines :, :] = jnp.broadcast_to(
        delta_ref[0 : out_ref.shape[1] - CHIPS * lines, :][None],
        (out_ref.shape[0], out_ref.shape[1] - CHIPS * lines, 128),
    )
    for k in range(CHIPS):
        q = q_ref[k]

        def chunk(j, carry, masked=False):
            top, total = carry
            s = dot_nt(cache_slice(kv_ref, j, blocks, rows, 0), q)
            if masked:
                seen = key_positions(place, j, blocks, rows, block_rows) <= pos
                s = jnp.where(seen, s, LOW)
            new = jnp.maximum(top, jnp.max(s, axis=0, keepdims=True))
            p = jnp.exp2((s - new) * scale)
            if masked:
                p = jnp.where(seen, p, 0.0)
            total = total * jnp.exp2((top - new) * scale) + jnp.sum(p, axis=0, keepdims=True)
            return new, total

        start = (jnp.full((1, width), LOW, F32), jnp.zeros((1, width), F32))
        top, total = chunk(full, lax.fori_loop(0, full, chunk, start), masked=True)
        lse = jnp.where(total > 0.0, top * factor + jnp.log(total), LOW)
        line = lax.rem(chip + k, CHIPS) * lines
        for n in range(lines):
            out_ref[:, pl.ds(line + n, 1), :] = jnp.broadcast_to(
                lse[:, n * 128 : (n + 1) * 128][None], (out_ref.shape[0], 1, 128)
            )


def grads_kernel(
    blocks, rows, block_rows, factor, where_ref, q_ref, g_ref, kv_ref, pos_ref, log_ref, delta_ref,
    dkv_ref, dq_ref, dk_total, dv_total,
):
    shard, chip, place = where_ref[0], where_ref[1], where_ref[2]
    width = q_ref.shape[1]
    size = blocks * rows
    full = shard // blocks
    pos = pos_ref[...]
    scale = factor * LOG2E
    dk_total[...] = jnp.zeros_like(dk_total)
    dv_total[...] = jnp.zeros_like(dv_total)
    for k in range(CHIPS):
        layer = lax.rem(chip + k, CHIPS)
        q = q_ref[k]
        g = g_ref[k]
        log_total = log_ref[layer] * LOG2E
        delta = delta_ref[layer]

        def chunk(j, dq, masked=False):
            keys = cache_slice(kv_ref, j, blocks, rows, 0)
            values = cache_slice(kv_ref, j, blocks, rows, 1)
            p = jnp.exp2(dot_nt(keys, q) * scale - log_total)
            if masked:
                seen = key_positions(place, j, blocks, rows, block_rows) <= pos
                p = jnp.where(seen, p, 0.0)
            ds = (p * (dot_nt(values, g) - delta)).astype(BF)
            at = pl.ds(pl.multiple_of(j * size, size), size)
            dk_total[at, :] += dot_nn(ds, q)
            dv_total[at, :] += dot_nn(p.astype(BF), g)
            return dq + dot_tn(keys, ds)

        dq = lax.fori_loop(0, full, chunk, jnp.zeros((kv_ref.shape[-1], width), F32))
        dq = chunk(full, dq, masked=True).T
        half = width // CORES
        for n in range(CORES):
            dq_ref[n, layer] = dq[n * half : (n + 1) * half]
    per = dkv_ref.shape[0] // blocks
    for j in range(HALVES * per):
        at = slice(j * size, (j + 1) * size)
        to = slice((j % per) * blocks, (j % per + 1) * blocks)
        line = (j // per) * 2 * rows
        dkv_ref[to, line : line + rows, :] = dk_total[at, :].astype(BF).reshape(blocks, rows, -1)
        line += rows
        dkv_ref[to, line : line + rows, :] = dv_total[at, :].astype(BF).reshape(blocks, rows, -1)


def total_kernel(factor, terms_ref, out_ref):
    total = jnp.sum(terms_ref[...].astype(F32), axis=0)
    lines = out_ref.shape[1]
    row = lax.broadcasted_iota(jnp.int32, (lines, 1), 0)
    scale = jnp.where(row < lines // 2, factor, 1.0)
    count = out_ref.shape[0] // HALVES
    for n in range(HALVES):
        part = (total[n * lines : (n + 1) * lines] * scale).astype(BF)
        out_ref[n * count : (n + 1) * count] = jnp.broadcast_to(part[None], (count,) + part.shape)


def states_kernel(
    heads, whole_ref, kp_ref, vp_ref, rq_ref, rk_ref, rv_ref, from_ref, to_ref, extra_ref,
    ck_ref, cv_ref, gr_ref, send_ref, wire,
):
    count = whole_ref.shape[0] // HALVES
    rows = whole_ref.shape[1] // 2
    both = (whole_ref[0:count].astype(F32) + whole_ref[count:].astype(F32)).astype(BF)
    ck = both[:, 0:rows, :].reshape(count * rows, -1)
    cv = both[:, rows:, :].reshape(count * rows, -1)
    ck_ref[...] = ck
    cv_ref[...] = cv
    plane = send_ref.shape[0]
    used = 2 * SLICE * heads
    wire[:, used:, :] = jnp.broadcast_to(extra_ref[...][None], (plane,) + extra_ref.shape)
    for i in range(heads):
        at = slice(i * 128, (i + 1) * 128)
        gr = (dot_nt(ck, kp_ref[at, :]) + dot_nt(cv, vp_ref[at, :])).astype(BF)
        gr_ref[:, at] = gr
        query_w = (rq_ref[:, at].astype(F32) * from_ref[:, i : i + 1]).astype(BF)
        key_w = (rk_ref[:, at].astype(F32) * to_ref[:, i : i + 1]).astype(BF)
        grad = dot_tn(query_w, gr)
        state = dot_tn(key_w, rv_ref[:, at])
        for k in range(SLICE):
            part = slice(k * plane, (k + 1) * plane)
            wire[:, SLICE * i + k, :] = grad[part]
            wire[:, SLICE * (heads + i) + k, :] = state[part]
    send_ref[...] = wire[...].astype(BF)


def totals_kernel(heads, part_ref, decay_ref, out_ref):
    count = part_ref.shape[0]
    zero = jnp.zeros(part_ref.shape[1:], F32)

    def step(b, carry):
        fore, back = carry
        fore = decay_ref[b] * fore + part_ref[b].astype(F32)
        r = count - 1 - b
        back = decay_ref[r] * back + part_ref[r].astype(F32)
        return fore, back

    fore, back = lax.fori_loop(0, count, step, (zero, zero), unroll=4)
    row = lax.broadcasted_iota(jnp.int32, zero.shape, 0)
    out_ref[...] = jnp.where(row < SLICE * heads, back, fore)


def scan_kernel(heads, where_ref, part_ref, decay_ref, other_ref, out_ref, ahead, behind):
    count = part_ref.shape[0]
    upper = where_ref[0] >= count
    other = other_ref[...]
    zero = jnp.zeros_like(other)

    def step(b, carry):
        fore, back = carry
        ahead[b] = fore
        fore = decay_ref[b] * fore + part_ref[b].astype(F32)
        r = count - 1 - b
        behind[r] = back
        back = decay_ref[r] * back + part_ref[r].astype(F32)
        return fore, back

    start = (jnp.where(upper, other, zero), jnp.where(upper, zero, other))
    lax.fori_loop(0, count, step, start, unroll=4)
    row = lax.broadcasted_iota(jnp.int32, part_ref.shape, 1)
    out_ref[...] = jnp.where(row < SLICE * heads, behind[...], ahead[...]).astype(BF)


def final_kernel(
    heads, rq_ref, rk_ref, rv_ref, gr_ref, cum_ref, cum_t_ref, from_ref, to_ref, wire_ref,
    q_ref, k_ref, v_ref, wire,
):
    wire[...] = wire_ref[...].astype(F32)

    def matrix(r):
        return jnp.concatenate([wire[:, r + k, :] for k in range(SLICE)], axis=0).astype(BF)

    size = rq_ref.shape[0]
    t = lax.broadcasted_iota(jnp.int32, (size, size), 0)
    u = lax.broadcasted_iota(jnp.int32, (size, size), 1)
    causal = t >= u
    for i in range(heads):
        at = slice(i * 128, (i + 1) * 128)
        qr, kr, vr, gr = rq_ref[:, at], rk_ref[:, at], rv_ref[:, at], gr_ref[:, at]
        grad_b, state_b = matrix(SLICE * i), matrix(SLICE * (heads + i))
        gap = cum_t_ref[:, i : i + 1] - cum_ref[i : i + 1, :]
        decay = jnp.where(causal, jnp.exp(jnp.where(causal, gap, 0.0)), 0.0)
        from_start, to_end = from_ref[:, i : i + 1], to_ref[:, i : i + 1]
        one = (decay * dot_nt(gr, vr)).astype(BF)
        three = (decay * dot_nt(qr, kr)).astype(BF)
        q_ref[:, at] = dot_nn(one, kr) + from_start * dot_nt(gr, state_b)
        k_ref[:, at] = dot_tn(one, qr) + to_end * dot_nt(vr, grad_b)
        v_ref[:, at] = dot_tn(three, gr) + to_end * dot_nn(kr, grad_b)


def query_grad_kernel(heads, factor, own_ref, a_ref, b_ref, c_ref, out_ref):
    rows = out_ref.shape[1]
    total = own_ref[...] + a_ref[...].astype(F32) + b_ref[...].astype(F32) + c_ref[...].astype(F32)
    total = (total * factor).astype(BF)
    for h in range(heads):
        out_ref[0, :, h * 128 : (h + 1) * 128] = total[h * rows : (h + 1) * rows]


def body(
    offsets,
    queries,
    output_grad,
    attention_out,
    cache_keys,
    cache_values,
    key_projection,
    value_projection,
    retention_query,
    retention_key,
    retention_value,
    retention_decay,
):
    core, chip = lax.axis_index("core"), lax.axis_index("zl")
    place = chip * CORES + core
    secs = CHIPS * CORES
    half = lax.axis_index("zh")
    shard = half * PLANE + lax.axis_index(PLANE_AXES)
    shards = HALVES * PLANE
    block_rows, head = cache_keys.shape
    _, query_rows, query_width = queries.shape
    heads = query_width // head
    flat = query_rows * heads
    width = CORES * flat
    rows = block_rows // secs
    factor = 1.0 / math.sqrt(head)
    blocks = 16
    where = jnp.stack([shard, chip, place, core]).astype(jnp.int32)

    kv_own = jnp.concatenate(
        [lax.dynamic_slice_in_dim(a, place * rows, rows, 0) for a in (cache_keys, cache_values)]
    )
    kv_own, queries, output_grad = lax.optimization_barrier((kv_own, queries, output_grad))
    kv_other = lax.ppermute(kv_own, "zh", [(0, 1), (1, 0)])
    own = call(
        functools.partial(pack_kernel, heads),
        shape((2 * flat, head), BF), (), (queries, output_grad),
    )
    parts = [own] + [
        lax.ppermute(own, "zl", [(i, (i - k) % CHIPS) for i in range(CHIPS)])
        for k in range(1, CHIPS)
    ]
    delta = call(
        functools.partial(delta_kernel, heads),
        shape((12, head), F32), (where,), (output_grad, attention_out),
        scratch=[pltpu.VMEM((width, head), F32)],
    )
    own_offset = jnp.sum(
        jnp.where(jnp.arange(shards, dtype=jnp.int32) == shard, offsets, 0)
    )
    row_of = jnp.arange(width, dtype=jnp.int32) % query_rows
    pos = (shard * block_rows + own_offset + row_of)[None]

    local = retention_decay.shape[0]
    cum = jnp.cumsum(retention_decay, axis=1)
    cum_t = cum.T
    last = cum[:, -1]
    from_start = jnp.exp(cum_t)
    to_end = jnp.exp(last[None] - cum_t)
    high = last.astype(BF)
    rest = last - high.astype(F32)
    middle = rest.astype(BF)
    low = (rest - middle.astype(F32)).astype(BF)
    extra = jnp.concatenate([high, middle, low]).astype(F32)
    used = 2 * SLICE * local
    extra = jnp.pad(extra[None], ((0, WIRE - used - 1), (0, head - extra.shape[0])))

    early = (where, pos, delta, cum, cum_t, from_start, to_end, extra)
    kv = jnp.where(
        half == 0,
        jnp.concatenate([kv_own, kv_other]),
        jnp.concatenate([kv_other, kv_own]),
    )
    kv = jnp.broadcast_to(kv[None], (PLANE,) + kv.shape)
    kv, early = pinned_exchange(kv, PLANE_AXES, early)
    where, pos, delta, cum, cum_t, from_start, to_end, extra = early

    kv, *parts = lax.optimization_barrier((kv, *parts))
    mine = jnp.stack(parts)
    other = lax.ppermute(mine, "core", [(0, 1), (1, 0)])
    first = jnp.where(core == 0, mine, other)
    second = jnp.where(core == 0, other, mine)
    q_all = jnp.concatenate([first[:, :flat], second[:, :flat]], axis=1)
    g_all = jnp.concatenate([first[:, flat:], second[:, flat:]], axis=1)

    sizes = (blocks, rows, block_rows, factor)
    both = call(
        functools.partial(stats_kernel, *sizes),
        shape((secs, 32, head), F32), (where,), (q_all, kv, pos, delta),
        flops=1 << 30,
    )
    both, (q_all, g_all, kv) = pinned_exchange(both, ("zl", "core"), (q_all, g_all, kv))
    lines = width // 128
    logs = both[:, : CHIPS * lines]
    top = jnp.max(logs, axis=0)
    log_total = top + jnp.log(jnp.sum(jnp.exp(logs - top), axis=0))
    log_total = log_total.reshape(CHIPS, 1, width)
    deltas = both[:, CHIPS * lines : (CHIPS + 1) * lines]
    deltas = (deltas[0::CORES] + deltas[1::CORES]).reshape(CHIPS, 1, width)

    dkv, dq = call(
        functools.partial(grads_kernel, *sizes),
        (shape(kv.shape, BF), shape((CORES, CHIPS, flat, head), F32)),
        (where,),
        (q_all, g_all, kv, pos, log_total, deltas),
        scratch=[pltpu.VMEM((shards * rows, head), F32)] * 2,
        flops=4 << 30,
    )
    dq_other = lax.ppermute(
        lax.dynamic_index_in_dim(dq, 1 - core, 0, False), "core", [(0, 1), (1, 0)]
    )
    dq_own = lax.dynamic_index_in_dim(dq, core, 0, False)
    terms, dq_own = pinned_exchange(dkv, PLANE_AXES, dq_own)
    total = call(
        functools.partial(total_kernel, factor),
        shape((HALVES * secs, 2 * rows, head), BF), (), (terms,),
    )
    whole, (dq_own, dq_other) = pinned_exchange(total, ("zh", "zl", "core"), (dq_own, dq_other))

    cache_key_grad, cache_value_grad, out_grad, send = call(
        functools.partial(states_kernel, local),
        (
            shape((block_rows, head), BF), shape((block_rows, head), BF),
            shape(retention_query.shape, BF), shape((PLANE, WIRE, head), BF),
        ),
        (),
        (
            whole, key_projection, value_projection,
            retention_query, retention_key, retention_value, from_start, to_end, extra,
        ),
        scratch=[pltpu.VMEM((PLANE, WIRE, head), F32)],
        flops=1 << 27,
    )
    part, (dq_own, dq_other) = pinned_exchange(send, PLANE_AXES, (dq_own, dq_other))
    lasts = part[:, used, : 3 * local].astype(F32).reshape(PLANE, 3, local)
    decays = jnp.exp(lasts[:, 0] + lasts[:, 1] + lasts[:, 2])
    decays = jnp.concatenate([decays, decays], axis=1)
    decays = jnp.broadcast_to(decays[:, :, None], (PLANE, 2 * local, SLICE))
    decays = decays.reshape(PLANE, used, 1)
    decays = jnp.pad(decays, ((0, 0), (0, WIRE - used), (0, 0)))
    decays = jnp.broadcast_to(decays, (PLANE, WIRE, head))
    totals = call(
        functools.partial(totals_kernel, local),
        shape((WIRE, head), F32), (), (part, decays),
    )
    dq_sum = dq_own + dq_other
    totals, dq_sum = lax.optimization_barrier((totals, dq_sum))
    totals = lax.ppermute(totals, "zh", [(0, 1), (1, 0)])
    pieces = [
        lax.ppermute(
            lax.dynamic_index_in_dim(dq_sum, lax.rem(chip + k, CHIPS), 0, False).astype(BF),
            "zl", [(i, (i + k) % CHIPS) for i in range(CHIPS)],
        )
        for k in range(1, CHIPS)
    ]
    dq_mine = lax.dynamic_index_in_dim(dq_sum, chip, 0, False)
    enter = call(
        functools.partial(scan_kernel, local),
        shape(part.shape, BF), (where,), (part, decays, totals),
        scratch=[pltpu.VMEM(part.shape, F32)] * 2,
    )
    enter, (dq_mine, pieces, out_grad) = pinned_exchange(
        enter, PLANE_AXES, (dq_mine, pieces, out_grad)
    )
    cross_query_grad = call(
        functools.partial(query_grad_kernel, heads, factor),
        shape(queries.shape, BF), (), (dq_mine, *pieces),
    )
    grads = call(
        functools.partial(final_kernel, local),
        (shape(retention_query.shape, F32),) * 3,
        (),
        (
            retention_query, retention_key, retention_value, out_grad, cum, cum_t,
            from_start, to_end, enter,
        ),
        scratch=[pltpu.VMEM(enter.shape, F32)],
        flops=1 << 28,
    )
    return (cross_query_grad, cache_key_grad, cache_value_grad) + tuple(grads)


def solution(mesh):
    sec, ctx = ("zl", "core"), ("zh", "x", "y")
    split = Mesh(mesh.devices.reshape(CHIPS, CORES, HALVES, 4, 8), sec + ctx)
    in_specs = (
        P(),
        P(sec, ctx, None),
        P(sec, ctx, None),
        P(sec, ctx, None),
        P(ctx, None),
        P(ctx, None),
        P(sec, None),
        P(sec, None),
        P(ctx, sec),
        P(ctx, sec),
        P(ctx, sec),
        P(sec, ctx),
    )
    out_specs = (
        P(sec, ctx, None),
        P(ctx, None),
        P(ctx, None),
        P(ctx, sec),
        P(ctx, sec),
        P(ctx, sec),
    )
    return jax.shard_map(body, mesh=split, in_specs=in_specs, out_specs=out_specs, check_vma=False)
```

time: 206 us -> 189 us (0.917)
  waiting for transfers between devices: 82.6 us -> 54.1 us
  between operations: 15.1 us -> 1.73 us
  blocking collectives: 24.4 us -> 37.1 us
  starting transfers between devices: 61.1 us -> 71.9 us
  Pallas kernels: 11.9 us -> 14.4 us
    all_to_all x5 -> x4, waiting for transfers between devices: 72.2 us -> 45 us  [pinned_exchange(): array = lax.all_to_all(array, axes, 0, 0, tiled=True)]
    ppermute x4 -> x10, starting transfers between devices: 14.2 us -> 38.6 us  [the longest x1 10.9 us: body(): kv_other = lax.ppermute(kv_own, 'zh', [(0, 1), (1, 0)])]
    all_to_all x5 -> x4, starting transfers between devices: 46.8 us -> 33.3 us  [pinned_exchange(): array = lax.all_to_all(array, axes, 0, 0, tiled=True)]
    all_to_all x1 -> x2, blocking collectives: 24.4 us -> 37.1 us  [pinned_exchange(): array = lax.all_to_all(array, axes, 0, 0, tiled=True)]
    reshape x6 -> x1, local copies, waits for them, and re-layouts: 2.89 us -> 0.01 us  [body(): deltas = (deltas[0::CORES] + deltas[1::CORES]).reshape(CHIPS, 1, width)]
    pallas_call x5 -> x10, Pallas kernels: 11.9 us -> 14.4 us  [call(): pl.pallas_call(kernel, out_shape=outs, in_specs=[smem] * len(in_smem) + [...]
    ppermute x4 -> x10, waiting for transfers between devices: 10.3 us -> 9.11 us  [the longest x1 5.4 us: body(): totals = lax.ppermute(totals, 'zh', [(0, 1), (1, 0)])]
  transfers between devices with their start and end apart: 10 -> 14, of which waited for: 7 -> 7; matrix products, arithmetic and copies ran while one was open for 3% -> 1% of each run, Pallas kernels for 1% -> 1%
where the time goes in v2:
time: 189 us; the launch traced here: 188 us
  starting transfers between devices  71.9 us (38%)
  waiting for transfers between devices  54.1 us (29%)
  blocking collectives  37.1 us (20%)
  Pallas kernels  14.4 us (8%)
  local copies, waits for them, and re-layouts  5.35 us (3%)
  other arithmetic  2.93 us (2%)
    all_to_all x4, waiting for transfers between devices, pinned_exchange(): array = lax.all_to_all(array, axes, 0, 0, tiled=True)  45 us
    all_to_all x2, blocking collectives, pinned_exchange(): array = lax.all_to_all(array, axes, 0, 0, tiled=True)  37.1 us
    all_to_all x4, starting transfers between devices, pinned_exchange(): array = lax.all_to_all(array, axes, 0, 0, tiled=True)  33.3 us
    pallas_call x10, Pallas kernels, call(): pl.pallas_call(kernel, out_shape=outs, in_specs=[smem] * len(in_smem) + [...  14.4 us
    ppermute x1, starting transfers between devices, body(): kv_other = lax.ppermute(kv_own, 'zh', [(0, 1), (1, 0)])  10.9 us
    ppermute x3, starting transfers between devices, body(): lax.ppermute(own, 'zl', [(i, (i - k) % CHIPS) for i in range(CHIPS)])  10.1 us
    ppermute x3, starting transfers between devices, body(): lax.ppermute(lax.dynamic_index_in_dim(dq_sum, lax.rem(chip + k, CHIPS), 0...  9.56 us
    ppermute x1, waiting for transfers between devices, body(): totals = lax.ppermute(totals, 'zh', [(0, 1), (1, 0)])  5.4 us
  transfers between devices with their start and end apart: 14, of which 7 were waited for; matrix products, arithmetic and copies ran while one was open for 1% of the time, Pallas kernels for 1%

profile of v2, /device:TPU:8, one launch (start us, length us, event | category | flops | bytes accessed | tf_op | source)
XLA Modules:
  0.0 187.5 jit_solution(7644351174633581834)
XLA Ops:
  1.4 10.9 %collective-permute-start = (bf16[32,128]{1,0:T(8,128)(2,1)S(1)}, bf16[32,128]{1,0:T(8,128)(2,1)S(1)}, u32[]{:S(2)}, u32[]{:S(2)}) collective-permute-start(bf16[32,128]{1,0:T(8,128)(2,1)S(1)} %pad_maximum_fusion.3), channel_id=1, source_target_pairs={{0,32},{32,0},{1,33},{33,1},{2,34},{34,2},{3,35},{35,3},{4,36},{36... | collective-permute-start | bytes 24584 | tf_op jit(solution)/shard_map/ppermute | solution.py:324
  12.3 1.0 reduce_window_sum.11.cum_ref
  13.6 1.3 fusion.16
  15.8 0.9 copy-done.3
  18.3 0.9 broadcast_in_dim.12
  19.2 10.2 %all-to-all-start = ((bf16[32,64,128]{2,1,0:T(8,128)(2,1)}), bf16[32,64,128]{2,1,0:T(8,128)(2,1)S(1)}, u32[]{:S(2)}, u32[]{:S(2)}) async-start(bf16[32,64,128]{2,1,0:T(8,128)(2,1)} %broadcast_in_dim.12), calls=%async_computation | async-start | bytes 1048576 | tf_op jit(solution)/shard_map/all_to_all | solution.py:56
  29.5 5.2 %collective-permute-start.1 = (bf16[640,128]{1,0:T(8,128)(2,1)S(1)}, bf16[640,128]{1,0:T(8,128)(2,1)S(1)}, u32[]{:S(2)}, u32[]{:S(2)}) collective-permute-start(bf16[640,128]{1,0:T(8,128)(2,1)S(1)} %shard_map.164), channel_id=1, source_target_pairs={{0,384},{128,0},{256,128},{384,256},{1,385},{129,1},{257,129},{385... | collective-permute-start | bytes 491528 | tf_op jit(solution)/shard_map/ppermute | solution.py:330
  34.7 1.9 %collective-permute-start.2 = (bf16[640,128]{1,0:T(8,128)(2,1)S(1)}, bf16[640,128]{1,0:T(8,128)(2,1)S(1)}, u32[]{:S(2)}, u32[]{:S(2)}) collective-permute-start(bf16[640,128]{1,0:T(8,128)(2,1)S(1)} %shard_map.164), channel_id=1, source_target_pairs={{0,256},{128,384},{256,0},{384,128},{1,257},{129,385},{257,1},{385... | collective-permute-start | bytes 491528 | tf_op jit(solution)/shard_map/ppermute | solution.py:330
  36.6 3.0 %collective-permute-start.3 = (bf16[640,128]{1,0:T(8,128)(2,1)S(1)}, bf16[640,128]{1,0:T(8,128)(2,1)S(1)}, u32[]{:S(2)}, u32[]{:S(2)}) collective-permute-start(bf16[640,128]{1,0:T(8,128)(2,1)S(1)} %shard_map.164), channel_id=1, source_target_pairs={{0,128},{128,256},{256,384},{384,0},{1,129},{129,257},{257,385},{3... | collective-permute-start | bytes 491528 | tf_op jit(solution)/shard_map/ppermute | solution.py:330
  39.6 7.1 %all-to-all-done.kv_ref = bf16[32,64,128]{2,1,0:T(8,128)(2,1)S(1)} async-done(((bf16[32,64,128]{2,1,0:T(8,128)(2,1)}), bf16[32,64,128]{2,1,0:T(8,128)(2,1)S(1)}, u32[]{:S(2)}, u32[]{:S(2)}) %all-to-all-start) | async-done | bytes 524320 | tf_op jit(solution)/shard_map/all_to_all | solution.py:56
  46.8 1.6 collective-permute-done.2
  48.5 1.9 %collective-permute-start.4 = (bf16[4,640,128]{2,1,0:T(8,128)(2,1)S(1)}, bf16[4,640,128]{2,1,0:T(8,128)(2,1)S(1)}, u32[]{:S(2)}, u32[]{:S(2)}) collective-permute-start(bf16[4,640,128]{2,1,0:T(8,128)(2,1)S(1)} %pad_maximum_fusion), channel_id=1, source_target_pairs={{0,64},{64,0},{1,65},{65,1},{2,66},{66,2},{3,67},{67,3},{4,68},{68... | collective-permute-start | bytes 1966088 | tf_op jit(solution)/shard_map/ppermute | solution.py:370
  50.4 2.1 %collective-permute-done.4 = bf16[4,640,128]{2,1,0:T(8,128)(2,1)S(1)} collective-permute-done((bf16[4,640,128]{2,1,0:T(8,128)(2,1)S(1)}, bf16[4,640,128]{2,1,0:T(8,128)(2,1)S(1)}, u32[]{:S(2)}, u32[]{:S(2)}) %collective-permute-start.4) | collective-permute-done | bytes 655392 | tf_op jit(solution)/shard_map/ppermute | solution.py:370
  52.8 3.0 %shard_map.165 = f32[8,32,128]{2,1,0:T(8,128)} custom-call(s32[4]{0:T(128)S(1)} %pad_add_fusion.where_ref, bf16[4,640,128]{2,1,0:T(8,128)(2,1)S(1)} %pad_maximum_fusion.1.q_ref, bf16[32,64,128]{2,1,0:T(8,128)(2,1)S(1)} %all-to-all-done.kv_ref, s32[1,640]{1,0:T(1,128)S(1)} %fusion.9.pos_ref, f32[12,128]{1,0:T(8,128)S(1)} %shard_map.163.delta_ref), custom_call_target="tpu_custom_call" | custom-call | flops 1073741824 | bytes 1048576 | tf_op jit(solution)/shard_map/pallas_call | solution.py:39
  55.9 4.1 %all-to-all-start.1 = ((f32[8,32,128]{2,1,0:T(8,128)}), f32[8,32,128]{2,1,0:T(8,128)S(1)}, u32[]{:S(2)}, u32[]{:S(2)}) async-start(f32[8,32,128]{2,1,0:T(8,128)} %shard_map.165), calls=%async_computation.1 | async-start | bytes 262144 | tf_op jit(solution)/shard_map/all_to_all | solution.py:56
  59.9 6.8 %all-to-all-done.1 = f32[8,32,128]{2,1,0:T(8,128)S(1)} async-done(((f32[8,32,128]{2,1,0:T(8,128)}), f32[8,32,128]{2,1,0:T(8,128)S(1)}, u32[]{:S(2)}, u32[]{:S(2)}) %all-to-all-start.1) | async-done | bytes 131104 | tf_op jit(solution)/shard_map/all_to_all | solution.py:56
  66.8 4.6 %shard_map.166 = (bf16[32,64,128]{2,1,0:T(8,128)(2,1)}, f32[2,4,320,128]{3,2,1,0:T(8,128)S(1)}) custom-call(s32[4]{0:T(128)S(1)} %pad_add_fusion.where_ref, bf16[4,640,128]{2,1,0:T(8,128)(2,1)S(1)} %pad_maximum_fusion.1.q_ref, bf16[4,640,128]{2,1,0:T(8,128)(2,1)S(1)} %pad_maximum_fusion.2.g_ref, bf16[32,64,128]{2,1,0:T(8,128)(2,1)S(1)} %all-to-all-done.kv_ref, ...), custom_call_target="tpu_custom_call" | custom-call | flops 4294967296 | bytes 1048576 | tf_op jit(solution)/shard_map/pallas_call | solution.py:39
  71.5 1.0 dynamic-slice_bitcast_fusion
  72.4 14.2 %all-to-all-start.2 = ((bf16[32,64,128]{2,1,0:T(8,128)(2,1)}), bf16[32,64,128]{2,1,0:T(8,128)(2,1)S(1)}, u32[]{:S(2)}, u32[]{:S(2)}) async-start(bf16[32,64,128]{2,1,0:T(8,128)(2,1)} %get-tuple-element.110), calls=%async_computation.2 | async-start | bytes 1048576 | tf_op jit(solution)/shard_map/all_to_all | solution.py:56
  86.6 1.9 %collective-permute-start.5 = (f32[4,320,128]{2,1,0:T(8,128)}, f32[4,320,128]{2,1,0:T(8,128)S(1)}, u32[]{:S(2)}, u32[]{:S(2)}) collective-permute-start(f32[4,320,128]{2,1,0:T(8,128)} %get-tuple-element.152), channel_id=1, source_target_pairs={{0,64},{64,0},{1,65},{65,1},{2,66},{66,2},{3,67},{67,3},{4,68},{68... | collective-permute-start | bytes 1966088 | tf_op jit(solution)/shard_map/ppermute | solution.py:399
  88.5 15.4 %all-to-all-done.2.terms_ref = bf16[32,64,128]{2,1,0:T(8,128)(2,1)S(1)} async-done(((bf16[32,64,128]{2,1,0:T(8,128)(2,1)}), bf16[32,64,128]{2,1,0:T(8,128)(2,1)S(1)}, u32[]{:S(2)}, u32[]{:S(2)}) %all-to-all-start.2) | async-done | bytes 524320 | tf_op jit(solution)/shard_map/all_to_all | solution.py:56
  104.1 19.0 %all_to_all.30.whole_ref = bf16[16,32,128]{2,1,0:T(8,128)(2,1)S(1)} all-to-all(bf16[16,32,128]{2,1,0:T(8,128)(2,1)S(1)} %shard_map.167), channel_id=1, replica_groups=mesh['zl'=4,'core'=2,'zh'=2,'x'=4,'y'=8] {'zh','zl','core'}, dimensions={0} | all-to-all | bytes 262144 | tf_op jit(solution)/shard_map/all_to_all | solution.py:56
  123.1 2.0 %shard_map.168 = (bf16[128,128]{1,0:T(8,128)(2,1)}, bf16[128,128]{1,0:T(8,128)(2,1)}, bf16[128,640]{1,0:T(8,128)(2,1)S(1)}, bf16[32,48,128]{2,1,0:T(8,128)(2,1)}) custom-call(bf16[16,32,128]{2,1,0:T(8,128)(2,1)S(1)} %all_to_all.30.whole_ref, bf16[640,128]{1,0:T(8,128)(2,1)S(1)} %copy-done.5, bf16[640,128]{1,0:T(8,128)(2,1)S(1)} %copy-done.6, ...), custom_call_target="tpu_custom_call" | custom-call | flops 134217728 | bytes 1048576 | tf_op jit(solution)/shard_map/pallas_call | solution.py:39
  125.1 4.8 %all-to-all-start.4 = ((bf16[32,48,128]{2,1,0:T(8,128)(2,1)}), bf16[32,48,128]{2,1,0:T(8,128)(2,1)S(1)}, u32[]{:S(2)}, u32[]{:S(2)}) async-start(bf16[32,48,128]{2,1,0:T(8,128)(2,1)} %get-tuple-element.124), calls=%async_computation.4 | async-start | bytes 786432 | tf_op jit(solution)/shard_map/all_to_all | solution.py:56
  129.9 15.7 %all-to-all-done.4.part_ref = bf16[32,48,128]{2,1,0:T(8,128)(2,1)S(1)} async-done(((bf16[32,48,128]{2,1,0:T(8,128)(2,1)}), bf16[32,48,128]{2,1,0:T(8,128)(2,1)S(1)}, u32[]{:S(2)}, u32[]{:S(2)}) %all-to-all-start.4) | async-done | bytes 393248 | tf_op jit(solution)/shard_map/all_to_all | solution.py:56
  146.4 2.2 %collective-permute-start.7 = (bf16[320,128]{1,0:T(8,128)(2,1)S(1)}, bf16[320,128]{1,0:T(8,128)(2,1)S(1)}, u32[]{:S(2)}, u32[]{:S(2)}) collective-permute-start(bf16[320,128]{1,0:T(8,128)(2,1)S(1)} %get-tuple-element.158), channel_id=1, source_target_pairs={{0,128},{128,256},{256,384},{384,0},{1,129},{129,257},{257,385},{3... | collective-permute-start | bytes 245768 | tf_op jit(solution)/shard_map/ppermute | solution.py:440
  148.6 3.1 %collective-permute-start.8 = (bf16[320,128]{1,0:T(8,128)(2,1)S(1)}, bf16[320,128]{1,0:T(8,128)(2,1)S(1)}, u32[]{:S(2)}, u32[]{:S(2)}) collective-permute-start(bf16[320,128]{1,0:T(8,128)(2,1)S(1)} %get-tuple-element.157), channel_id=1, source_target_pairs={{0,256},{128,384},{256,0},{384,128},{1,257},{129,385},{257,1},{385... | collective-permute-start | bytes 245768 | tf_op jit(solution)/shard_map/ppermute | solution.py:440
  151.7 4.2 %collective-permute-start.9 = (bf16[320,128]{1,0:T(8,128)(2,1)S(1)}, bf16[320,128]{1,0:T(8,128)(2,1)S(1)}, u32[]{:S(2)}, u32[]{:S(2)}) collective-permute-start(bf16[320,128]{1,0:T(8,128)(2,1)S(1)} %get-tuple-element.156), channel_id=1, source_target_pairs={{0,384},{128,0},{256,128},{384,256},{1,385},{129,1},{257,129},{385... | collective-permute-start | bytes 245768 | tf_op jit(solution)/shard_map/ppermute | solution.py:440
  156.0 4.2 %collective-permute-start.6 = (f32[48,128]{1,0:T(8,128)S(1)}, f32[48,128]{1,0:T(8,128)S(1)}, u32[]{:S(2)}, u32[]{:S(2)}) collective-permute-start(f32[48,128]{1,0:T(8,128)S(1)} %shard_map.169), channel_id=1, source_target_pairs={{0,32},{32,0},{1,33},{33,1},{2,34},{34,2},{3,35},{35,3},{4,36},{36... | collective-permute-start | bytes 73736 | tf_op jit(solution)/shard_map/ppermute | solution.py:438
  160.2 5.4 %collective-permute-done.6.other_ref = f32[48,128]{1,0:T(8,128)S(1)} collective-permute-done((f32[48,128]{1,0:T(8,128)S(1)}, f32[48,128]{1,0:T(8,128)S(1)}, u32[]{:S(2)}, u32[]{:S(2)}) %collective-permute-start.6) | collective-permute-done | bytes 24608 | tf_op jit(solution)/shard_map/ppermute | solution.py:438
  166.4 18.1 %all_to_all.31.wire_ref = bf16[32,48,128]{2,1,0:T(8,128)(2,1)S(1)} all-to-all(bf16[32,48,128]{2,1,0:T(8,128)(2,1)S(1)} %shard_map.170), channel_id=1, replica_groups=mesh['zl'=4,'core'=2,'zh'=2,'x'=4,'y'=8] {'x','y'}, dimensions={0} | all-to-all | bytes 786432 | tf_op jit(solution)/shard_map/all_to_all | solution.py:56
  184.5 2.3 %shard_map.172 = (f32[128,640]{1,0:T(8,128)}, f32[128,640]{1,0:T(8,128)}, f32[128,640]{1,0:T(8,128)}) custom-call(bf16[128,640]{1,0:T(8,128)(2,1)S(1)} %copy-done, bf16[128,640]{1,0:T(8,128)(2,1)S(1)} %copy-done.1, bf16[128,640]{1,0:T(8,128)(2,1)S(1)} %copy-done.2, bf16[128,640]{1,0:T(8,128)(2,1)S(1)} %get-tuple-element.145.gr_ref, ...), custom_call_target="tpu_custom_call" | custom-call | flops 268435456 | bytes 1048576 | tf_op jit(solution)/shard_map/pallas_call | solution.py:39
  (65 shorter events, 5.7 us)
Async XLA Ops:
  0.6 28.8 %copy-start.7 = (bf16[1,16,2560]{2,1,0:T(8,128)(2,1)S(1)}, bf16[1,16,2560]{2,1,0:T(8,128)(2,1)}, u32[]{:S(2)}) copy-start(bf16[1,16,2560]{2,1,0:T(8,128)(2,1)} %q_ref) | copy-start | bytes 245764
  0.6 28.8 %copy-start.4 = (bf16[1,16,2560]{2,1,0:T(8,128)(2,1)S(1)}, bf16[1,16,2560]{2,1,0:T(8,128)(2,1)}, u32[]{:S(2)}) copy-start(bf16[1,16,2560]{2,1,0:T(8,128)(2,1)} %g_ref.1) | copy-start | bytes 245764
  1.4 16.9 %collective-permute-start = (bf16[32,128]{1,0:T(8,128)(2,1)S(1)}, bf16[32,128]{1,0:T(8,128)(2,1)S(1)}, u32[]{:S(2)}, u32[]{:S(2)}) collective-permute-start(bf16[32,128]{1,0:T(8,128)(2,1)S(1)} %pad_maximum_fusion.3), channel_id=1, source_target_pairs={{0,32},{32,0},{1,33},{33,1},{2,34},{34,2},{3,35},{35,3},{4,36},{36... | collective-permute-start | bytes 24584 | tf_op jit(solution)/shard_map/ppermute | solution.py:324
  15.8 0.9 copy-start.3
  16.7 0.9 copy-start.8
  19.2 27.5 %all-to-all-start = ((bf16[32,64,128]{2,1,0:T(8,128)(2,1)}), bf16[32,64,128]{2,1,0:T(8,128)(2,1)S(1)}, u32[]{:S(2)}, u32[]{:S(2)}) async-start(bf16[32,64,128]{2,1,0:T(8,128)(2,1)} %broadcast_in_dim.12), calls=%async_computation | async-start | bytes 1048576 | tf_op jit(solution)/shard_map/all_to_all | solution.py:56
  29.5 17.3 %collective-permute-start.1 = (bf16[640,128]{1,0:T(8,128)(2,1)S(1)}, bf16[640,128]{1,0:T(8,128)(2,1)S(1)}, u32[]{:S(2)}, u32[]{:S(2)}) collective-permute-start(bf16[640,128]{1,0:T(8,128)(2,1)S(1)} %shard_map.164), channel_id=1, source_target_pairs={{0,384},{128,0},{256,128},{384,256},{1,385},{129,1},{257,129},{385... | collective-permute-start | bytes 491528 | tf_op jit(solution)/shard_map/ppermute | solution.py:330
  34.7 13.7 %collective-permute-start.2 = (bf16[640,128]{1,0:T(8,128)(2,1)S(1)}, bf16[640,128]{1,0:T(8,128)(2,1)S(1)}, u32[]{:S(2)}, u32[]{:S(2)}) collective-permute-start(bf16[640,128]{1,0:T(8,128)(2,1)S(1)} %shard_map.164), channel_id=1, source_target_pairs={{0,256},{128,384},{256,0},{384,128},{1,257},{129,385},{257,1},{385... | collective-permute-start | bytes 491528 | tf_op jit(solution)/shard_map/ppermute | solution.py:330
  36.6 11.8 %collective-permute-start.3 = (bf16[640,128]{1,0:T(8,128)(2,1)S(1)}, bf16[640,128]{1,0:T(8,128)(2,1)S(1)}, u32[]{:S(2)}, u32[]{:S(2)}) collective-permute-start(bf16[640,128]{1,0:T(8,128)(2,1)S(1)} %shard_map.164), channel_id=1, source_target_pairs={{0,128},{128,256},{256,384},{384,0},{1,129},{129,257},{257,385},{3... | collective-permute-start | bytes 491528 | tf_op jit(solution)/shard_map/ppermute | solution.py:330
  48.5 4.0 %collective-permute-start.4 = (bf16[4,640,128]{2,1,0:T(8,128)(2,1)S(1)}, bf16[4,640,128]{2,1,0:T(8,128)(2,1)S(1)}, u32[]{:S(2)}, u32[]{:S(2)}) collective-permute-start(bf16[4,640,128]{2,1,0:T(8,128)(2,1)S(1)} %pad_maximum_fusion), channel_id=1, source_target_pairs={{0,64},{64,0},{1,65},{65,1},{2,66},{66,2},{3,67},{67,3},{4,68},{68... | collective-permute-start | bytes 1966088 | tf_op jit(solution)/shard_map/ppermute | solution.py:370
  55.9 10.9 %all-to-all-start.1 = ((f32[8,32,128]{2,1,0:T(8,128)}), f32[8,32,128]{2,1,0:T(8,128)S(1)}, u32[]{:S(2)}, u32[]{:S(2)}) async-start(f32[8,32,128]{2,1,0:T(8,128)} %shard_map.165), calls=%async_computation.1 | async-start | bytes 262144 | tf_op jit(solution)/shard_map/all_to_all | solution.py:56
  72.4 50.7 %copy-start = (bf16[128,640]{1,0:T(8,128)(2,1)S(1)}, bf16[128,640]{1,0:T(8,128)(2,1)}, u32[]{:S(2)}) copy-start(bf16[128,640]{1,0:T(8,128)(2,1)} %rq_ref.3) | copy-start | bytes 491524
  72.4 50.7 %copy-start.1 = (bf16[128,640]{1,0:T(8,128)(2,1)S(1)}, bf16[128,640]{1,0:T(8,128)(2,1)}, u32[]{:S(2)}) copy-start(bf16[128,640]{1,0:T(8,128)(2,1)} %rk_ref.3) | copy-start | bytes 491524
  72.4 50.7 %copy-start.2 = (bf16[128,640]{1,0:T(8,128)(2,1)S(1)}, bf16[128,640]{1,0:T(8,128)(2,1)}, u32[]{:S(2)}) copy-start(bf16[128,640]{1,0:T(8,128)(2,1)} %rv_ref.3) | copy-start | bytes 491524
  72.4 50.7 %copy-start.5 = (bf16[640,128]{1,0:T(8,128)(2,1)S(1)}, bf16[640,128]{1,0:T(8,128)(2,1)}, u32[]{:S(2)}) copy-start(bf16[640,128]{1,0:T(8,128)(2,1)} %kp_ref.1) | copy-start | bytes 491524
  72.4 50.7 %copy-start.6 = (bf16[640,128]{1,0:T(8,128)(2,1)S(1)}, bf16[640,128]{1,0:T(8,128)(2,1)}, u32[]{:S(2)}) copy-start(bf16[640,128]{1,0:T(8,128)(2,1)} %vp_ref.1) | copy-start | bytes 491524
  72.4 31.5 %all-to-all-start.2 = ((bf16[32,64,128]{2,1,0:T(8,128)(2,1)}), bf16[32,64,128]{2,1,0:T(8,128)(2,1)S(1)}, u32[]{:S(2)}, u32[]{:S(2)}) async-start(bf16[32,64,128]{2,1,0:T(8,128)(2,1)} %get-tuple-element.110), calls=%async_computation.2 | async-start | bytes 1048576 | tf_op jit(solution)/shard_map/all_to_all | solution.py:56
  86.6 17.4 %collective-permute-start.5 = (f32[4,320,128]{2,1,0:T(8,128)}, f32[4,320,128]{2,1,0:T(8,128)S(1)}, u32[]{:S(2)}, u32[]{:S(2)}) collective-permute-start(f32[4,320,128]{2,1,0:T(8,128)} %get-tuple-element.152), channel_id=1, source_target_pairs={{0,64},{64,0},{1,65},{65,1},{2,66},{66,2},{3,67},{67,3},{4,68},{68... | collective-permute-start | bytes 1966088 | tf_op jit(solution)/shard_map/ppermute | solution.py:399
  125.1 20.6 %all-to-all-start.4 = ((bf16[32,48,128]{2,1,0:T(8,128)(2,1)}), bf16[32,48,128]{2,1,0:T(8,128)(2,1)S(1)}, u32[]{:S(2)}, u32[]{:S(2)}) async-start(bf16[32,48,128]{2,1,0:T(8,128)(2,1)} %get-tuple-element.124), calls=%async_computation.4 | async-start | bytes 786432 | tf_op jit(solution)/shard_map/all_to_all | solution.py:56
  146.4 20.0 %collective-permute-start.7 = (bf16[320,128]{1,0:T(8,128)(2,1)S(1)}, bf16[320,128]{1,0:T(8,128)(2,1)S(1)}, u32[]{:S(2)}, u32[]{:S(2)}) collective-permute-start(bf16[320,128]{1,0:T(8,128)(2,1)S(1)} %get-tuple-element.158), channel_id=1, source_target_pairs={{0,128},{128,256},{256,384},{384,0},{1,129},{129,257},{257,385},{3... | collective-permute-start | bytes 245768 | tf_op jit(solution)/shard_map/ppermute | solution.py:440
  148.6 17.8 %collective-permute-start.8 = (bf16[320,128]{1,0:T(8,128)(2,1)S(1)}, bf16[320,128]{1,0:T(8,128)(2,1)S(1)}, u32[]{:S(2)}, u32[]{:S(2)}) collective-permute-start(bf16[320,128]{1,0:T(8,128)(2,1)S(1)} %get-tuple-element.157), channel_id=1, source_target_pairs={{0,256},{128,384},{256,0},{384,128},{1,257},{129,385},{257,1},{385... | collective-permute-start | bytes 245768 | tf_op jit(solution)/shard_map/ppermute | solution.py:440
  151.7 14.7 %collective-permute-start.9 = (bf16[320,128]{1,0:T(8,128)(2,1)S(1)}, bf16[320,128]{1,0:T(8,128)(2,1)S(1)}, u32[]{:S(2)}, u32[]{:S(2)}) collective-permute-start(bf16[320,128]{1,0:T(8,128)(2,1)S(1)} %get-tuple-element.156), channel_id=1, source_target_pairs={{0,384},{128,0},{256,128},{384,256},{1,385},{129,1},{257,129},{385... | collective-permute-start | bytes 245768 | tf_op jit(solution)/shard_map/ppermute | solution.py:440
  156.0 9.6 %collective-permute-start.6 = (f32[48,128]{1,0:T(8,128)S(1)}, f32[48,128]{1,0:T(8,128)S(1)}, u32[]{:S(2)}, u32[]{:S(2)}) collective-permute-start(f32[48,128]{1,0:T(8,128)S(1)} %shard_map.169), channel_id=1, source_target_pairs={{0,32},{32,0},{1,33},{33,1},{2,34},{34,2},{3,35},{35,3},{4,36},{36... | collective-permute-start | bytes 73736 | tf_op jit(solution)/shard_map/ppermute | solution.py:438

commit v3 on v2

--- a/solution.py
+++ b/solution.py
@@ -67,7 +67,7 @@
 
 def delta_kernel(heads, where_ref, g_ref, o_ref, out_ref, product):
     rows = g_ref.shape[1]
-    base = where_ref[3] * (heads * rows)
+    base = lax.rem(where_ref[1], 2) * (heads * rows)
     product[...] = jnp.zeros_like(product)
     for h in range(heads):
         at = slice(h * 128, (h + 1) * 128)
@@ -79,6 +79,20 @@
         out_ref[n : n + 1, :] = sums[:, n * 128 : (n + 1) * 128]
 
 
+def gather_kernel(where_ref, a_ref, b_ref, c_ref, d_ref, out_ref):
+    flat = out_ref.shape[2]
+    for k, ref in enumerate((a_ref, b_ref, c_ref, d_ref)):
+        chip = lax.rem(where_ref[1] + k, CHIPS)
+        out_ref[0, chip] = ref[0:flat]
+        out_ref[1, chip] = ref[flat:]
+
+
+def row_positions(where_ref, offset_ref, width, rows, block_rows):
+    lane = lax.broadcasted_iota(jnp.int32, (1, width), 1)
+    shard = where_ref[0]
+    return lax.rem(lane, rows) + (shard * block_rows + offset_ref[shard])
+
+
 def key_positions(place, chunk, blocks, rows, block_rows):
     at = lax.broadcasted_iota(jnp.int32, (blocks * rows, 1), 0)
     return (chunk * blocks + at // rows) * block_rows + place * rows + at % rows
@@ -91,110 +105,122 @@
     return kv_ref[at, pl.ds(line, rows), :].reshape(blocks * rows, -1)
 
 
-def stats_kernel(blocks, rows, block_rows, factor, where_ref, q_ref, kv_ref, pos_ref, delta_ref, out_ref):
-    shard, chip, place = where_ref[0], where_ref[1], where_ref[2]
-    width = q_ref.shape[1]
+def tile(refs, which, n, t):
+    return refs[n][which, 2 * t : 2 * t + 2].reshape(2 * refs[n].shape[2], -1)
+
+
+def stats_kernel(
+    blocks, rows, query_rows, block_rows, factor,
+    where_ref, offset_ref, mine_ref, other_ref, kv_ref, delta_ref, out_ref,
+):
+    shard, place, core = where_ref[0], where_ref[2], where_ref[3]
+    width = 2 * mine_ref.shape[2]
     lines = width // 128
     full = shard // blocks
-    pos = pos_ref[...]
+    pos = row_positions(where_ref, offset_ref, width, query_rows, block_rows)
     scale = factor * LOG2E
+    count, total_lines = out_ref.shape[0], out_ref.shape[1]
     out_ref[:, CHIPS * lines :, :] = jnp.broadcast_to(
-        delta_ref[0 : out_ref.shape[1] - CHIPS * lines, :][None],
-        (out_ref.shape[0], out_ref.shape[1] - CHIPS * lines, 128),
-    )
-    for k in range(CHIPS):
-        q = q_ref[k]
-
-        def chunk(j, carry, masked=False):
-            top, total = carry
-            s = dot_nt(cache_slice(kv_ref, j, blocks, rows, 0), q)
-            if masked:
-                seen = key_positions(place, j, blocks, rows, block_rows) <= pos
-                s = jnp.where(seen, s, LOW)
-            new = jnp.maximum(top, jnp.max(s, axis=0, keepdims=True))
-            p = jnp.exp2((s - new) * scale)
-            if masked:
-                p = jnp.where(seen, p, 0.0)
-            total = total * jnp.exp2((top - new) * scale) + jnp.sum(p, axis=0, keepdims=True)
-            return new, total
-
-        start = (jnp.full((1, width), LOW, F32), jnp.zeros((1, width), F32))
-        top, total = chunk(full, lax.fori_loop(0, full, chunk, start), masked=True)
-        lse = jnp.where(total > 0.0, top * factor + jnp.log(total), LOW)
-        line = lax.rem(chip + k, CHIPS) * lines
-        for n in range(lines):
-            out_ref[:, pl.ds(line + n, 1), :] = jnp.broadcast_to(
-                lse[:, n * 128 : (n + 1) * 128][None], (out_ref.shape[0], 1, 128)
-            )
+        delta_ref[...][None], (count, total_lines - CHIPS * lines, 128)
+    )
+    for n in range(CORES):
+        for t in range(CHIPS // 2):
+            q = tile((mine_ref, other_ref), 0, n, t)
+
+            def chunk(j, carry, masked=False):
+                top, total = carry
+                s = dot_nt(cache_slice(kv_ref, j, blocks, rows, 0), q)
+                if masked:
+                    seen = key_positions(place, j, blocks, rows, block_rows) <= pos
+                    s = jnp.where(seen, s, LOW)
+                new = jnp.maximum(top, jnp.max(s, axis=0, keepdims=True))
+                p = jnp.exp2((s - new) * scale)
+                if masked:
+                    p = jnp.where(seen, p, 0.0)
+                total = total * jnp.exp2((top - new) * scale) + jnp.sum(p, axis=0, keepdims=True)
+                return new, total
+
+            start = (jnp.full((1, width), LOW, F32), jnp.zeros((1, width), F32))
+            top, total = chunk(full, lax.fori_loop(0, full, chunk, start), masked=True)
+            lse = jnp.where(total > 0.0, top * factor + jnp.log(total), LOW)
+            line = lax.rem(core + n, CORES) * (CHIPS // 2 * lines) + t * lines
+            for m in range(lines):
+                out_ref[:, pl.ds(line + m, 1), :] = jnp.broadcast_to(
+                    lse[:, m * 128 : (m + 1) * 128][None], (count, 1, 128)
+                )
 
 
 def grads_kernel(
-    blocks, rows, block_rows, factor, where_ref, q_ref, g_ref, kv_ref, pos_ref, log_ref, delta_ref,
-    dkv_ref, dq_ref, dk_total, dv_total,
+    blocks, rows, query_rows, block_rows, factor,
+    where_ref, offset_ref, mine_ref, other_ref, kv_ref, log_ref, delta_ref,
+    dkv_ref, dq_own_ref, dq_other_ref, dk_total, dv_total,
 ):
-    shard, chip, place = where_ref[0], where_ref[1], where_ref[2]
-    width = q_ref.shape[1]
+    shard, place, core = where_ref[0], where_ref[2], where_ref[3]
+    flat = mine_ref.shape[2]
+    width = 2 * flat
     size = blocks * rows
     full = shard // blocks
-    pos = pos_ref[...]
+    pos = row_positions(where_ref, offset_ref, width, query_rows, block_rows)
     scale = factor * LOG2E
     dk_total[...] = jnp.zeros_like(dk_total)
     dv_total[...] = jnp.zeros_like(dv_total)
-    for k in range(CHIPS):
-        layer = lax.rem(chip + k, CHIPS)
-        q = q_ref[k]
-        g = g_ref[k]
-        log_total = log_ref[layer] * LOG2E
-        delta = delta_ref[layer]
-
-        def chunk(j, dq, masked=False):
-            keys = cache_slice(kv_ref, j, blocks, rows, 0)
-            values = cache_slice(kv_ref, j, blocks, rows, 1)
-            p = jnp.exp2(dot_nt(keys, q) * scale - log_total)
-            if masked:
-                seen = key_positions(place, j, blocks, rows, block_rows) <= pos
-                p = jnp.where(seen, p, 0.0)
-            ds = (p * (dot_nt(values, g) - delta)).astype(BF)
-            at = pl.ds(pl.multiple_of(j * size, size), size)
-            dk_total[at, :] += dot_nn(ds, q)
-            dv_total[at, :] += dot_nn(p.astype(BF), g)
-            return dq + dot_tn(keys, ds)
-
-        dq = lax.fori_loop(0, full, chunk, jnp.zeros((kv_ref.shape[-1], width), F32))
-        dq = chunk(full, dq, masked=True).T
-        half = width // CORES
-        for n in range(CORES):
-            dq_ref[n, layer] = dq[n * half : (n + 1) * half]
-    per = dkv_ref.shape[0] // blocks
+    for n in range(CORES):
+        for t in range(CHIPS // 2):
+            q = tile((mine_ref, other_ref), 0, n, t)
+            g = tile((mine_ref, other_ref), 1, n, t)
+            at_core = lax.rem(core + n, CORES)
+            log_total = log_ref[at_core, t] * LOG2E
+            delta = delta_ref[at_core, t]
+
+            def chunk(j, dq, masked=False):
+                keys = cache_slice(kv_ref, j, blocks, rows, 0)
+                values = cache_slice(kv_ref, j, blocks, rows, 1)
+                p = jnp.exp2(dot_nt(keys, q) * scale - log_total)
+                if masked:
+                    seen = key_positions(place, j, blocks, rows, block_rows) <= pos
+                    p = jnp.where(seen, p, 0.0)
+                ds = (p * (dot_nt(values, g) - delta)).astype(BF)
+                at = pl.ds(pl.multiple_of(j * size, size), size)
+                dk_total[at, :] += dot_nn(ds, q)
+                dv_total[at, :] += dot_nn(p.astype(BF), g)
+                return dq + dot_tn(keys, ds)
+
+            dq = lax.fori_loop(0, full, chunk, jnp.zeros((kv_ref.shape[-1], width), F32))
+            dq = chunk(full, dq, masked=True).T
+            dq_ref = (dq_own_ref, dq_other_ref)[n]
+            for m in range(2):
+                dq_ref[2 * t + m] = dq[m * flat : (m + 1) * flat]
+    per = kv_ref.shape[0] // blocks
     for j in range(HALVES * per):
         at = slice(j * size, (j + 1) * size)
-        to = slice((j % per) * blocks, (j % per + 1) * blocks)
-        line = (j // per) * 2 * rows
-        dkv_ref[to, line : line + rows, :] = dk_total[at, :].astype(BF).reshape(blocks, rows, -1)
-        line += rows
-        dkv_ref[to, line : line + rows, :] = dv_total[at, :].astype(BF).reshape(blocks, rows, -1)
+        to = slice(j * blocks, (j + 1) * blocks)
+        dkv_ref[to, 0:rows, :] = dk_total[at, :].astype(BF).reshape(blocks, rows, -1)
+        dkv_ref[to, rows : 2 * rows, :] = dv_total[at, :].astype(BF).reshape(blocks, rows, -1)
+
+
+def pieces_kernel(where_ref, own_ref, other_ref, mine_ref, a_ref, b_ref, c_ref):
+    chip = where_ref[1]
+    mine_ref[...] = own_ref[chip] + other_ref[chip]
+    for k, ref in ((1, a_ref), (2, b_ref), (3, c_ref)):
+        to = lax.rem(chip + k, CHIPS)
+        ref[...] = (own_ref[to] + other_ref[to]).astype(BF)
 
 
 def total_kernel(factor, terms_ref, out_ref):
     total = jnp.sum(terms_ref[...].astype(F32), axis=0)
-    lines = out_ref.shape[1]
-    row = lax.broadcasted_iota(jnp.int32, (lines, 1), 0)
-    scale = jnp.where(row < lines // 2, factor, 1.0)
-    count = out_ref.shape[0] // HALVES
-    for n in range(HALVES):
-        part = (total[n * lines : (n + 1) * lines] * scale).astype(BF)
-        out_ref[n * count : (n + 1) * count] = jnp.broadcast_to(part[None], (count,) + part.shape)
+    row = lax.broadcasted_iota(jnp.int32, (total.shape[0], 1), 0)
+    total = (total * jnp.where(row < total.shape[0] // 2, factor, 1.0)).astype(BF)
+    out_ref[...] = jnp.broadcast_to(total[None], out_ref.shape)
 
 
 def states_kernel(
     heads, whole_ref, kp_ref, vp_ref, rq_ref, rk_ref, rv_ref, from_ref, to_ref, extra_ref,
     ck_ref, cv_ref, gr_ref, send_ref, wire,
 ):
-    count = whole_ref.shape[0] // HALVES
+    count = whole_ref.shape[0]
     rows = whole_ref.shape[1] // 2
-    both = (whole_ref[0:count].astype(F32) + whole_ref[count:].astype(F32)).astype(BF)
-    ck = both[:, 0:rows, :].reshape(count * rows, -1)
-    cv = both[:, rows:, :].reshape(count * rows, -1)
+    ck = whole_ref[:, 0:rows, :].reshape(count * rows, -1)
+    cv = whole_ref[:, rows:, :].reshape(count * rows, -1)
     ck_ref[...] = ck
     cv_ref[...] = cv
     plane = send_ref.shape[0]
@@ -311,17 +337,24 @@
     _, query_rows, query_width = queries.shape
     heads = query_width // head
     flat = query_rows * heads
-    width = CORES * flat
+    width = 2 * flat
+    lines = width // 128
     rows = block_rows // secs
     factor = 1.0 / math.sqrt(head)
     blocks = 16
+    sizes = (blocks, rows, query_rows, block_rows, factor)
     where = jnp.stack([shard, chip, place, core]).astype(jnp.int32)
 
     kv_own = jnp.concatenate(
         [lax.dynamic_slice_in_dim(a, place * rows, rows, 0) for a in (cache_keys, cache_values)]
     )
-    kv_own, queries, output_grad = lax.optimization_barrier((kv_own, queries, output_grad))
     kv_other = lax.ppermute(kv_own, "zh", [(0, 1), (1, 0)])
+    kv = jnp.where(
+        half == 0,
+        jnp.concatenate([kv_own, kv_other]),
+        jnp.concatenate([kv_other, kv_own]),
+    )
+    kv = jnp.broadcast_to(kv[None], (PLANE,) + kv.shape)
     own = call(
         functools.partial(pack_kernel, heads),
         shape((2 * flat, head), BF), (), (queries, output_grad),
@@ -332,16 +365,12 @@
     ]
     delta = call(
         functools.partial(delta_kernel, heads),
-        shape((12, head), F32), (where,), (output_grad, attention_out),
+        shape((32 - CHIPS * lines, head), F32), (where,), (output_grad, attention_out),
         scratch=[pltpu.VMEM((width, head), F32)],
     )
-    own_offset = jnp.sum(
-        jnp.where(jnp.arange(shards, dtype=jnp.int32) == shard, offsets, 0)
-    )
-    row_of = jnp.arange(width, dtype=jnp.int32) % query_rows
-    pos = (shard * block_rows + own_offset + row_of)[None]
 
     local = retention_decay.shape[0]
+    used = 2 * SLICE * local
     cum = jnp.cumsum(retention_decay, axis=1)
     cum_t = cum.T
     last = cum[:, -1]
@@ -352,60 +381,50 @@
     middle = rest.astype(BF)
     low = (rest - middle.astype(F32)).astype(BF)
     extra = jnp.concatenate([high, middle, low]).astype(F32)
-    used = 2 * SLICE * local
     extra = jnp.pad(extra[None], ((0, WIRE - used - 1), (0, head - extra.shape[0])))
 
-    early = (where, pos, delta, cum, cum_t, from_start, to_end, extra)
-    kv = jnp.where(
-        half == 0,
-        jnp.concatenate([kv_own, kv_other]),
-        jnp.concatenate([kv_other, kv_own]),
-    )
-    kv = jnp.broadcast_to(kv[None], (PLANE,) + kv.shape)
-    kv, early = pinned_exchange(kv, PLANE_AXES, early)
-    where, pos, delta, cum, cum_t, from_start, to_end, extra = early
-
-    kv, *parts = lax.optimization_barrier((kv, *parts))
-    mine = jnp.stack(parts)
+    env = (where, offsets, delta, cum, cum_t, from_start, to_end, extra)
+    mine = call(gather_kernel, shape((2, CHIPS, flat, head), BF), (where,), tuple(parts))
+    mine, kv, env = lax.optimization_barrier((mine, kv, env))
     other = lax.ppermute(mine, "core", [(0, 1), (1, 0)])
-    first = jnp.where(core == 0, mine, other)
-    second = jnp.where(core == 0, other, mine)
-    q_all = jnp.concatenate([first[:, :flat], second[:, :flat]], axis=1)
-    g_all = jnp.concatenate([first[:, flat:], second[:, flat:]], axis=1)
-
-    sizes = (blocks, rows, block_rows, factor)
+    kv = lax.all_to_all(kv, PLANE_AXES, 0, 0, tiled=True)
+    mine, other, kv, env = lax.optimization_barrier((mine, other, kv, env))
+    where, offsets, delta = env[:3]
+
     both = call(
         functools.partial(stats_kernel, *sizes),
-        shape((secs, 32, head), F32), (where,), (q_all, kv, pos, delta),
+        shape((secs, 32, head), F32), (where, offsets), (mine, other, kv, delta),
         flops=1 << 30,
     )
-    both, (q_all, g_all, kv) = pinned_exchange(both, ("zl", "core"), (q_all, g_all, kv))
-    lines = width // 128
+    both, (mine, other, kv, env) = pinned_exchange(both, ("zl", "core"), (mine, other, kv, env))
+    where, offsets = env[:2]
+    tiles = (CORES, CHIPS // 2, 1, width)
     logs = both[:, : CHIPS * lines]
     top = jnp.max(logs, axis=0)
-    log_total = top + jnp.log(jnp.sum(jnp.exp(logs - top), axis=0))
-    log_total = log_total.reshape(CHIPS, 1, width)
+    log_total = (top + jnp.log(jnp.sum(jnp.exp(logs - top), axis=0))).reshape(tiles)
     deltas = both[:, CHIPS * lines : (CHIPS + 1) * lines]
-    deltas = (deltas[0::CORES] + deltas[1::CORES]).reshape(CHIPS, 1, width)
-
-    dkv, dq = call(
+    deltas = deltas.reshape(CHIPS // 2, 2, CORES, lines, head)
+    deltas = (deltas[:, 0] + deltas[:, 1]).transpose(1, 0, 2, 3).reshape(tiles)
+
+    dkv, dq_own, dq_other = call(
         functools.partial(grads_kernel, *sizes),
-        (shape(kv.shape, BF), shape((CORES, CHIPS, flat, head), F32)),
-        (where,),
-        (q_all, g_all, kv, pos, log_total, deltas),
+        (shape((shards, 2 * rows, head), BF),) + (shape((CHIPS, flat, head), F32),) * 2,
+        (where, offsets),
+        (mine, other, kv, log_total, deltas),
         scratch=[pltpu.VMEM((shards * rows, head), F32)] * 2,
         flops=4 << 30,
     )
-    dq_other = lax.ppermute(
-        lax.dynamic_index_in_dim(dq, 1 - core, 0, False), "core", [(0, 1), (1, 0)]
-    )
-    dq_own = lax.dynamic_index_in_dim(dq, core, 0, False)
-    terms, dq_own = pinned_exchange(dkv, PLANE_AXES, dq_own)
+    terms, (dq_own, dq_other, env) = pinned_exchange(
+        dkv, ("zh",) + PLANE_AXES, (dq_own, dq_other, env)
+    )
     total = call(
         functools.partial(total_kernel, factor),
-        shape((HALVES * secs, 2 * rows, head), BF), (), (terms,),
-    )
-    whole, (dq_own, dq_other) = pinned_exchange(total, ("zh", "zl", "core"), (dq_own, dq_other))
+        shape((secs, 2 * rows, head), BF), (), (terms,),
+    )
+    whole, (dq_own, dq_other, env) = pinned_exchange(
+        total, ("zl", "core"), (dq_own, dq_other, env)
+    )
+    where, offsets, delta, cum, cum_t, from_start, to_end, extra = env
 
     cache_key_grad, cache_value_grad, out_grad, send = call(
         functools.partial(states_kernel, local),
@@ -421,7 +440,10 @@
         scratch=[pltpu.VMEM((PLANE, WIRE, head), F32)],
         flops=1 << 27,
     )
-    part, (dq_own, dq_other) = pinned_exchange(send, PLANE_AXES, (dq_own, dq_other))
+    send, dq_own, dq_other = lax.optimization_barrier((send, dq_own, dq_other))
+    dq_other = lax.ppermute(dq_other, "core", [(0, 1), (1, 0)])
+    part = lax.all_to_all(send, PLANE_AXES, 0, 0, tiled=True)
+    part, dq_own, dq_other, where = lax.optimization_barrier((part, dq_own, dq_other, where))
     lasts = part[:, used, : 3 * local].astype(F32).reshape(PLANE, 3, local)
     decays = jnp.exp(lasts[:, 0] + lasts[:, 1] + lasts[:, 2])
     decays = jnp.concatenate([decays, decays], axis=1)
@@ -433,25 +455,24 @@
         functools.partial(totals_kernel, local),
         shape((WIRE, head), F32), (), (part, decays),
     )
-    dq_sum = dq_own + dq_other
-    totals, dq_sum = lax.optimization_barrier((totals, dq_sum))
+    totals, dq_own, dq_other = lax.optimization_barrier((totals, dq_own, dq_other))
     totals = lax.ppermute(totals, "zh", [(0, 1), (1, 0)])
-    pieces = [
-        lax.ppermute(
-            lax.dynamic_index_in_dim(dq_sum, lax.rem(chip + k, CHIPS), 0, False).astype(BF),
-            "zl", [(i, (i + k) % CHIPS) for i in range(CHIPS)],
-        )
-        for k in range(1, CHIPS)
-    ]
-    dq_mine = lax.dynamic_index_in_dim(dq_sum, chip, 0, False)
+    piece = shape((flat, head), BF)
+    dq_mine, *pieces = call(
+        pieces_kernel, (shape((flat, head), F32), piece, piece, piece),
+        (where,), (dq_own, dq_other), flops=4 << 30,
+    )
     enter = call(
         functools.partial(scan_kernel, local),
         shape(part.shape, BF), (where,), (part, decays, totals),
         scratch=[pltpu.VMEM(part.shape, F32)] * 2,
     )
-    enter, (dq_mine, pieces, out_grad) = pinned_exchange(
-        enter, PLANE_AXES, (dq_mine, pieces, out_grad)
-    )
+    enter, dq_mine, pieces = lax.optimization_barrier((enter, dq_mine, pieces))
+    pieces = [
+        lax.ppermute(piece, "zl", [(i, (i + k) % CHIPS) for i in range(CHIPS)])
+        for k, piece in enumerate(pieces, 1)
+    ]
+    enter = lax.all_to_all(enter, PLANE_AXES, 0, 0, tiled=True)
     cross_query_grad = call(
         functools.partial(query_grad_kernel, heads, factor),
         shape(queries.shape, BF), (), (dq_mine, *pieces),

time: 189 us -> 180 us (0.952)
  the two profiles are of different devices: /device:TPU:8 before, /device:TPU:2 now
where the time goes in v3:
time: 180 us; the launch traced here: 179 us
  starting transfers between devices  62.6 us (35%)
  blocking collectives  62.2 us (35%)
  waiting for transfers between devices  32.3 us (18%)
  Pallas kernels  14.8 us (8%)
  local copies, waits for them, and re-layouts  5.77 us (3%)
    all_to_all x3, blocking collectives, pinned_exchange(): array = lax.all_to_all(array, axes, 0, 0, tiled=True)  62.2 us
    pallas_call x12, Pallas kernels, call(): pl.pallas_call(kernel, out_shape=outs, in_specs=[smem] * len(in_smem) + [...  14.8 us
    ppermute x3, starting transfers between devices, body(): lax.ppermute(own, 'zl', [(i, (i - k) % CHIPS) for i in range(CHIPS)])  12.8 us
    all_to_all x1, starting transfers between devices, body(): kv = lax.all_to_all(kv, PLANE_AXES, 0, 0, tiled=True)  10.4 us
    all_to_all x1, waiting for transfers between devices, body(): kv = lax.all_to_all(kv, PLANE_AXES, 0, 0, tiled=True)  10.3 us
    ppermute x3, starting transfers between devices, body(): lax.ppermute(piece, 'zl', [(i, (i + k) % CHIPS) for i in range(CHIPS)])  9.56 us
    ppermute x1, starting transfers between devices, body(): kv_other = lax.ppermute(kv_own, 'zh', [(0, 1), (1, 0)])  9.24 us
    all_to_all x1, waiting for transfers between devices, body(): part = lax.all_to_all(send, PLANE_AXES, 0, 0, tiled=True)  9.23 us
  transfers between devices with their start and end apart: 13, of which 7 were waited for; matrix products, arithmetic and copies ran while one was open for 1% of the time, Pallas kernels for 1%

profile of v3, /device:TPU:2, one launch (start us, length us, event | category | flops | bytes accessed | tf_op | source)
XLA Modules:
  0.0 179.4 jit_solution(18046292439811353670)
XLA Ops:
  0.6 0.9 copy-done.3
  1.5 0.9 copy-done.7
  2.4 4.3 %collective-permute-start.2 = (bf16[640,128]{1,0:T(8,128)(2,1)S(1)}, bf16[640,128]{1,0:T(8,128)(2,1)S(1)}, u32[]{:S(2)}, u32[]{:S(2)}) collective-permute-start(bf16[640,128]{1,0:T(8,128)(2,1)S(1)} %shard_map.163.a_ref), channel_id=1, source_target_pairs={{0,128},{128,256},{256,384},{384,0},{1,129},{129,257},{257,385},{3... | collective-permute-start | bytes 491528 | tf_op jit(solution)/shard_map/ppermute | solution.py:363
  6.7 6.1 %collective-permute-start.1 = (bf16[640,128]{1,0:T(8,128)(2,1)S(1)}, bf16[640,128]{1,0:T(8,128)(2,1)S(1)}, u32[]{:S(2)}, u32[]{:S(2)}) collective-permute-start(bf16[640,128]{1,0:T(8,128)(2,1)S(1)} %shard_map.163.a_ref), channel_id=1, source_target_pairs={{0,256},{128,384},{256,0},{384,128},{1,257},{129,385},{257,1},{385... | collective-permute-start | bytes 491528 | tf_op jit(solution)/shard_map/ppermute | solution.py:363
  12.8 2.5 %collective-permute-start = (bf16[640,128]{1,0:T(8,128)(2,1)S(1)}, bf16[640,128]{1,0:T(8,128)(2,1)S(1)}, u32[]{:S(2)}, u32[]{:S(2)}) collective-permute-start(bf16[640,128]{1,0:T(8,128)(2,1)S(1)} %shard_map.163.a_ref), channel_id=1, source_target_pairs={{0,384},{128,0},{256,128},{384,256},{1,385},{129,1},{257,129},{385... | collective-permute-start | bytes 491528 | tf_op jit(solution)/shard_map/ppermute | solution.py:363
  16.0 9.2 %collective-permute-start.3 = (bf16[32,128]{1,0:T(8,128)(2,1)S(1)}, bf16[32,128]{1,0:T(8,128)(2,1)S(1)}, u32[]{:S(2)}, u32[]{:S(2)}) collective-permute-start(bf16[32,128]{1,0:T(8,128)(2,1)S(1)} %pad_maximum_fusion), channel_id=1, source_target_pairs={{0,32},{32,0},{1,33},{33,1},{2,34},{34,2},{3,35},{35,3},{4,36},{36... | collective-permute-start | bytes 24584 | tf_op jit(solution)/shard_map/ppermute | solution.py:351
  28.2 0.9 broadcast_in_dim.8
  29.1 10.4 %all-to-all-start = ((bf16[32,64,128]{2,1,0:T(8,128)(2,1)}), bf16[32,64,128]{2,1,0:T(8,128)(2,1)S(1)}, u32[]{:S(2)}, u32[]{:S(2)}) async-start(bf16[32,64,128]{2,1,0:T(8,128)(2,1)} %broadcast_in_dim.8), calls=%async_computation | async-start | bytes 1048576 | tf_op jit(solution)/shard_map/all_to_all | solution.py:390
  39.5 1.9 %collective-permute-start.4 = (bf16[2,4,320,128]{3,2,1,0:T(8,128)(2,1)S(1)}, bf16[2,4,320,128]{3,2,1,0:T(8,128)(2,1)S(1)}, u32[]{:S(2)}, u32[]{:S(2)}) collective-permute-start(bf16[2,4,320,128]{3,2,1,0:T(8,128)(2,1)S(1)} %shard_map.164.mine_ref), channel_id=1, source_target_pairs={{0,64},{64,0},{1,65},{65,1},{2,66},{66,2},{3,67},{67,3},{4,68},{68... | collective-permute-start | bytes 1966088 | tf_op jit(solution)/shard_map/ppermute | solution.py:389
  41.4 2.1 %collective-permute-done.4.other_ref = bf16[2,4,320,128]{3,2,1,0:T(8,128)(2,1)S(1)} collective-permute-done((bf16[2,4,320,128]{3,2,1,0:T(8,128)(2,1)S(1)}, bf16[2,4,320,128]{3,2,1,0:T(8,128)(2,1)S(1)}, u32[]{:S(2)}, u32[]{:S(2)}) %collective-permute-start.4) | collective-permute-done | bytes 655392 | tf_op jit(solution)/shard_map/ppermute | solution.py:389
  43.5 10.3 %all-to-all-done.kv_ref = bf16[32,64,128]{2,1,0:T(8,128)(2,1)S(1)} async-done(((bf16[32,64,128]{2,1,0:T(8,128)(2,1)}), bf16[32,64,128]{2,1,0:T(8,128)(2,1)S(1)}, u32[]{:S(2)}, u32[]{:S(2)}) %all-to-all-start) | async-done | bytes 524320 | tf_op jit(solution)/shard_map/all_to_all | solution.py:390
  53.8 2.4 %shard_map.166 = f32[8,32,128]{2,1,0:T(8,128)S(1)} custom-call(s32[4]{0:T(128)S(1)} %pad_add_fusion.where_ref, s32[64]{0:T(128)S(1)} %copy-done.9, bf16[2,4,320,128]{3,2,1,0:T(8,128)(2,1)S(1)} %shard_map.164.mine_ref, bf16[2,4,320,128]{3,2,1,0:T(8,128)(2,1)S(1)} %collective-permute-done.4.other_ref, bf16[32,64,128]{2,1,0:T(8,128)(2,1)S(1)} %all-to-all-done.kv_ref, ...), custom_call_target="tpu_custom_call" | custom-call | flops 1073741824 | bytes 1048576 | tf_op jit(solution)/shard_map/pallas_call | solution.py:39
  56.2 10.3 %all_to_all.30 = f32[8,32,128]{2,1,0:T(8,128)S(1)} all-to-all(f32[8,32,128]{2,1,0:T(8,128)S(1)} %shard_map.166), channel_id=1, replica_groups=mesh['zl'=4,'core'=2,'zh'=2,'x'=4,'y'=8] {'zl','core'}, dimensions={0} | all-to-all | bytes 262144 | tf_op jit(solution)/shard_map/all_to_all | solution.py:56
  66.6 3.8 %shard_map.167 = (bf16[64,32,128]{2,1,0:T(8,128)(2,1)S(1)}, f32[4,320,128]{2,1,0:T(8,128)S(1)}, f32[4,320,128]{2,1,0:T(8,128)S(1)}) custom-call(s32[4]{0:T(128)S(1)} %pad_add_fusion.where_ref, s32[64]{0:T(128)S(1)} %copy-done.9, bf16[2,4,320,128]{3,2,1,0:T(8,128)(2,1)S(1)} %shard_map.164.mine_ref, ...), custom_call_target="tpu_custom_call" | custom-call | flops 4294967296 | bytes 1048576 | tf_op jit(solution)/shard_map/pallas_call | solution.py:39
  70.5 0.9 copy-done.10
  71.3 43.2 %all_to_all.31.terms_ref = bf16[64,32,128]{2,1,0:T(8,128)(2,1)S(1)} all-to-all(bf16[64,32,128]{2,1,0:T(8,128)(2,1)S(1)} %get-tuple-element.160), channel_id=1, replica_groups=mesh['zl'=4,'core'=2,'zh'=2,'x'=4,'y'=8] {'zh','x','y'}, dimensions={0} | all-to-all | bytes 1048576 | tf_op jit(solution)/shard_map/all_to_all | solution.py:56
  114.6 8.8 %all_to_all.32.whole_ref = bf16[8,32,128]{2,1,0:T(8,128)(2,1)S(1)} all-to-all(bf16[8,32,128]{2,1,0:T(8,128)(2,1)S(1)} %shard_map.168), channel_id=1, replica_groups=mesh['zl'=4,'core'=2,'zh'=2,'x'=4,'y'=8] {'zl','core'}, dimensions={0} | all-to-all | bytes 131072 | tf_op jit(solution)/shard_map/all_to_all | solution.py:56
  123.4 1.9 %shard_map.169 = (bf16[128,128]{1,0:T(8,128)(2,1)}, bf16[128,128]{1,0:T(8,128)(2,1)}, bf16[128,640]{1,0:T(8,128)(2,1)S(1)}, bf16[32,48,128]{2,1,0:T(8,128)(2,1)}) custom-call(bf16[8,32,128]{2,1,0:T(8,128)(2,1)S(1)} %all_to_all.32.whole_ref, bf16[640,128]{1,0:T(8,128)(2,1)S(1)} %copy-done.5, bf16[640,128]{1,0:T(8,128)(2,1)S(1)} %copy-done.6, ...), custom_call_target="tpu_custom_call" | custom-call | flops 134217728 | bytes 1048576 | tf_op jit(solution)/shard_map/pallas_call | solution.py:39
  125.3 7.0 %all-to-all-start.4 = ((bf16[32,48,128]{2,1,0:T(8,128)(2,1)}), bf16[32,48,128]{2,1,0:T(8,128)(2,1)S(1)}, u32[]{:S(2)}, u32[]{:S(2)}) async-start(bf16[32,48,128]{2,1,0:T(8,128)(2,1)} %get-tuple-element.194), calls=%async_computation.4 | async-start | bytes 786432 | tf_op jit(solution)/shard_map/all_to_all | solution.py:445
  132.3 1.9 %collective-permute-start.5 = (f32[4,320,128]{2,1,0:T(8,128)S(1)}, f32[4,320,128]{2,1,0:T(8,128)S(1)}, u32[]{:S(2)}, u32[]{:S(2)}) collective-permute-start(f32[4,320,128]{2,1,0:T(8,128)S(1)} %get-tuple-element.196), channel_id=1, source_target_pairs={{0,64},{64,0},{1,65},{65,1},{2,66},{66,2},{3,67},{67,3},{4,68},{68... | collective-permute-start | bytes 1966088 | tf_op jit(solution)/shard_map/ppermute | solution.py:444
  134.3 2.1 %collective-permute-done.5.other_ref = f32[4,320,128]{2,1,0:T(8,128)S(1)} collective-permute-done((f32[4,320,128]{2,1,0:T(8,128)S(1)}, f32[4,320,128]{2,1,0:T(8,128)S(1)}, u32[]{:S(2)}, u32[]{:S(2)}) %collective-permute-start.5) | collective-permute-done | bytes 655392 | tf_op jit(solution)/shard_map/ppermute | solution.py:444
  136.3 9.2 %all-to-all-done.4.part_ref = bf16[32,48,128]{2,1,0:T(8,128)(2,1)S(1)} async-done(((bf16[32,48,128]{2,1,0:T(8,128)(2,1)}), bf16[32,48,128]{2,1,0:T(8,128)(2,1)S(1)}, u32[]{:S(2)}, u32[]{:S(2)}) %all-to-all-start.4) | async-done | bytes 393248 | tf_op jit(solution)/shard_map/all_to_all | solution.py:445
  146.2 3.5 %collective-permute-start.6 = (f32[48,128]{1,0:T(8,128)S(1)}, f32[48,128]{1,0:T(8,128)S(1)}, u32[]{:S(2)}, u32[]{:S(2)}) collective-permute-start(f32[48,128]{1,0:T(8,128)S(1)} %shard_map.170), channel_id=1, source_target_pairs={{0,32},{32,0},{1,33},{33,1},{2,34},{34,2},{3,35},{35,3},{4,36},{36... | collective-permute-start | bytes 73736 | tf_op jit(solution)/shard_map/ppermute | solution.py:459
  150.4 5.6 %collective-permute-done.6.other_ref = f32[48,128]{1,0:T(8,128)S(1)} collective-permute-done((f32[48,128]{1,0:T(8,128)S(1)}, f32[48,128]{1,0:T(8,128)S(1)}, u32[]{:S(2)}, u32[]{:S(2)}) %collective-permute-start.6) | collective-permute-done | bytes 24608 | tf_op jit(solution)/shard_map/ppermute | solution.py:459
  156.0 1.5 shard_map.171
  157.5 6.3 %all-to-all-start.5 = ((bf16[32,48,128]{2,1,0:T(8,128)(2,1)}), bf16[32,48,128]{2,1,0:T(8,128)(2,1)S(1)}, u32[]{:S(2)}, u32[]{:S(2)}) async-start(bf16[32,48,128]{2,1,0:T(8,128)(2,1)} %shard_map.171), calls=%async_computation.5 | async-start | bytes 786432 | tf_op jit(solution)/shard_map/all_to_all | solution.py:475
  163.8 3.0 %collective-permute-start.7 = (bf16[320,128]{1,0:T(8,128)(2,1)S(1)}, bf16[320,128]{1,0:T(8,128)(2,1)S(1)}, u32[]{:S(2)}, u32[]{:S(2)}) collective-permute-start(bf16[320,128]{1,0:T(8,128)(2,1)S(1)} %get-tuple-element.210), channel_id=1, source_target_pairs={{0,128},{128,256},{256,384},{384,0},{1,129},{129,257},{257,385},{3... | collective-permute-start | bytes 245768 | tf_op jit(solution)/shard_map/ppermute | solution.py:472
  166.8 2.5 %collective-permute-start.8 = (bf16[320,128]{1,0:T(8,128)(2,1)S(1)}, bf16[320,128]{1,0:T(8,128)(2,1)S(1)}, u32[]{:S(2)}, u32[]{:S(2)}) collective-permute-start(bf16[320,128]{1,0:T(8,128)(2,1)S(1)} %get-tuple-element.211), channel_id=1, source_target_pairs={{0,256},{128,384},{256,0},{384,128},{1,257},{129,385},{257,1},{385... | collective-permute-start | bytes 245768 | tf_op jit(solution)/shard_map/ppermute | solution.py:472
  169.3 4.1 %collective-permute-start.9 = (bf16[320,128]{1,0:T(8,128)(2,1)S(1)}, bf16[320,128]{1,0:T(8,128)(2,1)S(1)}, u32[]{:S(2)}, u32[]{:S(2)}) collective-permute-start(bf16[320,128]{1,0:T(8,128)(2,1)S(1)} %get-tuple-element.212), channel_id=1, source_target_pairs={{0,384},{128,0},{256,128},{384,256},{1,385},{129,1},{257,129},{385... | collective-permute-start | bytes 245768 | tf_op jit(solution)/shard_map/ppermute | solution.py:472
  173.4 2.2 %collective-permute-done.8.b_ref = bf16[320,128]{1,0:T(8,128)(2,1)S(1)} collective-permute-done((bf16[320,128]{1,0:T(8,128)(2,1)S(1)}, bf16[320,128]{1,0:T(8,128)(2,1)S(1)}, u32[]{:S(2)}, u32[]{:S(2)}) %collective-permute-start.8) | collective-permute-done | bytes 81952 | tf_op jit(solution)/shard_map/ppermute | solution.py:472
  175.5 0.9 collective-permute-done.9.c_ref
  177.1 2.3 %shard_map.174 = (f32[128,640]{1,0:T(8,128)}, f32[128,640]{1,0:T(8,128)}, f32[128,640]{1,0:T(8,128)}) custom-call(bf16[128,640]{1,0:T(8,128)(2,1)S(1)} %copy-done, bf16[128,640]{1,0:T(8,128)(2,1)S(1)} %copy-done.1, bf16[128,640]{1,0:T(8,128)(2,1)S(1)} %copy-done.2, bf16[128,640]{1,0:T(8,128)(2,1)S(1)} %get-tuple-element.215.gr_ref, ...), custom_call_target="tpu_custom_call" | custom-call | flops 268435456 | bytes 1048576 | tf_op jit(solution)/shard_map/pallas_call | solution.py:39
  (63 shorter events, 5.7 us)
Async XLA Ops:
  0.6 0.9 copy-start.3
  1.5 0.9 copy-start.7
  2.4 25.1 %collective-permute-start.2 = (bf16[640,128]{1,0:T(8,128)(2,1)S(1)}, bf16[640,128]{1,0:T(8,128)(2,1)S(1)}, u32[]{:S(2)}, u32[]{:S(2)}) collective-permute-start(bf16[640,128]{1,0:T(8,128)(2,1)S(1)} %shard_map.163.a_ref), channel_id=1, source_target_pairs={{0,128},{128,256},{256,384},{384,0},{1,129},{129,257},{257,385},{3... | collective-permute-start | bytes 491528 | tf_op jit(solution)/shard_map/ppermute | solution.py:363
  6.7 20.9 %collective-permute-start.1 = (bf16[640,128]{1,0:T(8,128)(2,1)S(1)}, bf16[640,128]{1,0:T(8,128)(2,1)S(1)}, u32[]{:S(2)}, u32[]{:S(2)}) collective-permute-start(bf16[640,128]{1,0:T(8,128)(2,1)S(1)} %shard_map.163.a_ref), channel_id=1, source_target_pairs={{0,256},{128,384},{256,0},{384,128},{1,257},{129,385},{257,1},{385... | collective-permute-start | bytes 491528 | tf_op jit(solution)/shard_map/ppermute | solution.py:363
  12.8 14.8 %collective-permute-start = (bf16[640,128]{1,0:T(8,128)(2,1)S(1)}, bf16[640,128]{1,0:T(8,128)(2,1)S(1)}, u32[]{:S(2)}, u32[]{:S(2)}) collective-permute-start(bf16[640,128]{1,0:T(8,128)(2,1)S(1)} %shard_map.163.a_ref), channel_id=1, source_target_pairs={{0,384},{128,0},{256,128},{384,256},{1,385},{129,1},{257,129},{385... | collective-permute-start | bytes 491528 | tf_op jit(solution)/shard_map/ppermute | solution.py:363
  16.0 9.3 %copy-start.12 = (f32[5,128]{1,0:T(8,128)S(1)}, f32[5,128]{1,0:T(8,128)}, u32[]{:S(2)}) copy-start(f32[5,128]{1,0:T(8,128)} %param.23) | copy-start | bytes 7684
  16.0 11.5 %collective-permute-start.3 = (bf16[32,128]{1,0:T(8,128)(2,1)S(1)}, bf16[32,128]{1,0:T(8,128)(2,1)S(1)}, u32[]{:S(2)}, u32[]{:S(2)}) collective-permute-start(bf16[32,128]{1,0:T(8,128)(2,1)S(1)} %pad_maximum_fusion), channel_id=1, source_target_pairs={{0,32},{32,0},{1,33},{33,1},{2,34},{34,2},{3,35},{35,3},{4,36},{36... | collective-permute-start | bytes 24584 | tf_op jit(solution)/shard_map/ppermute | solution.py:351
  25.9 0.9 copy-start.4
  25.9 0.9 copy-start.8
  29.1 24.7 %copy-start.9 = (s32[64]{0:T(128)S(1)}, s32[64]{0:T(128)}, u32[]{:S(2)}) copy-start(s32[64]{0:T(128)} %offset_ref.1) | copy-start | bytes 772
  29.1 24.7 %all-to-all-start = ((bf16[32,64,128]{2,1,0:T(8,128)(2,1)}), bf16[32,64,128]{2,1,0:T(8,128)(2,1)S(1)}, u32[]{:S(2)}, u32[]{:S(2)}) async-start(bf16[32,64,128]{2,1,0:T(8,128)(2,1)} %broadcast_in_dim.8), calls=%async_computation | async-start | bytes 1048576 | tf_op jit(solution)/shard_map/all_to_all | solution.py:390
  39.5 4.0 %collective-permute-start.4 = (bf16[2,4,320,128]{3,2,1,0:T(8,128)(2,1)S(1)}, bf16[2,4,320,128]{3,2,1,0:T(8,128)(2,1)S(1)}, u32[]{:S(2)}, u32[]{:S(2)}) collective-permute-start(bf16[2,4,320,128]{3,2,1,0:T(8,128)(2,1)S(1)} %shard_map.164.mine_ref), channel_id=1, source_target_pairs={{0,64},{64,0},{1,65},{65,1},{2,66},{66,2},{3,67},{67,3},{4,68},{68... | collective-permute-start | bytes 1966088 | tf_op jit(solution)/shard_map/ppermute | solution.py:389
  70.5 0.9 copy-start.10
  71.3 52.0 %copy-start.6 = (bf16[640,128]{1,0:T(8,128)(2,1)S(1)}, bf16[640,128]{1,0:T(8,128)(2,1)}, u32[]{:S(2)}) copy-start(bf16[640,128]{1,0:T(8,128)(2,1)} %vp_ref.1) | copy-start | bytes 491524
  114.5 8.9 %copy-start = (bf16[128,640]{1,0:T(8,128)(2,1)S(1)}, bf16[128,640]{1,0:T(8,128)(2,1)}, u32[]{:S(2)}) copy-start(bf16[128,640]{1,0:T(8,128)(2,1)} %rq_ref.3) | copy-start | bytes 491524
  114.5 8.9 %copy-start.1 = (bf16[128,640]{1,0:T(8,128)(2,1)S(1)}, bf16[128,640]{1,0:T(8,128)(2,1)}, u32[]{:S(2)}) copy-start(bf16[128,640]{1,0:T(8,128)(2,1)} %rk_ref.3) | copy-start | bytes 491524
  114.5 8.9 %copy-start.2 = (bf16[128,640]{1,0:T(8,128)(2,1)S(1)}, bf16[128,640]{1,0:T(8,128)(2,1)}, u32[]{:S(2)}) copy-start(bf16[128,640]{1,0:T(8,128)(2,1)} %rv_ref.3) | copy-start | bytes 491524
  114.5 8.9 %copy-start.5 = (bf16[640,128]{1,0:T(8,128)(2,1)S(1)}, bf16[640,128]{1,0:T(8,128)(2,1)}, u32[]{:S(2)}) copy-start(bf16[640,128]{1,0:T(8,128)(2,1)} %kp_ref.1) | copy-start | bytes 491524
  125.3 20.2 %all-to-all-start.4 = ((bf16[32,48,128]{2,1,0:T(8,128)(2,1)}), bf16[32,48,128]{2,1,0:T(8,128)(2,1)S(1)}, u32[]{:S(2)}, u32[]{:S(2)}) async-start(bf16[32,48,128]{2,1,0:T(8,128)(2,1)} %get-tuple-element.194), calls=%async_computation.4 | async-start | bytes 786432 | tf_op jit(solution)/shard_map/all_to_all | solution.py:445
  132.3 4.0 %collective-permute-start.5 = (f32[4,320,128]{2,1,0:T(8,128)S(1)}, f32[4,320,128]{2,1,0:T(8,128)S(1)}, u32[]{:S(2)}, u32[]{:S(2)}) collective-permute-start(f32[4,320,128]{2,1,0:T(8,128)S(1)} %get-tuple-element.196), channel_id=1, source_target_pairs={{0,64},{64,0},{1,65},{65,1},{2,66},{66,2},{3,67},{67,3},{4,68},{68... | collective-permute-start | bytes 1966088 | tf_op jit(solution)/shard_map/ppermute | solution.py:444
  146.1 3.7 %copy-start.11 = (f32[4,320,128]{2,1,0:T(8,128)S(1)}, f32[4,320,128]{2,1,0:T(8,128)}, u32[]{:S(2)}) copy-start(f32[4,320,128]{2,1,0:T(8,128)} %copy-done.10) | copy-start | bytes 1966084
  146.2 9.8 %collective-permute-start.6 = (f32[48,128]{1,0:T(8,128)S(1)}, f32[48,128]{1,0:T(8,128)S(1)}, u32[]{:S(2)}, u32[]{:S(2)}) collective-permute-start(f32[48,128]{1,0:T(8,128)S(1)} %shard_map.170), channel_id=1, source_target_pairs={{0,32},{32,0},{1,33},{33,1},{2,34},{34,2},{3,35},{35,3},{4,36},{36... | collective-permute-start | bytes 73736 | tf_op jit(solution)/shard_map/ppermute | solution.py:459
  157.5 19.6 %all-to-all-start.5 = ((bf16[32,48,128]{2,1,0:T(8,128)(2,1)}), bf16[32,48,128]{2,1,0:T(8,128)(2,1)S(1)}, u32[]{:S(2)}, u32[]{:S(2)}) async-start(bf16[32,48,128]{2,1,0:T(8,128)(2,1)} %shard_map.171), calls=%async_computation.5 | async-start | bytes 786432 | tf_op jit(solution)/shard_map/all_to_all | solution.py:475
  163.8 9.6 %collective-permute-start.7 = (bf16[320,128]{1,0:T(8,128)(2,1)S(1)}, bf16[320,128]{1,0:T(8,128)(2,1)S(1)}, u32[]{:S(2)}, u32[]{:S(2)}) collective-permute-start(bf16[320,128]{1,0:T(8,128)(2,1)S(1)} %get-tuple-element.210), channel_id=1, source_target_pairs={{0,128},{128,256},{256,384},{384,0},{1,129},{129,257},{257,385},{3... | collective-permute-start | bytes 245768 | tf_op jit(solution)/shard_map/ppermute | solution.py:472
  166.8 8.8 %collective-permute-start.8 = (bf16[320,128]{1,0:T(8,128)(2,1)S(1)}, bf16[320,128]{1,0:T(8,128)(2,1)S(1)}, u32[]{:S(2)}, u32[]{:S(2)}) collective-permute-start(bf16[320,128]{1,0:T(8,128)(2,1)S(1)} %get-tuple-element.211), channel_id=1, source_target_pairs={{0,256},{128,384},{256,0},{384,128},{1,257},{129,385},{257,1},{385... | collective-permute-start | bytes 245768 | tf_op jit(solution)/shard_map/ppermute | solution.py:472
  169.3 7.2 %collective-permute-start.9 = (bf16[320,128]{1,0:T(8,128)(2,1)S(1)}, bf16[320,128]{1,0:T(8,128)(2,1)S(1)}, u32[]{:S(2)}, u32[]{:S(2)}) collective-permute-start(bf16[320,128]{1,0:T(8,128)(2,1)S(1)} %get-tuple-element.212), channel_id=1, source_target_pairs={{0,384},{128,0},{256,128},{384,256},{1,385},{129,1},{257,129},{385... | collective-permute-start | bytes 245768 | tf_op jit(solution)/shard_map/ppermute | solution.py:472

commit v4 on v3

--- a/solution.py
+++ b/solution.py
@@ -110,50 +110,45 @@
 
 
 def stats_kernel(
-    blocks, rows, query_rows, block_rows, factor,
-    where_ref, offset_ref, mine_ref, other_ref, kv_ref, delta_ref, out_ref,
+    blocks, rows, query_rows, block_rows, factor, where_ref, offset_ref, rows_ref, kv_ref, out_ref,
 ):
-    shard, place, core = where_ref[0], where_ref[2], where_ref[3]
-    width = 2 * mine_ref.shape[2]
+    shard, place = where_ref[0], where_ref[2]
+    width = 2 * rows_ref.shape[2]
     lines = width // 128
     full = shard // blocks
     pos = row_positions(where_ref, offset_ref, width, query_rows, block_rows)
     scale = factor * LOG2E
-    count, total_lines = out_ref.shape[0], out_ref.shape[1]
-    out_ref[:, CHIPS * lines :, :] = jnp.broadcast_to(
-        delta_ref[...][None], (count, total_lines - CHIPS * lines, 128)
-    )
-    for n in range(CORES):
-        for t in range(CHIPS // 2):
-            q = tile((mine_ref, other_ref), 0, n, t)
-
-            def chunk(j, carry, masked=False):
-                top, total = carry
-                s = dot_nt(cache_slice(kv_ref, j, blocks, rows, 0), q)
-                if masked:
-                    seen = key_positions(place, j, blocks, rows, block_rows) <= pos
-                    s = jnp.where(seen, s, LOW)
-                new = jnp.maximum(top, jnp.max(s, axis=0, keepdims=True))
-                p = jnp.exp2((s - new) * scale)
-                if masked:
-                    p = jnp.where(seen, p, 0.0)
-                total = total * jnp.exp2((top - new) * scale) + jnp.sum(p, axis=0, keepdims=True)
-                return new, total
-
-            start = (jnp.full((1, width), LOW, F32), jnp.zeros((1, width), F32))
-            top, total = chunk(full, lax.fori_loop(0, full, chunk, start), masked=True)
-            lse = jnp.where(total > 0.0, top * factor + jnp.log(total), LOW)
-            line = lax.rem(core + n, CORES) * (CHIPS // 2 * lines) + t * lines
-            for m in range(lines):
-                out_ref[:, pl.ds(line + m, 1), :] = jnp.broadcast_to(
-                    lse[:, m * 128 : (m + 1) * 128][None], (count, 1, 128)
-                )
+    tiles = range(CHIPS // 2)
+
+    def chunk(j, carry, masked=False):
+        keys = cache_slice(kv_ref, j, blocks, rows, 0)
+        if masked:
+            seen = key_positions(place, j, blocks, rows, block_rows) <= pos
+        out = []
+        for t, (top, total) in zip(tiles, carry):
+            s = dot_nt(keys, tile((rows_ref,), 0, 0, t))
+            if masked:
+                s = jnp.where(seen, s, LOW)
+            new = jnp.maximum(top, jnp.max(s, axis=0, keepdims=True))
+            p = jnp.exp2((s - new) * scale)
+            if masked:
+                p = jnp.where(seen, p, 0.0)
+            total = total * jnp.exp2((top - new) * scale) + jnp.sum(p, axis=0, keepdims=True)
+            out.append((new, total))
+        return tuple(out)
+
+    start = ((jnp.full((1, width), LOW, F32), jnp.zeros((1, width), F32)),) * len(tiles)
+    done = chunk(full, lax.fori_loop(0, full, chunk, start), masked=True)
+    for t, (top, total) in zip(tiles, done):
+        lse = jnp.where(total > 0.0, top * factor + jnp.log(total), LOW)
+        for m in range(lines):
+            out_ref[t * lines + m : t * lines + m + 1, :] = lse[:, m * 128 : (m + 1) * 128]
 
 
 def grads_kernel(
     blocks, rows, query_rows, block_rows, factor,
     where_ref, offset_ref, mine_ref, other_ref, kv_ref, log_ref, delta_ref,
-    dkv_ref, dq_own_ref, dq_other_ref, dk_total, dv_total,
+    dkv_ref, dq_own_ref, dq_other_ref, dq_total,
 ):
     shard, place, core = where_ref[0], where_ref[2], where_ref[3]
     flat = mine_ref.shape[2]
@@ -162,40 +157,48 @@
     full = shard // blocks
     pos = row_positions(where_ref, offset_ref, width, query_rows, block_rows)
     scale = factor * LOG2E
-    dk_total[...] = jnp.zeros_like(dk_total)
-    dv_total[...] = jnp.zeros_like(dv_total)
-    for n in range(CORES):
-        for t in range(CHIPS // 2):
+    tiles = [(n, t) for n in range(CORES) for t in range(CHIPS // 2)]
+    dq_total[...] = jnp.zeros_like(dq_total)
+
+    def chunk(j, masked=False):
+        keys = cache_slice(kv_ref, j, blocks, rows, 0)
+        values = cache_slice(kv_ref, j, blocks, rows, 1)
+        if masked:
+            seen = key_positions(place, j, blocks, rows, block_rows) <= pos
+        dk = dv = 0.0
+        for i, (n, t) in enumerate(tiles):
             q = tile((mine_ref, other_ref), 0, n, t)
             g = tile((mine_ref, other_ref), 1, n, t)
             at_core = lax.rem(core + n, CORES)
-            log_total = log_ref[at_core, t] * LOG2E
-            delta = delta_ref[at_core, t]
-
-            def chunk(j, dq, masked=False):
-                keys = cache_slice(kv_ref, j, blocks, rows, 0)
-                values = cache_slice(kv_ref, j, blocks, rows, 1)
-                p = jnp.exp2(dot_nt(keys, q) * scale - log_total)
-                if masked:
-                    seen = key_positions(place, j, blocks, rows, block_rows) <= pos
-                    p = jnp.where(seen, p, 0.0)
-                ds = (p * (dot_nt(values, g) - delta)).astype(BF)
-                at = pl.ds(pl.multiple_of(j * size, size), size)
-                dk_total[at, :] += dot_nn(ds, q)
-                dv_total[at, :] += dot_nn(p.astype(BF), g)
-                return dq + dot_tn(keys, ds)
-
-            dq = lax.fori_loop(0, full, chunk, jnp.zeros((kv_ref.shape[-1], width), F32))
-            dq = chunk(full, dq, masked=True).T
-            dq_ref = (dq_own_ref, dq_other_ref)[n]
-            for m in range(2):
-                dq_ref[2 * t + m] = dq[m * flat : (m + 1) * flat]
-    per = kv_ref.shape[0] // blocks
-    for j in range(HALVES * per):
-        at = slice(j * size, (j + 1) * size)
-        to = slice(j * blocks, (j + 1) * blocks)
-        dkv_ref[to, 0:rows, :] = dk_total[at, :].astype(BF).reshape(blocks, rows, -1)
-        dkv_ref[to, rows : 2 * rows, :] = dv_total[at, :].astype(BF).reshape(blocks, rows, -1)
+            p = jnp.exp2(dot_nt(keys, q) * scale - log_ref[at_core, t] * LOG2E)
+            if masked:
+                p = jnp.where(seen, p, 0.0)
+            ds = (p * (dot_nt(values, g) - delta_ref[at_core, t])).astype(BF)
+            dk = dk + dot_nn(ds, q)
+            dv = dv + dot_nn(p.astype(BF), g)
+            dq_total[i] += dot_tn(keys, ds)
+        at = pl.ds(pl.multiple_of(j * blocks, blocks), blocks)
+        dkv_ref[at, 0:rows, :] = dk.astype(BF).reshape(blocks, rows, -1)
+        dkv_ref[at, rows : 2 * rows, :] = dv.astype(BF).reshape(blocks, rows, -1)
+
+    def step(j, _):
+        chunk(j)
+        return 0
+
+    lax.fori_loop(0, full, step, 0)
+    chunk(full, masked=True)
+
+    def clear(j, _):
+        at = pl.ds(pl.multiple_of(j * blocks, blocks), blocks)
+        dkv_ref[at] = jnp.zeros((blocks, 2 * rows, kv_ref.shape[-1]), BF)
+        return 0
+
+    lax.fori_loop(full + 1, dkv_ref.shape[0] // blocks, clear, 0)
+    for i, (n, t) in enumerate(tiles):
+        dq = dq_total[i].T
+        dq_ref = (dq_own_ref, dq_other_ref)[n]
+        for m in range(2):
+            dq_ref[2 * t + m] = dq[m * flat : (m + 1) * flat]
 
 
 def pieces_kernel(where_ref, own_ref, other_ref, mine_ref, a_ref, b_ref, c_ref):
@@ -341,7 +344,7 @@
     lines = width // 128
     rows = block_rows // secs
     factor = 1.0 / math.sqrt(head)
-    blocks = 16
+    blocks = 32
     sizes = (blocks, rows, query_rows, block_rows, factor)
     where = jnp.stack([shard, chip, place, core]).astype(jnp.int32)
 
@@ -385,17 +388,27 @@
 
     env = (where, offsets, delta, cum, cum_t, from_start, to_end, extra)
     mine = call(gather_kernel, shape((2, CHIPS, flat, head), BF), (where,), tuple(parts))
-    mine, kv, env = lax.optimization_barrier((mine, kv, env))
+    kv, env = lax.optimization_barrier((kv, env))
+    kv = lax.all_to_all(kv, PLANE_AXES, 0, 0, tiled=True)
+    kv, env = lax.optimization_barrier((kv, env))
+    where, offsets, delta = env[:3]
     other = lax.ppermute(mine, "core", [(0, 1), (1, 0)])
-    kv = lax.all_to_all(kv, PLANE_AXES, 0, 0, tiled=True)
-    mine, other, kv, env = lax.optimization_barrier((mine, other, kv, env))
-    where, offsets, delta = env[:3]
-
-    both = call(
-        functools.partial(stats_kernel, *sizes),
-        shape((secs, 32, head), F32), (where, offsets), (mine, other, kv, delta),
-        flops=1 << 30,
-    )
+
+    stats = [
+        call(
+            functools.partial(stats_kernel, *sizes),
+            shape((CHIPS // 2 * lines, head), F32), (where, offsets), (part, kv),
+            flops=4 << 30,
+        )
+        for part in (mine, other)
+    ]
+    own_stats, other_stats = stats
+    both = jnp.concatenate([
+        jnp.where(core == 0, own_stats, other_stats),
+        jnp.where(core == 0, other_stats, own_stats),
+        delta,
+    ])
+    both = jnp.broadcast_to(both[None], (secs,) + both.shape)
     both, (mine, other, kv, env) = pinned_exchange(both, ("zl", "core"), (mine, other, kv, env))
     where, offsets = env[:2]
     tiles = (CORES, CHIPS // 2, 1, width)
@@ -411,19 +424,15 @@
         (shape((shards, 2 * rows, head), BF),) + (shape((CHIPS, flat, head), F32),) * 2,
         (where, offsets),
         (mine, other, kv, log_total, deltas),
-        scratch=[pltpu.VMEM((shards * rows, head), F32)] * 2,
+        scratch=[pltpu.VMEM((CORES * CHIPS // 2, head, width), F32)],
         flops=4 << 30,
     )
-    terms, (dq_own, dq_other, env) = pinned_exchange(
-        dkv, ("zh",) + PLANE_AXES, (dq_own, dq_other, env)
-    )
+    terms, env = pinned_exchange(dkv, ("zh",) + PLANE_AXES, env)
     total = call(
         functools.partial(total_kernel, factor),
         shape((secs, 2 * rows, head), BF), (), (terms,),
     )
-    whole, (dq_own, dq_other, env) = pinned_exchange(
-        total, ("zl", "core"), (dq_own, dq_other, env)
-    )
+    whole, env = pinned_exchange(total, ("zl", "core"), env)
     where, offsets, delta, cum, cum_t, from_start, to_end, extra = env
 
     cache_key_grad, cache_value_grad, out_grad, send = call(

time: 180 us -> 173 us (0.961)
  waiting for transfers between devices: 32.3 us -> 26.8 us
  blocking collectives: 62.2 us -> 59.7 us
  Pallas kernels: 14.8 us -> 17.1 us
    all_to_all x1, waiting for transfers between devices: 10.3 us -> 0.01 us  [body(): kv = lax.all_to_all(kv, PLANE_AXES, 0, 0, tiled=True)]
    ppermute x3, waiting for transfers between devices: 0.01 us -> 6.47 us  [body(): lax.ppermute(own, 'zl', [(i, (i - k) % CHIPS) for i in range(CHIPS)])]
    all_to_all x3, blocking collectives: 62.2 us -> 59.7 us  [pinned_exchange(): array = lax.all_to_all(array, axes, 0, 0, tiled=True)]
    pallas_call x12 -> x13, Pallas kernels: 14.8 us -> 17.1 us  [call(): pl.pallas_call(kernel, out_shape=outs, in_specs=[smem] * len(in_smem) + [...]
  transfers between devices with their start and end apart: 13 -> 13, of which waited for: 7 -> 8; matrix products, arithmetic and copies ran while one was open for 1% -> 0% of each run, Pallas kernels for 1% -> 3%
where the time goes in v4:
time: 173 us; the launch traced here: 172 us
  starting transfers between devices  62.6 us (36%)
  blocking collectives  59.7 us (35%)
  waiting for transfers between devices  26.8 us (15%)
  Pallas kernels  17.1 us (10%)
  local copies, waits for them, and re-layouts  4.03 us (2%)
    all_to_all x3, blocking collectives, pinned_exchange(): array = lax.all_to_all(array, axes, 0, 0, tiled=True)  59.7 us
    pallas_call x13, Pallas kernels, call(): pl.pallas_call(kernel, out_shape=outs, in_specs=[smem] * len(in_smem) + [...  17.1 us
    ppermute x1, starting transfers between devices, body(): kv_other = lax.ppermute(kv_own, 'zh', [(0, 1), (1, 0)])  11 us
    ppermute x3, starting transfers between devices, body(): lax.ppermute(own, 'zl', [(i, (i - k) % CHIPS) for i in range(CHIPS)])  11 us
    all_to_all x1, starting transfers between devices, body(): kv = lax.all_to_all(kv, PLANE_AXES, 0, 0, tiled=True)  10.4 us
    ppermute x3, starting transfers between devices, body(): lax.ppermute(piece, 'zl', [(i, (i + k) % CHIPS) for i in range(CHIPS)])  9.56 us
    all_to_all x1, waiting for transfers between devices, body(): part = lax.all_to_all(send, PLANE_AXES, 0, 0, tiled=True)  9.23 us
    all_to_all x1, starting transfers between devices, body(): part = lax.all_to_all(send, PLANE_AXES, 0, 0, tiled=True)  7.02 us
  transfers between devices with their start and end apart: 13, of which 8 were waited for; matrix products, arithmetic and copies ran while one was open for 0% of the time, Pallas kernels for 3%

profile of v4, /device:TPU:2, one launch (start us, length us, event | category | flops | bytes accessed | tf_op | source)
XLA Modules:
  0.0 171.9 jit_solution(13476768905368006408)
XLA Ops:
  1.4 11.0 %collective-permute-start = (bf16[32,128]{1,0:T(8,128)(2,1)S(1)}, bf16[32,128]{1,0:T(8,128)(2,1)S(1)}, u32[]{:S(2)}, u32[]{:S(2)}) collective-permute-start(bf16[32,128]{1,0:T(8,128)(2,1)S(1)} %pad_maximum_fusion.1), channel_id=1, source_target_pairs={{0,32},{32,0},{1,33},{33,1},{2,34},{34,2},{3,35},{35,3},{4,36},{36... | collective-permute-start | bytes 24584 | tf_op jit(solution)/shard_map/ppermute | solution.py:354
  13.9 0.7 shard_map.163
  14.7 0.9 broadcast_in_dim.10
  15.6 10.4 %all-to-all-start = ((bf16[32,64,128]{2,1,0:T(8,128)(2,1)}), bf16[32,64,128]{2,1,0:T(8,128)(2,1)S(1)}, u32[]{:S(2)}, u32[]{:S(2)}) async-start(bf16[32,64,128]{2,1,0:T(8,128)(2,1)} %broadcast_in_dim.10), calls=%async_computation | async-start | bytes 1048576 | tf_op jit(solution)/shard_map/all_to_all | solution.py:392
  26.1 3.4 %collective-permute-start.3 = (bf16[640,128]{1,0:T(8,128)(2,1)S(1)}, bf16[640,128]{1,0:T(8,128)(2,1)S(1)}, u32[]{:S(2)}, u32[]{:S(2)}) collective-permute-start(bf16[640,128]{1,0:T(8,128)(2,1)S(1)} %shard_map.164.a_ref), channel_id=1, source_target_pairs={{0,128},{128,256},{256,384},{384,0},{1,129},{129,257},{257,385},{3... | collective-permute-start | bytes 491528 | tf_op jit(solution)/shard_map/ppermute | solution.py:366
  29.5 4.3 %collective-permute-start.2 = (bf16[640,128]{1,0:T(8,128)(2,1)S(1)}, bf16[640,128]{1,0:T(8,128)(2,1)S(1)}, u32[]{:S(2)}, u32[]{:S(2)}) collective-permute-start(bf16[640,128]{1,0:T(8,128)(2,1)S(1)} %shard_map.164.a_ref), channel_id=1, source_target_pairs={{0,256},{128,384},{256,0},{384,128},{1,257},{129,385},{257,1},{385... | collective-permute-start | bytes 491528 | tf_op jit(solution)/shard_map/ppermute | solution.py:366
  33.8 3.4 %collective-permute-start.1 = (bf16[640,128]{1,0:T(8,128)(2,1)S(1)}, bf16[640,128]{1,0:T(8,128)(2,1)S(1)}, u32[]{:S(2)}, u32[]{:S(2)}) collective-permute-start(bf16[640,128]{1,0:T(8,128)(2,1)S(1)} %shard_map.164.a_ref), channel_id=1, source_target_pairs={{0,384},{128,0},{256,128},{384,256},{1,385},{129,1},{257,129},{385... | collective-permute-start | bytes 491528 | tf_op jit(solution)/shard_map/ppermute | solution.py:366
  37.1 5.1 %collective-permute-done.2.c_ref = bf16[640,128]{1,0:T(8,128)(2,1)S(1)} collective-permute-done((bf16[640,128]{1,0:T(8,128)(2,1)S(1)}, bf16[640,128]{1,0:T(8,128)(2,1)S(1)}, u32[]{:S(2)}, u32[]{:S(2)}) %collective-permute-start.2) | collective-permute-done | bytes 163872 | tf_op jit(solution)/shard_map/ppermute | solution.py:366
  42.2 1.4 collective-permute-done.1.b_ref
  44.2 1.9 %collective-permute-start.4 = (bf16[2,4,320,128]{3,2,1,0:T(8,128)(2,1)S(1)}, bf16[2,4,320,128]{3,2,1,0:T(8,128)(2,1)S(1)}, u32[]{:S(2)}, u32[]{:S(2)}) collective-permute-start(bf16[2,4,320,128]{3,2,1,0:T(8,128)(2,1)S(1)} %shard_map.165.rows_ref.mine_ref), channel_id=1, source_target_pairs={{0,64},{64,0},{1,65},{65,1},{2,66},{66,2},{3,67},{67,3},{4,68},{68... | collective-permute-start | bytes 1966088 | tf_op jit(solution)/shard_map/ppermute | solution.py:395
  46.2 1.7 shard_map.166
  48.2 1.7 shard_map.167
  49.9 11.3 %all_to_all.30 = f32[8,32,128]{2,1,0:T(8,128)S(1)} all-to-all(f32[8,32,128]{2,1,0:T(8,128)S(1)} %broadcast_in_dim.11), channel_id=1, replica_groups=mesh['zl'=4,'core'=2,'zh'=2,'x'=4,'y'=8] {'zl','core'}, dimensions={0} | all-to-all | bytes 262144 | tf_op jit(solution)/shard_map/all_to_all | solution.py:56
  61.4 5.1 %shard_map.168 = (bf16[64,32,128]{2,1,0:T(8,128)(2,1)S(1)}, f32[4,320,128]{2,1,0:T(8,128)S(1)}, f32[4,320,128]{2,1,0:T(8,128)S(1)}) custom-call(s32[4]{0:T(128)S(1)} %pad_add_fusion.where_ref, s32[64]{0:T(128)S(1)} %copy-done.8, bf16[2,4,320,128]{3,2,1,0:T(8,128)(2,1)S(1)} %shard_map.165.rows_ref.mine_ref, ...), custom_call_target="tpu_custom_call" | custom-call | flops 4294967296 | bytes 1048576 | tf_op jit(solution)/shard_map/pallas_call | solution.py:39
  66.6 0.9 copy-done.9
  67.4 39.6 %all_to_all.31.terms_ref = bf16[64,32,128]{2,1,0:T(8,128)(2,1)S(1)} all-to-all(bf16[64,32,128]{2,1,0:T(8,128)(2,1)S(1)} %get-tuple-element.144), channel_id=1, replica_groups=mesh['zl'=4,'core'=2,'zh'=2,'x'=4,'y'=8] {'zh','x','y'}, dimensions={0} | all-to-all | bytes 1048576 | tf_op jit(solution)/shard_map/all_to_all | solution.py:56
  107.1 8.7 %all_to_all.32.whole_ref = bf16[8,32,128]{2,1,0:T(8,128)(2,1)S(1)} all-to-all(bf16[8,32,128]{2,1,0:T(8,128)(2,1)S(1)} %shard_map.169), channel_id=1, replica_groups=mesh['zl'=4,'core'=2,'zh'=2,'x'=4,'y'=8] {'zl','core'}, dimensions={0} | all-to-all | bytes 131072 | tf_op jit(solution)/shard_map/all_to_all | solution.py:56
  115.9 2.0 %shard_map.170 = (bf16[128,128]{1,0:T(8,128)(2,1)}, bf16[128,128]{1,0:T(8,128)(2,1)}, bf16[128,640]{1,0:T(8,128)(2,1)S(1)}, bf16[32,48,128]{2,1,0:T(8,128)(2,1)}) custom-call(bf16[8,32,128]{2,1,0:T(8,128)(2,1)S(1)} %all_to_all.32.whole_ref, bf16[640,128]{1,0:T(8,128)(2,1)S(1)} %copy-done.4, bf16[640,128]{1,0:T(8,128)(2,1)S(1)} %copy-done.5, ...), custom_call_target="tpu_custom_call" | custom-call | flops 134217728 | bytes 1048576 | tf_op jit(solution)/shard_map/pallas_call | solution.py:39
  117.9 7.0 %all-to-all-start.4 = ((bf16[32,48,128]{2,1,0:T(8,128)(2,1)}), bf16[32,48,128]{2,1,0:T(8,128)(2,1)S(1)}, u32[]{:S(2)}, u32[]{:S(2)}) async-start(bf16[32,48,128]{2,1,0:T(8,128)(2,1)} %get-tuple-element.172), calls=%async_computation.4 | async-start | bytes 786432 | tf_op jit(solution)/shard_map/all_to_all | solution.py:454
  124.9 1.9 %collective-permute-start.5 = (f32[4,320,128]{2,1,0:T(8,128)S(1)}, f32[4,320,128]{2,1,0:T(8,128)S(1)}, u32[]{:S(2)}, u32[]{:S(2)}) collective-permute-start(f32[4,320,128]{2,1,0:T(8,128)S(1)} %get-tuple-element.174), channel_id=1, source_target_pairs={{0,64},{64,0},{1,65},{65,1},{2,66},{66,2},{3,67},{67,3},{4,68},{68... | collective-permute-start | bytes 1966088 | tf_op jit(solution)/shard_map/ppermute | solution.py:453
  126.8 2.1 %collective-permute-done.5.other_ref = f32[4,320,128]{2,1,0:T(8,128)S(1)} collective-permute-done((f32[4,320,128]{2,1,0:T(8,128)S(1)}, f32[4,320,128]{2,1,0:T(8,128)S(1)}, u32[]{:S(2)}, u32[]{:S(2)}) %collective-permute-start.5) | collective-permute-done | bytes 655392 | tf_op jit(solution)/shard_map/ppermute | solution.py:453
  128.9 9.2 %all-to-all-done.4.part_ref = bf16[32,48,128]{2,1,0:T(8,128)(2,1)S(1)} async-done(((bf16[32,48,128]{2,1,0:T(8,128)(2,1)}), bf16[32,48,128]{2,1,0:T(8,128)(2,1)S(1)}, u32[]{:S(2)}, u32[]{:S(2)}) %all-to-all-start.4) | async-done | bytes 393248 | tf_op jit(solution)/shard_map/all_to_all | solution.py:454
  138.8 3.5 %collective-permute-start.6 = (f32[48,128]{1,0:T(8,128)S(1)}, f32[48,128]{1,0:T(8,128)S(1)}, u32[]{:S(2)}, u32[]{:S(2)}) collective-permute-start(f32[48,128]{1,0:T(8,128)S(1)} %shard_map.171), channel_id=1, source_target_pairs={{0,32},{32,0},{1,33},{33,1},{2,34},{34,2},{3,35},{35,3},{4,36},{36... | collective-permute-start | bytes 73736 | tf_op jit(solution)/shard_map/ppermute | solution.py:468
  142.9 5.6 %collective-permute-done.6.other_ref = f32[48,128]{1,0:T(8,128)S(1)} collective-permute-done((f32[48,128]{1,0:T(8,128)S(1)}, f32[48,128]{1,0:T(8,128)S(1)}, u32[]{:S(2)}, u32[]{:S(2)}) %collective-permute-start.6) | collective-permute-done | bytes 24608 | tf_op jit(solution)/shard_map/ppermute | solution.py:468
  148.5 1.6 shard_map.172
  150.1 6.3 %all-to-all-start.5 = ((bf16[32,48,128]{2,1,0:T(8,128)(2,1)}), bf16[32,48,128]{2,1,0:T(8,128)(2,1)S(1)}, u32[]{:S(2)}, u32[]{:S(2)}) async-start(bf16[32,48,128]{2,1,0:T(8,128)(2,1)} %shard_map.172), calls=%async_computation.5 | async-start | bytes 786432 | tf_op jit(solution)/shard_map/all_to_all | solution.py:484
  156.4 3.0 %collective-permute-start.7 = (bf16[320,128]{1,0:T(8,128)(2,1)S(1)}, bf16[320,128]{1,0:T(8,128)(2,1)S(1)}, u32[]{:S(2)}, u32[]{:S(2)}) collective-permute-start(bf16[320,128]{1,0:T(8,128)(2,1)S(1)} %get-tuple-element.188), channel_id=1, source_target_pairs={{0,128},{128,256},{256,384},{384,0},{1,129},{129,257},{257,385},{3... | collective-permute-start | bytes 245768 | tf_op jit(solution)/shard_map/ppermute | solution.py:481
  159.4 2.5 %collective-permute-start.8 = (bf16[320,128]{1,0:T(8,128)(2,1)S(1)}, bf16[320,128]{1,0:T(8,128)(2,1)S(1)}, u32[]{:S(2)}, u32[]{:S(2)}) collective-permute-start(bf16[320,128]{1,0:T(8,128)(2,1)S(1)} %get-tuple-element.189), channel_id=1, source_target_pairs={{0,256},{128,384},{256,0},{384,128},{1,257},{129,385},{257,1},{385... | collective-permute-start | bytes 245768 | tf_op jit(solution)/shard_map/ppermute | solution.py:481
  161.8 4.1 %collective-permute-start.9 = (bf16[320,128]{1,0:T(8,128)(2,1)S(1)}, bf16[320,128]{1,0:T(8,128)(2,1)S(1)}, u32[]{:S(2)}, u32[]{:S(2)}) collective-permute-start(bf16[320,128]{1,0:T(8,128)(2,1)S(1)} %get-tuple-element.190), channel_id=1, source_target_pairs={{0,384},{128,0},{256,128},{384,256},{1,385},{129,1},{257,129},{385... | collective-permute-start | bytes 245768 | tf_op jit(solution)/shard_map/ppermute | solution.py:481
  166.0 2.2 %collective-permute-done.8.b_ref = bf16[320,128]{1,0:T(8,128)(2,1)S(1)} collective-permute-done((bf16[320,128]{1,0:T(8,128)(2,1)S(1)}, bf16[320,128]{1,0:T(8,128)(2,1)S(1)}, u32[]{:S(2)}, u32[]{:S(2)}) %collective-permute-start.8) | collective-permute-done | bytes 81952 | tf_op jit(solution)/shard_map/ppermute | solution.py:481
  168.1 0.9 collective-permute-done.9.c_ref
  169.7 2.3 %shard_map.175 = (f32[128,640]{1,0:T(8,128)}, f32[128,640]{1,0:T(8,128)}, f32[128,640]{1,0:T(8,128)}) custom-call(bf16[128,640]{1,0:T(8,128)(2,1)S(1)} %copy-done, bf16[128,640]{1,0:T(8,128)(2,1)S(1)} %copy-done.1, bf16[128,640]{1,0:T(8,128)(2,1)S(1)} %copy-done.2, bf16[128,640]{1,0:T(8,128)(2,1)S(1)} %get-tuple-element.193.gr_ref, ...), custom_call_target="tpu_custom_call" | custom-call | flops 268435456 | bytes 1048576 | tf_op jit(solution)/shard_map/pallas_call | solution.py:39
  (66 shorter events, 5.4 us)
Async XLA Ops:
  1.4 11.1 %copy-start.11 = (f32[5,128]{1,0:T(8,128)S(1)}, f32[5,128]{1,0:T(8,128)}, u32[]{:S(2)}) copy-start(f32[5,128]{1,0:T(8,128)} %param.23) | copy-start | bytes 7684
  1.4 13.3 %collective-permute-start = (bf16[32,128]{1,0:T(8,128)(2,1)S(1)}, bf16[32,128]{1,0:T(8,128)(2,1)S(1)}, u32[]{:S(2)}, u32[]{:S(2)}) collective-permute-start(bf16[32,128]{1,0:T(8,128)(2,1)S(1)} %pad_maximum_fusion.1), channel_id=1, source_target_pairs={{0,32},{32,0},{1,33},{33,1},{2,34},{34,2},{3,35},{35,3},{4,36},{36... | collective-permute-start | bytes 24584 | tf_op jit(solution)/shard_map/ppermute | solution.py:354
  13.0 0.9 copy-start.3
  13.0 0.9 copy-start.7
  15.6 10.4 %copy-start.6 = (bf16[1,16,2560]{2,1,0:T(8,128)(2,1)S(1)}, bf16[1,16,2560]{2,1,0:T(8,128)(2,1)}, u32[]{:S(2)}) copy-start(bf16[1,16,2560]{2,1,0:T(8,128)(2,1)} %q_ref.1) | copy-start | bytes 245764
  15.6 30.5 %all-to-all-start = ((bf16[32,64,128]{2,1,0:T(8,128)(2,1)}), bf16[32,64,128]{2,1,0:T(8,128)(2,1)S(1)}, u32[]{:S(2)}, u32[]{:S(2)}) async-start(bf16[32,64,128]{2,1,0:T(8,128)(2,1)} %broadcast_in_dim.10), calls=%async_computation | async-start | bytes 1048576 | tf_op jit(solution)/shard_map/all_to_all | solution.py:392
  26.1 11.1 %collective-permute-start.3 = (bf16[640,128]{1,0:T(8,128)(2,1)S(1)}, bf16[640,128]{1,0:T(8,128)(2,1)S(1)}, u32[]{:S(2)}, u32[]{:S(2)}) collective-permute-start(bf16[640,128]{1,0:T(8,128)(2,1)S(1)} %shard_map.164.a_ref), channel_id=1, source_target_pairs={{0,128},{128,256},{256,384},{384,0},{1,129},{129,257},{257,385},{3... | collective-permute-start | bytes 491528 | tf_op jit(solution)/shard_map/ppermute | solution.py:366
  29.5 12.8 %collective-permute-start.2 = (bf16[640,128]{1,0:T(8,128)(2,1)S(1)}, bf16[640,128]{1,0:T(8,128)(2,1)S(1)}, u32[]{:S(2)}, u32[]{:S(2)}) collective-permute-start(bf16[640,128]{1,0:T(8,128)(2,1)S(1)} %shard_map.164.a_ref), channel_id=1, source_target_pairs={{0,256},{128,384},{256,0},{384,128},{1,257},{129,385},{257,1},{385... | collective-permute-start | bytes 491528 | tf_op jit(solution)/shard_map/ppermute | solution.py:366
  33.8 9.8 %collective-permute-start.1 = (bf16[640,128]{1,0:T(8,128)(2,1)S(1)}, bf16[640,128]{1,0:T(8,128)(2,1)S(1)}, u32[]{:S(2)}, u32[]{:S(2)}) collective-permute-start(bf16[640,128]{1,0:T(8,128)(2,1)S(1)} %shard_map.164.a_ref), channel_id=1, source_target_pairs={{0,384},{128,0},{256,128},{384,256},{1,385},{129,1},{257,129},{385... | collective-permute-start | bytes 491528 | tf_op jit(solution)/shard_map/ppermute | solution.py:366
  44.2 2.0 %copy-start.8 = (s32[64]{0:T(128)S(1)}, s32[64]{0:T(128)}, u32[]{:S(2)}) copy-start(s32[64]{0:T(128)} %offset_ref.2) | copy-start | bytes 772
  44.2 4.0 %collective-permute-start.4 = (bf16[2,4,320,128]{3,2,1,0:T(8,128)(2,1)S(1)}, bf16[2,4,320,128]{3,2,1,0:T(8,128)(2,1)S(1)}, u32[]{:S(2)}, u32[]{:S(2)}) collective-permute-start(bf16[2,4,320,128]{3,2,1,0:T(8,128)(2,1)S(1)} %shard_map.165.rows_ref.mine_ref), channel_id=1, source_target_pairs={{0,64},{64,0},{1,65},{65,1},{2,66},{66,2},{3,67},{67,3},{4,68},{68... | collective-permute-start | bytes 1966088 | tf_op jit(solution)/shard_map/ppermute | solution.py:395
  66.6 0.9 copy-start.9
  67.4 48.5 %copy-start.5 = (bf16[640,128]{1,0:T(8,128)(2,1)S(1)}, bf16[640,128]{1,0:T(8,128)(2,1)}, u32[]{:S(2)}) copy-start(bf16[640,128]{1,0:T(8,128)(2,1)} %vp_ref.1) | copy-start | bytes 491524
  107.0 8.8 %copy-start = (bf16[128,640]{1,0:T(8,128)(2,1)S(1)}, bf16[128,640]{1,0:T(8,128)(2,1)}, u32[]{:S(2)}) copy-start(bf16[128,640]{1,0:T(8,128)(2,1)} %rq_ref.3) | copy-start | bytes 491524
  107.0 8.8 %copy-start.1 = (bf16[128,640]{1,0:T(8,128)(2,1)S(1)}, bf16[128,640]{1,0:T(8,128)(2,1)}, u32[]{:S(2)}) copy-start(bf16[128,640]{1,0:T(8,128)(2,1)} %rk_ref.3) | copy-start | bytes 491524
  107.1 8.8 %copy-start.2 = (bf16[128,640]{1,0:T(8,128)(2,1)S(1)}, bf16[128,640]{1,0:T(8,128)(2,1)}, u32[]{:S(2)}) copy-start(bf16[128,640]{1,0:T(8,128)(2,1)} %rv_ref.3) | copy-start | bytes 491524
  107.1 8.9 %copy-start.4 = (bf16[640,128]{1,0:T(8,128)(2,1)S(1)}, bf16[640,128]{1,0:T(8,128)(2,1)}, u32[]{:S(2)}) copy-start(bf16[640,128]{1,0:T(8,128)(2,1)} %kp_ref.1) | copy-start | bytes 491524
  117.9 20.2 %all-to-all-start.4 = ((bf16[32,48,128]{2,1,0:T(8,128)(2,1)}), bf16[32,48,128]{2,1,0:T(8,128)(2,1)S(1)}, u32[]{:S(2)}, u32[]{:S(2)}) async-start(bf16[32,48,128]{2,1,0:T(8,128)(2,1)} %get-tuple-element.172), calls=%async_computation.4 | async-start | bytes 786432 | tf_op jit(solution)/shard_map/all_to_all | solution.py:454
  124.9 4.0 %collective-permute-start.5 = (f32[4,320,128]{2,1,0:T(8,128)S(1)}, f32[4,320,128]{2,1,0:T(8,128)S(1)}, u32[]{:S(2)}, u32[]{:S(2)}) collective-permute-start(f32[4,320,128]{2,1,0:T(8,128)S(1)} %get-tuple-element.174), channel_id=1, source_target_pairs={{0,64},{64,0},{1,65},{65,1},{2,66},{66,2},{3,67},{67,3},{4,68},{68... | collective-permute-start | bytes 1966088 | tf_op jit(solution)/shard_map/ppermute | solution.py:453
  138.6 3.7 %copy-start.10 = (f32[4,320,128]{2,1,0:T(8,128)S(1)}, f32[4,320,128]{2,1,0:T(8,128)}, u32[]{:S(2)}) copy-start(f32[4,320,128]{2,1,0:T(8,128)} %copy-done.9) | copy-start | bytes 1966084
  138.8 9.8 %collective-permute-start.6 = (f32[48,128]{1,0:T(8,128)S(1)}, f32[48,128]{1,0:T(8,128)S(1)}, u32[]{:S(2)}, u32[]{:S(2)}) collective-permute-start(f32[48,128]{1,0:T(8,128)S(1)} %shard_map.171), channel_id=1, source_target_pairs={{0,32},{32,0},{1,33},{33,1},{2,34},{34,2},{3,35},{35,3},{4,36},{36... | collective-permute-start | bytes 73736 | tf_op jit(solution)/shard_map/ppermute | solution.py:468
  150.1 19.6 %all-to-all-start.5 = ((bf16[32,48,128]{2,1,0:T(8,128)(2,1)}), bf16[32,48,128]{2,1,0:T(8,128)(2,1)S(1)}, u32[]{:S(2)}, u32[]{:S(2)}) async-start(bf16[32,48,128]{2,1,0:T(8,128)(2,1)} %shard_map.172), calls=%async_computation.5 | async-start | bytes 786432 | tf_op jit(solution)/shard_map/all_to_all | solution.py:484
  156.4 9.6 %collective-permute-start.7 = (bf16[320,128]{1,0:T(8,128)(2,1)S(1)}, bf16[320,128]{1,0:T(8,128)(2,1)S(1)}, u32[]{:S(2)}, u32[]{:S(2)}) collective-permute-start(bf16[320,128]{1,0:T(8,128)(2,1)S(1)} %get-tuple-element.188), channel_id=1, source_target_pairs={{0,128},{128,256},{256,384},{384,0},{1,129},{129,257},{257,385},{3... | collective-permute-start | bytes 245768 | tf_op jit(solution)/shard_map/ppermute | solution.py:481
  159.4 8.8 %collective-permute-start.8 = (bf16[320,128]{1,0:T(8,128)(2,1)S(1)}, bf16[320,128]{1,0:T(8,128)(2,1)S(1)}, u32[]{:S(2)}, u32[]{:S(2)}) collective-permute-start(bf16[320,128]{1,0:T(8,128)(2,1)S(1)} %get-tuple-element.189), channel_id=1, source_target_pairs={{0,256},{128,384},{256,0},{384,128},{1,257},{129,385},{257,1},{385... | collective-permute-start | bytes 245768 | tf_op jit(solution)/shard_map/ppermute | solution.py:481
  161.8 7.2 %collective-permute-start.9 = (bf16[320,128]{1,0:T(8,128)(2,1)S(1)}, bf16[320,128]{1,0:T(8,128)(2,1)S(1)}, u32[]{:S(2)}, u32[]{:S(2)}) collective-permute-start(bf16[320,128]{1,0:T(8,128)(2,1)S(1)} %get-tuple-element.190), channel_id=1, source_target_pairs={{0,384},{128,0},{256,128},{384,256},{1,385},{129,1},{257,129},{385... | collective-permute-start | bytes 245768 | tf_op jit(solution)/shard_map/ppermute | solution.py:481

commit v5 on v4

--- a/solution.py
+++ b/solution.py
@@ -98,10 +98,15 @@
     return (chunk * blocks + at // rows) * block_rows + place * rows + at % rows
 
 
+def cache_place(kv_ref, chunk, blocks, rows):
+    per = kv_ref.shape[0] // blocks
+    line = pl.multiple_of((chunk // per) * (2 * rows), 2 * rows)
+    return pl.ds(pl.multiple_of(lax.rem(chunk, per) * blocks, blocks), blocks), line
+
+
 def cache_slice(kv_ref, chunk, blocks, rows, values):
-    per = kv_ref.shape[0] // blocks
-    line = pl.multiple_of((chunk // per) * (2 * rows) + values * rows, rows)
-    at = pl.ds(lax.rem(chunk, per) * blocks, blocks)
+    at, line = cache_place(kv_ref, chunk, blocks, rows)
+    line = pl.multiple_of(line + values * rows, rows)
     return kv_ref[at, pl.ds(line, rows), :].reshape(blocks * rows, -1)
 
 
@@ -177,9 +182,9 @@
             dk = dk + dot_nn(ds, q)
             dv = dv + dot_nn(p.astype(BF), g)
             dq_total[i] += dot_tn(keys, ds)
-        at = pl.ds(pl.multiple_of(j * blocks, blocks), blocks)
-        dkv_ref[at, 0:rows, :] = dk.astype(BF).reshape(blocks, rows, -1)
-        dkv_ref[at, rows : 2 * rows, :] = dv.astype(BF).reshape(blocks, rows, -1)
+        at, line = cache_place(kv_ref, j, blocks, rows)
+        dkv_ref[at, pl.ds(line, rows), :] = dk.astype(BF).reshape(blocks, rows, -1)
+        dkv_ref[at, pl.ds(line + rows, rows), :] = dv.astype(BF).reshape(blocks, rows, -1)
 
     def step(j, _):
         chunk(j)
@@ -189,41 +194,53 @@
     chunk(full, masked=True)
 
     def clear(j, _):
-        at = pl.ds(pl.multiple_of(j * blocks, blocks), blocks)
-        dkv_ref[at] = jnp.zeros((blocks, 2 * rows, kv_ref.shape[-1]), BF)
+        at, line = cache_place(kv_ref, j, blocks, rows)
+        dkv_ref[at, pl.ds(line, 2 * rows), :] = jnp.zeros((blocks, 2 * rows, kv_ref.shape[-1]), BF)
         return 0
 
-    lax.fori_loop(full + 1, dkv_ref.shape[0] // blocks, clear, 0)
+    lax.fori_loop(full + 1, HALVES * kv_ref.shape[0] // blocks, clear, 0)
     for i, (n, t) in enumerate(tiles):
         dq = dq_total[i].T
         dq_ref = (dq_own_ref, dq_other_ref)[n]
         for m in range(2):
-            dq_ref[2 * t + m] = dq[m * flat : (m + 1) * flat]
-
-
-def pieces_kernel(where_ref, own_ref, other_ref, mine_ref, a_ref, b_ref, c_ref):
-    chip = where_ref[1]
-    mine_ref[...] = own_ref[chip] + other_ref[chip]
-    for k, ref in ((1, a_ref), (2, b_ref), (3, c_ref)):
-        to = lax.rem(chip + k, CHIPS)
-        ref[...] = (own_ref[to] + other_ref[to]).astype(BF)
+            dq_ref[2 * t + m] = dq[m * flat : (m + 1) * flat].astype(dq_ref.dtype)
+
+
+def chip_pairs_kernel(where_ref, own_ref, other_ref, keep_ref, send_ref):
+    pair = where_ref[1] // 2
+    for m in range(2):
+        to = 2 * pair + m
+        keep_ref[m] = own_ref[to] + other_ref[to].astype(F32)
+        to = 2 * (1 - pair) + m
+        send_ref[m] = (own_ref[to] + other_ref[to].astype(F32)).astype(BF)
+
+
+def chips_kernel(where_ref, keep_ref, got_ref, own_ref, send_ref):
+    own = lax.rem(where_ref[1], 2)
+    own_ref[...] = keep_ref[own] + got_ref[own].astype(F32)
+    send_ref[...] = (keep_ref[1 - own] + got_ref[1 - own].astype(F32)).astype(BF)
 
 
 def total_kernel(factor, terms_ref, out_ref):
     total = jnp.sum(terms_ref[...].astype(F32), axis=0)
-    row = lax.broadcasted_iota(jnp.int32, (total.shape[0], 1), 0)
-    total = (total * jnp.where(row < total.shape[0] // 2, factor, 1.0)).astype(BF)
-    out_ref[...] = jnp.broadcast_to(total[None], out_ref.shape)
+    lines = out_ref.shape[1]
+    row = lax.broadcasted_iota(jnp.int32, (lines, 1), 0)
+    scale = jnp.where(row < lines // 2, factor, 1.0)
+    count = out_ref.shape[0] // HALVES
+    for n in range(HALVES):
+        part = (total[n * lines : (n + 1) * lines] * scale).astype(BF)
+        out_ref[n * count : (n + 1) * count] = jnp.broadcast_to(part[None], (count,) + part.shape)
 
 
 def states_kernel(
     heads, whole_ref, kp_ref, vp_ref, rq_ref, rk_ref, rv_ref, from_ref, to_ref, extra_ref,
     ck_ref, cv_ref, gr_ref, send_ref, wire,
 ):
-    count = whole_ref.shape[0]
+    count = whole_ref.shape[0] // HALVES
     rows = whole_ref.shape[1] // 2
-    ck = whole_ref[:, 0:rows, :].reshape(count * rows, -1)
-    cv = whole_ref[:, rows:, :].reshape(count * rows, -1)
+    both = (whole_ref[0:count].astype(F32) + whole_ref[count:].astype(F32)).astype(BF)
+    ck = both[:, 0:rows, :].reshape(count * rows, -1)
+    cv = both[:, rows:, :].reshape(count * rows, -1)
     ck_ref[...] = ck
     cv_ref[...] = cv
     plane = send_ref.shape[0]
@@ -308,10 +325,9 @@
         v_ref[:, at] = dot_tn(three, gr) + to_end * dot_nn(kr, grad_b)
 
 
-def query_grad_kernel(heads, factor, own_ref, a_ref, b_ref, c_ref, out_ref):
+def query_grad_kernel(heads, factor, own_ref, got_ref, out_ref):
     rows = out_ref.shape[1]
-    total = own_ref[...] + a_ref[...].astype(F32) + b_ref[...].astype(F32) + c_ref[...].astype(F32)
-    total = (total * factor).astype(BF)
+    total = ((own_ref[...] + got_ref[...].astype(F32)) * factor).astype(BF)
     for h in range(heads):
         out_ref[0, :, h * 128 : (h + 1) * 128] = total[h * rows : (h + 1) * rows]
 
@@ -387,8 +403,8 @@
     extra = jnp.pad(extra[None], ((0, WIRE - used - 1), (0, head - extra.shape[0])))
 
     env = (where, offsets, delta, cum, cum_t, from_start, to_end, extra)
+    kv, parts[2], env = lax.optimization_barrier((kv, parts[2], env))
     mine = call(gather_kernel, shape((2, CHIPS, flat, head), BF), (where,), tuple(parts))
-    kv, env = lax.optimization_barrier((kv, env))
     kv = lax.all_to_all(kv, PLANE_AXES, 0, 0, tiled=True)
     kv, env = lax.optimization_barrier((kv, env))
     where, offsets, delta = env[:3]
@@ -421,18 +437,18 @@
 
     dkv, dq_own, dq_other = call(
         functools.partial(grads_kernel, *sizes),
-        (shape((shards, 2 * rows, head), BF),) + (shape((CHIPS, flat, head), F32),) * 2,
+        (shape(kv.shape, BF), shape((CHIPS, flat, head), F32), shape((CHIPS, flat, head), BF)),
         (where, offsets),
         (mine, other, kv, log_total, deltas),
         scratch=[pltpu.VMEM((CORES * CHIPS // 2, head, width), F32)],
         flops=4 << 30,
     )
-    terms, env = pinned_exchange(dkv, ("zh",) + PLANE_AXES, env)
+    terms, env = pinned_exchange(dkv, PLANE_AXES, env)
     total = call(
         functools.partial(total_kernel, factor),
-        shape((secs, 2 * rows, head), BF), (), (terms,),
-    )
-    whole, env = pinned_exchange(total, ("zl", "core"), env)
+        shape((HALVES * secs, 2 * rows, head), BF), (), (terms,),
+    )
+    whole, env = pinned_exchange(total, ("zh", "zl", "core"), env)
     where, offsets, delta, cum, cum_t, from_start, to_end, extra = env
 
     cache_key_grad, cache_value_grad, out_grad, send = call(
@@ -451,8 +467,13 @@
     )
     send, dq_own, dq_other = lax.optimization_barrier((send, dq_own, dq_other))
     dq_other = lax.ppermute(dq_other, "core", [(0, 1), (1, 0)])
+    keep, away = call(
+        chip_pairs_kernel, (shape((2, flat, head), F32), shape((2, flat, head), BF)),
+        (where,), (dq_own, dq_other),
+    )
+    away = lax.ppermute(away, "zl", [(i, i ^ 2) for i in range(CHIPS)])
     part = lax.all_to_all(send, PLANE_AXES, 0, 0, tiled=True)
-    part, dq_own, dq_other, where = lax.optimization_barrier((part, dq_own, dq_other, where))
+    part, keep, away, where = lax.optimization_barrier((part, keep, away, where))
     lasts = part[:, used, : 3 * local].astype(F32).reshape(PLANE, 3, local)
     decays = jnp.exp(lasts[:, 0] + lasts[:, 1] + lasts[:, 2])
     decays = jnp.concatenate([decays, decays], axis=1)
@@ -464,27 +485,21 @@
         functools.partial(totals_kernel, local),
         shape((WIRE, head), F32), (), (part, decays),
     )
-    totals, dq_own, dq_other = lax.optimization_barrier((totals, dq_own, dq_other))
     totals = lax.ppermute(totals, "zh", [(0, 1), (1, 0)])
-    piece = shape((flat, head), BF)
-    dq_mine, *pieces = call(
-        pieces_kernel, (shape((flat, head), F32), piece, piece, piece),
-        (where,), (dq_own, dq_other), flops=4 << 30,
-    )
     enter = call(
         functools.partial(scan_kernel, local),
         shape(part.shape, BF), (where,), (part, decays, totals),
         scratch=[pltpu.VMEM(part.shape, F32)] * 2,
     )
-    enter, dq_mine, pieces = lax.optimization_barrier((enter, dq_mine, pieces))
-    pieces = [
-        lax.ppermute(piece, "zl", [(i, (i + k) % CHIPS) for i in range(CHIPS)])
-        for k, piece in enumerate(pieces, 1)
-    ]
+    enter, keep, away = lax.optimization_barrier((enter, keep, away))
+    dq_mine, piece = call(
+        chips_kernel, (shape((flat, head), F32), shape((flat, head), BF)), (where,), (keep, away),
+    )
+    piece = lax.ppermute(piece, "zl", [(i, i ^ 1) for i in range(CHIPS)])
     enter = lax.all_to_all(enter, PLANE_AXES, 0, 0, tiled=True)
     cross_query_grad = call(
         functools.partial(query_grad_kernel, heads, factor),
-        shape(queries.shape, BF), (), (dq_mine, *pieces),
+        shape(queries.shape, BF), (), (dq_mine, piece),
     )
     grads = call(
         functools.partial(final_kernel, local),

time: 173 us -> 176 us (1.017)
  the two profiles are of different devices: /device:TPU:2 before, /device:TPU:8 now
where the time goes in v5:
time: 176 us; the launch traced here: 175 us
  starting transfers between devices  59.9 us (34%)
  blocking collectives  51.2 us (29%)
  waiting for transfers between devices  40.1 us (23%)
  Pallas kernels  17.6 us (10%)
  local copies, waits for them, and re-layouts  4.93 us (3%)
    all_to_all x3, blocking collectives, pinned_exchange(): array = lax.all_to_all(array, axes, 0, 0, tiled=True)  51.2 us
    pallas_call x14, Pallas kernels, call(): pl.pallas_call(kernel, out_shape=outs, in_specs=[smem] * len(in_smem) + [...  17.6 us
    ppermute x3, starting transfers between devices, body(): lax.ppermute(own, 'zl', [(i, (i - k) % CHIPS) for i in range(CHIPS)])  11.9 us
    ppermute x1, starting transfers between devices, body(): kv_other = lax.ppermute(kv_own, 'zh', [(0, 1), (1, 0)])  10.9 us
    ppermute x3, waiting for transfers between devices, body(): lax.ppermute(own, 'zl', [(i, (i - k) % CHIPS) for i in range(CHIPS)])  10.2 us
    all_to_all x1, starting transfers between devices, body(): kv = lax.all_to_all(kv, PLANE_AXES, 0, 0, tiled=True)  10.2 us
    ppermute x1, waiting for transfers between devices, body(): away = lax.ppermute(away, 'zl', [(i, i ^ 2) for i in range(CHIPS)])  9.83 us
    all_to_all x1, starting transfers between devices, body(): enter = lax.all_to_all(enter, PLANE_AXES, 0, 0, tiled=True)  9.78 us
  transfers between devices with their start and end apart: 12, of which 9 were waited for; matrix products, arithmetic and copies ran while one was open for 0% of the time, Pallas kernels for 3%

profile of v5, /device:TPU:8, one launch (start us, length us, event | category | flops | bytes accessed | tf_op | source)
XLA Modules:
  0.0 175.4 jit_solution(9055594912536133833)
XLA Ops:
  1.4 10.9 %collective-permute-start = (bf16[32,128]{1,0:T(8,128)(2,1)S(1)}, bf16[32,128]{1,0:T(8,128)(2,1)S(1)}, u32[]{:S(2)}, u32[]{:S(2)}) collective-permute-start(bf16[32,128]{1,0:T(8,128)(2,1)S(1)} %pad_maximum_fusion.1), channel_id=1, source_target_pairs={{0,32},{32,0},{1,33},{33,1},{2,34},{34,2},{3,35},{35,3},{4,36},{36... | collective-permute-start | bytes 24584 | tf_op jit(solution)/shard_map/ppermute | solution.py:370
  13.2 0.9 copy-done.7
  14.1 4.3 %collective-permute-start.1 = (bf16[640,128]{1,0:T(8,128)(2,1)S(1)}, bf16[640,128]{1,0:T(8,128)(2,1)S(1)}, u32[]{:S(2)}, u32[]{:S(2)}) collective-permute-start(bf16[640,128]{1,0:T(8,128)(2,1)S(1)} %shard_map.163.a_ref), channel_id=1, source_target_pairs={{0,256},{128,384},{256,0},{384,128},{1,257},{129,385},{257,1},{385... | collective-permute-start | bytes 491528 | tf_op jit(solution)/shard_map/ppermute | solution.py:382
  20.7 5.4 %collective-permute-done.1.c_ref = bf16[640,128]{1,0:T(8,128)(2,1)S(1)} collective-permute-done((bf16[640,128]{1,0:T(8,128)(2,1)S(1)}, bf16[640,128]{1,0:T(8,128)(2,1)S(1)}, u32[]{:S(2)}, u32[]{:S(2)}) %collective-permute-start.1) | collective-permute-done | bytes 163872 | tf_op jit(solution)/shard_map/ppermute | solution.py:382
  26.0 0.9 broadcast_in_dim.10
  27.0 10.2 %all-to-all-start = ((bf16[32,64,128]{2,1,0:T(8,128)(2,1)}), bf16[32,64,128]{2,1,0:T(8,128)(2,1)S(1)}, u32[]{:S(2)}, u32[]{:S(2)}) async-start(bf16[32,64,128]{2,1,0:T(8,128)(2,1)} %broadcast_in_dim.10), calls=%async_computation | async-start | bytes 1048576 | tf_op jit(solution)/shard_map/all_to_all | solution.py:408
  37.1 2.4 %collective-permute-start.3 = (bf16[640,128]{1,0:T(8,128)(2,1)S(1)}, bf16[640,128]{1,0:T(8,128)(2,1)S(1)}, u32[]{:S(2)}, u32[]{:S(2)}) collective-permute-start(bf16[640,128]{1,0:T(8,128)(2,1)S(1)} %shard_map.163.a_ref), channel_id=1, source_target_pairs={{0,128},{128,256},{256,384},{384,0},{1,129},{129,257},{257,385},{3... | collective-permute-start | bytes 491528 | tf_op jit(solution)/shard_map/ppermute | solution.py:382
  39.5 5.3 %collective-permute-start.2 = (bf16[640,128]{1,0:T(8,128)(2,1)S(1)}, bf16[640,128]{1,0:T(8,128)(2,1)S(1)}, u32[]{:S(2)}, u32[]{:S(2)}) collective-permute-start(bf16[640,128]{1,0:T(8,128)(2,1)S(1)} %shard_map.163.a_ref), channel_id=1, source_target_pairs={{0,384},{128,0},{256,128},{384,256},{1,385},{129,1},{257,129},{385... | collective-permute-start | bytes 491528 | tf_op jit(solution)/shard_map/ppermute | solution.py:382
  44.8 1.5 collective-permute-done.3.d_ref
  46.3 3.3 %collective-permute-done.2.b_ref = bf16[640,128]{1,0:T(8,128)(2,1)S(1)} collective-permute-done((bf16[640,128]{1,0:T(8,128)(2,1)S(1)}, bf16[640,128]{1,0:T(8,128)(2,1)S(1)}, u32[]{:S(2)}, u32[]{:S(2)}) %collective-permute-start.2) | collective-permute-done | bytes 163872 | tf_op jit(solution)/shard_map/ppermute | solution.py:382
  50.3 1.9 %collective-permute-start.4 = (bf16[2,4,320,128]{3,2,1,0:T(8,128)(2,1)S(1)}, bf16[2,4,320,128]{3,2,1,0:T(8,128)(2,1)S(1)}, u32[]{:S(2)}, u32[]{:S(2)}) collective-permute-start(bf16[2,4,320,128]{3,2,1,0:T(8,128)(2,1)S(1)} %shard_map.165.rows_ref.mine_ref), channel_id=1, source_target_pairs={{0,64},{64,0},{1,65},{65,1},{2,66},{66,2},{3,67},{67,3},{4,68},{68... | collective-permute-start | bytes 1966088 | tf_op jit(solution)/shard_map/ppermute | solution.py:411
  52.2 1.8 %all-to-all-done.kv_ref = bf16[32,64,128]{2,1,0:T(8,128)(2,1)S(1)} async-done(((bf16[32,64,128]{2,1,0:T(8,128)(2,1)}), bf16[32,64,128]{2,1,0:T(8,128)(2,1)S(1)}, u32[]{:S(2)}, u32[]{:S(2)}) %all-to-all-start) | async-done | bytes 524320 | tf_op jit(solution)/shard_map/all_to_all | solution.py:408
  54.0 1.7 shard_map.166
  55.6 1.6 shard_map.167
  57.3 12.1 %all_to_all.30 = f32[8,32,128]{2,1,0:T(8,128)S(1)} all-to-all(f32[8,32,128]{2,1,0:T(8,128)S(1)} %broadcast_in_dim.11), channel_id=1, replica_groups=mesh['zl'=4,'core'=2,'zh'=2,'x'=4,'y'=8] {'zl','core'}, dimensions={0} | all-to-all | bytes 262144 | tf_op jit(solution)/shard_map/all_to_all | solution.py:56
  69.6 5.1 %shard_map.168 = (bf16[32,64,128]{2,1,0:T(8,128)(2,1)S(1)}, f32[4,320,128]{2,1,0:T(8,128)S(1)}, bf16[4,320,128]{2,1,0:T(8,128)(2,1)S(1)}) custom-call(s32[4]{0:T(128)S(1)} %pad_add_fusion.where_ref, s32[64]{0:T(128)S(1)} %copy-done.9, bf16[2,4,320,128]{3,2,1,0:T(8,128)(2,1)S(1)} %shard_map.165.rows_ref.mine_ref, ...), custom_call_target="tpu_custom_call" | custom-call | flops 4294967296 | bytes 1048576 | tf_op jit(solution)/shard_map/pallas_call | solution.py:39
  74.7 23.5 %all_to_all.31.terms_ref = bf16[32,64,128]{2,1,0:T(8,128)(2,1)S(1)} all-to-all(bf16[32,64,128]{2,1,0:T(8,128)(2,1)S(1)} %get-tuple-element.141), channel_id=1, replica_groups=mesh['zl'=4,'core'=2,'zh'=2,'x'=4,'y'=8] {'x','y'}, dimensions={0} | all-to-all | bytes 1048576 | tf_op jit(solution)/shard_map/all_to_all | solution.py:56
  98.3 15.6 %all_to_all.32.whole_ref = bf16[16,32,128]{2,1,0:T(8,128)(2,1)S(1)} all-to-all(bf16[16,32,128]{2,1,0:T(8,128)(2,1)S(1)} %shard_map.169), channel_id=1, replica_groups=mesh['zl'=4,'core'=2,'zh'=2,'x'=4,'y'=8] {'zh','zl','core'}, dimensions={0} | all-to-all | bytes 262144 | tf_op jit(solution)/shard_map/all_to_all | solution.py:56
  113.9 1.9 %shard_map.170 = (bf16[128,128]{1,0:T(8,128)(2,1)}, bf16[128,128]{1,0:T(8,128)(2,1)}, bf16[128,640]{1,0:T(8,128)(2,1)S(1)}, bf16[32,48,128]{2,1,0:T(8,128)(2,1)}) custom-call(bf16[16,32,128]{2,1,0:T(8,128)(2,1)S(1)} %all_to_all.32.whole_ref, bf16[640,128]{1,0:T(8,128)(2,1)S(1)} %copy-done.5, bf16[640,128]{1,0:T(8,128)(2,1)S(1)} %copy-done.6, ...), custom_call_target="tpu_custom_call" | custom-call | flops 134217728 | bytes 1048576 | tf_op jit(solution)/shard_map/pallas_call | solution.py:39
  115.9 4.8 %all-to-all-start.4 = ((bf16[32,48,128]{2,1,0:T(8,128)(2,1)}), bf16[32,48,128]{2,1,0:T(8,128)(2,1)S(1)}, u32[]{:S(2)}, u32[]{:S(2)}) async-start(bf16[32,48,128]{2,1,0:T(8,128)(2,1)} %get-tuple-element.169), calls=%async_computation.4 | async-start | bytes 786432 | tf_op jit(solution)/shard_map/all_to_all | solution.py:475
  120.7 2.2 %collective-permute-start.5 = (bf16[4,320,128]{2,1,0:T(8,128)(2,1)S(1)}, bf16[4,320,128]{2,1,0:T(8,128)(2,1)S(1)}, u32[]{:S(2)}, u32[]{:S(2)}) collective-permute-start(bf16[4,320,128]{2,1,0:T(8,128)(2,1)S(1)} %get-tuple-element.172), channel_id=1, source_target_pairs={{0,64},{64,0},{1,65},{65,1},{2,66},{66,2},{3,67},{67,3},{4,68},{68... | collective-permute-start | bytes 983048 | tf_op jit(solution)/shard_map/ppermute | solution.py:469
  122.9 1.3 collective-permute-done.5.other_ref
  124.9 2.7 %collective-permute-start.6 = (bf16[2,320,128]{2,1,0:T(8,128)(2,1)S(1)}, bf16[2,320,128]{2,1,0:T(8,128)(2,1)S(1)}, u32[]{:S(2)}, u32[]{:S(2)}) collective-permute-start(bf16[2,320,128]{2,1,0:T(8,128)(2,1)S(1)} %get-tuple-element.174), channel_id=1, source_target_pairs={{0,256},{128,384},{256,0},{384,128},{1,257},{129,385},{257,1},{385... | collective-permute-start | bytes 491528 | tf_op jit(solution)/shard_map/ppermute | solution.py:474
  127.6 9.8 %collective-permute-done.6.got_ref = bf16[2,320,128]{2,1,0:T(8,128)(2,1)S(1)} collective-permute-done((bf16[2,320,128]{2,1,0:T(8,128)(2,1)S(1)}, bf16[2,320,128]{2,1,0:T(8,128)(2,1)S(1)}, u32[]{:S(2)}, u32[]{:S(2)}) %collective-permute-start.6) | collective-permute-done | bytes 163872 | tf_op jit(solution)/shard_map/ppermute | solution.py:474
  138.0 3.6 %collective-permute-start.7 = (f32[48,128]{1,0:T(8,128)S(1)}, f32[48,128]{1,0:T(8,128)S(1)}, u32[]{:S(2)}, u32[]{:S(2)}) collective-permute-start(f32[48,128]{1,0:T(8,128)S(1)} %shard_map.172), channel_id=1, source_target_pairs={{0,32},{32,0},{1,33},{33,1},{2,34},{34,2},{3,35},{35,3},{4,36},{36... | collective-permute-start | bytes 73736 | tf_op jit(solution)/shard_map/ppermute | solution.py:488
  141.6 6.1 %collective-permute-done.7.other_ref = f32[48,128]{1,0:T(8,128)S(1)} collective-permute-done((f32[48,128]{1,0:T(8,128)S(1)}, f32[48,128]{1,0:T(8,128)S(1)}, u32[]{:S(2)}, u32[]{:S(2)}) %collective-permute-start.7) | collective-permute-done | bytes 24608 | tf_op jit(solution)/shard_map/ppermute | solution.py:488
  147.7 1.6 shard_map.173
  149.2 9.8 %all-to-all-start.5 = ((bf16[32,48,128]{2,1,0:T(8,128)(2,1)}), bf16[32,48,128]{2,1,0:T(8,128)(2,1)S(1)}, u32[]{:S(2)}, u32[]{:S(2)}) async-start(bf16[32,48,128]{2,1,0:T(8,128)(2,1)} %shard_map.173), calls=%async_computation.5 | async-start | bytes 786432 | tf_op jit(solution)/shard_map/all_to_all | solution.py:499
  159.6 1.9 %collective-permute-start.8 = (bf16[320,128]{1,0:T(8,128)(2,1)S(1)}, bf16[320,128]{1,0:T(8,128)(2,1)S(1)}, u32[]{:S(2)}, u32[]{:S(2)}) collective-permute-start(bf16[320,128]{1,0:T(8,128)(2,1)S(1)} %get-tuple-element.182), channel_id=1, source_target_pairs={{0,128},{128,0},{256,384},{384,256},{1,129},{129,1},{257,385},{385... | collective-permute-start | bytes 245768 | tf_op jit(solution)/shard_map/ppermute | solution.py:498
  161.5 4.4 %collective-permute-done.8.got_ref = bf16[320,128]{1,0:T(8,128)(2,1)S(1)} collective-permute-done((bf16[320,128]{1,0:T(8,128)(2,1)S(1)}, bf16[320,128]{1,0:T(8,128)(2,1)S(1)}, u32[]{:S(2)}, u32[]{:S(2)}) %collective-permute-start.8) | collective-permute-done | bytes 81952 | tf_op jit(solution)/shard_map/ppermute | solution.py:498
  166.6 6.5 %all-to-all-done.5.wire_ref = bf16[32,48,128]{2,1,0:T(8,128)(2,1)S(1)} async-done(((bf16[32,48,128]{2,1,0:T(8,128)(2,1)}), bf16[32,48,128]{2,1,0:T(8,128)(2,1)S(1)}, u32[]{:S(2)}, u32[]{:S(2)}) %all-to-all-start.5) | async-done | bytes 393248 | tf_op jit(solution)/shard_map/all_to_all | solution.py:499
  173.1 2.3 %shard_map.176 = (f32[128,640]{1,0:T(8,128)}, f32[128,640]{1,0:T(8,128)}, f32[128,640]{1,0:T(8,128)}) custom-call(bf16[128,640]{1,0:T(8,128)(2,1)S(1)} %copy-done, bf16[128,640]{1,0:T(8,128)(2,1)S(1)} %copy-done.1, bf16[128,640]{1,0:T(8,128)(2,1)S(1)} %copy-done.2, bf16[128,640]{1,0:T(8,128)(2,1)S(1)} %get-tuple-element.185.gr_ref, ...), custom_call_target="tpu_custom_call" | custom-call | flops 268435456 | bytes 1048576 | tf_op jit(solution)/shard_map/pallas_call | solution.py:39
  (63 shorter events, 7.2 us)
Async XLA Ops:
  1.4 19.3 %collective-permute-start = (bf16[32,128]{1,0:T(8,128)(2,1)S(1)}, bf16[32,128]{1,0:T(8,128)(2,1)S(1)}, u32[]{:S(2)}, u32[]{:S(2)}) collective-permute-start(bf16[32,128]{1,0:T(8,128)(2,1)S(1)} %pad_maximum_fusion.1), channel_id=1, source_target_pairs={{0,32},{32,0},{1,33},{33,1},{2,34},{34,2},{3,35},{35,3},{4,36},{36... | collective-permute-start | bytes 24584 | tf_op jit(solution)/shard_map/ppermute | solution.py:370
  12.3 0.9 copy-start.3
  13.2 0.9 copy-start.7
  14.0 4.3 %copy-start.10 = (f32[5,128]{1,0:T(8,128)S(1)}, f32[5,128]{1,0:T(8,128)}, u32[]{:S(2)}) copy-start(f32[5,128]{1,0:T(8,128)} %param.23) | copy-start | bytes 7684
  14.1 12.0 %collective-permute-start.1 = (bf16[640,128]{1,0:T(8,128)(2,1)S(1)}, bf16[640,128]{1,0:T(8,128)(2,1)S(1)}, u32[]{:S(2)}, u32[]{:S(2)}) collective-permute-start(bf16[640,128]{1,0:T(8,128)(2,1)S(1)} %shard_map.163.a_ref), channel_id=1, source_target_pairs={{0,256},{128,384},{256,0},{384,128},{1,257},{129,385},{257,1},{385... | collective-permute-start | bytes 491528 | tf_op jit(solution)/shard_map/ppermute | solution.py:382
  19.0 0.9 copy-start.4
  19.0 0.9 copy-start.8
  27.0 27.0 %all-to-all-start = ((bf16[32,64,128]{2,1,0:T(8,128)(2,1)}), bf16[32,64,128]{2,1,0:T(8,128)(2,1)S(1)}, u32[]{:S(2)}, u32[]{:S(2)}) async-start(bf16[32,64,128]{2,1,0:T(8,128)(2,1)} %broadcast_in_dim.10), calls=%async_computation | async-start | bytes 1048576 | tf_op jit(solution)/shard_map/all_to_all | solution.py:408
  37.1 9.2 %collective-permute-start.3 = (bf16[640,128]{1,0:T(8,128)(2,1)S(1)}, bf16[640,128]{1,0:T(8,128)(2,1)S(1)}, u32[]{:S(2)}, u32[]{:S(2)}) collective-permute-start(bf16[640,128]{1,0:T(8,128)(2,1)S(1)} %shard_map.163.a_ref), channel_id=1, source_target_pairs={{0,128},{128,256},{256,384},{384,0},{1,129},{129,257},{257,385},{3... | collective-permute-start | bytes 491528 | tf_op jit(solution)/shard_map/ppermute | solution.py:382
  39.5 10.1 %collective-permute-start.2 = (bf16[640,128]{1,0:T(8,128)(2,1)S(1)}, bf16[640,128]{1,0:T(8,128)(2,1)S(1)}, u32[]{:S(2)}, u32[]{:S(2)}) collective-permute-start(bf16[640,128]{1,0:T(8,128)(2,1)S(1)} %shard_map.163.a_ref), channel_id=1, source_target_pairs={{0,384},{128,0},{256,128},{384,256},{1,385},{129,1},{257,129},{385... | collective-permute-start | bytes 491528 | tf_op jit(solution)/shard_map/ppermute | solution.py:382
  50.3 3.7 %copy-start.9 = (s32[64]{0:T(128)S(1)}, s32[64]{0:T(128)}, u32[]{:S(2)}) copy-start(s32[64]{0:T(128)} %offset_ref.2) | copy-start | bytes 772
  50.3 5.4 %collective-permute-start.4 = (bf16[2,4,320,128]{3,2,1,0:T(8,128)(2,1)S(1)}, bf16[2,4,320,128]{3,2,1,0:T(8,128)(2,1)S(1)}, u32[]{:S(2)}, u32[]{:S(2)}) collective-permute-start(bf16[2,4,320,128]{3,2,1,0:T(8,128)(2,1)S(1)} %shard_map.165.rows_ref.mine_ref), channel_id=1, source_target_pairs={{0,64},{64,0},{1,65},{65,1},{2,66},{66,2},{3,67},{67,3},{4,68},{68... | collective-permute-start | bytes 1966088 | tf_op jit(solution)/shard_map/ppermute | solution.py:411
  98.2 15.7 %copy-start.1 = (bf16[128,640]{1,0:T(8,128)(2,1)S(1)}, bf16[128,640]{1,0:T(8,128)(2,1)}, u32[]{:S(2)}) copy-start(bf16[128,640]{1,0:T(8,128)(2,1)} %rk_ref.3) | copy-start | bytes 491524
  98.2 15.7 %copy-start.2 = (bf16[128,640]{1,0:T(8,128)(2,1)S(1)}, bf16[128,640]{1,0:T(8,128)(2,1)}, u32[]{:S(2)}) copy-start(bf16[128,640]{1,0:T(8,128)(2,1)} %rv_ref.3) | copy-start | bytes 491524
  98.2 15.7 %copy-start.5 = (bf16[640,128]{1,0:T(8,128)(2,1)S(1)}, bf16[640,128]{1,0:T(8,128)(2,1)}, u32[]{:S(2)}) copy-start(bf16[640,128]{1,0:T(8,128)(2,1)} %kp_ref.1) | copy-start | bytes 491524
  98.2 15.7 %copy-start.6 = (bf16[640,128]{1,0:T(8,128)(2,1)S(1)}, bf16[640,128]{1,0:T(8,128)(2,1)}, u32[]{:S(2)}) copy-start(bf16[640,128]{1,0:T(8,128)(2,1)} %vp_ref.1) | copy-start | bytes 491524
  98.3 15.6 %copy-start = (bf16[128,640]{1,0:T(8,128)(2,1)S(1)}, bf16[128,640]{1,0:T(8,128)(2,1)}, u32[]{:S(2)}) copy-start(bf16[128,640]{1,0:T(8,128)(2,1)} %rq_ref.3) | copy-start | bytes 491524
  115.9 21.5 %all-to-all-start.4 = ((bf16[32,48,128]{2,1,0:T(8,128)(2,1)}), bf16[32,48,128]{2,1,0:T(8,128)(2,1)S(1)}, u32[]{:S(2)}, u32[]{:S(2)}) async-start(bf16[32,48,128]{2,1,0:T(8,128)(2,1)} %get-tuple-element.169), calls=%async_computation.4 | async-start | bytes 786432 | tf_op jit(solution)/shard_map/all_to_all | solution.py:475
  120.7 3.5 %collective-permute-start.5 = (bf16[4,320,128]{2,1,0:T(8,128)(2,1)S(1)}, bf16[4,320,128]{2,1,0:T(8,128)(2,1)S(1)}, u32[]{:S(2)}, u32[]{:S(2)}) collective-permute-start(bf16[4,320,128]{2,1,0:T(8,128)(2,1)S(1)} %get-tuple-element.172), channel_id=1, source_target_pairs={{0,64},{64,0},{1,65},{65,1},{2,66},{66,2},{3,67},{67,3},{4,68},{68... | collective-permute-start | bytes 983048 | tf_op jit(solution)/shard_map/ppermute | solution.py:469
  124.9 12.5 %collective-permute-start.6 = (bf16[2,320,128]{2,1,0:T(8,128)(2,1)S(1)}, bf16[2,320,128]{2,1,0:T(8,128)(2,1)S(1)}, u32[]{:S(2)}, u32[]{:S(2)}) collective-permute-start(bf16[2,320,128]{2,1,0:T(8,128)(2,1)S(1)} %get-tuple-element.174), channel_id=1, source_target_pairs={{0,256},{128,384},{256,0},{384,128},{1,257},{129,385},{257,1},{385... | collective-permute-start | bytes 491528 | tf_op jit(solution)/shard_map/ppermute | solution.py:474
  138.0 9.6 %collective-permute-start.7 = (f32[48,128]{1,0:T(8,128)S(1)}, f32[48,128]{1,0:T(8,128)S(1)}, u32[]{:S(2)}, u32[]{:S(2)}) collective-permute-start(f32[48,128]{1,0:T(8,128)S(1)} %shard_map.172), channel_id=1, source_target_pairs={{0,32},{32,0},{1,33},{33,1},{2,34},{34,2},{3,35},{35,3},{4,36},{36... | collective-permute-start | bytes 73736 | tf_op jit(solution)/shard_map/ppermute | solution.py:488
  149.2 23.9 %all-to-all-start.5 = ((bf16[32,48,128]{2,1,0:T(8,128)(2,1)}), bf16[32,48,128]{2,1,0:T(8,128)(2,1)S(1)}, u32[]{:S(2)}, u32[]{:S(2)}) async-start(bf16[32,48,128]{2,1,0:T(8,128)(2,1)} %shard_map.173), calls=%async_computation.5 | async-start | bytes 786432 | tf_op jit(solution)/shard_map/all_to_all | solution.py:499
  159.6 6.3 %collective-permute-start.8 = (bf16[320,128]{1,0:T(8,128)(2,1)S(1)}, bf16[320,128]{1,0:T(8,128)(2,1)S(1)}, u32[]{:S(2)}, u32[]{:S(2)}) collective-permute-start(bf16[320,128]{1,0:T(8,128)(2,1)S(1)} %get-tuple-element.182), channel_id=1, source_target_pairs={{0,128},{128,0},{256,384},{384,256},{1,129},{129,1},{257,385},{385... | collective-permute-start | bytes 245768 | tf_op jit(solution)/shard_map/ppermute | solution.py:498

commit v6 on v5

--- a/solution.py
+++ b/solution.py
@@ -18,7 +18,7 @@
 PLANE_AXES = ("x", "y")
 SLICE = 4
 WIRE = 48
-SCOPED = 32 * 1024 * 1024
+SCOPED = 16 * 1024 * 1024
 
 
 def dot_nt(a, b):
@@ -367,6 +367,7 @@
     kv_own = jnp.concatenate(
         [lax.dynamic_slice_in_dim(a, place * rows, rows, 0) for a in (cache_keys, cache_values)]
     )
+    kv_own, queries, output_grad = lax.optimization_barrier((kv_own, queries, output_grad))
     kv_other = lax.ppermute(kv_own, "zh", [(0, 1), (1, 0)])
     kv = jnp.where(
         half == 0,
@@ -403,8 +404,10 @@
     extra = jnp.pad(extra[None], ((0, WIRE - used - 1), (0, head - extra.shape[0])))
 
     env = (where, offsets, delta, cum, cum_t, from_start, to_end, extra)
-    kv, parts[2], env = lax.optimization_barrier((kv, parts[2], env))
-    mine = call(gather_kernel, shape((2, CHIPS, flat, head), BF), (where,), tuple(parts))
+    mine = call(
+        gather_kernel, shape((2, CHIPS, flat, head), BF), (where,), tuple(parts), flops=16 << 30
+    )
+    kv, env = lax.optimization_barrier((kv, env))
     kv = lax.all_to_all(kv, PLANE_AXES, 0, 0, tiled=True)
     kv, env = lax.optimization_barrier((kv, env))
     where, offsets, delta = env[:3]
@@ -425,7 +428,7 @@
         delta,
     ])
     both = jnp.broadcast_to(both[None], (secs,) + both.shape)
-    both, (mine, other, kv, env) = pinned_exchange(both, ("zl", "core"), (mine, other, kv, env))
+    both, env = pinned_exchange(both, ("zl", "core"), env)
     where, offsets = env[:2]
     tiles = (CORES, CHIPS // 2, 1, width)
     logs = both[:, : CHIPS * lines]
@@ -473,7 +476,7 @@
     )
     away = lax.ppermute(away, "zl", [(i, i ^ 2) for i in range(CHIPS)])
     part = lax.all_to_all(send, PLANE_AXES, 0, 0, tiled=True)
-    part, keep, away, where = lax.optimization_barrier((part, keep, away, where))
+    part, where = lax.optimization_barrier((part, where))
     lasts = part[:, used, : 3 * local].astype(F32).reshape(PLANE, 3, local)
     decays = jnp.exp(lasts[:, 0] + lasts[:, 1] + lasts[:, 2])
     decays = jnp.concatenate([decays, decays], axis=1)
@@ -497,10 +500,6 @@
     )
     piece = lax.ppermute(piece, "zl", [(i, i ^ 1) for i in range(CHIPS)])
     enter = lax.all_to_all(enter, PLANE_AXES, 0, 0, tiled=True)
-    cross_query_grad = call(
-        functools.partial(query_grad_kernel, heads, factor),
-        shape(queries.shape, BF), (), (dq_mine, piece),
-    )
     grads = call(
         functools.partial(final_kernel, local),
         (shape(retention_query.shape, F32),) * 3,
@@ -511,6 +510,11 @@
         ),
         scratch=[pltpu.VMEM(enter.shape, F32)],
         flops=1 << 28,
+    )
+    grads, dq_mine, piece = lax.optimization_barrier((grads, dq_mine, piece))
+    cross_query_grad = call(
+        functools.partial(query_grad_kernel, heads, factor),
+        shape(queries.shape, BF), (), (dq_mine, piece),
     )
     return (cross_query_grad, cache_key_grad, cache_value_grad) + tuple(grads)
 

time: 176 us -> 173 us (0.983)
  starting transfers between devices: 59.9 us -> 54.1 us
    all_to_all x1, waiting for transfers between devices: 1.77 us -> 13.9 us  [body(): kv = lax.all_to_all(kv, PLANE_AXES, 0, 0, tiled=True)]
    ppermute x3, waiting for transfers between devices: 10.2 us -> 0.01 us  [body(): lax.ppermute(own, 'zl', [(i, (i - k) % CHIPS) for i in range(CHIPS)])]
    ppermute x1, waiting for transfers between devices: 9.83 us -> 0.01 us  [body(): away = lax.ppermute(away, 'zl', [(i, i ^ 2) for i in range(CHIPS)])]
    all_to_all x1, waiting for transfers between devices: 0.01 us -> 8.86 us  [body(): part = lax.all_to_all(send, PLANE_AXES, 0, 0, tiled=True)]
    all_to_all x1, starting transfers between devices: 9.78 us -> 5.18 us  [body(): enter = lax.all_to_all(enter, PLANE_AXES, 0, 0, tiled=True)]
    all_to_all x1, waiting for transfers between devices: 6.51 us -> 11 us  [body(): enter = lax.all_to_all(enter, PLANE_AXES, 0, 0, tiled=True)]
    ppermute x1, waiting for transfers between devices: 4.41 us -> 0.01 us  [body(): piece = lax.ppermute(piece, 'zl', [(i, i ^ 1) for i in range(CHIPS)])]
    ppermute x1, starting transfers between devices: 10.9 us -> 9.12 us  [body(): kv_other = lax.ppermute(kv_own, 'zh', [(0, 1), (1, 0)])]
  transfers between devices with their start and end apart: 12 -> 12, of which waited for: 9 -> 5; matrix products, arithmetic and copies ran while one was open for 0% -> 1% of each run, Pallas kernels for 3% -> 5%
where the time goes in v6:
time: 173 us; the launch traced here: 172 us
  starting transfers between devices  54.1 us (31%)
  blocking collectives  51 us (29%)
  waiting for transfers between devices  41.7 us (24%)
  Pallas kernels  17.6 us (10%)
  local copies, waits for them, and re-layouts  6.03 us (3%)
    all_to_all x3, blocking collectives, pinned_exchange(): array = lax.all_to_all(array, axes, 0, 0, tiled=True)  51 us
    pallas_call x14, Pallas kernels, call(): pl.pallas_call(kernel, out_shape=outs, in_specs=[smem] * len(in_smem) + [...  17.6 us
    all_to_all x1, waiting for transfers between devices, body(): kv = lax.all_to_all(kv, PLANE_AXES, 0, 0, tiled=True)  13.9 us
    ppermute x3, starting transfers between devices, body(): lax.ppermute(own, 'zl', [(i, (i - k) % CHIPS) for i in range(CHIPS)])  12.8 us
    all_to_all x1, waiting for transfers between devices, body(): enter = lax.all_to_all(enter, PLANE_AXES, 0, 0, tiled=True)  11 us
    all_to_all x1, starting transfers between devices, body(): kv = lax.all_to_all(kv, PLANE_AXES, 0, 0, tiled=True)  10.2 us
    ppermute x1, starting transfers between devices, body(): kv_other = lax.ppermute(kv_own, 'zh', [(0, 1), (1, 0)])  9.12 us
    all_to_all x1, waiting for transfers between devices, body(): part = lax.all_to_all(send, PLANE_AXES, 0, 0, tiled=True)  8.86 us
  transfers between devices with their start and end apart: 12, of which 5 were waited for; matrix products, arithmetic and copies ran while one was open for 1% of the time, Pallas kernels for 5%

profile of v6, /device:TPU:8, one launch (start us, length us, event | category | flops | bytes accessed | tf_op | source)
XLA Modules:
  0.0 172.1 jit_solution(6444858799798165277)
XLA Ops:
  0.6 0.7 constant_dynamic-slice_fusion
  1.4 0.9 copy-done.3
  2.2 0.9 copy-done.7
  3.2 4.3 %collective-permute-start.3 = (bf16[640,128]{1,0:T(8,128)(2,1)S(1)}, bf16[640,128]{1,0:T(8,128)(2,1)S(1)}, u32[]{:S(2)}, u32[]{:S(2)}) collective-permute-start(bf16[640,128]{1,0:T(8,128)(2,1)S(1)} %shard_map.164.a_ref), channel_id=1, source_target_pairs={{0,128},{128,256},{256,384},{384,0},{1,129},{129,257},{257,385},{3... | collective-permute-start | bytes 491528 | tf_op jit(solution)/shard_map/ppermute | solution.py:383
  7.5 6.1 %collective-permute-start.2 = (bf16[640,128]{1,0:T(8,128)(2,1)S(1)}, bf16[640,128]{1,0:T(8,128)(2,1)S(1)}, u32[]{:S(2)}, u32[]{:S(2)}) collective-permute-start(bf16[640,128]{1,0:T(8,128)(2,1)S(1)} %shard_map.164.a_ref), channel_id=1, source_target_pairs={{0,256},{128,384},{256,0},{384,128},{1,257},{129,385},{257,1},{385... | collective-permute-start | bytes 491528 | tf_op jit(solution)/shard_map/ppermute | solution.py:383
  13.6 2.5 %collective-permute-start.1 = (bf16[640,128]{1,0:T(8,128)(2,1)S(1)}, bf16[640,128]{1,0:T(8,128)(2,1)S(1)}, u32[]{:S(2)}, u32[]{:S(2)}) collective-permute-start(bf16[640,128]{1,0:T(8,128)(2,1)S(1)} %shard_map.164.a_ref), channel_id=1, source_target_pairs={{0,384},{128,0},{256,128},{384,256},{1,385},{129,1},{257,129},{385... | collective-permute-start | bytes 491528 | tf_op jit(solution)/shard_map/ppermute | solution.py:383
  16.0 9.1 %collective-permute-start = (bf16[32,128]{1,0:T(8,128)(2,1)S(1)}, bf16[32,128]{1,0:T(8,128)(2,1)S(1)}, u32[]{:S(2)}, u32[]{:S(2)}) collective-permute-start(bf16[32,128]{1,0:T(8,128)(2,1)S(1)} %pad_maximum_fusion.1), channel_id=1, source_target_pairs={{0,32},{32,0},{1,33},{33,1},{2,34},{34,2},{3,35},{35,3},{4,36},{36... | collective-permute-start | bytes 24584 | tf_op jit(solution)/shard_map/ppermute | solution.py:371
  26.7 0.7 shard_map.163
  27.5 0.9 broadcast_in_dim.10
  28.4 10.2 %all-to-all-start = ((bf16[32,64,128]{2,1,0:T(8,128)(2,1)}), bf16[32,64,128]{2,1,0:T(8,128)(2,1)S(1)}, u32[]{:S(2)}, u32[]{:S(2)}) async-start(bf16[32,64,128]{2,1,0:T(8,128)(2,1)} %broadcast_in_dim.10), calls=%async_computation | async-start | bytes 1048576 | tf_op jit(solution)/shard_map/all_to_all | solution.py:411
  39.2 1.9 %collective-permute-start.4 = (bf16[2,4,320,128]{3,2,1,0:T(8,128)(2,1)S(1)}, bf16[2,4,320,128]{3,2,1,0:T(8,128)(2,1)S(1)}, u32[]{:S(2)}, u32[]{:S(2)}) collective-permute-start(bf16[2,4,320,128]{3,2,1,0:T(8,128)(2,1)S(1)} %shard_map.165.rows_ref.mine_ref), channel_id=1, source_target_pairs={{0,64},{64,0},{1,65},{65,1},{2,66},{66,2},{3,67},{67,3},{4,68},{68... | collective-permute-start | bytes 1966088 | tf_op jit(solution)/shard_map/ppermute | solution.py:414
  41.1 13.9 %all-to-all-done.kv_ref = bf16[32,64,128]{2,1,0:T(8,128)(2,1)S(1)} async-done(((bf16[32,64,128]{2,1,0:T(8,128)(2,1)}), bf16[32,64,128]{2,1,0:T(8,128)(2,1)S(1)}, u32[]{:S(2)}, u32[]{:S(2)}) %all-to-all-start) | async-done | bytes 524320 | tf_op jit(solution)/shard_map/all_to_all | solution.py:411
  55.1 1.6 shard_map.166
  56.7 1.7 shard_map.167
  58.4 11.1 %all_to_all.30 = f32[8,32,128]{2,1,0:T(8,128)S(1)} all-to-all(f32[8,32,128]{2,1,0:T(8,128)S(1)} %broadcast_in_dim.11), channel_id=1, replica_groups=mesh['zl'=4,'core'=2,'zh'=2,'x'=4,'y'=8] {'zl','core'}, dimensions={0} | all-to-all | bytes 262144 | tf_op jit(solution)/shard_map/all_to_all | solution.py:56
  69.7 1.1 copy-done.10
  70.8 5.1 %shard_map.168 = (bf16[32,64,128]{2,1,0:T(8,128)(2,1)S(1)}, f32[4,320,128]{2,1,0:T(8,128)S(1)}, bf16[4,320,128]{2,1,0:T(8,128)(2,1)S(1)}) custom-call(s32[4]{0:T(128)S(1)} %pad_add_fusion.where_ref, s32[64]{0:T(128)S(1)} %copy-done.11, bf16[2,4,320,128]{3,2,1,0:T(8,128)(2,1)S(1)} %shard_map.165.rows_ref.mine_ref, bf16[2,4,320,128]{3,2,1,0:T(8,128)(2,1)S(1)} %copy-done.10, ...), custom_call_target="tpu_custom_call" | custom-call | flops 4294967296 | bytes 1048576 | tf_op jit(solution)/shard_map/pallas_call | solution.py:39
  75.9 22.1 %all_to_all.31.terms_ref = bf16[32,64,128]{2,1,0:T(8,128)(2,1)S(1)} all-to-all(bf16[32,64,128]{2,1,0:T(8,128)(2,1)S(1)} %get-tuple-element.136), channel_id=1, replica_groups=mesh['zl'=4,'core'=2,'zh'=2,'x'=4,'y'=8] {'x','y'}, dimensions={0} | all-to-all | bytes 1048576 | tf_op jit(solution)/shard_map/all_to_all | solution.py:56
  98.1 17.8 %all_to_all.32.whole_ref = bf16[16,32,128]{2,1,0:T(8,128)(2,1)S(1)} all-to-all(bf16[16,32,128]{2,1,0:T(8,128)(2,1)S(1)} %shard_map.169), channel_id=1, replica_groups=mesh['zl'=4,'core'=2,'zh'=2,'x'=4,'y'=8] {'zh','zl','core'}, dimensions={0} | all-to-all | bytes 262144 | tf_op jit(solution)/shard_map/all_to_all | solution.py:56
  116.0 1.9 %shard_map.170 = (bf16[128,128]{1,0:T(8,128)(2,1)}, bf16[128,128]{1,0:T(8,128)(2,1)}, bf16[128,640]{1,0:T(8,128)(2,1)S(1)}, bf16[32,48,128]{2,1,0:T(8,128)(2,1)}) custom-call(bf16[16,32,128]{2,1,0:T(8,128)(2,1)S(1)} %all_to_all.32.whole_ref, bf16[640,128]{1,0:T(8,128)(2,1)S(1)} %copy-done.5, bf16[640,128]{1,0:T(8,128)(2,1)S(1)} %copy-done.6, ...), custom_call_target="tpu_custom_call" | custom-call | flops 134217728 | bytes 1048576 | tf_op jit(solution)/shard_map/pallas_call | solution.py:39
  117.9 4.8 %all-to-all-start.4 = ((bf16[32,48,128]{2,1,0:T(8,128)(2,1)}), bf16[32,48,128]{2,1,0:T(8,128)(2,1)S(1)}, u32[]{:S(2)}, u32[]{:S(2)}) async-start(bf16[32,48,128]{2,1,0:T(8,128)(2,1)} %get-tuple-element.167), calls=%async_computation.4 | async-start | bytes 786432 | tf_op jit(solution)/shard_map/all_to_all | solution.py:478
  122.8 2.2 %collective-permute-start.6 = (bf16[4,320,128]{2,1,0:T(8,128)(2,1)S(1)}, bf16[4,320,128]{2,1,0:T(8,128)(2,1)S(1)}, u32[]{:S(2)}, u32[]{:S(2)}) collective-permute-start(bf16[4,320,128]{2,1,0:T(8,128)(2,1)S(1)} %get-tuple-element.172), channel_id=1, source_target_pairs={{0,64},{64,0},{1,65},{65,1},{2,66},{66,2},{3,67},{67,3},{4,68},{68... | collective-permute-start | bytes 983048 | tf_op jit(solution)/shard_map/ppermute | solution.py:472
  125.0 1.3 collective-permute-done.6.other_ref
  126.9 2.7 %collective-permute-start.7 = (bf16[2,320,128]{2,1,0:T(8,128)(2,1)S(1)}, bf16[2,320,128]{2,1,0:T(8,128)(2,1)S(1)}, u32[]{:S(2)}, u32[]{:S(2)}) collective-permute-start(bf16[2,320,128]{2,1,0:T(8,128)(2,1)S(1)} %get-tuple-element.174), channel_id=1, source_target_pairs={{0,256},{128,384},{256,0},{384,128},{1,257},{129,385},{257,1},{385... | collective-permute-start | bytes 491528 | tf_op jit(solution)/shard_map/ppermute | solution.py:477
  129.6 8.9 %all-to-all-done.4.part_ref = bf16[32,48,128]{2,1,0:T(8,128)(2,1)S(1)} async-done(((bf16[32,48,128]{2,1,0:T(8,128)(2,1)}), bf16[32,48,128]{2,1,0:T(8,128)(2,1)S(1)}, u32[]{:S(2)}, u32[]{:S(2)}) %all-to-all-start.4) | async-done | bytes 393248 | tf_op jit(solution)/shard_map/all_to_all | solution.py:478
  139.1 3.1 %collective-permute-start.5 = (f32[48,128]{1,0:T(8,128)S(1)}, f32[48,128]{1,0:T(8,128)S(1)}, u32[]{:S(2)}, u32[]{:S(2)}) collective-permute-start(f32[48,128]{1,0:T(8,128)S(1)} %shard_map.171), channel_id=1, source_target_pairs={{0,32},{32,0},{1,33},{33,1},{2,34},{34,2},{3,35},{35,3},{4,36},{36... | collective-permute-start | bytes 73736 | tf_op jit(solution)/shard_map/ppermute | solution.py:491
  142.3 6.5 %collective-permute-done.5.other_ref = f32[48,128]{1,0:T(8,128)S(1)} collective-permute-done((f32[48,128]{1,0:T(8,128)S(1)}, f32[48,128]{1,0:T(8,128)S(1)}, u32[]{:S(2)}, u32[]{:S(2)}) %collective-permute-start.5) | collective-permute-done | bytes 24608 | tf_op jit(solution)/shard_map/ppermute | solution.py:491
  148.7 1.6 shard_map.172
  150.3 5.2 %all-to-all-start.5 = ((bf16[32,48,128]{2,1,0:T(8,128)(2,1)}), bf16[32,48,128]{2,1,0:T(8,128)(2,1)S(1)}, u32[]{:S(2)}, u32[]{:S(2)}) async-start(bf16[32,48,128]{2,1,0:T(8,128)(2,1)} %shard_map.172), calls=%async_computation.5 | async-start | bytes 786432 | tf_op jit(solution)/shard_map/all_to_all | solution.py:502
  156.1 2.0 %collective-permute-start.8 = (bf16[320,128]{1,0:T(8,128)(2,1)S(1)}, bf16[320,128]{1,0:T(8,128)(2,1)S(1)}, u32[]{:S(2)}, u32[]{:S(2)}) collective-permute-start(bf16[320,128]{1,0:T(8,128)(2,1)S(1)} %get-tuple-element.182), channel_id=1, source_target_pairs={{0,128},{128,0},{256,384},{384,256},{1,129},{129,1},{257,385},{385... | collective-permute-start | bytes 245768 | tf_op jit(solution)/shard_map/ppermute | solution.py:501
  158.1 11.0 %all-to-all-done.5.wire_ref = bf16[32,48,128]{2,1,0:T(8,128)(2,1)S(1)} async-done(((bf16[32,48,128]{2,1,0:T(8,128)(2,1)}), bf16[32,48,128]{2,1,0:T(8,128)(2,1)S(1)}, u32[]{:S(2)}, u32[]{:S(2)}) %all-to-all-start.5) | async-done | bytes 393248 | tf_op jit(solution)/shard_map/all_to_all | solution.py:502
  169.2 2.3 %shard_map.174 = (f32[128,640]{1,0:T(8,128)}, f32[128,640]{1,0:T(8,128)}, f32[128,640]{1,0:T(8,128)}) custom-call(bf16[128,640]{1,0:T(8,128)(2,1)S(1)} %copy-done, bf16[128,640]{1,0:T(8,128)(2,1)S(1)} %copy-done.1, bf16[128,640]{1,0:T(8,128)(2,1)S(1)} %copy-done.2, bf16[128,640]{1,0:T(8,128)(2,1)S(1)} %get-tuple-element.161.gr_ref, ...), custom_call_target="tpu_custom_call" | custom-call | flops 268435456 | bytes 1048576 | tf_op jit(solution)/shard_map/pallas_call | solution.py:39
  (67 shorter events, 4.9 us)
Async XLA Ops:
  1.4 0.9 copy-start.3
  2.2 0.9 copy-start.7
  3.1 22.0 %copy-start.12 = (f32[5,128]{1,0:T(8,128)S(1)}, f32[5,128]{1,0:T(8,128)}, u32[]{:S(2)}) copy-start(f32[5,128]{1,0:T(8,128)} %param.23) | copy-start | bytes 7684
  3.2 35.4 %collective-permute-start.3 = (bf16[640,128]{1,0:T(8,128)(2,1)S(1)}, bf16[640,128]{1,0:T(8,128)(2,1)S(1)}, u32[]{:S(2)}, u32[]{:S(2)}) collective-permute-start(bf16[640,128]{1,0:T(8,128)(2,1)S(1)} %shard_map.164.a_ref), channel_id=1, source_target_pairs={{0,128},{128,256},{256,384},{384,0},{1,129},{129,257},{257,385},{3... | collective-permute-start | bytes 491528 | tf_op jit(solution)/shard_map/ppermute | solution.py:383
  7.5 31.1 %collective-permute-start.2 = (bf16[640,128]{1,0:T(8,128)(2,1)S(1)}, bf16[640,128]{1,0:T(8,128)(2,1)S(1)}, u32[]{:S(2)}, u32[]{:S(2)}) collective-permute-start(bf16[640,128]{1,0:T(8,128)(2,1)S(1)} %shard_map.164.a_ref), channel_id=1, source_target_pairs={{0,256},{128,384},{256,0},{384,128},{1,257},{129,385},{257,1},{385... | collective-permute-start | bytes 491528 | tf_op jit(solution)/shard_map/ppermute | solution.py:383
  13.6 25.0 %collective-permute-start.1 = (bf16[640,128]{1,0:T(8,128)(2,1)S(1)}, bf16[640,128]{1,0:T(8,128)(2,1)S(1)}, u32[]{:S(2)}, u32[]{:S(2)}) collective-permute-start(bf16[640,128]{1,0:T(8,128)(2,1)S(1)} %shard_map.164.a_ref), channel_id=1, source_target_pairs={{0,384},{128,0},{256,128},{384,256},{1,385},{129,1},{257,129},{385... | collective-permute-start | bytes 491528 | tf_op jit(solution)/shard_map/ppermute | solution.py:383
  16.0 11.4 %collective-permute-start = (bf16[32,128]{1,0:T(8,128)(2,1)S(1)}, bf16[32,128]{1,0:T(8,128)(2,1)S(1)}, u32[]{:S(2)}, u32[]{:S(2)}) collective-permute-start(bf16[32,128]{1,0:T(8,128)(2,1)S(1)} %pad_maximum_fusion.1), channel_id=1, source_target_pairs={{0,32},{32,0},{1,33},{33,1},{2,34},{34,2},{3,35},{35,3},{4,36},{36... | collective-permute-start | bytes 24584 | tf_op jit(solution)/shard_map/ppermute | solution.py:371
  25.8 0.9 copy-start.4
  25.8 0.9 copy-start.8
  28.4 26.7 %all-to-all-start = ((bf16[32,64,128]{2,1,0:T(8,128)(2,1)}), bf16[32,64,128]{2,1,0:T(8,128)(2,1)S(1)}, u32[]{:S(2)}, u32[]{:S(2)}) async-start(bf16[32,64,128]{2,1,0:T(8,128)(2,1)} %broadcast_in_dim.10), calls=%async_computation | async-start | bytes 1048576 | tf_op jit(solution)/shard_map/all_to_all | solution.py:411
  39.2 15.9 %copy-start.11 = (s32[64]{0:T(128)S(1)}, s32[64]{0:T(128)}, u32[]{:S(2)}) copy-start(s32[64]{0:T(128)} %offset_ref.2) | copy-start | bytes 772
  39.2 17.5 %collective-permute-start.4 = (bf16[2,4,320,128]{3,2,1,0:T(8,128)(2,1)S(1)}, bf16[2,4,320,128]{3,2,1,0:T(8,128)(2,1)S(1)}, u32[]{:S(2)}, u32[]{:S(2)}) collective-permute-start(bf16[2,4,320,128]{3,2,1,0:T(8,128)(2,1)S(1)} %shard_map.165.rows_ref.mine_ref), channel_id=1, source_target_pairs={{0,64},{64,0},{1,65},{65,1},{2,66},{66,2},{3,67},{67,3},{4,68},{68... | collective-permute-start | bytes 1966088 | tf_op jit(solution)/shard_map/ppermute | solution.py:414
  56.7 1.7 copy-start.9
  69.7 1.1 copy-start.10
  75.9 40.1 %copy-start.1 = (bf16[128,640]{1,0:T(8,128)(2,1)S(1)}, bf16[128,640]{1,0:T(8,128)(2,1)}, u32[]{:S(2)}) copy-start(bf16[128,640]{1,0:T(8,128)(2,1)} %rk_ref.3) | copy-start | bytes 491524
  75.9 40.1 %copy-start.2 = (bf16[128,640]{1,0:T(8,128)(2,1)S(1)}, bf16[128,640]{1,0:T(8,128)(2,1)}, u32[]{:S(2)}) copy-start(bf16[128,640]{1,0:T(8,128)(2,1)} %rv_ref.3) | copy-start | bytes 491524
  75.9 40.1 %copy-start.5 = (bf16[640,128]{1,0:T(8,128)(2,1)S(1)}, bf16[640,128]{1,0:T(8,128)(2,1)}, u32[]{:S(2)}) copy-start(bf16[640,128]{1,0:T(8,128)(2,1)} %kp_ref.1) | copy-start | bytes 491524
  75.9 40.1 %copy-start.6 = (bf16[640,128]{1,0:T(8,128)(2,1)S(1)}, bf16[640,128]{1,0:T(8,128)(2,1)}, u32[]{:S(2)}) copy-start(bf16[640,128]{1,0:T(8,128)(2,1)} %vp_ref.1) | copy-start | bytes 491524
  98.1 17.9 %copy-start = (bf16[128,640]{1,0:T(8,128)(2,1)S(1)}, bf16[128,640]{1,0:T(8,128)(2,1)}, u32[]{:S(2)}) copy-start(bf16[128,640]{1,0:T(8,128)(2,1)} %rq_ref.3) | copy-start | bytes 491524
  117.9 20.6 %all-to-all-start.4 = ((bf16[32,48,128]{2,1,0:T(8,128)(2,1)}), bf16[32,48,128]{2,1,0:T(8,128)(2,1)S(1)}, u32[]{:S(2)}, u32[]{:S(2)}) async-start(bf16[32,48,128]{2,1,0:T(8,128)(2,1)} %get-tuple-element.167), calls=%async_computation.4 | async-start | bytes 786432 | tf_op jit(solution)/shard_map/all_to_all | solution.py:478
  122.8 3.5 %collective-permute-start.6 = (bf16[4,320,128]{2,1,0:T(8,128)(2,1)S(1)}, bf16[4,320,128]{2,1,0:T(8,128)(2,1)S(1)}, u32[]{:S(2)}, u32[]{:S(2)}) collective-permute-start(bf16[4,320,128]{2,1,0:T(8,128)(2,1)S(1)} %get-tuple-element.172), channel_id=1, source_target_pairs={{0,64},{64,0},{1,65},{65,1},{2,66},{66,2},{3,67},{67,3},{4,68},{68... | collective-permute-start | bytes 983048 | tf_op jit(solution)/shard_map/ppermute | solution.py:472
  126.9 23.4 %collective-permute-start.7 = (bf16[2,320,128]{2,1,0:T(8,128)(2,1)S(1)}, bf16[2,320,128]{2,1,0:T(8,128)(2,1)S(1)}, u32[]{:S(2)}, u32[]{:S(2)}) collective-permute-start(bf16[2,320,128]{2,1,0:T(8,128)(2,1)S(1)} %get-tuple-element.174), channel_id=1, source_target_pairs={{0,256},{128,384},{256,0},{384,128},{1,257},{129,385},{257,1},{385... | collective-permute-start | bytes 491528 | tf_op jit(solution)/shard_map/ppermute | solution.py:477
  139.1 9.6 %collective-permute-start.5 = (f32[48,128]{1,0:T(8,128)S(1)}, f32[48,128]{1,0:T(8,128)S(1)}, u32[]{:S(2)}, u32[]{:S(2)}) collective-permute-start(f32[48,128]{1,0:T(8,128)S(1)} %shard_map.171), channel_id=1, source_target_pairs={{0,32},{32,0},{1,33},{33,1},{2,34},{34,2},{3,35},{35,3},{4,36},{36... | collective-permute-start | bytes 73736 | tf_op jit(solution)/shard_map/ppermute | solution.py:491
  150.3 18.9 %all-to-all-start.5 = ((bf16[32,48,128]{2,1,0:T(8,128)(2,1)}), bf16[32,48,128]{2,1,0:T(8,128)(2,1)S(1)}, u32[]{:S(2)}, u32[]{:S(2)}) async-start(bf16[32,48,128]{2,1,0:T(8,128)(2,1)} %shard_map.172), calls=%async_computation.5 | async-start | bytes 786432 | tf_op jit(solution)/shard_map/all_to_all | solution.py:502
  156.1 15.3 %collective-permute-start.8 = (bf16[320,128]{1,0:T(8,128)(2,1)S(1)}, bf16[320,128]{1,0:T(8,128)(2,1)S(1)}, u32[]{:S(2)}, u32[]{:S(2)}) collective-permute-start(bf16[320,128]{1,0:T(8,128)(2,1)S(1)} %get-tuple-element.182), channel_id=1, source_target_pairs={{0,128},{128,0},{256,384},{384,256},{1,129},{129,1},{257,385},{385... | collective-permute-start | bytes 245768 | tf_op jit(solution)/shard_map/ppermute | solution.py:501

commit v7 on v6

--- a/solution.py
+++ b/solution.py
@@ -232,9 +232,21 @@
         out_ref[n * count : (n + 1) * count] = jnp.broadcast_to(part[None], (count,) + part.shape)
 
 
+def early_kernel(heads, rk_ref, rv_ref, to_ref, extra_ref, out_ref, wire):
+    plane = wire.shape[0]
+    used = SLICE * heads
+    wire[:, used:, :] = jnp.broadcast_to(extra_ref[...][None], (plane,) + extra_ref.shape)
+    for i in range(heads):
+        at = slice(i * 128, (i + 1) * 128)
+        key_w = (rk_ref[:, at].astype(F32) * to_ref[:, i : i + 1]).astype(BF)
+        state = dot_tn(key_w, rv_ref[:, at])
+        for k in range(SLICE):
+            wire[:, SLICE * i + k, :] = state[k * plane : (k + 1) * plane]
+    out_ref[...] = wire[...].astype(BF)
+
+
 def states_kernel(
-    heads, whole_ref, kp_ref, vp_ref, rq_ref, rk_ref, rv_ref, from_ref, to_ref, extra_ref,
-    ck_ref, cv_ref, gr_ref, send_ref, wire,
+    heads, whole_ref, kp_ref, vp_ref, rq_ref, from_ref, early_ref, ck_ref, cv_ref, gr_ref, send_ref, wire,
 ):
     count = whole_ref.shape[0] // HALVES
     rows = whole_ref.shape[1] // 2
@@ -244,21 +256,18 @@
     ck_ref[...] = ck
     cv_ref[...] = cv
     plane = send_ref.shape[0]
-    used = 2 * SLICE * heads
-    wire[:, used:, :] = jnp.broadcast_to(extra_ref[...][None], (plane,) + extra_ref.shape)
+    lines = send_ref.shape[1] - early_ref.shape[1]
+    wire[:, SLICE * heads :, :] = jnp.zeros((plane, lines - SLICE * heads, 128), F32)
     for i in range(heads):
         at = slice(i * 128, (i + 1) * 128)
         gr = (dot_nt(ck, kp_ref[at, :]) + dot_nt(cv, vp_ref[at, :])).astype(BF)
         gr_ref[:, at] = gr
         query_w = (rq_ref[:, at].astype(F32) * from_ref[:, i : i + 1]).astype(BF)
-        key_w = (rk_ref[:, at].astype(F32) * to_ref[:, i : i + 1]).astype(BF)
         grad = dot_tn(query_w, gr)
-        state = dot_tn(key_w, rv_ref[:, at])
         for k in range(SLICE):
-            part = slice(k * plane, (k + 1) * plane)
-            wire[:, SLICE * i + k, :] = grad[part]
-            wire[:, SLICE * (heads + i) + k, :] = state[part]
-    send_ref[...] = wire[...].astype(BF)
+            wire[:, SLICE * i + k, :] = grad[k * plane : (k + 1) * plane]
+    send_ref[:, 0:lines, :] = wire[...].astype(BF)
+    send_ref[:, lines:, :] = early_ref[...]
 
 
 def totals_kernel(heads, part_ref, decay_ref, out_ref):
@@ -274,7 +283,7 @@
 
     fore, back = lax.fori_loop(0, count, step, (zero, zero), unroll=4)
     row = lax.broadcasted_iota(jnp.int32, zero.shape, 0)
-    out_ref[...] = jnp.where(row < SLICE * heads, back, fore)
+    out_ref[...] = jnp.where(row < WIRE // 2, back, fore)
 
 
 def scan_kernel(heads, where_ref, part_ref, decay_ref, other_ref, out_ref, ahead, behind):
@@ -295,18 +304,12 @@
     start = (jnp.where(upper, other, zero), jnp.where(upper, zero, other))
     lax.fori_loop(0, count, step, start, unroll=4)
     row = lax.broadcasted_iota(jnp.int32, part_ref.shape, 1)
-    out_ref[...] = jnp.where(row < SLICE * heads, behind[...], ahead[...]).astype(BF)
-
-
-def final_kernel(
-    heads, rq_ref, rk_ref, rv_ref, gr_ref, cum_ref, cum_t_ref, from_ref, to_ref, wire_ref,
-    q_ref, k_ref, v_ref, wire,
+    out_ref[...] = jnp.where(row < WIRE // 2, behind[...], ahead[...]).astype(BF)
+
+
+def within_kernel(
+    heads, rq_ref, rk_ref, rv_ref, gr_ref, cum_ref, cum_t_ref, q_ref, k_ref, v_ref,
 ):
-    wire[...] = wire_ref[...].astype(F32)
-
-    def matrix(r):
-        return jnp.concatenate([wire[:, r + k, :] for k in range(SLICE)], axis=0).astype(BF)
-
     size = rq_ref.shape[0]
     t = lax.broadcasted_iota(jnp.int32, (size, size), 0)
     u = lax.broadcasted_iota(jnp.int32, (size, size), 1)
@@ -314,15 +317,31 @@
     for i in range(heads):
         at = slice(i * 128, (i + 1) * 128)
         qr, kr, vr, gr = rq_ref[:, at], rk_ref[:, at], rv_ref[:, at], gr_ref[:, at]
-        grad_b, state_b = matrix(SLICE * i), matrix(SLICE * (heads + i))
         gap = cum_t_ref[:, i : i + 1] - cum_ref[i : i + 1, :]
         decay = jnp.where(causal, jnp.exp(jnp.where(causal, gap, 0.0)), 0.0)
-        from_start, to_end = from_ref[:, i : i + 1], to_ref[:, i : i + 1]
         one = (decay * dot_nt(gr, vr)).astype(BF)
         three = (decay * dot_nt(qr, kr)).astype(BF)
-        q_ref[:, at] = dot_nn(one, kr) + from_start * dot_nt(gr, state_b)
-        k_ref[:, at] = dot_tn(one, qr) + to_end * dot_nt(vr, grad_b)
-        v_ref[:, at] = dot_tn(three, gr) + to_end * dot_nn(kr, grad_b)
+        q_ref[:, at] = dot_nn(one, kr)
+        k_ref[:, at] = dot_tn(one, qr)
+        v_ref[:, at] = dot_tn(three, gr)
+
+
+def final_kernel(
+    heads, rk_ref, rv_ref, gr_ref, from_ref, to_ref, q_in_ref, k_in_ref, v_in_ref, wire_ref,
+    q_ref, k_ref, v_ref, wire,
+):
+    wire[...] = wire_ref[...].astype(F32)
+
+    def matrix(r):
+        return jnp.concatenate([wire[:, r + k, :] for k in range(SLICE)], axis=0).astype(BF)
+
+    for i in range(heads):
+        at = slice(i * 128, (i + 1) * 128)
+        grad_b, state_b = matrix(SLICE * i), matrix(WIRE // 2 + SLICE * i)
+        from_start, to_end = from_ref[:, i : i + 1], to_ref[:, i : i + 1]
+        q_ref[:, at] = q_in_ref[:, at] + from_start * dot_nt(gr_ref[:, at], state_b)
+        k_ref[:, at] = k_in_ref[:, at] + to_end * dot_nt(rv_ref[:, at], grad_b)
+        v_ref[:, at] = v_in_ref[:, at] + to_end * dot_nn(rk_ref[:, at], grad_b)
 
 
 def query_grad_kernel(heads, factor, own_ref, got_ref, out_ref):
@@ -367,7 +386,6 @@
     kv_own = jnp.concatenate(
         [lax.dynamic_slice_in_dim(a, place * rows, rows, 0) for a in (cache_keys, cache_values)]
     )
-    kv_own, queries, output_grad = lax.optimization_barrier((kv_own, queries, output_grad))
     kv_other = lax.ppermute(kv_own, "zh", [(0, 1), (1, 0)])
     kv = jnp.where(
         half == 0,
@@ -390,7 +408,8 @@
     )
 
     local = retention_decay.shape[0]
-    used = 2 * SLICE * local
+    used = SLICE * local
+    lines_half = WIRE // 2
     cum = jnp.cumsum(retention_decay, axis=1)
     cum_t = cum.T
     last = cum[:, -1]
@@ -401,11 +420,19 @@
     middle = rest.astype(BF)
     low = (rest - middle.astype(F32)).astype(BF)
     extra = jnp.concatenate([high, middle, low]).astype(F32)
-    extra = jnp.pad(extra[None], ((0, WIRE - used - 1), (0, head - extra.shape[0])))
-
-    env = (where, offsets, delta, cum, cum_t, from_start, to_end, extra)
+    extra = jnp.pad(extra[None], ((0, lines_half - used - 1), (0, head - extra.shape[0])))
+
+    wide = retention_query.shape
+    early = call(
+        functools.partial(early_kernel, local),
+        shape((PLANE, WIRE // 2, head), BF), (),
+        (retention_key, retention_value, to_end, extra),
+        scratch=[pltpu.VMEM((PLANE, WIRE // 2, head), F32)], flops=1 << 26,
+    )
+
+    env = (where, offsets, delta, cum, cum_t, from_start, to_end, early)
     mine = call(
-        gather_kernel, shape((2, CHIPS, flat, head), BF), (where,), tuple(parts), flops=16 << 30
+        gather_kernel, shape((2, CHIPS, flat, head), BF), (where,), tuple(parts)
     )
     kv, env = lax.optimization_barrier((kv, env))
     kv = lax.all_to_all(kv, PLANE_AXES, 0, 0, tiled=True)
@@ -452,20 +479,17 @@
         shape((HALVES * secs, 2 * rows, head), BF), (), (terms,),
     )
     whole, env = pinned_exchange(total, ("zh", "zl", "core"), env)
-    where, offsets, delta, cum, cum_t, from_start, to_end, extra = env
+    where, offsets, delta, cum, cum_t, from_start, to_end, early = env
 
     cache_key_grad, cache_value_grad, out_grad, send = call(
         functools.partial(states_kernel, local),
         (
             shape((block_rows, head), BF), shape((block_rows, head), BF),
-            shape(retention_query.shape, BF), shape((PLANE, WIRE, head), BF),
+            shape(wide, BF), shape((PLANE, WIRE, head), BF),
         ),
         (),
-        (
-            whole, key_projection, value_projection,
-            retention_query, retention_key, retention_value, from_start, to_end, extra,
-        ),
-        scratch=[pltpu.VMEM((PLANE, WIRE, head), F32)],
+        (whole, key_projection, value_projection, retention_query, from_start, early),
+        scratch=[pltpu.VMEM((PLANE, WIRE // 2, head), F32)],
         flops=1 << 27,
     )
     send, dq_own, dq_other = lax.optimization_barrier((send, dq_own, dq_other))
@@ -477,12 +501,11 @@
     away = lax.ppermute(away, "zl", [(i, i ^ 2) for i in range(CHIPS)])
     part = lax.all_to_all(send, PLANE_AXES, 0, 0, tiled=True)
     part, where = lax.optimization_barrier((part, where))
-    lasts = part[:, used, : 3 * local].astype(F32).reshape(PLANE, 3, local)
+    lasts = part[:, lines_half + used, : 3 * local].astype(F32).reshape(PLANE, 3, local)
     decays = jnp.exp(lasts[:, 0] + lasts[:, 1] + lasts[:, 2])
-    decays = jnp.concatenate([decays, decays], axis=1)
-    decays = jnp.broadcast_to(decays[:, :, None], (PLANE, 2 * local, SLICE))
-    decays = decays.reshape(PLANE, used, 1)
-    decays = jnp.pad(decays, ((0, 0), (0, WIRE - used), (0, 0)))
+    decays = jnp.broadcast_to(decays[:, :, None], (PLANE, local, SLICE))
+    decays = jnp.pad(decays.reshape(PLANE, used), ((0, 0), (0, lines_half - used)))
+    decays = jnp.concatenate([decays, decays], axis=1)[:, :, None]
     decays = jnp.broadcast_to(decays, (PLANE, WIRE, head))
     totals = call(
         functools.partial(totals_kernel, local),
@@ -500,16 +523,16 @@
     )
     piece = lax.ppermute(piece, "zl", [(i, i ^ 1) for i in range(CHIPS)])
     enter = lax.all_to_all(enter, PLANE_AXES, 0, 0, tiled=True)
+    within = call(
+        functools.partial(within_kernel, local), (shape(wide, F32),) * 3, (),
+        (retention_query, retention_key, retention_value, out_grad, cum, cum_t),
+        flops=1 << 28,
+    )
     grads = call(
-        functools.partial(final_kernel, local),
-        (shape(retention_query.shape, F32),) * 3,
-        (),
-        (
-            retention_query, retention_key, retention_value, out_grad, cum, cum_t,
-            from_start, to_end, enter,
-        ),
+        functools.partial(final_kernel, local), (shape(wide, F32),) * 3, (),
+        (retention_key, retention_value, out_grad, from_start, to_end, *within, enter),
         scratch=[pltpu.VMEM(enter.shape, F32)],
-        flops=1 << 28,
+        flops=1 << 27,
     )
     grads, dq_mine, piece = lax.optimization_barrier((grads, dq_mine, piece))
     cross_query_grad = call(

time: 173 us -> 171 us (0.988)
  waiting for transfers between devices: 41.7 us -> 33.4 us
  blocking collectives: 51 us -> 58.2 us
  local copies, waits for them, and re-layouts: 6.03 us -> 3.85 us
    all_to_all x1, waiting for transfers between devices: 13.9 us -> 0.01 us  [body(): kv = lax.all_to_all(kv, PLANE_AXES, 0, 0, tiled=True)]
    all_to_all x3, blocking collectives: 51 us -> 58.2 us  [pinned_exchange(): array = lax.all_to_all(array, axes, 0, 0, tiled=True)]
    ppermute x3, waiting for transfers between devices: 0.01 us -> 6.47 us  [body(): lax.ppermute(own, 'zl', [(i, (i - k) % CHIPS) for i in range(CHIPS)])]
    unnamed x26 -> x24, local copies, waits for them, and re-layouts: 3.61 us -> 1.42 us
    ppermute x1, starting transfers between devices: 9.12 us -> 11 us  [body(): kv_other = lax.ppermute(kv_own, 'zh', [(0, 1), (1, 0)])]
    ppermute x3, starting transfers between devices: 12.8 us -> 11 us  [body(): lax.ppermute(own, 'zl', [(i, (i - k) % CHIPS) for i in range(CHIPS)])]
    pallas_call x14 -> x16, Pallas kernels: 17.6 us -> 18.5 us  [call(): pl.pallas_call(kernel, out_shape=outs, in_specs=[smem] * len(in_smem) + [...]
  transfers between devices with their start and end apart: 12 -> 12, of which waited for: 5 -> 7; matrix products, arithmetic and copies ran while one was open for 1% -> 1% of each run, Pallas kernels for 5% -> 5%
where the time goes in v7:
time: 171 us; the launch traced here: 170 us
  blocking collectives  58.2 us (34%)
  starting transfers between devices  54.5 us (32%)
  waiting for transfers between devices  33.4 us (20%)
  Pallas kernels  18.5 us (11%)
  local copies, waits for them, and re-layouts  3.85 us (2%)
    all_to_all x3, blocking collectives, pinned_exchange(): array = lax.all_to_all(array, axes, 0, 0, tiled=True)  58.2 us
    pallas_call x16, Pallas kernels, call(): pl.pallas_call(kernel, out_shape=outs, in_specs=[smem] * len(in_smem) + [...  18.5 us
    ppermute x1, starting transfers between devices, body(): kv_other = lax.ppermute(kv_own, 'zh', [(0, 1), (1, 0)])  11 us
    ppermute x3, starting transfers between devices, body(): lax.ppermute(own, 'zl', [(i, (i - k) % CHIPS) for i in range(CHIPS)])  11 us
    all_to_all x1, starting transfers between devices, body(): kv = lax.all_to_all(kv, PLANE_AXES, 0, 0, tiled=True)  10.3 us
    all_to_all x1, waiting for transfers between devices, body(): enter = lax.all_to_all(enter, PLANE_AXES, 0, 0, tiled=True)  9.81 us
    all_to_all x1, waiting for transfers between devices, body(): part = lax.all_to_all(send, PLANE_AXES, 0, 0, tiled=True)  8.87 us
    ppermute x1, waiting for transfers between devices, body(): totals = lax.ppermute(totals, 'zh', [(0, 1), (1, 0)])  6.5 us
  transfers between devices with their start and end apart: 12, of which 7 were waited for; matrix products, arithmetic and copies ran while one was open for 1% of the time, Pallas kernels for 5%

profile of v7, /device:TPU:8, one launch (start us, length us, event | category | flops | bytes accessed | tf_op | source)
XLA Modules:
  0.0 170.1 jit_solution(4904088938729888128)
XLA Ops:
  0.6 0.7 constant_dynamic-slice_fusion
  1.4 11.0 %collective-permute-start = (bf16[32,128]{1,0:T(8,128)(2,1)S(1)}, bf16[32,128]{1,0:T(8,128)(2,1)S(1)}, u32[]{:S(2)}, u32[]{:S(2)}) collective-permute-start(bf16[32,128]{1,0:T(8,128)(2,1)S(1)} %pad_maximum_fusion.2), channel_id=1, source_target_pairs={{0,32},{32,0},{1,33},{33,1},{2,34},{34,2},{3,35},{35,3},{4,36},{36... | collective-permute-start | bytes 24584 | tf_op jit(solution)/shard_map/ppermute | solution.py:389
  13.9 0.7 shard_map.163
  15.2 0.9 broadcast_in_dim.8
  16.1 10.3 %all-to-all-start = ((bf16[32,64,128]{2,1,0:T(8,128)(2,1)}), bf16[32,64,128]{2,1,0:T(8,128)(2,1)S(1)}, u32[]{:S(2)}, u32[]{:S(2)}) async-start(bf16[32,64,128]{2,1,0:T(8,128)(2,1)} %broadcast_in_dim.8), calls=%async_computation | async-start | bytes 1048576 | tf_op jit(solution)/shard_map/all_to_all | solution.py:438
  26.5 3.4 %collective-permute-start.3 = (bf16[640,128]{1,0:T(8,128)(2,1)S(1)}, bf16[640,128]{1,0:T(8,128)(2,1)S(1)}, u32[]{:S(2)}, u32[]{:S(2)}) collective-permute-start(bf16[640,128]{1,0:T(8,128)(2,1)S(1)} %shard_map.165.a_ref), channel_id=1, source_target_pairs={{0,128},{128,256},{256,384},{384,0},{1,129},{129,257},{257,385},{3... | collective-permute-start | bytes 491528 | tf_op jit(solution)/shard_map/ppermute | solution.py:401
  29.8 4.3 %collective-permute-start.2 = (bf16[640,128]{1,0:T(8,128)(2,1)S(1)}, bf16[640,128]{1,0:T(8,128)(2,1)S(1)}, u32[]{:S(2)}, u32[]{:S(2)}) collective-permute-start(bf16[640,128]{1,0:T(8,128)(2,1)S(1)} %shard_map.165.a_ref), channel_id=1, source_target_pairs={{0,256},{128,384},{256,0},{384,128},{1,257},{129,385},{257,1},{385... | collective-permute-start | bytes 491528 | tf_op jit(solution)/shard_map/ppermute | solution.py:401
  34.1 3.4 %collective-permute-start.1 = (bf16[640,128]{1,0:T(8,128)(2,1)S(1)}, bf16[640,128]{1,0:T(8,128)(2,1)S(1)}, u32[]{:S(2)}, u32[]{:S(2)}) collective-permute-start(bf16[640,128]{1,0:T(8,128)(2,1)S(1)} %shard_map.165.a_ref), channel_id=1, source_target_pairs={{0,384},{128,0},{256,128},{384,256},{1,385},{129,1},{257,129},{385... | collective-permute-start | bytes 491528 | tf_op jit(solution)/shard_map/ppermute | solution.py:401
  37.5 5.1 %collective-permute-done.2.c_ref = bf16[640,128]{1,0:T(8,128)(2,1)S(1)} collective-permute-done((bf16[640,128]{1,0:T(8,128)(2,1)S(1)}, bf16[640,128]{1,0:T(8,128)(2,1)S(1)}, u32[]{:S(2)}, u32[]{:S(2)}) %collective-permute-start.2) | collective-permute-done | bytes 163872 | tf_op jit(solution)/shard_map/ppermute | solution.py:401
  42.6 1.4 collective-permute-done.1.b_ref
  44.6 1.9 %collective-permute-start.4 = (bf16[2,4,320,128]{3,2,1,0:T(8,128)(2,1)S(1)}, bf16[2,4,320,128]{3,2,1,0:T(8,128)(2,1)S(1)}, u32[]{:S(2)}, u32[]{:S(2)}) collective-permute-start(bf16[2,4,320,128]{3,2,1,0:T(8,128)(2,1)S(1)} %shard_map.166.rows_ref.mine_ref), channel_id=1, source_target_pairs={{0,64},{64,0},{1,65},{65,1},{2,66},{66,2},{3,67},{67,3},{4,68},{68... | collective-permute-start | bytes 1966088 | tf_op jit(solution)/shard_map/ppermute | solution.py:441
  46.6 1.6 shard_map.167
  48.6 1.6 shard_map.168
  50.3 11.4 %all_to_all.30 = f32[8,32,128]{2,1,0:T(8,128)S(1)} all-to-all(f32[8,32,128]{2,1,0:T(8,128)S(1)} %broadcast_in_dim.9), channel_id=1, replica_groups=mesh['zl'=4,'core'=2,'zh'=2,'x'=4,'y'=8] {'zl','core'}, dimensions={0} | all-to-all | bytes 262144 | tf_op jit(solution)/shard_map/all_to_all | solution.py:56
  61.8 5.1 %shard_map.169 = (bf16[32,64,128]{2,1,0:T(8,128)(2,1)S(1)}, f32[4,320,128]{2,1,0:T(8,128)S(1)}, bf16[4,320,128]{2,1,0:T(8,128)(2,1)S(1)}) custom-call(s32[4]{0:T(128)S(1)} %pad_add_fusion.where_ref, s32[64]{0:T(128)S(1)} %copy-done.10, bf16[2,4,320,128]{3,2,1,0:T(8,128)(2,1)S(1)} %shard_map.166.rows_ref.mine_ref, ...), custom_call_target="tpu_custom_call" | custom-call | flops 4294967296 | bytes 1048576 | tf_op jit(solution)/shard_map/pallas_call | solution.py:39
  66.9 0.7 copy-done.8
  67.6 26.9 %all_to_all.31.terms_ref = bf16[32,64,128]{2,1,0:T(8,128)(2,1)S(1)} all-to-all(bf16[32,64,128]{2,1,0:T(8,128)(2,1)S(1)} %get-tuple-element.133), channel_id=1, replica_groups=mesh['zl'=4,'core'=2,'zh'=2,'x'=4,'y'=8] {'x','y'}, dimensions={0} | all-to-all | bytes 1048576 | tf_op jit(solution)/shard_map/all_to_all | solution.py:56
  94.6 19.9 %all_to_all.32.whole_ref = bf16[16,32,128]{2,1,0:T(8,128)(2,1)S(1)} all-to-all(bf16[16,32,128]{2,1,0:T(8,128)(2,1)S(1)} %shard_map.170), channel_id=1, replica_groups=mesh['zl'=4,'core'=2,'zh'=2,'x'=4,'y'=8] {'zh','zl','core'}, dimensions={0} | all-to-all | bytes 262144 | tf_op jit(solution)/shard_map/all_to_all | solution.py:56
  114.5 1.9 %shard_map.171 = (bf16[128,128]{1,0:T(8,128)(2,1)}, bf16[128,128]{1,0:T(8,128)(2,1)}, bf16[128,640]{1,0:T(8,128)(2,1)S(1)}, bf16[32,48,128]{2,1,0:T(8,128)(2,1)}) custom-call(bf16[16,32,128]{2,1,0:T(8,128)(2,1)S(1)} %all_to_all.32.whole_ref, bf16[640,128]{1,0:T(8,128)(2,1)S(1)} %copy-done.3, bf16[640,128]{1,0:T(8,128)(2,1)S(1)} %copy-done.4, ...), custom_call_target="tpu_custom_call" | custom-call | flops 134217728 | bytes 1048576 | tf_op jit(solution)/shard_map/pallas_call | solution.py:39
  116.5 5.0 %all-to-all-start.4 = ((bf16[32,48,128]{2,1,0:T(8,128)(2,1)}), bf16[32,48,128]{2,1,0:T(8,128)(2,1)S(1)}, u32[]{:S(2)}, u32[]{:S(2)}) async-start(bf16[32,48,128]{2,1,0:T(8,128)(2,1)} %get-tuple-element.167), calls=%async_computation.4 | async-start | bytes 786432 | tf_op jit(solution)/shard_map/all_to_all | solution.py:502
  121.5 2.2 %collective-permute-start.6 = (bf16[4,320,128]{2,1,0:T(8,128)(2,1)S(1)}, bf16[4,320,128]{2,1,0:T(8,128)(2,1)S(1)}, u32[]{:S(2)}, u32[]{:S(2)}) collective-permute-start(bf16[4,320,128]{2,1,0:T(8,128)(2,1)S(1)} %copy-done.9), channel_id=1, source_target_pairs={{0,64},{64,0},{1,65},{65,1},{2,66},{66,2},{3,67},{67,3},{4,68},{68... | collective-permute-start | bytes 983048 | tf_op jit(solution)/shard_map/ppermute | solution.py:496
  123.7 1.3 collective-permute-done.6.other_ref
  125.6 2.7 %collective-permute-start.7 = (bf16[2,320,128]{2,1,0:T(8,128)(2,1)S(1)}, bf16[2,320,128]{2,1,0:T(8,128)(2,1)S(1)}, u32[]{:S(2)}, u32[]{:S(2)}) collective-permute-start(bf16[2,320,128]{2,1,0:T(8,128)(2,1)S(1)} %get-tuple-element.174), channel_id=1, source_target_pairs={{0,256},{128,384},{256,0},{384,128},{1,257},{129,385},{257,1},{385... | collective-permute-start | bytes 491528 | tf_op jit(solution)/shard_map/ppermute | solution.py:501
  128.3 8.9 %all-to-all-done.4.part_ref = bf16[32,48,128]{2,1,0:T(8,128)(2,1)S(1)} async-done(((bf16[32,48,128]{2,1,0:T(8,128)(2,1)}), bf16[32,48,128]{2,1,0:T(8,128)(2,1)S(1)}, u32[]{:S(2)}, u32[]{:S(2)}) %all-to-all-start.4) | async-done | bytes 393248 | tf_op jit(solution)/shard_map/all_to_all | solution.py:502
  137.8 3.1 %collective-permute-start.5 = (f32[48,128]{1,0:T(8,128)S(1)}, f32[48,128]{1,0:T(8,128)S(1)}, u32[]{:S(2)}, u32[]{:S(2)}) collective-permute-start(f32[48,128]{1,0:T(8,128)S(1)} %shard_map.173), channel_id=1, source_target_pairs={{0,32},{32,0},{1,33},{33,1},{2,34},{34,2},{3,35},{35,3},{4,36},{36... | collective-permute-start | bytes 73736 | tf_op jit(solution)/shard_map/ppermute | solution.py:514
  141.0 6.5 %collective-permute-done.5.other_ref = f32[48,128]{1,0:T(8,128)S(1)} collective-permute-done((f32[48,128]{1,0:T(8,128)S(1)}, f32[48,128]{1,0:T(8,128)S(1)}, u32[]{:S(2)}, u32[]{:S(2)}) %collective-permute-start.5) | collective-permute-done | bytes 24608 | tf_op jit(solution)/shard_map/ppermute | solution.py:514
  147.4 1.6 shard_map.174
  149.0 5.2 %all-to-all-start.5 = ((bf16[32,48,128]{2,1,0:T(8,128)(2,1)}), bf16[32,48,128]{2,1,0:T(8,128)(2,1)S(1)}, u32[]{:S(2)}, u32[]{:S(2)}) async-start(bf16[32,48,128]{2,1,0:T(8,128)(2,1)} %shard_map.174), calls=%async_computation.5 | async-start | bytes 786432 | tf_op jit(solution)/shard_map/all_to_all | solution.py:525
  154.8 2.0 %collective-permute-start.8 = (bf16[320,128]{1,0:T(8,128)(2,1)S(1)}, bf16[320,128]{1,0:T(8,128)(2,1)S(1)}, u32[]{:S(2)}, u32[]{:S(2)}) collective-permute-start(bf16[320,128]{1,0:T(8,128)(2,1)S(1)} %get-tuple-element.182), channel_id=1, source_target_pairs={{0,128},{128,0},{256,384},{384,256},{1,129},{129,1},{257,385},{385... | collective-permute-start | bytes 245768 | tf_op jit(solution)/shard_map/ppermute | solution.py:524
  156.8 1.2 shard_map.172
  158.0 9.8 %all-to-all-done.5.wire_ref = bf16[32,48,128]{2,1,0:T(8,128)(2,1)S(1)} async-done(((bf16[32,48,128]{2,1,0:T(8,128)(2,1)}), bf16[32,48,128]{2,1,0:T(8,128)(2,1)S(1)}, u32[]{:S(2)}, u32[]{:S(2)}) %all-to-all-start.5) | async-done | bytes 393248 | tf_op jit(solution)/shard_map/all_to_all | solution.py:525
  167.9 1.5 shard_map.176
  (68 shorter events, 5.6 us)
Async XLA Ops:
  1.4 11.1 %copy-start.11 = (f32[5,128]{1,0:T(8,128)S(1)}, f32[5,128]{1,0:T(8,128)}, u32[]{:S(2)}) copy-start(f32[5,128]{1,0:T(8,128)} %param.23) | copy-start | bytes 7684
  1.4 13.8 %collective-permute-start = (bf16[32,128]{1,0:T(8,128)(2,1)S(1)}, bf16[32,128]{1,0:T(8,128)(2,1)S(1)}, u32[]{:S(2)}, u32[]{:S(2)}) collective-permute-start(bf16[32,128]{1,0:T(8,128)(2,1)S(1)} %pad_maximum_fusion.2), channel_id=1, source_target_pairs={{0,32},{32,0},{1,33},{33,1},{2,34},{34,2},{3,35},{35,3},{4,36},{36... | collective-permute-start | bytes 24584 | tf_op jit(solution)/shard_map/ppermute | solution.py:389
  12.4 0.9 copy-start.7
  13.0 0.9 copy-start.2
  13.0 1.6 copy-start
  13.0 1.6 copy-start.1
  16.1 10.3 %copy-start.6 = (bf16[1,16,2560]{2,1,0:T(8,128)(2,1)S(1)}, bf16[1,16,2560]{2,1,0:T(8,128)(2,1)}, u32[]{:S(2)}) copy-start(bf16[1,16,2560]{2,1,0:T(8,128)(2,1)} %q_ref.1) | copy-start | bytes 245764
  16.1 30.4 %all-to-all-start = ((bf16[32,64,128]{2,1,0:T(8,128)(2,1)}), bf16[32,64,128]{2,1,0:T(8,128)(2,1)S(1)}, u32[]{:S(2)}, u32[]{:S(2)}) async-start(bf16[32,64,128]{2,1,0:T(8,128)(2,1)} %broadcast_in_dim.8), calls=%async_computation | async-start | bytes 1048576 | tf_op jit(solution)/shard_map/all_to_all | solution.py:438
  26.5 11.1 %collective-permute-start.3 = (bf16[640,128]{1,0:T(8,128)(2,1)S(1)}, bf16[640,128]{1,0:T(8,128)(2,1)S(1)}, u32[]{:S(2)}, u32[]{:S(2)}) collective-permute-start(bf16[640,128]{1,0:T(8,128)(2,1)S(1)} %shard_map.165.a_ref), channel_id=1, source_target_pairs={{0,128},{128,256},{256,384},{384,0},{1,129},{129,257},{257,385},{3... | collective-permute-start | bytes 491528 | tf_op jit(solution)/shard_map/ppermute | solution.py:401
  29.8 12.8 %collective-permute-start.2 = (bf16[640,128]{1,0:T(8,128)(2,1)S(1)}, bf16[640,128]{1,0:T(8,128)(2,1)S(1)}, u32[]{:S(2)}, u32[]{:S(2)}) collective-permute-start(bf16[640,128]{1,0:T(8,128)(2,1)S(1)} %shard_map.165.a_ref), channel_id=1, source_target_pairs={{0,256},{128,384},{256,0},{384,128},{1,257},{129,385},{257,1},{385... | collective-permute-start | bytes 491528 | tf_op jit(solution)/shard_map/ppermute | solution.py:401
  34.1 9.8 %collective-permute-start.1 = (bf16[640,128]{1,0:T(8,128)(2,1)S(1)}, bf16[640,128]{1,0:T(8,128)(2,1)S(1)}, u32[]{:S(2)}, u32[]{:S(2)}) collective-permute-start(bf16[640,128]{1,0:T(8,128)(2,1)S(1)} %shard_map.165.a_ref), channel_id=1, source_target_pairs={{0,384},{128,0},{256,128},{384,256},{1,385},{129,1},{257,129},{385... | collective-permute-start | bytes 491528 | tf_op jit(solution)/shard_map/ppermute | solution.py:401
  44.6 2.0 %copy-start.10 = (s32[64]{0:T(128)S(1)}, s32[64]{0:T(128)}, u32[]{:S(2)}) copy-start(s32[64]{0:T(128)} %offset_ref.2) | copy-start | bytes 772
  44.6 4.0 %collective-permute-start.4 = (bf16[2,4,320,128]{3,2,1,0:T(8,128)(2,1)S(1)}, bf16[2,4,320,128]{3,2,1,0:T(8,128)(2,1)S(1)}, u32[]{:S(2)}, u32[]{:S(2)}) collective-permute-start(bf16[2,4,320,128]{3,2,1,0:T(8,128)(2,1)S(1)} %shard_map.166.rows_ref.mine_ref), channel_id=1, source_target_pairs={{0,64},{64,0},{1,65},{65,1},{2,66},{66,2},{3,67},{67,3},{4,68},{68... | collective-permute-start | bytes 1966088 | tf_op jit(solution)/shard_map/ppermute | solution.py:441
  66.9 0.7 copy-start.8
  94.5 20.0 %copy-start.4 = (bf16[640,128]{1,0:T(8,128)(2,1)S(1)}, bf16[640,128]{1,0:T(8,128)(2,1)}, u32[]{:S(2)}) copy-start(bf16[640,128]{1,0:T(8,128)(2,1)} %vp_ref.1) | copy-start | bytes 491524
  94.5 20.0 %copy-start.5 = (bf16[128,640]{1,0:T(8,128)(2,1)S(1)}, bf16[128,640]{1,0:T(8,128)(2,1)}, u32[]{:S(2)}) copy-start(bf16[128,640]{1,0:T(8,128)(2,1)} %rq_ref.3) | copy-start | bytes 491524
  94.6 19.9 %copy-start.3 = (bf16[640,128]{1,0:T(8,128)(2,1)S(1)}, bf16[640,128]{1,0:T(8,128)(2,1)}, u32[]{:S(2)}) copy-start(bf16[640,128]{1,0:T(8,128)(2,1)} %kp_ref.1) | copy-start | bytes 491524
  116.5 5.0 %copy-start.9 = (bf16[4,320,128]{2,1,0:T(8,128)(2,1)S(1)}, bf16[4,320,128]{2,1,0:T(8,128)(2,1)}, u32[]{:S(2)}) copy-start(bf16[4,320,128]{2,1,0:T(8,128)(2,1)} %copy-done.8) | copy-start | bytes 983044
  116.5 20.7 %all-to-all-start.4 = ((bf16[32,48,128]{2,1,0:T(8,128)(2,1)}), bf16[32,48,128]{2,1,0:T(8,128)(2,1)S(1)}, u32[]{:S(2)}, u32[]{:S(2)}) async-start(bf16[32,48,128]{2,1,0:T(8,128)(2,1)} %get-tuple-element.167), calls=%async_computation.4 | async-start | bytes 786432 | tf_op jit(solution)/shard_map/all_to_all | solution.py:502
  121.5 3.5 %collective-permute-start.6 = (bf16[4,320,128]{2,1,0:T(8,128)(2,1)S(1)}, bf16[4,320,128]{2,1,0:T(8,128)(2,1)S(1)}, u32[]{:S(2)}, u32[]{:S(2)}) collective-permute-start(bf16[4,320,128]{2,1,0:T(8,128)(2,1)S(1)} %copy-done.9), channel_id=1, source_target_pairs={{0,64},{64,0},{1,65},{65,1},{2,66},{66,2},{3,67},{67,3},{4,68},{68... | collective-permute-start | bytes 983048 | tf_op jit(solution)/shard_map/ppermute | solution.py:496
  125.6 23.4 %collective-permute-start.7 = (bf16[2,320,128]{2,1,0:T(8,128)(2,1)S(1)}, bf16[2,320,128]{2,1,0:T(8,128)(2,1)S(1)}, u32[]{:S(2)}, u32[]{:S(2)}) collective-permute-start(bf16[2,320,128]{2,1,0:T(8,128)(2,1)S(1)} %get-tuple-element.174), channel_id=1, source_target_pairs={{0,256},{128,384},{256,0},{384,128},{1,257},{129,385},{257,1},{385... | collective-permute-start | bytes 491528 | tf_op jit(solution)/shard_map/ppermute | solution.py:501
  137.8 9.6 %collective-permute-start.5 = (f32[48,128]{1,0:T(8,128)S(1)}, f32[48,128]{1,0:T(8,128)S(1)}, u32[]{:S(2)}, u32[]{:S(2)}) collective-permute-start(f32[48,128]{1,0:T(8,128)S(1)} %shard_map.173), channel_id=1, source_target_pairs={{0,32},{32,0},{1,33},{33,1},{2,34},{34,2},{3,35},{35,3},{4,36},{36... | collective-permute-start | bytes 73736 | tf_op jit(solution)/shard_map/ppermute | solution.py:514
  149.0 18.9 %all-to-all-start.5 = ((bf16[32,48,128]{2,1,0:T(8,128)(2,1)}), bf16[32,48,128]{2,1,0:T(8,128)(2,1)S(1)}, u32[]{:S(2)}, u32[]{:S(2)}) async-start(bf16[32,48,128]{2,1,0:T(8,128)(2,1)} %shard_map.174), calls=%async_computation.5 | async-start | bytes 786432 | tf_op jit(solution)/shard_map/all_to_all | solution.py:525
  154.8 14.6 %collective-permute-start.8 = (bf16[320,128]{1,0:T(8,128)(2,1)S(1)}, bf16[320,128]{1,0:T(8,128)(2,1)S(1)}, u32[]{:S(2)}, u32[]{:S(2)}) collective-permute-start(bf16[320,128]{1,0:T(8,128)(2,1)S(1)} %get-tuple-element.182), channel_id=1, source_target_pairs={{0,128},{128,0},{256,384},{384,256},{1,129},{129,1},{257,385},{385... | collective-permute-start | bytes 245768 | tf_op jit(solution)/shard_map/ppermute | solution.py:524

commit v8 on v7

--- a/solution.py
+++ b/solution.py
@@ -33,14 +33,17 @@
     return lax.dot_general(a, b, (((0,), (0,)), ((), ())), preferred_element_type=F32)
 
 
-def call(kernel, outs, in_smem, ins, scratch=(), flops=0):
+def call(kernel, outs, in_smem, ins, scratch=(), flops=0, smem_outs=0):
     vmem = pl.BlockSpec(memory_space=pltpu.VMEM)
     smem = pl.BlockSpec(memory_space=pltpu.SMEM)
+    out_specs = jax.tree.map(lambda _: vmem, outs)
+    if smem_outs:
+        out_specs = (vmem,) * (len(outs) - smem_outs) + (smem,) * smem_outs
     return pl.pallas_call(
         kernel,
         out_shape=outs,
         in_specs=[smem] * len(in_smem) + [vmem] * len(ins),
-        out_specs=jax.tree.map(lambda _: vmem, outs),
+        out_specs=out_specs,
         scratch_shapes=list(scratch),
         compiler_params=pltpu.CompilerParams(vmem_limit_bytes=SCOPED),
         cost_estimate=pl.CostEstimate(flops=flops, bytes_accessed=1 << 20, transcendentals=0),
@@ -65,7 +68,17 @@
         out_ref[(heads + h) * rows : (heads + h + 1) * rows, :] = g_ref[0, :, at]
 
 
-def delta_kernel(heads, where_ref, g_ref, o_ref, out_ref, product):
+def spread_kernel(where_ref, own_ref, other_ref, out_ref):
+    plane = out_ref.shape[0]
+    half = where_ref[0] // plane
+    out_ref[:, half] = jnp.broadcast_to(own_ref[...][None], (plane,) + own_ref.shape)
+    out_ref[:, 1 - half] = jnp.broadcast_to(other_ref[...][None], (plane,) + other_ref.shape)
+
+
+def delta_kernel(heads, where_ref, offset_ref, g_ref, o_ref, out_ref, place_ref, product):
+    for n in range(4):
+        place_ref[n] = where_ref[n]
+    place_ref[4] = offset_ref[where_ref[0]]
     rows = g_ref.shape[1]
     base = lax.rem(where_ref[1], 2) * (heads * rows)
     product[...] = jnp.zeros_like(product)
@@ -87,10 +100,10 @@
         out_ref[1, chip] = ref[flat:]
 
 
-def row_positions(where_ref, offset_ref, width, rows, block_rows):
+def row_positions(where_ref, width, rows, block_rows):
     lane = lax.broadcasted_iota(jnp.int32, (1, width), 1)
     shard = where_ref[0]
-    return lax.rem(lane, rows) + (shard * block_rows + offset_ref[shard])
+    return lax.rem(lane, rows) + (shard * block_rows + where_ref[4])
 
 
 def key_positions(place, chunk, blocks, rows, block_rows):
@@ -104,10 +117,9 @@
     return pl.ds(pl.multiple_of(lax.rem(chunk, per) * blocks, blocks), blocks), line
 
 
-def cache_slice(kv_ref, chunk, blocks, rows, values):
-    at, line = cache_place(kv_ref, chunk, blocks, rows)
-    line = pl.multiple_of(line + values * rows, rows)
-    return kv_ref[at, pl.ds(line, rows), :].reshape(blocks * rows, -1)
+def keys_slice(kv_ref, chunk, blocks, rows, values):
+    at = pl.ds(pl.multiple_of(chunk * blocks, blocks), blocks)
+    return kv_ref[at, values * rows : (values + 1) * rows, :].reshape(blocks * rows, -1)
 
 
 def tile(refs, which, n, t):
@@ -115,18 +127,18 @@
 
 
 def stats_kernel(
-    blocks, rows, query_rows, block_rows, factor, where_ref, offset_ref, rows_ref, kv_ref, out_ref,
+    blocks, rows, query_rows, block_rows, factor, where_ref, rows_ref, kv_ref, out_ref,
 ):
     shard, place = where_ref[0], where_ref[2]
     width = 2 * rows_ref.shape[2]
     lines = width // 128
     full = shard // blocks
-    pos = row_positions(where_ref, offset_ref, width, query_rows, block_rows)
+    pos = row_positions(where_ref, width, query_rows, block_rows)
     scale = factor * LOG2E
     tiles = range(CHIPS // 2)
 
     def chunk(j, carry, masked=False):
-        keys = cache_slice(kv_ref, j, blocks, rows, 0)
+        keys = keys_slice(kv_ref, j, blocks, rows, 0)
         if masked:
             seen = key_positions(place, j, blocks, rows, block_rows) <= pos
         out = []
@@ -152,7 +164,7 @@
 
 def grads_kernel(
     blocks, rows, query_rows, block_rows, factor,
-    where_ref, offset_ref, mine_ref, other_ref, kv_ref, log_ref, delta_ref,
+    where_ref, mine_ref, other_ref, kv_ref, log_ref, delta_ref,
     dkv_ref, dq_own_ref, dq_other_ref, dq_total,
 ):
     shard, place, core = where_ref[0], where_ref[2], where_ref[3]
@@ -160,14 +172,14 @@
     width = 2 * flat
     size = blocks * rows
     full = shard // blocks
-    pos = row_positions(where_ref, offset_ref, width, query_rows, block_rows)
+    pos = row_positions(where_ref, width, query_rows, block_rows)
     scale = factor * LOG2E
     tiles = [(n, t) for n in range(CORES) for t in range(CHIPS // 2)]
     dq_total[...] = jnp.zeros_like(dq_total)
 
     def chunk(j, masked=False):
-        keys = cache_slice(kv_ref, j, blocks, rows, 0)
-        values = cache_slice(kv_ref, j, blocks, rows, 1)
+        keys = keys_slice(kv_ref, j, blocks, rows, 0)
+        values = keys_slice(kv_ref, j, blocks, rows, 1)
         if masked:
             seen = key_positions(place, j, blocks, rows, block_rows) <= pos
         dk = dv = 0.0
@@ -182,7 +194,7 @@
             dk = dk + dot_nn(ds, q)
             dv = dv + dot_nn(p.astype(BF), g)
             dq_total[i] += dot_tn(keys, ds)
-        at, line = cache_place(kv_ref, j, blocks, rows)
+        at, line = cache_place(dkv_ref, j, blocks, rows)
         dkv_ref[at, pl.ds(line, rows), :] = dk.astype(BF).reshape(blocks, rows, -1)
         dkv_ref[at, pl.ds(line + rows, rows), :] = dv.astype(BF).reshape(blocks, rows, -1)
 
@@ -194,11 +206,11 @@
     chunk(full, masked=True)
 
     def clear(j, _):
-        at, line = cache_place(kv_ref, j, blocks, rows)
+        at, line = cache_place(dkv_ref, j, blocks, rows)
         dkv_ref[at, pl.ds(line, 2 * rows), :] = jnp.zeros((blocks, 2 * rows, kv_ref.shape[-1]), BF)
         return 0
 
-    lax.fori_loop(full + 1, HALVES * kv_ref.shape[0] // blocks, clear, 0)
+    lax.fori_loop(full + 1, HALVES * dkv_ref.shape[0] // blocks, clear, 0)
     for i, (n, t) in enumerate(tiles):
         dq = dq_total[i].T
         dq_ref = (dq_own_ref, dq_other_ref)[n]
@@ -303,8 +315,10 @@
 
     start = (jnp.where(upper, other, zero), jnp.where(upper, zero, other))
     lax.fori_loop(0, count, step, start, unroll=4)
-    row = lax.broadcasted_iota(jnp.int32, part_ref.shape, 1)
-    out_ref[...] = jnp.where(row < WIRE // 2, behind[...], ahead[...]).astype(BF)
+    used = SLICE * heads
+    at = WIRE // 2
+    both = jnp.concatenate([behind[:, 0:used, :], ahead[:, at : at + used, :]], axis=1)
+    out_ref[...] = both.astype(BF)
 
 
 def within_kernel(
@@ -337,7 +351,7 @@
 
     for i in range(heads):
         at = slice(i * 128, (i + 1) * 128)
-        grad_b, state_b = matrix(SLICE * i), matrix(WIRE // 2 + SLICE * i)
+        grad_b, state_b = matrix(SLICE * i), matrix(SLICE * (heads + i))
         from_start, to_end = from_ref[:, i : i + 1], to_ref[:, i : i + 1]
         q_ref[:, at] = q_in_ref[:, at] + from_start * dot_nt(gr_ref[:, at], state_b)
         k_ref[:, at] = k_in_ref[:, at] + to_end * dot_nt(rv_ref[:, at], grad_b)
@@ -386,24 +400,19 @@
     kv_own = jnp.concatenate(
         [lax.dynamic_slice_in_dim(a, place * rows, rows, 0) for a in (cache_keys, cache_values)]
     )
-    kv_other = lax.ppermute(kv_own, "zh", [(0, 1), (1, 0)])
-    kv = jnp.where(
-        half == 0,
-        jnp.concatenate([kv_own, kv_other]),
-        jnp.concatenate([kv_other, kv_own]),
-    )
-    kv = jnp.broadcast_to(kv[None], (PLANE,) + kv.shape)
+    kv = jnp.broadcast_to(kv_own[None], (shards,) + kv_own.shape)
     own = call(
         functools.partial(pack_kernel, heads),
-        shape((2 * flat, head), BF), (), (queries, output_grad),
+        shape((2 * flat, head), BF), (), (queries, output_grad), flops=1 << 20,
     )
     parts = [own] + [
         lax.ppermute(own, "zl", [(i, (i - k) % CHIPS) for i in range(CHIPS)])
         for k in range(1, CHIPS)
     ]
-    delta = call(
+    delta, where = call(
         functools.partial(delta_kernel, heads),
-        shape((32 - CHIPS * lines, head), F32), (where,), (output_grad, attention_out),
+        (shape((32 - CHIPS * lines, head), F32), shape((5,), jnp.int32)),
+        (where, offsets), (output_grad, attention_out), smem_outs=1,
         scratch=[pltpu.VMEM((width, head), F32)],
     )
 
@@ -430,21 +439,20 @@
         scratch=[pltpu.VMEM((PLANE, WIRE // 2, head), F32)], flops=1 << 26,
     )
 
-    env = (where, offsets, delta, cum, cum_t, from_start, to_end, early)
+    env = (where, delta, cum, cum_t, from_start, to_end, early)
     mine = call(
-        gather_kernel, shape((2, CHIPS, flat, head), BF), (where,), tuple(parts)
-    )
+        gather_kernel, shape((2, CHIPS, flat, head), BF), (where,), tuple(parts), flops=4 << 30
+    )
+    kv = lax.all_to_all(kv, ("zh",) + PLANE_AXES, 0, 0, tiled=True)
     kv, env = lax.optimization_barrier((kv, env))
-    kv = lax.all_to_all(kv, PLANE_AXES, 0, 0, tiled=True)
-    kv, env = lax.optimization_barrier((kv, env))
-    where, offsets, delta = env[:3]
+    where, delta = env[:2]
     other = lax.ppermute(mine, "core", [(0, 1), (1, 0)])
 
     stats = [
         call(
             functools.partial(stats_kernel, *sizes),
-            shape((CHIPS // 2 * lines, head), F32), (where, offsets), (part, kv),
-            flops=4 << 30,
+            shape((CHIPS // 2 * lines, head), F32), (where,), (part, kv),
+            flops=1 << 28,
         )
         for part in (mine, other)
     ]
@@ -456,7 +464,7 @@
     ])
     both = jnp.broadcast_to(both[None], (secs,) + both.shape)
     both, env = pinned_exchange(both, ("zl", "core"), env)
-    where, offsets = env[:2]
+    where = env[0]
     tiles = (CORES, CHIPS // 2, 1, width)
     logs = both[:, : CHIPS * lines]
     top = jnp.max(logs, axis=0)
@@ -467,8 +475,8 @@
 
     dkv, dq_own, dq_other = call(
         functools.partial(grads_kernel, *sizes),
-        (shape(kv.shape, BF), shape((CHIPS, flat, head), F32), shape((CHIPS, flat, head), BF)),
-        (where, offsets),
+        (shape((PLANE, HALVES * 2 * rows, head), BF), shape((CHIPS, flat, head), F32), shape((CHIPS, flat, head), BF)),
+        (where,),
         (mine, other, kv, log_total, deltas),
         scratch=[pltpu.VMEM((CORES * CHIPS // 2, head, width), F32)],
         flops=4 << 30,
@@ -479,7 +487,7 @@
         shape((HALVES * secs, 2 * rows, head), BF), (), (terms,),
     )
     whole, env = pinned_exchange(total, ("zh", "zl", "core"), env)
-    where, offsets, delta, cum, cum_t, from_start, to_end, early = env
+    where, delta, cum, cum_t, from_start, to_end, early = env
 
     cache_key_grad, cache_value_grad, out_grad, send = call(
         functools.partial(states_kernel, local),
@@ -514,7 +522,7 @@
     totals = lax.ppermute(totals, "zh", [(0, 1), (1, 0)])
     enter = call(
         functools.partial(scan_kernel, local),
-        shape(part.shape, BF), (where,), (part, decays, totals),
+        shape((PLANE, 2 * used, head), BF), (where,), (part, decays, totals),
         scratch=[pltpu.VMEM(part.shape, F32)] * 2,
     )
     enter, keep, away = lax.optimization_barrier((enter, keep, away))

time: 171 us -> 167 us (0.977)
  blocking collectives: 58.2 us -> 47.3 us
  waiting for transfers between devices: 33.4 us -> 40.8 us
  starting transfers between devices: 54.5 us -> 52.4 us
    all_to_all x1, waiting for transfers between devices: 0.01 us -> 15.6 us  [body(): kv = lax.all_to_all(kv, ('zh',) + PLANE_AXES, 0, 0, tiled=True)]
    ppermute x1 -> x0, starting transfers between devices: 11 us -> none  [body(): kv_other = lax.ppermute(kv_own, 'zh', [(0, 1), (1, 0)])]
    all_to_all x3, blocking collectives: 58.2 us -> 47.3 us  [pinned_exchange(): array = lax.all_to_all(array, axes, 0, 0, tiled=True)]
    all_to_all x1, starting transfers between devices: 10.3 us -> 17.3 us  [body(): kv = lax.all_to_all(kv, ('zh',) + PLANE_AXES, 0, 0, tiled=True)]
    ppermute x3, waiting for transfers between devices: 6.47 us -> 0.01 us  [body(): lax.ppermute(own, 'zl', [(i, (i - k) % CHIPS) for i in range(CHIPS)])]
    ppermute x3, starting transfers between devices: 11 us -> 12.8 us  [body(): lax.ppermute(own, 'zl', [(i, (i - k) % CHIPS) for i in range(CHIPS)])]
  transfers between devices with their start and end apart: 12 -> 11, of which waited for: 7 -> 5; matrix products, arithmetic and copies ran while one was open for 1% -> 2% of each run, Pallas kernels for 5% -> 6%
where the time goes in v8:
time: 167 us
  starting transfers between devices  52.4 us (31%)
  blocking collectives  47.3 us (28%)
  waiting for transfers between devices  40.8 us (24%)
  Pallas kernels  18.9 us (11%)
  local copies, waits for them, and re-layouts  5.49 us (3%)
    all_to_all x3, blocking collectives, pinned_exchange(): array = lax.all_to_all(array, axes, 0, 0, tiled=True)  47.3 us
    pallas_call x16, Pallas kernels, call(): pl.pallas_call(kernel, out_shape=outs, in_specs=[smem] * len(in_smem) + [...  18.9 us
    all_to_all x1, starting transfers between devices, body(): kv = lax.all_to_all(kv, ('zh',) + PLANE_AXES, 0, 0, tiled=True)  17.3 us
    all_to_all x1, waiting for transfers between devices, body(): kv = lax.all_to_all(kv, ('zh',) + PLANE_AXES, 0, 0, tiled=True)  15.6 us
    ppermute x3, starting transfers between devices, body(): lax.ppermute(own, 'zl', [(i, (i - k) % CHIPS) for i in range(CHIPS)])  12.8 us
    all_to_all x1, waiting for transfers between devices, body(): part = lax.all_to_all(send, PLANE_AXES, 0, 0, tiled=True)  8.87 us
    all_to_all x1, waiting for transfers between devices, body(): enter = lax.all_to_all(enter, PLANE_AXES, 0, 0, tiled=True)  8.49 us
    ppermute x1, waiting for transfers between devices, body(): totals = lax.ppermute(totals, 'zh', [(0, 1), (1, 0)])  6.49 us
  transfers between devices with their start and end apart: 11, of which 5 were waited for; matrix products, arithmetic and copies ran while one was open for 2% of the time, Pallas kernels for 6%

profile of v8, /device:TPU:8, one launch (start us, length us, event | category | flops | bytes accessed | tf_op | source)
XLA Modules:
  0.0 166.6 jit_solution(4533723134284099273)
XLA Ops:
  0.6 0.9 copy-done.2
  1.5 0.9 copy-done.7
  2.4 4.3 %collective-permute-start.2 = (bf16[640,128]{1,0:T(8,128)(2,1)S(1)}, bf16[640,128]{1,0:T(8,128)(2,1)S(1)}, u32[]{:S(2)}, u32[]{:S(2)}) collective-permute-start(bf16[640,128]{1,0:T(8,128)(2,1)S(1)} %shard_map.165.a_ref), channel_id=1, source_target_pairs={{0,128},{128,256},{256,384},{384,0},{1,129},{129,257},{257,385},{3... | collective-permute-start | bytes 491528 | tf_op jit(solution)/shard_map/ppermute | solution.py:409
  6.7 6.1 %collective-permute-start.1 = (bf16[640,128]{1,0:T(8,128)(2,1)S(1)}, bf16[640,128]{1,0:T(8,128)(2,1)S(1)}, u32[]{:S(2)}, u32[]{:S(2)}) collective-permute-start(bf16[640,128]{1,0:T(8,128)(2,1)S(1)} %shard_map.165.a_ref), channel_id=1, source_target_pairs={{0,256},{128,384},{256,0},{384,128},{1,257},{129,385},{257,1},{385... | collective-permute-start | bytes 491528 | tf_op jit(solution)/shard_map/ppermute | solution.py:409
  12.8 2.5 %collective-permute-start = (bf16[640,128]{1,0:T(8,128)(2,1)S(1)}, bf16[640,128]{1,0:T(8,128)(2,1)S(1)}, u32[]{:S(2)}, u32[]{:S(2)}) collective-permute-start(bf16[640,128]{1,0:T(8,128)(2,1)S(1)} %shard_map.165.a_ref), channel_id=1, source_target_pairs={{0,384},{128,0},{256,128},{384,256},{1,385},{129,1},{257,129},{385... | collective-permute-start | bytes 491528 | tf_op jit(solution)/shard_map/ppermute | solution.py:409
  15.3 0.7 constant_dynamic-slice_fusion
  16.0 0.9 broadcast_in_dim.8
  16.9 17.3 %all-to-all-start = ((bf16[64,32,128]{2,1,0:T(8,128)(2,1)}), bf16[64,32,128]{2,1,0:T(8,128)(2,1)S(1)}, u32[]{:S(2)}, u32[]{:S(2)}) async-start(bf16[64,32,128]{2,1,0:T(8,128)(2,1)} %broadcast_in_dim.8), calls=%async_computation | async-start | bytes 1048576 | tf_op jit(solution)/shard_map/all_to_all | solution.py:446
  35.4 1.2 shard_map.163
  37.2 2.1 %collective-permute-start.3 = (bf16[2,4,320,128]{3,2,1,0:T(8,128)(2,1)S(1)}, bf16[2,4,320,128]{3,2,1,0:T(8,128)(2,1)S(1)}, u32[]{:S(2)}, u32[]{:S(2)}) collective-permute-start(bf16[2,4,320,128]{3,2,1,0:T(8,128)(2,1)S(1)} %shard_map.166.rows_ref.mine_ref), channel_id=1, source_target_pairs={{0,64},{64,0},{1,65},{65,1},{2,66},{66,2},{3,67},{67,3},{4,68},{68... | collective-permute-start | bytes 1966088 | tf_op jit(solution)/shard_map/ppermute | solution.py:449
  40.1 15.6 %all-to-all-done.kv_ref = bf16[64,32,128]{2,1,0:T(8,128)(2,1)S(1)} async-done(((bf16[64,32,128]{2,1,0:T(8,128)(2,1)}), bf16[64,32,128]{2,1,0:T(8,128)(2,1)S(1)}, u32[]{:S(2)}, u32[]{:S(2)}) %all-to-all-start) | async-done | bytes 524320 | tf_op jit(solution)/shard_map/all_to_all | solution.py:446
  55.7 1.6 shard_map.167
  57.4 1.6 shard_map.168
  59.1 9.2 %all_to_all.30 = f32[8,32,128]{2,1,0:T(8,128)S(1)} all-to-all(f32[8,32,128]{2,1,0:T(8,128)S(1)} %broadcast_in_dim.9), channel_id=1, replica_groups=mesh['zl'=4,'core'=2,'zh'=2,'x'=4,'y'=8] {'zl','core'}, dimensions={0} | all-to-all | bytes 262144 | tf_op jit(solution)/shard_map/all_to_all | solution.py:59
  68.4 5.0 %shard_map.169 = (bf16[32,64,128]{2,1,0:T(8,128)(2,1)S(1)}, f32[4,320,128]{2,1,0:T(8,128)S(1)}, bf16[4,320,128]{2,1,0:T(8,128)(2,1)S(1)}) custom-call(s32[5]{0:T(128)S(1)} %get-tuple-element.149.where_ref, bf16[2,4,320,128]{3,2,1,0:T(8,128)(2,1)S(1)} %shard_map.166.rows_ref.mine_ref, bf16[2,4,320,128]{3,2,1,0:T(8,128)(2,1)S(1)} %collective-permute-done.3.rows_ref.other_ref, ...), custom_call_target="tpu_custom_call" | custom-call | flops 4294967296 | bytes 1048576 | tf_op jit(solution)/shard_map/pallas_call | solution.py:42
  73.4 0.7 copy-done.10
  74.1 22.0 %all_to_all.31.terms_ref = bf16[32,64,128]{2,1,0:T(8,128)(2,1)S(1)} all-to-all(bf16[32,64,128]{2,1,0:T(8,128)(2,1)S(1)} %get-tuple-element.113), channel_id=1, replica_groups=mesh['zl'=4,'core'=2,'zh'=2,'x'=4,'y'=8] {'x','y'}, dimensions={0} | all-to-all | bytes 1048576 | tf_op jit(solution)/shard_map/all_to_all | solution.py:59
  96.2 16.2 %all_to_all.32.whole_ref = bf16[16,32,128]{2,1,0:T(8,128)(2,1)S(1)} all-to-all(bf16[16,32,128]{2,1,0:T(8,128)(2,1)S(1)} %shard_map.170), channel_id=1, replica_groups=mesh['zl'=4,'core'=2,'zh'=2,'x'=4,'y'=8] {'zh','zl','core'}, dimensions={0} | all-to-all | bytes 262144 | tf_op jit(solution)/shard_map/all_to_all | solution.py:59
  112.4 1.9 %shard_map.171 = (bf16[128,128]{1,0:T(8,128)(2,1)}, bf16[128,128]{1,0:T(8,128)(2,1)}, bf16[128,640]{1,0:T(8,128)(2,1)S(1)}, bf16[32,48,128]{2,1,0:T(8,128)(2,1)}) custom-call(bf16[16,32,128]{2,1,0:T(8,128)(2,1)S(1)} %all_to_all.32.whole_ref, bf16[640,128]{1,0:T(8,128)(2,1)S(1)} %copy-done.4, bf16[640,128]{1,0:T(8,128)(2,1)S(1)} %copy-done.5, ...), custom_call_target="tpu_custom_call" | custom-call | flops 134217728 | bytes 1048576 | tf_op jit(solution)/shard_map/pallas_call | solution.py:42
  114.3 5.0 %all-to-all-start.4 = ((bf16[32,48,128]{2,1,0:T(8,128)(2,1)}), bf16[32,48,128]{2,1,0:T(8,128)(2,1)S(1)}, u32[]{:S(2)}, u32[]{:S(2)}) async-start(bf16[32,48,128]{2,1,0:T(8,128)(2,1)} %get-tuple-element.147), calls=%async_computation.4 | async-start | bytes 786432 | tf_op jit(solution)/shard_map/all_to_all | solution.py:510
  119.3 2.2 %collective-permute-start.5 = (bf16[4,320,128]{2,1,0:T(8,128)(2,1)S(1)}, bf16[4,320,128]{2,1,0:T(8,128)(2,1)S(1)}, u32[]{:S(2)}, u32[]{:S(2)}) collective-permute-start(bf16[4,320,128]{2,1,0:T(8,128)(2,1)S(1)} %copy-done.11), channel_id=1, source_target_pairs={{0,64},{64,0},{1,65},{65,1},{2,66},{66,2},{3,67},{67,3},{4,68},{68... | collective-permute-start | bytes 983048 | tf_op jit(solution)/shard_map/ppermute | solution.py:504
  121.5 1.3 collective-permute-done.5.other_ref
  123.5 2.7 %collective-permute-start.6 = (bf16[2,320,128]{2,1,0:T(8,128)(2,1)S(1)}, bf16[2,320,128]{2,1,0:T(8,128)(2,1)S(1)}, u32[]{:S(2)}, u32[]{:S(2)}) collective-permute-start(bf16[2,320,128]{2,1,0:T(8,128)(2,1)S(1)} %get-tuple-element.154), channel_id=1, source_target_pairs={{0,256},{128,384},{256,0},{384,128},{1,257},{129,385},{257,1},{385... | collective-permute-start | bytes 491528 | tf_op jit(solution)/shard_map/ppermute | solution.py:509
  126.2 8.9 %all-to-all-done.4.part_ref = bf16[32,48,128]{2,1,0:T(8,128)(2,1)S(1)} async-done(((bf16[32,48,128]{2,1,0:T(8,128)(2,1)}), bf16[32,48,128]{2,1,0:T(8,128)(2,1)S(1)}, u32[]{:S(2)}, u32[]{:S(2)}) %all-to-all-start.4) | async-done | bytes 393248 | tf_op jit(solution)/shard_map/all_to_all | solution.py:510
  135.7 3.1 %collective-permute-start.4 = (f32[48,128]{1,0:T(8,128)S(1)}, f32[48,128]{1,0:T(8,128)S(1)}, u32[]{:S(2)}, u32[]{:S(2)}) collective-permute-start(f32[48,128]{1,0:T(8,128)S(1)} %shard_map.173), channel_id=1, source_target_pairs={{0,32},{32,0},{1,33},{33,1},{2,34},{34,2},{3,35},{35,3},{4,36},{36... | collective-permute-start | bytes 73736 | tf_op jit(solution)/shard_map/ppermute | solution.py:522
  138.8 6.5 %collective-permute-done.4.other_ref = f32[48,128]{1,0:T(8,128)S(1)} collective-permute-done((f32[48,128]{1,0:T(8,128)S(1)}, f32[48,128]{1,0:T(8,128)S(1)}, u32[]{:S(2)}, u32[]{:S(2)}) %collective-permute-start.4) | collective-permute-done | bytes 24608 | tf_op jit(solution)/shard_map/ppermute | solution.py:522
  145.3 1.5 shard_map.174
  146.9 5.2 %all-to-all-start.5 = ((bf16[32,40,128]{2,1,0:T(8,128)(2,1)}), bf16[32,40,128]{2,1,0:T(8,128)(2,1)S(1)}, u32[]{:S(2)}, u32[]{:S(2)}) async-start(bf16[32,40,128]{2,1,0:T(8,128)(2,1)} %shard_map.174), calls=%async_computation.5 | async-start | bytes 655360 | tf_op jit(solution)/shard_map/all_to_all | solution.py:533
  152.6 2.0 %collective-permute-start.7 = (bf16[320,128]{1,0:T(8,128)(2,1)S(1)}, bf16[320,128]{1,0:T(8,128)(2,1)S(1)}, u32[]{:S(2)}, u32[]{:S(2)}) collective-permute-start(bf16[320,128]{1,0:T(8,128)(2,1)S(1)} %get-tuple-element.162), channel_id=1, source_target_pairs={{0,128},{128,0},{256,384},{384,256},{1,129},{129,1},{257,385},{385... | collective-permute-start | bytes 245768 | tf_op jit(solution)/shard_map/ppermute | solution.py:532
  154.7 1.2 shard_map.172
  155.9 8.5 %all-to-all-done.5.wire_ref = bf16[32,40,128]{2,1,0:T(8,128)(2,1)S(1)} async-done(((bf16[32,40,128]{2,1,0:T(8,128)(2,1)}), bf16[32,40,128]{2,1,0:T(8,128)(2,1)S(1)}, u32[]{:S(2)}, u32[]{:S(2)}) %all-to-all-start.5) | async-done | bytes 327712 | tf_op jit(solution)/shard_map/all_to_all | solution.py:533
  164.4 1.5 shard_map.176
  (67 shorter events, 5.2 us)
Async XLA Ops:
  0.6 0.9 copy-start.2
  1.5 0.9 copy-start.7
  2.4 34.1 %collective-permute-start.2 = (bf16[640,128]{1,0:T(8,128)(2,1)S(1)}, bf16[640,128]{1,0:T(8,128)(2,1)S(1)}, u32[]{:S(2)}, u32[]{:S(2)}) collective-permute-start(bf16[640,128]{1,0:T(8,128)(2,1)S(1)} %shard_map.165.a_ref), channel_id=1, source_target_pairs={{0,128},{128,256},{256,384},{384,0},{1,129},{129,257},{257,385},{3... | collective-permute-start | bytes 491528 | tf_op jit(solution)/shard_map/ppermute | solution.py:409
  6.7 29.8 %collective-permute-start.1 = (bf16[640,128]{1,0:T(8,128)(2,1)S(1)}, bf16[640,128]{1,0:T(8,128)(2,1)S(1)}, u32[]{:S(2)}, u32[]{:S(2)}) collective-permute-start(bf16[640,128]{1,0:T(8,128)(2,1)S(1)} %shard_map.165.a_ref), channel_id=1, source_target_pairs={{0,256},{128,384},{256,0},{384,128},{1,257},{129,385},{257,1},{385... | collective-permute-start | bytes 491528 | tf_op jit(solution)/shard_map/ppermute | solution.py:409
  12.8 23.7 %collective-permute-start = (bf16[640,128]{1,0:T(8,128)(2,1)S(1)}, bf16[640,128]{1,0:T(8,128)(2,1)S(1)}, u32[]{:S(2)}, u32[]{:S(2)}) collective-permute-start(bf16[640,128]{1,0:T(8,128)(2,1)S(1)} %shard_map.165.a_ref), channel_id=1, source_target_pairs={{0,384},{128,0},{256,128},{384,256},{1,385},{129,1},{257,129},{385... | collective-permute-start | bytes 491528 | tf_op jit(solution)/shard_map/ppermute | solution.py:409
  16.9 17.4 %copy-start.12 = (f32[5,128]{1,0:T(8,128)S(1)}, f32[5,128]{1,0:T(8,128)}, u32[]{:S(2)}) copy-start(f32[5,128]{1,0:T(8,128)} %param.23) | copy-start | bytes 7684
  16.9 17.9 %copy-start.8 = (bf16[1,16,2560]{2,1,0:T(8,128)(2,1)S(1)}, bf16[1,16,2560]{2,1,0:T(8,128)(2,1)}, u32[]{:S(2)}) copy-start(bf16[1,16,2560]{2,1,0:T(8,128)(2,1)} %o_ref.1) | copy-start | bytes 245764
  16.9 38.8 %all-to-all-start = ((bf16[64,32,128]{2,1,0:T(8,128)(2,1)}), bf16[64,32,128]{2,1,0:T(8,128)(2,1)S(1)}, u32[]{:S(2)}, u32[]{:S(2)}) async-start(bf16[64,32,128]{2,1,0:T(8,128)(2,1)} %broadcast_in_dim.8), calls=%async_computation | async-start | bytes 1048576 | tf_op jit(solution)/shard_map/all_to_all | solution.py:446
  34.2 0.9 copy-start.3
  34.7 0.7 copy-start.9
  36.6 3.0 %copy-start.1 = (bf16[128,640]{1,0:T(8,128)(2,1)S(1)}, bf16[128,640]{1,0:T(8,128)(2,1)}, u32[]{:S(2)}) copy-start(bf16[128,640]{1,0:T(8,128)(2,1)} %rv_ref.5) | copy-start | bytes 491524
  37.2 2.4 %copy-start = (bf16[128,640]{1,0:T(8,128)(2,1)S(1)}, bf16[128,640]{1,0:T(8,128)(2,1)}, u32[]{:S(2)}) copy-start(bf16[128,640]{1,0:T(8,128)(2,1)} %rk_ref.5) | copy-start | bytes 491524
  37.2 20.1 %collective-permute-start.3 = (bf16[2,4,320,128]{3,2,1,0:T(8,128)(2,1)S(1)}, bf16[2,4,320,128]{3,2,1,0:T(8,128)(2,1)S(1)}, u32[]{:S(2)}, u32[]{:S(2)}) collective-permute-start(bf16[2,4,320,128]{3,2,1,0:T(8,128)(2,1)S(1)} %shard_map.166.rows_ref.mine_ref), channel_id=1, source_target_pairs={{0,64},{64,0},{1,65},{65,1},{2,66},{66,2},{3,67},{67,3},{4,68},{68... | collective-permute-start | bytes 1966088 | tf_op jit(solution)/shard_map/ppermute | solution.py:449
  73.4 0.7 copy-start.10
  96.1 16.3 %copy-start.5 = (bf16[640,128]{1,0:T(8,128)(2,1)S(1)}, bf16[640,128]{1,0:T(8,128)(2,1)}, u32[]{:S(2)}) copy-start(bf16[640,128]{1,0:T(8,128)(2,1)} %vp_ref.1) | copy-start | bytes 491524
  96.1 16.3 %copy-start.6 = (bf16[128,640]{1,0:T(8,128)(2,1)S(1)}, bf16[128,640]{1,0:T(8,128)(2,1)}, u32[]{:S(2)}) copy-start(bf16[128,640]{1,0:T(8,128)(2,1)} %rq_ref.3) | copy-start | bytes 491524
  96.2 16.2 %copy-start.4 = (bf16[640,128]{1,0:T(8,128)(2,1)S(1)}, bf16[640,128]{1,0:T(8,128)(2,1)}, u32[]{:S(2)}) copy-start(bf16[640,128]{1,0:T(8,128)(2,1)} %kp_ref.1) | copy-start | bytes 491524
  114.3 5.0 %copy-start.11 = (bf16[4,320,128]{2,1,0:T(8,128)(2,1)S(1)}, bf16[4,320,128]{2,1,0:T(8,128)(2,1)}, u32[]{:S(2)}) copy-start(bf16[4,320,128]{2,1,0:T(8,128)(2,1)} %copy-done.10) | copy-start | bytes 983044
  114.3 20.7 %all-to-all-start.4 = ((bf16[32,48,128]{2,1,0:T(8,128)(2,1)}), bf16[32,48,128]{2,1,0:T(8,128)(2,1)S(1)}, u32[]{:S(2)}, u32[]{:S(2)}) async-start(bf16[32,48,128]{2,1,0:T(8,128)(2,1)} %get-tuple-element.147), calls=%async_computation.4 | async-start | bytes 786432 | tf_op jit(solution)/shard_map/all_to_all | solution.py:510
  119.3 3.5 %collective-permute-start.5 = (bf16[4,320,128]{2,1,0:T(8,128)(2,1)S(1)}, bf16[4,320,128]{2,1,0:T(8,128)(2,1)S(1)}, u32[]{:S(2)}, u32[]{:S(2)}) collective-permute-start(bf16[4,320,128]{2,1,0:T(8,128)(2,1)S(1)} %copy-done.11), channel_id=1, source_target_pairs={{0,64},{64,0},{1,65},{65,1},{2,66},{66,2},{3,67},{67,3},{4,68},{68... | collective-permute-start | bytes 983048 | tf_op jit(solution)/shard_map/ppermute | solution.py:504
  123.5 23.4 %collective-permute-start.6 = (bf16[2,320,128]{2,1,0:T(8,128)(2,1)S(1)}, bf16[2,320,128]{2,1,0:T(8,128)(2,1)S(1)}, u32[]{:S(2)}, u32[]{:S(2)}) collective-permute-start(bf16[2,320,128]{2,1,0:T(8,128)(2,1)S(1)} %get-tuple-element.154), channel_id=1, source_target_pairs={{0,256},{128,384},{256,0},{384,128},{1,257},{129,385},{257,1},{385... | collective-permute-start | bytes 491528 | tf_op jit(solution)/shard_map/ppermute | solution.py:509
  135.7 9.6 %collective-permute-start.4 = (f32[48,128]{1,0:T(8,128)S(1)}, f32[48,128]{1,0:T(8,128)S(1)}, u32[]{:S(2)}, u32[]{:S(2)}) collective-permute-start(f32[48,128]{1,0:T(8,128)S(1)} %shard_map.173), channel_id=1, source_target_pairs={{0,32},{32,0},{1,33},{33,1},{2,34},{34,2},{3,35},{35,3},{4,36},{36... | collective-permute-start | bytes 73736 | tf_op jit(solution)/shard_map/ppermute | solution.py:522
  146.9 17.5 %all-to-all-start.5 = ((bf16[32,40,128]{2,1,0:T(8,128)(2,1)}), bf16[32,40,128]{2,1,0:T(8,128)(2,1)S(1)}, u32[]{:S(2)}, u32[]{:S(2)}) async-start(bf16[32,40,128]{2,1,0:T(8,128)(2,1)} %shard_map.174), calls=%async_computation.5 | async-start | bytes 655360 | tf_op jit(solution)/shard_map/all_to_all | solution.py:533
  152.6 13.3 %collective-permute-start.7 = (bf16[320,128]{1,0:T(8,128)(2,1)S(1)}, bf16[320,128]{1,0:T(8,128)(2,1)S(1)}, u32[]{:S(2)}, u32[]{:S(2)}) collective-permute-start(bf16[320,128]{1,0:T(8,128)(2,1)S(1)} %get-tuple-element.162), channel_id=1, source_target_pairs={{0,128},{128,0},{256,384},{384,256},{1,129},{129,1},{257,385},{385... | collective-permute-start | bytes 245768 | tf_op jit(solution)/shard_map/ppermute | solution.py:532

commit v9 on v8

--- a/solution.py
+++ b/solution.py
@@ -33,7 +33,7 @@
     return lax.dot_general(a, b, (((0,), (0,)), ((), ())), preferred_element_type=F32)
 
 
-def call(kernel, outs, in_smem, ins, scratch=(), flops=0, smem_outs=0):
+def call(kernel, outs, in_smem, ins, scratch=(), flops=0, smem_outs=0, space=pltpu.VMEM, scoped=SCOPED):
     vmem = pl.BlockSpec(memory_space=pltpu.VMEM)
     smem = pl.BlockSpec(memory_space=pltpu.SMEM)
     out_specs = jax.tree.map(lambda _: vmem, outs)
@@ -42,10 +42,10 @@
     return pl.pallas_call(
         kernel,
         out_shape=outs,
-        in_specs=[smem] * len(in_smem) + [vmem] * len(ins),
+        in_specs=[smem] * len(in_smem) + [pl.BlockSpec(memory_space=space)] * len(ins),
         out_specs=out_specs,
         scratch_shapes=list(scratch),
-        compiler_params=pltpu.CompilerParams(vmem_limit_bytes=SCOPED),
+        compiler_params=pltpu.CompilerParams(vmem_limit_bytes=scoped),
         cost_estimate=pl.CostEstimate(flops=flops, bytes_accessed=1 << 20, transcendentals=0),
     )(*in_smem, *ins)
 
@@ -60,19 +60,20 @@
     return lax.optimization_barrier((array, later))
 
 
-def pack_kernel(heads, q_ref, g_ref, out_ref):
+def pack_kernel(heads, q_hbm, g_hbm, out_ref, q_ref, g_ref, sems):
     rows = q_ref.shape[1]
+    copies = [
+        pltpu.make_async_copy(q_hbm, q_ref, sems.at[0]),
+        pltpu.make_async_copy(g_hbm, g_ref, sems.at[1]),
+    ]
+    for copy in copies:
+        copy.start()
+    for copy in copies:
+        copy.wait()
     for h in range(heads):
         at = slice(h * 128, (h + 1) * 128)
         out_ref[h * rows : (h + 1) * rows, :] = q_ref[0, :, at]
         out_ref[(heads + h) * rows : (heads + h + 1) * rows, :] = g_ref[0, :, at]
-
-
-def spread_kernel(where_ref, own_ref, other_ref, out_ref):
-    plane = out_ref.shape[0]
-    half = where_ref[0] // plane
-    out_ref[:, half] = jnp.broadcast_to(own_ref[...][None], (plane,) + own_ref.shape)
-    out_ref[:, 1 - half] = jnp.broadcast_to(other_ref[...][None], (plane,) + other_ref.shape)
 
 
 def delta_kernel(heads, where_ref, offset_ref, g_ref, o_ref, out_ref, place_ref, product):
@@ -270,10 +271,13 @@
     plane = send_ref.shape[0]
     lines = send_ref.shape[1] - early_ref.shape[1]
     wire[:, SLICE * heads :, :] = jnp.zeros((plane, lines - SLICE * heads, 128), F32)
+    both = jnp.concatenate([ck, cv], axis=1)
+    projection = jnp.concatenate([kp_ref[...], vp_ref[...]], axis=1)
+    out_grad = dot_nt(both, projection).astype(BF)
+    gr_ref[...] = out_grad
     for i in range(heads):
         at = slice(i * 128, (i + 1) * 128)
-        gr = (dot_nt(ck, kp_ref[at, :]) + dot_nt(cv, vp_ref[at, :])).astype(BF)
-        gr_ref[:, at] = gr
+        gr = out_grad[:, at]
         query_w = (rq_ref[:, at].astype(F32) * from_ref[:, i : i + 1]).astype(BF)
         grad = dot_tn(query_w, gr)
         for k in range(SLICE):
@@ -341,9 +345,13 @@
 
 
 def final_kernel(
-    heads, rk_ref, rv_ref, gr_ref, from_ref, to_ref, q_in_ref, k_in_ref, v_in_ref, wire_ref,
-    q_ref, k_ref, v_ref, wire,
+    heads, query_heads, factor, rk_ref, rv_ref, gr_ref, from_ref, to_ref, q_in_ref, k_in_ref, v_in_ref,
+    wire_ref, own_ref, got_ref, q_ref, k_ref, v_ref, cross_ref, wire,
 ):
+    rows = cross_ref.shape[1]
+    total = ((own_ref[...] + got_ref[...].astype(F32)) * factor).astype(BF)
+    for h in range(query_heads):
+        cross_ref[0, :, h * 128 : (h + 1) * 128] = total[h * rows : (h + 1) * rows]
     wire[...] = wire_ref[...].astype(F32)
 
     def matrix(r):
@@ -356,13 +364,6 @@
         q_ref[:, at] = q_in_ref[:, at] + from_start * dot_nt(gr_ref[:, at], state_b)
         k_ref[:, at] = k_in_ref[:, at] + to_end * dot_nt(rv_ref[:, at], grad_b)
         v_ref[:, at] = v_in_ref[:, at] + to_end * dot_nn(rk_ref[:, at], grad_b)
-
-
-def query_grad_kernel(heads, factor, own_ref, got_ref, out_ref):
-    rows = out_ref.shape[1]
-    total = ((own_ref[...] + got_ref[...].astype(F32)) * factor).astype(BF)
-    for h in range(heads):
-        out_ref[0, :, h * 128 : (h + 1) * 128] = total[h * rows : (h + 1) * rows]
 
 
 def body(
@@ -403,7 +404,9 @@
     kv = jnp.broadcast_to(kv_own[None], (shards,) + kv_own.shape)
     own = call(
         functools.partial(pack_kernel, heads),
-        shape((2 * flat, head), BF), (), (queries, output_grad), flops=1 << 20,
+        shape((2 * flat, head), BF), (), (queries, output_grad),
+        scratch=[pltpu.VMEM(queries.shape, BF)] * 2 + [pltpu.SemaphoreType.DMA((2,))],
+        space=pltpu.HBM, scoped=56 * 1024 * 1024,
     )
     parts = [own] + [
         lax.ppermute(own, "zl", [(i, (i - k) % CHIPS) for i in range(CHIPS)])
@@ -536,16 +539,16 @@
         (retention_query, retention_key, retention_value, out_grad, cum, cum_t),
         flops=1 << 28,
     )
-    grads = call(
-        functools.partial(final_kernel, local), (shape(wide, F32),) * 3, (),
-        (retention_key, retention_value, out_grad, from_start, to_end, *within, enter),
+    *grads, cross_query_grad = call(
+        functools.partial(final_kernel, local, heads, factor),
+        (shape(wide, F32),) * 3 + (shape(queries.shape, BF),),
+        (),
+        (
+            retention_key, retention_value, out_grad, from_start, to_end, *within, enter,
+            dq_mine, piece,
+        ),
         scratch=[pltpu.VMEM(enter.shape, F32)],
         flops=1 << 27,
-    )
-    grads, dq_mine, piece = lax.optimization_barrier((grads, dq_mine, piece))
-    cross_query_grad = call(
-        functools.partial(query_grad_kernel, heads, factor),
-        shape(queries.shape, BF), (), (dq_mine, piece),
     )
     return (cross_query_grad, cache_key_grad, cache_value_grad) + tuple(grads)
 

time: 167 us -> 165 us (0.988)
  local copies, waits for them, and re-layouts: 5.49 us -> 2.8 us
    ppermute x1, waiting for transfers between devices: 0.01 us -> 3.07 us  [body(): piece = lax.ppermute(piece, 'zl', [(i, i ^ 1) for i in range(CHIPS)])]
    all_to_all x1, waiting for transfers between devices: 8.49 us -> 5.42 us  [body(): enter = lax.all_to_all(enter, PLANE_AXES, 0, 0, tiled=True)]
    unnamed x26 -> x24, local copies, waits for them, and re-layouts: 3.11 us -> 0.41 us
    pallas_call x16 -> x15, Pallas kernels: 18.9 us -> 19.2 us  [call(): pl.pallas_call(kernel, out_shape=outs, in_specs=[smem] * len(in_smem) + [...]
  transfers between devices with their start and end apart: 11 -> 11, of which waited for: 5 -> 6; matrix products, arithmetic and copies ran while one was open for 2% -> 2% of each run, Pallas kernels for 6% -> 5%
where the time goes in v9:
time: 165 us; the launch traced here: 164 us
  starting transfers between devices  52.4 us (32%)
  blocking collectives  47.3 us (29%)
  waiting for transfers between devices  41 us (25%)
  Pallas kernels  19.2 us (12%)
  local copies, waits for them, and re-layouts  2.8 us (2%)
    all_to_all x3, blocking collectives, pinned_exchange(): array = lax.all_to_all(array, axes, 0, 0, tiled=True)  47.3 us
    pallas_call x15, Pallas kernels, call(): pl.pallas_call(kernel, out_shape=outs, in_specs=[smem] * len(in_smem) + [...  19.2 us
    all_to_all x1, starting transfers between devices, body(): kv = lax.all_to_all(kv, ('zh',) + PLANE_AXES, 0, 0, tiled=True)  17.3 us
    all_to_all x1, waiting for transfers between devices, body(): kv = lax.all_to_all(kv, ('zh',) + PLANE_AXES, 0, 0, tiled=True)  15.8 us
    ppermute x3, starting transfers between devices, body(): lax.ppermute(own, 'zl', [(i, (i - k) % CHIPS) for i in range(CHIPS)])  12.8 us
    all_to_all x1, waiting for transfers between devices, body(): part = lax.all_to_all(send, PLANE_AXES, 0, 0, tiled=True)  8.87 us
    ppermute x1, waiting for transfers between devices, body(): totals = lax.ppermute(totals, 'zh', [(0, 1), (1, 0)])  6.5 us
    all_to_all x1, waiting for transfers between devices, body(): enter = lax.all_to_all(enter, PLANE_AXES, 0, 0, tiled=True)  5.42 us
  transfers between devices with their start and end apart: 11, of which 6 were waited for; matrix products, arithmetic and copies ran while one was open for 2% of the time, Pallas kernels for 5%

profile of v9, /device:TPU:8, one launch (start us, length us, event | category | flops | bytes accessed | tf_op | source)
XLA Modules:
  0.0 164.4 jit_solution(4564760233343432168)
XLA Ops:
  0.6 1.6 shard_map.165.a_ref
  2.3 4.3 %collective-permute-start.2 = (bf16[640,128]{1,0:T(8,128)(2,1)}, bf16[640,128]{1,0:T(8,128)(2,1)S(1)}, u32[]{:S(2)}, u32[]{:S(2)}) collective-permute-start(bf16[640,128]{1,0:T(8,128)(2,1)} %shard_map.165.a_ref), channel_id=1, source_target_pairs={{0,128},{128,256},{256,384},{384,0},{1,129},{129,257},{257,385},{3... | collective-permute-start | bytes 491528 | tf_op jit(solution)/shard_map/ppermute | solution.py:412
  6.6 6.1 %collective-permute-start.1 = (bf16[640,128]{1,0:T(8,128)(2,1)}, bf16[640,128]{1,0:T(8,128)(2,1)S(1)}, u32[]{:S(2)}, u32[]{:S(2)}) collective-permute-start(bf16[640,128]{1,0:T(8,128)(2,1)} %shard_map.165.a_ref), channel_id=1, source_target_pairs={{0,256},{128,384},{256,0},{384,128},{1,257},{129,385},{257,1},{385... | collective-permute-start | bytes 491528 | tf_op jit(solution)/shard_map/ppermute | solution.py:412
  12.7 2.5 %collective-permute-start = (bf16[640,128]{1,0:T(8,128)(2,1)}, bf16[640,128]{1,0:T(8,128)(2,1)S(1)}, u32[]{:S(2)}, u32[]{:S(2)}) collective-permute-start(bf16[640,128]{1,0:T(8,128)(2,1)} %shard_map.165.a_ref), channel_id=1, source_target_pairs={{0,384},{128,0},{256,128},{384,256},{1,385},{129,1},{257,129},{385... | collective-permute-start | bytes 491528 | tf_op jit(solution)/shard_map/ppermute | solution.py:412
  15.1 0.7 constant_dynamic-slice_fusion
  15.9 0.9 broadcast_in_dim.8
  16.7 17.3 %all-to-all-start = ((bf16[64,32,128]{2,1,0:T(8,128)(2,1)}), bf16[64,32,128]{2,1,0:T(8,128)(2,1)S(1)}, u32[]{:S(2)}, u32[]{:S(2)}) async-start(bf16[64,32,128]{2,1,0:T(8,128)(2,1)} %broadcast_in_dim.8), calls=%async_computation | async-start | bytes 1048576 | tf_op jit(solution)/shard_map/all_to_all | solution.py:449
  35.0 1.2 shard_map.163
  36.8 2.1 %collective-permute-start.3 = (bf16[2,4,320,128]{3,2,1,0:T(8,128)(2,1)S(1)}, bf16[2,4,320,128]{3,2,1,0:T(8,128)(2,1)S(1)}, u32[]{:S(2)}, u32[]{:S(2)}) collective-permute-start(bf16[2,4,320,128]{3,2,1,0:T(8,128)(2,1)S(1)} %shard_map.166.rows_ref.mine_ref), channel_id=1, source_target_pairs={{0,64},{64,0},{1,65},{65,1},{2,66},{66,2},{3,67},{67,3},{4,68},{68... | collective-permute-start | bytes 1966088 | tf_op jit(solution)/shard_map/ppermute | solution.py:452
  39.7 15.8 %all-to-all-done.kv_ref = bf16[64,32,128]{2,1,0:T(8,128)(2,1)S(1)} async-done(((bf16[64,32,128]{2,1,0:T(8,128)(2,1)}), bf16[64,32,128]{2,1,0:T(8,128)(2,1)S(1)}, u32[]{:S(2)}, u32[]{:S(2)}) %all-to-all-start) | async-done | bytes 524320 | tf_op jit(solution)/shard_map/all_to_all | solution.py:449
  55.5 1.6 %shard_map.167 = f32[10,128]{1,0:T(8,128)S(1)} custom-call(s32[5]{0:T(128)S(1)} %get-tuple-element.145.where_ref, bf16[2,4,320,128]{3,2,1,0:T(8,128)(2,1)S(1)} %shard_map.166.rows_ref.mine_ref, bf16[64,32,128]{2,1,0:T(8,128)(2,1)S(1)} %all-to-all-done.kv_ref), custom_call_target="tpu_custom_call" | custom-call | flops 268435456 | bytes 1048576 | tf_op jit(solution)/shard_map/pallas_call | solution.py:42
  57.2 1.6 %shard_map.168 = f32[10,128]{1,0:T(8,128)S(1)} custom-call(s32[5]{0:T(128)S(1)} %get-tuple-element.145.where_ref, bf16[2,4,320,128]{3,2,1,0:T(8,128)(2,1)S(1)} %collective-permute-done.3.rows_ref.other_ref, bf16[64,32,128]{2,1,0:T(8,128)(2,1)S(1)} %all-to-all-done.kv_ref), custom_call_target="tpu_custom_call" | custom-call | flops 268435456 | bytes 1048576 | tf_op jit(solution)/shard_map/pallas_call | solution.py:42
  58.9 9.2 %all_to_all.30 = f32[8,32,128]{2,1,0:T(8,128)S(1)} all-to-all(f32[8,32,128]{2,1,0:T(8,128)S(1)} %broadcast_in_dim.9), channel_id=1, replica_groups=mesh['zl'=4,'core'=2,'zh'=2,'x'=4,'y'=8] {'zl','core'}, dimensions={0} | all-to-all | bytes 262144 | tf_op jit(solution)/shard_map/all_to_all | solution.py:59
  68.2 5.0 %shard_map.169 = (bf16[32,64,128]{2,1,0:T(8,128)(2,1)S(1)}, f32[4,320,128]{2,1,0:T(8,128)S(1)}, bf16[4,320,128]{2,1,0:T(8,128)(2,1)S(1)}) custom-call(s32[5]{0:T(128)S(1)} %get-tuple-element.145.where_ref, bf16[2,4,320,128]{3,2,1,0:T(8,128)(2,1)S(1)} %shard_map.166.rows_ref.mine_ref, bf16[2,4,320,128]{3,2,1,0:T(8,128)(2,1)S(1)} %collective-permute-done.3.rows_ref.other_ref, ...), custom_call_target="tpu_custom_call" | custom-call | flops 4294967296 | bytes 1048576 | tf_op jit(solution)/shard_map/pallas_call | solution.py:42
  73.2 22.0 %all_to_all.31.terms_ref = bf16[32,64,128]{2,1,0:T(8,128)(2,1)S(1)} all-to-all(bf16[32,64,128]{2,1,0:T(8,128)(2,1)S(1)} %get-tuple-element.109), channel_id=1, replica_groups=mesh['zl'=4,'core'=2,'zh'=2,'x'=4,'y'=8] {'x','y'}, dimensions={0} | all-to-all | bytes 1048576 | tf_op jit(solution)/shard_map/all_to_all | solution.py:59
  95.3 16.2 %all_to_all.32.whole_ref = bf16[16,32,128]{2,1,0:T(8,128)(2,1)S(1)} all-to-all(bf16[16,32,128]{2,1,0:T(8,128)(2,1)S(1)} %shard_map.170), channel_id=1, replica_groups=mesh['zl'=4,'core'=2,'zh'=2,'x'=4,'y'=8] {'zh','zl','core'}, dimensions={0} | all-to-all | bytes 262144 | tf_op jit(solution)/shard_map/all_to_all | solution.py:59
  111.5 1.3 shard_map.171
  112.8 5.0 %all-to-all-start.4 = ((bf16[32,48,128]{2,1,0:T(8,128)(2,1)}), bf16[32,48,128]{2,1,0:T(8,128)(2,1)S(1)}, u32[]{:S(2)}, u32[]{:S(2)}) async-start(bf16[32,48,128]{2,1,0:T(8,128)(2,1)} %get-tuple-element.143), calls=%async_computation.4 | async-start | bytes 786432 | tf_op jit(solution)/shard_map/all_to_all | solution.py:513
  117.9 2.2 %collective-permute-start.5 = (bf16[4,320,128]{2,1,0:T(8,128)(2,1)S(1)}, bf16[4,320,128]{2,1,0:T(8,128)(2,1)S(1)}, u32[]{:S(2)}, u32[]{:S(2)}) collective-permute-start(bf16[4,320,128]{2,1,0:T(8,128)(2,1)S(1)} %copy-done.10), channel_id=1, source_target_pairs={{0,64},{64,0},{1,65},{65,1},{2,66},{66,2},{3,67},{67,3},{4,68},{68... | collective-permute-start | bytes 983048 | tf_op jit(solution)/shard_map/ppermute | solution.py:507
  120.1 1.3 collective-permute-done.5.other_ref
  121.4 0.6 shard_map.175
  122.0 2.7 %collective-permute-start.6 = (bf16[2,320,128]{2,1,0:T(8,128)(2,1)S(1)}, bf16[2,320,128]{2,1,0:T(8,128)(2,1)S(1)}, u32[]{:S(2)}, u32[]{:S(2)}) collective-permute-start(bf16[2,320,128]{2,1,0:T(8,128)(2,1)S(1)} %get-tuple-element.150), channel_id=1, source_target_pairs={{0,256},{128,384},{256,0},{384,128},{1,257},{129,385},{257,1},{385... | collective-permute-start | bytes 491528 | tf_op jit(solution)/shard_map/ppermute | solution.py:512
  124.7 8.9 %all-to-all-done.4.part_ref = bf16[32,48,128]{2,1,0:T(8,128)(2,1)S(1)} async-done(((bf16[32,48,128]{2,1,0:T(8,128)(2,1)}), bf16[32,48,128]{2,1,0:T(8,128)(2,1)S(1)}, u32[]{:S(2)}, u32[]{:S(2)}) %all-to-all-start.4) | async-done | bytes 393248 | tf_op jit(solution)/shard_map/all_to_all | solution.py:513
  134.2 3.1 %collective-permute-start.4 = (f32[48,128]{1,0:T(8,128)S(1)}, f32[48,128]{1,0:T(8,128)S(1)}, u32[]{:S(2)}, u32[]{:S(2)}) collective-permute-start(f32[48,128]{1,0:T(8,128)S(1)} %shard_map.173), channel_id=1, source_target_pairs={{0,32},{32,0},{1,33},{33,1},{2,34},{34,2},{3,35},{35,3},{4,36},{36... | collective-permute-start | bytes 73736 | tf_op jit(solution)/shard_map/ppermute | solution.py:525
  137.3 6.5 %collective-permute-done.4.other_ref = f32[48,128]{1,0:T(8,128)S(1)} collective-permute-done((f32[48,128]{1,0:T(8,128)S(1)}, f32[48,128]{1,0:T(8,128)S(1)}, u32[]{:S(2)}, u32[]{:S(2)}) %collective-permute-start.4) | collective-permute-done | bytes 24608 | tf_op jit(solution)/shard_map/ppermute | solution.py:525
  143.8 1.5 shard_map.174
  145.3 5.2 %all-to-all-start.5 = ((bf16[32,40,128]{2,1,0:T(8,128)(2,1)}), bf16[32,40,128]{2,1,0:T(8,128)(2,1)S(1)}, u32[]{:S(2)}, u32[]{:S(2)}) async-start(bf16[32,40,128]{2,1,0:T(8,128)(2,1)} %shard_map.174), calls=%async_computation.5 | async-start | bytes 655360 | tf_op jit(solution)/shard_map/all_to_all | solution.py:536
  151.1 2.0 %collective-permute-start.7 = (bf16[320,128]{1,0:T(8,128)(2,1)S(1)}, bf16[320,128]{1,0:T(8,128)(2,1)S(1)}, u32[]{:S(2)}, u32[]{:S(2)}) collective-permute-start(bf16[320,128]{1,0:T(8,128)(2,1)S(1)} %get-tuple-element.155), channel_id=1, source_target_pairs={{0,128},{128,0},{256,384},{384,256},{1,129},{129,1},{257,385},{385... | collective-permute-start | bytes 245768 | tf_op jit(solution)/shard_map/ppermute | solution.py:535
  153.2 1.2 shard_map.172
  154.4 3.1 %collective-permute-done.7.got_ref = bf16[320,128]{1,0:T(8,128)(2,1)S(1)} collective-permute-done((bf16[320,128]{1,0:T(8,128)(2,1)S(1)}, bf16[320,128]{1,0:T(8,128)(2,1)S(1)}, u32[]{:S(2)}, u32[]{:S(2)}) %collective-permute-start.7) | collective-permute-done | bytes 81952 | tf_op jit(solution)/shard_map/ppermute | solution.py:535
  157.5 5.4 %all-to-all-done.5.wire_ref = bf16[32,40,128]{2,1,0:T(8,128)(2,1)S(1)} async-done(((bf16[32,40,128]{2,1,0:T(8,128)(2,1)}), bf16[32,40,128]{2,1,0:T(8,128)(2,1)S(1)}, u32[]{:S(2)}, u32[]{:S(2)}) %all-to-all-start.5) | async-done | bytes 327712 | tf_op jit(solution)/shard_map/all_to_all | solution.py:536
  162.9 1.5 shard_map.177
  (64 shorter events, 3.7 us)
Async XLA Ops:
  2.3 33.9 %collective-permute-start.2 = (bf16[640,128]{1,0:T(8,128)(2,1)}, bf16[640,128]{1,0:T(8,128)(2,1)S(1)}, u32[]{:S(2)}, u32[]{:S(2)}) collective-permute-start(bf16[640,128]{1,0:T(8,128)(2,1)} %shard_map.165.a_ref), channel_id=1, source_target_pairs={{0,128},{128,256},{256,384},{384,0},{1,129},{129,257},{257,385},{3... | collective-permute-start | bytes 491528 | tf_op jit(solution)/shard_map/ppermute | solution.py:412
  6.6 29.6 %collective-permute-start.1 = (bf16[640,128]{1,0:T(8,128)(2,1)}, bf16[640,128]{1,0:T(8,128)(2,1)S(1)}, u32[]{:S(2)}, u32[]{:S(2)}) collective-permute-start(bf16[640,128]{1,0:T(8,128)(2,1)} %shard_map.165.a_ref), channel_id=1, source_target_pairs={{0,256},{128,384},{256,0},{384,128},{1,257},{129,385},{257,1},{385... | collective-permute-start | bytes 491528 | tf_op jit(solution)/shard_map/ppermute | solution.py:412
  12.7 23.5 %collective-permute-start = (bf16[640,128]{1,0:T(8,128)(2,1)}, bf16[640,128]{1,0:T(8,128)(2,1)S(1)}, u32[]{:S(2)}, u32[]{:S(2)}) collective-permute-start(bf16[640,128]{1,0:T(8,128)(2,1)} %shard_map.165.a_ref), channel_id=1, source_target_pairs={{0,384},{128,0},{256,128},{384,256},{1,385},{129,1},{257,129},{385... | collective-permute-start | bytes 491528 | tf_op jit(solution)/shard_map/ppermute | solution.py:412
  16.7 17.4 %copy-start.11 = (f32[5,128]{1,0:T(8,128)S(1)}, f32[5,128]{1,0:T(8,128)}, u32[]{:S(2)}) copy-start(f32[5,128]{1,0:T(8,128)} %param.23) | copy-start | bytes 7684
  16.7 17.9 %copy-start.7 = (bf16[1,16,2560]{2,1,0:T(8,128)(2,1)S(1)}, bf16[1,16,2560]{2,1,0:T(8,128)(2,1)}, u32[]{:S(2)}) copy-start(bf16[1,16,2560]{2,1,0:T(8,128)(2,1)} %o_ref.1) | copy-start | bytes 245764
  16.7 17.9 %copy-start.8 = (s32[64]{0:T(128)S(1)}, s32[64]{0:T(128)}, u32[]{:S(2)}) copy-start(s32[64]{0:T(128)} %offset_ref.1) | copy-start | bytes 772
  16.7 38.8 %all-to-all-start = ((bf16[64,32,128]{2,1,0:T(8,128)(2,1)}), bf16[64,32,128]{2,1,0:T(8,128)(2,1)S(1)}, u32[]{:S(2)}, u32[]{:S(2)}) async-start(bf16[64,32,128]{2,1,0:T(8,128)(2,1)} %broadcast_in_dim.8), calls=%async_computation | async-start | bytes 1048576 | tf_op jit(solution)/shard_map/all_to_all | solution.py:449
  34.1 0.9 copy-start.2
  34.1 2.1 %copy-start.6 = (bf16[640,128]{1,0:T(8,128)(2,1)S(1)}, bf16[640,128]{1,0:T(8,128)(2,1)}, u32[]{:S(2)}) copy-start(bf16[640,128]{1,0:T(8,128)(2,1)} %shard_map.165.a_ref) | copy-start | bytes 491524
  36.2 3.0 %copy-start.1 = (bf16[128,640]{1,0:T(8,128)(2,1)S(1)}, bf16[128,640]{1,0:T(8,128)(2,1)}, u32[]{:S(2)}) copy-start(bf16[128,640]{1,0:T(8,128)(2,1)} %rv_ref.5) | copy-start | bytes 491524
  36.8 2.4 %copy-start = (bf16[128,640]{1,0:T(8,128)(2,1)S(1)}, bf16[128,640]{1,0:T(8,128)(2,1)}, u32[]{:S(2)}) copy-start(bf16[128,640]{1,0:T(8,128)(2,1)} %rk_ref.5) | copy-start | bytes 491524
  36.8 20.4 %collective-permute-start.3 = (bf16[2,4,320,128]{3,2,1,0:T(8,128)(2,1)S(1)}, bf16[2,4,320,128]{3,2,1,0:T(8,128)(2,1)S(1)}, u32[]{:S(2)}, u32[]{:S(2)}) collective-permute-start(bf16[2,4,320,128]{3,2,1,0:T(8,128)(2,1)S(1)} %shard_map.166.rows_ref.mine_ref), channel_id=1, source_target_pairs={{0,64},{64,0},{1,65},{65,1},{2,66},{66,2},{3,67},{67,3},{4,68},{68... | collective-permute-start | bytes 1966088 | tf_op jit(solution)/shard_map/ppermute | solution.py:452
  73.2 22.0 %copy-start.9 = (bf16[4,320,128]{2,1,0:T(8,128)(2,1)}, bf16[4,320,128]{2,1,0:T(8,128)(2,1)S(1)}, u32[]{:S(2)}) copy-start(bf16[4,320,128]{2,1,0:T(8,128)(2,1)S(1)} %get-tuple-element.148) | copy-start | bytes 983044
  95.2 16.3 %copy-start.4 = (bf16[640,128]{1,0:T(8,128)(2,1)S(1)}, bf16[640,128]{1,0:T(8,128)(2,1)}, u32[]{:S(2)}) copy-start(bf16[640,128]{1,0:T(8,128)(2,1)} %vp_ref.1) | copy-start | bytes 491524
  95.2 16.3 %copy-start.5 = (bf16[128,640]{1,0:T(8,128)(2,1)S(1)}, bf16[128,640]{1,0:T(8,128)(2,1)}, u32[]{:S(2)}) copy-start(bf16[128,640]{1,0:T(8,128)(2,1)} %rq_ref.3) | copy-start | bytes 491524
  95.3 16.2 %copy-start.3 = (bf16[640,128]{1,0:T(8,128)(2,1)S(1)}, bf16[640,128]{1,0:T(8,128)(2,1)}, u32[]{:S(2)}) copy-start(bf16[640,128]{1,0:T(8,128)(2,1)} %kp_ref.1) | copy-start | bytes 491524
  112.8 5.0 %copy-start.10 = (bf16[4,320,128]{2,1,0:T(8,128)(2,1)S(1)}, bf16[4,320,128]{2,1,0:T(8,128)(2,1)}, u32[]{:S(2)}) copy-start(bf16[4,320,128]{2,1,0:T(8,128)(2,1)} %copy-done.9) | copy-start | bytes 983044
  112.8 20.7 %all-to-all-start.4 = ((bf16[32,48,128]{2,1,0:T(8,128)(2,1)}), bf16[32,48,128]{2,1,0:T(8,128)(2,1)S(1)}, u32[]{:S(2)}, u32[]{:S(2)}) async-start(bf16[32,48,128]{2,1,0:T(8,128)(2,1)} %get-tuple-element.143), calls=%async_computation.4 | async-start | bytes 786432 | tf_op jit(solution)/shard_map/all_to_all | solution.py:513
  117.9 3.5 %collective-permute-start.5 = (bf16[4,320,128]{2,1,0:T(8,128)(2,1)S(1)}, bf16[4,320,128]{2,1,0:T(8,128)(2,1)S(1)}, u32[]{:S(2)}, u32[]{:S(2)}) collective-permute-start(bf16[4,320,128]{2,1,0:T(8,128)(2,1)S(1)} %copy-done.10), channel_id=1, source_target_pairs={{0,64},{64,0},{1,65},{65,1},{2,66},{66,2},{3,67},{67,3},{4,68},{68... | collective-permute-start | bytes 983048 | tf_op jit(solution)/shard_map/ppermute | solution.py:507
  122.0 23.3 %collective-permute-start.6 = (bf16[2,320,128]{2,1,0:T(8,128)(2,1)S(1)}, bf16[2,320,128]{2,1,0:T(8,128)(2,1)S(1)}, u32[]{:S(2)}, u32[]{:S(2)}) collective-permute-start(bf16[2,320,128]{2,1,0:T(8,128)(2,1)S(1)} %get-tuple-element.150), channel_id=1, source_target_pairs={{0,256},{128,384},{256,0},{384,128},{1,257},{129,385},{257,1},{385... | collective-permute-start | bytes 491528 | tf_op jit(solution)/shard_map/ppermute | solution.py:512
  134.2 9.6 %collective-permute-start.4 = (f32[48,128]{1,0:T(8,128)S(1)}, f32[48,128]{1,0:T(8,128)S(1)}, u32[]{:S(2)}, u32[]{:S(2)}) collective-permute-start(f32[48,128]{1,0:T(8,128)S(1)} %shard_map.173), channel_id=1, source_target_pairs={{0,32},{32,0},{1,33},{33,1},{2,34},{34,2},{3,35},{35,3},{4,36},{36... | collective-permute-start | bytes 73736 | tf_op jit(solution)/shard_map/ppermute | solution.py:525
  145.3 17.5 %all-to-all-start.5 = ((bf16[32,40,128]{2,1,0:T(8,128)(2,1)}), bf16[32,40,128]{2,1,0:T(8,128)(2,1)S(1)}, u32[]{:S(2)}, u32[]{:S(2)}) async-start(bf16[32,40,128]{2,1,0:T(8,128)(2,1)} %shard_map.174), calls=%async_computation.5 | async-start | bytes 655360 | tf_op jit(solution)/shard_map/all_to_all | solution.py:536
  151.1 6.3 %collective-permute-start.7 = (bf16[320,128]{1,0:T(8,128)(2,1)S(1)}, bf16[320,128]{1,0:T(8,128)(2,1)S(1)}, u32[]{:S(2)}, u32[]{:S(2)}) collective-permute-start(bf16[320,128]{1,0:T(8,128)(2,1)S(1)} %get-tuple-element.155), channel_id=1, source_target_pairs={{0,128},{128,0},{256,384},{384,256},{1,129},{129,1},{257,385},{385... | collective-permute-start | bytes 245768 | tf_op jit(solution)/shard_map/ppermute | solution.py:535

commit v10 on v9

--- a/solution.py
+++ b/solution.py
@@ -149,8 +149,6 @@
                 s = jnp.where(seen, s, LOW)
             new = jnp.maximum(top, jnp.max(s, axis=0, keepdims=True))
             p = jnp.exp2((s - new) * scale)
-            if masked:
-                p = jnp.where(seen, p, 0.0)
             total = total * jnp.exp2((top - new) * scale) + jnp.sum(p, axis=0, keepdims=True)
             out.append((new, total))
         return tuple(out)
@@ -158,7 +156,7 @@
     start = ((jnp.full((1, width), LOW, F32), jnp.zeros((1, width), F32)),) * len(tiles)
     done = chunk(full, lax.fori_loop(0, full, chunk, start), masked=True)
     for t, (top, total) in zip(tiles, done):
-        lse = jnp.where(total > 0.0, top * factor + jnp.log(total), LOW)
+        lse = jnp.where(top > LOW, top * factor + jnp.log(total), LOW)
         for m in range(lines):
             out_ref[t * lines + m : t * lines + m + 1, :] = lse[:, m * 128 : (m + 1) * 128]
 
@@ -282,8 +280,7 @@
         grad = dot_tn(query_w, gr)
         for k in range(SLICE):
             wire[:, SLICE * i + k, :] = grad[k * plane : (k + 1) * plane]
-    send_ref[:, 0:lines, :] = wire[...].astype(BF)
-    send_ref[:, lines:, :] = early_ref[...]
+    send_ref[...] = jnp.concatenate([wire[...], early_ref[...].astype(F32)], axis=1).astype(BF)
 
 
 def totals_kernel(heads, part_ref, decay_ref, out_ref):
@@ -297,7 +294,7 @@
         back = decay_ref[r] * back + part_ref[r].astype(F32)
         return fore, back
 
-    fore, back = lax.fori_loop(0, count, step, (zero, zero), unroll=4)
+    fore, back = lax.fori_loop(0, count, step, (zero, zero), unroll=8)
     row = lax.broadcasted_iota(jnp.int32, zero.shape, 0)
     out_ref[...] = jnp.where(row < WIRE // 2, back, fore)
 
@@ -318,7 +315,7 @@
         return fore, back
 
     start = (jnp.where(upper, other, zero), jnp.where(upper, zero, other))
-    lax.fori_loop(0, count, step, start, unroll=4)
+    lax.fori_loop(0, count, step, start, unroll=8)
     used = SLICE * heads
     at = WIRE // 2
     both = jnp.concatenate([behind[:, 0:used, :], ahead[:, at : at + used, :]], axis=1)

time: 165 us -> 165 us (level)
  no operation moved by 1% of the time
where the time goes in v10:
time: 165 us; the launch traced here: 164 us
  starting transfers between devices  52.4 us (32%)
  blocking collectives  47.3 us (29%)
  waiting for transfers between devices  41 us (25%)
  Pallas kernels  18.9 us (11%)
  local copies, waits for them, and re-layouts  2.8 us (2%)
    all_to_all x3, blocking collectives, pinned_exchange(): array = lax.all_to_all(array, axes, 0, 0, tiled=True)  47.3 us
    pallas_call x15, Pallas kernels, call(): pl.pallas_call(kernel, out_shape=outs, in_specs=[smem] * len(in_smem) + [...  18.9 us
    all_to_all x1, starting transfers between devices, body(): kv = lax.all_to_all(kv, ('zh',) + PLANE_AXES, 0, 0, tiled=True)  17.3 us
    all_to_all x1, waiting for transfers between devices, body(): kv = lax.all_to_all(kv, ('zh',) + PLANE_AXES, 0, 0, tiled=True)  15.8 us
    ppermute x3, starting transfers between devices, body(): lax.ppermute(own, 'zl', [(i, (i - k) % CHIPS) for i in range(CHIPS)])  12.8 us
    all_to_all x1, waiting for transfers between devices, body(): part = lax.all_to_all(send, PLANE_AXES, 0, 0, tiled=True)  8.87 us
    ppermute x1, waiting for transfers between devices, body(): totals = lax.ppermute(totals, 'zh', [(0, 1), (1, 0)])  6.5 us
    all_to_all x1, waiting for transfers between devices, body(): enter = lax.all_to_all(enter, PLANE_AXES, 0, 0, tiled=True)  5.42 us
  transfers between devices with their start and end apart: 11, of which 6 were waited for; matrix products, arithmetic and copies ran while one was open for 2% of the time, Pallas kernels for 5%

profile of v10, /device:TPU:8, one launch (start us, length us, event | category | flops | bytes accessed | tf_op | source)
XLA Modules:
  0.0 164.1 jit_solution(153866704221603876)
XLA Ops:
  0.6 1.6 shard_map.165.a_ref
  2.3 4.3 %collective-permute-start.2 = (bf16[640,128]{1,0:T(8,128)(2,1)}, bf16[640,128]{1,0:T(8,128)(2,1)S(1)}, u32[]{:S(2)}, u32[]{:S(2)}) collective-permute-start(bf16[640,128]{1,0:T(8,128)(2,1)} %shard_map.165.a_ref), channel_id=1, source_target_pairs={{0,128},{128,256},{256,384},{384,0},{1,129},{129,257},{257,385},{3... | collective-permute-start | bytes 491528 | tf_op jit(solution)/shard_map/ppermute | solution.py:409
  6.6 6.1 %collective-permute-start.1 = (bf16[640,128]{1,0:T(8,128)(2,1)}, bf16[640,128]{1,0:T(8,128)(2,1)S(1)}, u32[]{:S(2)}, u32[]{:S(2)}) collective-permute-start(bf16[640,128]{1,0:T(8,128)(2,1)} %shard_map.165.a_ref), channel_id=1, source_target_pairs={{0,256},{128,384},{256,0},{384,128},{1,257},{129,385},{257,1},{385... | collective-permute-start | bytes 491528 | tf_op jit(solution)/shard_map/ppermute | solution.py:409
  12.7 2.5 %collective-permute-start = (bf16[640,128]{1,0:T(8,128)(2,1)}, bf16[640,128]{1,0:T(8,128)(2,1)S(1)}, u32[]{:S(2)}, u32[]{:S(2)}) collective-permute-start(bf16[640,128]{1,0:T(8,128)(2,1)} %shard_map.165.a_ref), channel_id=1, source_target_pairs={{0,384},{128,0},{256,128},{384,256},{1,385},{129,1},{257,129},{385... | collective-permute-start | bytes 491528 | tf_op jit(solution)/shard_map/ppermute | solution.py:409
  15.1 0.7 constant_dynamic-slice_fusion
  15.9 0.9 broadcast_in_dim.8
  16.7 17.3 %all-to-all-start = ((bf16[64,32,128]{2,1,0:T(8,128)(2,1)}), bf16[64,32,128]{2,1,0:T(8,128)(2,1)S(1)}, u32[]{:S(2)}, u32[]{:S(2)}) async-start(bf16[64,32,128]{2,1,0:T(8,128)(2,1)} %broadcast_in_dim.8), calls=%async_computation | async-start | bytes 1048576 | tf_op jit(solution)/shard_map/all_to_all | solution.py:446
  35.0 1.2 shard_map.163
  36.8 2.1 %collective-permute-start.3 = (bf16[2,4,320,128]{3,2,1,0:T(8,128)(2,1)S(1)}, bf16[2,4,320,128]{3,2,1,0:T(8,128)(2,1)S(1)}, u32[]{:S(2)}, u32[]{:S(2)}) collective-permute-start(bf16[2,4,320,128]{3,2,1,0:T(8,128)(2,1)S(1)} %shard_map.166.rows_ref.mine_ref), channel_id=1, source_target_pairs={{0,64},{64,0},{1,65},{65,1},{2,66},{66,2},{3,67},{67,3},{4,68},{68... | collective-permute-start | bytes 1966088 | tf_op jit(solution)/shard_map/ppermute | solution.py:449
  39.7 15.8 %all-to-all-done.kv_ref = bf16[64,32,128]{2,1,0:T(8,128)(2,1)S(1)} async-done(((bf16[64,32,128]{2,1,0:T(8,128)(2,1)}), bf16[64,32,128]{2,1,0:T(8,128)(2,1)S(1)}, u32[]{:S(2)}, u32[]{:S(2)}) %all-to-all-start) | async-done | bytes 524320 | tf_op jit(solution)/shard_map/all_to_all | solution.py:446
  55.5 1.5 shard_map.167
  57.1 1.5 shard_map.168
  58.6 9.2 %all_to_all.30 = f32[8,32,128]{2,1,0:T(8,128)S(1)} all-to-all(f32[8,32,128]{2,1,0:T(8,128)S(1)} %broadcast_in_dim.9), channel_id=1, replica_groups=mesh['zl'=4,'core'=2,'zh'=2,'x'=4,'y'=8] {'zl','core'}, dimensions={0} | all-to-all | bytes 262144 | tf_op jit(solution)/shard_map/all_to_all | solution.py:59
  68.0 5.0 %shard_map.169 = (bf16[32,64,128]{2,1,0:T(8,128)(2,1)S(1)}, f32[4,320,128]{2,1,0:T(8,128)S(1)}, bf16[4,320,128]{2,1,0:T(8,128)(2,1)S(1)}) custom-call(s32[5]{0:T(128)S(1)} %get-tuple-element.145.where_ref, bf16[2,4,320,128]{3,2,1,0:T(8,128)(2,1)S(1)} %shard_map.166.rows_ref.mine_ref, bf16[2,4,320,128]{3,2,1,0:T(8,128)(2,1)S(1)} %collective-permute-done.3.rows_ref.other_ref, ...), custom_call_target="tpu_custom_call" | custom-call | flops 4294967296 | bytes 1048576 | tf_op jit(solution)/shard_map/pallas_call | solution.py:42
  73.0 22.0 %all_to_all.31.terms_ref = bf16[32,64,128]{2,1,0:T(8,128)(2,1)S(1)} all-to-all(bf16[32,64,128]{2,1,0:T(8,128)(2,1)S(1)} %get-tuple-element.109), channel_id=1, replica_groups=mesh['zl'=4,'core'=2,'zh'=2,'x'=4,'y'=8] {'x','y'}, dimensions={0} | all-to-all | bytes 1048576 | tf_op jit(solution)/shard_map/all_to_all | solution.py:59
  95.1 16.2 %all_to_all.32.whole_ref = bf16[16,32,128]{2,1,0:T(8,128)(2,1)S(1)} all-to-all(bf16[16,32,128]{2,1,0:T(8,128)(2,1)S(1)} %shard_map.170), channel_id=1, replica_groups=mesh['zl'=4,'core'=2,'zh'=2,'x'=4,'y'=8] {'zh','zl','core'}, dimensions={0} | all-to-all | bytes 262144 | tf_op jit(solution)/shard_map/all_to_all | solution.py:59
  111.3 1.3 shard_map.171
  112.6 5.0 %all-to-all-start.4 = ((bf16[32,48,128]{2,1,0:T(8,128)(2,1)}), bf16[32,48,128]{2,1,0:T(8,128)(2,1)S(1)}, u32[]{:S(2)}, u32[]{:S(2)}) async-start(bf16[32,48,128]{2,1,0:T(8,128)(2,1)} %get-tuple-element.143), calls=%async_computation.4 | async-start | bytes 786432 | tf_op jit(solution)/shard_map/all_to_all | solution.py:510
  117.6 2.2 %collective-permute-start.5 = (bf16[4,320,128]{2,1,0:T(8,128)(2,1)S(1)}, bf16[4,320,128]{2,1,0:T(8,128)(2,1)S(1)}, u32[]{:S(2)}, u32[]{:S(2)}) collective-permute-start(bf16[4,320,128]{2,1,0:T(8,128)(2,1)S(1)} %copy-done.10), channel_id=1, source_target_pairs={{0,64},{64,0},{1,65},{65,1},{2,66},{66,2},{3,67},{67,3},{4,68},{68... | collective-permute-start | bytes 983048 | tf_op jit(solution)/shard_map/ppermute | solution.py:504
  119.8 1.3 collective-permute-done.5.other_ref
  121.2 0.6 shard_map.175
  121.8 2.7 %collective-permute-start.6 = (bf16[2,320,128]{2,1,0:T(8,128)(2,1)S(1)}, bf16[2,320,128]{2,1,0:T(8,128)(2,1)S(1)}, u32[]{:S(2)}, u32[]{:S(2)}) collective-permute-start(bf16[2,320,128]{2,1,0:T(8,128)(2,1)S(1)} %get-tuple-element.150), channel_id=1, source_target_pairs={{0,256},{128,384},{256,0},{384,128},{1,257},{129,385},{257,1},{385... | collective-permute-start | bytes 491528 | tf_op jit(solution)/shard_map/ppermute | solution.py:509
  124.5 8.9 %all-to-all-done.4.part_ref = bf16[32,48,128]{2,1,0:T(8,128)(2,1)S(1)} async-done(((bf16[32,48,128]{2,1,0:T(8,128)(2,1)}), bf16[32,48,128]{2,1,0:T(8,128)(2,1)S(1)}, u32[]{:S(2)}, u32[]{:S(2)}) %all-to-all-start.4) | async-done | bytes 393248 | tf_op jit(solution)/shard_map/all_to_all | solution.py:510
  134.0 3.1 %collective-permute-start.4 = (f32[48,128]{1,0:T(8,128)S(1)}, f32[48,128]{1,0:T(8,128)S(1)}, u32[]{:S(2)}, u32[]{:S(2)}) collective-permute-start(f32[48,128]{1,0:T(8,128)S(1)} %shard_map.173), channel_id=1, source_target_pairs={{0,32},{32,0},{1,33},{33,1},{2,34},{34,2},{3,35},{35,3},{4,36},{36... | collective-permute-start | bytes 73736 | tf_op jit(solution)/shard_map/ppermute | solution.py:522
  137.1 6.5 %collective-permute-done.4.other_ref = f32[48,128]{1,0:T(8,128)S(1)} collective-permute-done((f32[48,128]{1,0:T(8,128)S(1)}, f32[48,128]{1,0:T(8,128)S(1)}, u32[]{:S(2)}, u32[]{:S(2)}) %collective-permute-start.4) | collective-permute-done | bytes 24608 | tf_op jit(solution)/shard_map/ppermute | solution.py:522
  143.6 1.5 shard_map.174
  145.1 5.2 %all-to-all-start.5 = ((bf16[32,40,128]{2,1,0:T(8,128)(2,1)}), bf16[32,40,128]{2,1,0:T(8,128)(2,1)S(1)}, u32[]{:S(2)}, u32[]{:S(2)}) async-start(bf16[32,40,128]{2,1,0:T(8,128)(2,1)} %shard_map.174), calls=%async_computation.5 | async-start | bytes 655360 | tf_op jit(solution)/shard_map/all_to_all | solution.py:533
  150.9 2.0 %collective-permute-start.7 = (bf16[320,128]{1,0:T(8,128)(2,1)S(1)}, bf16[320,128]{1,0:T(8,128)(2,1)S(1)}, u32[]{:S(2)}, u32[]{:S(2)}) collective-permute-start(bf16[320,128]{1,0:T(8,128)(2,1)S(1)} %get-tuple-element.155), channel_id=1, source_target_pairs={{0,128},{128,0},{256,384},{384,256},{1,129},{129,1},{257,385},{385... | collective-permute-start | bytes 245768 | tf_op jit(solution)/shard_map/ppermute | solution.py:532
  152.9 1.2 shard_map.172
  154.1 3.1 %collective-permute-done.7.got_ref = bf16[320,128]{1,0:T(8,128)(2,1)S(1)} collective-permute-done((bf16[320,128]{1,0:T(8,128)(2,1)S(1)}, bf16[320,128]{1,0:T(8,128)(2,1)S(1)}, u32[]{:S(2)}, u32[]{:S(2)}) %collective-permute-start.7) | collective-permute-done | bytes 81952 | tf_op jit(solution)/shard_map/ppermute | solution.py:532
  157.2 5.4 %all-to-all-done.5.wire_ref = bf16[32,40,128]{2,1,0:T(8,128)(2,1)S(1)} async-done(((bf16[32,40,128]{2,1,0:T(8,128)(2,1)}), bf16[32,40,128]{2,1,0:T(8,128)(2,1)S(1)}, u32[]{:S(2)}, u32[]{:S(2)}) %all-to-all-start.5) | async-done | bytes 327712 | tf_op jit(solution)/shard_map/all_to_all | solution.py:533
  162.6 1.5 shard_map.177
  (64 shorter events, 3.6 us)
Async XLA Ops:
  2.3 33.9 %collective-permute-start.2 = (bf16[640,128]{1,0:T(8,128)(2,1)}, bf16[640,128]{1,0:T(8,128)(2,1)S(1)}, u32[]{:S(2)}, u32[]{:S(2)}) collective-permute-start(bf16[640,128]{1,0:T(8,128)(2,1)} %shard_map.165.a_ref), channel_id=1, source_target_pairs={{0,128},{128,256},{256,384},{384,0},{1,129},{129,257},{257,385},{3... | collective-permute-start | bytes 491528 | tf_op jit(solution)/shard_map/ppermute | solution.py:409
  6.6 29.6 %collective-permute-start.1 = (bf16[640,128]{1,0:T(8,128)(2,1)}, bf16[640,128]{1,0:T(8,128)(2,1)S(1)}, u32[]{:S(2)}, u32[]{:S(2)}) collective-permute-start(bf16[640,128]{1,0:T(8,128)(2,1)} %shard_map.165.a_ref), channel_id=1, source_target_pairs={{0,256},{128,384},{256,0},{384,128},{1,257},{129,385},{257,1},{385... | collective-permute-start | bytes 491528 | tf_op jit(solution)/shard_map/ppermute | solution.py:409
  12.7 23.5 %collective-permute-start = (bf16[640,128]{1,0:T(8,128)(2,1)}, bf16[640,128]{1,0:T(8,128)(2,1)S(1)}, u32[]{:S(2)}, u32[]{:S(2)}) collective-permute-start(bf16[640,128]{1,0:T(8,128)(2,1)} %shard_map.165.a_ref), channel_id=1, source_target_pairs={{0,384},{128,0},{256,128},{384,256},{1,385},{129,1},{257,129},{385... | collective-permute-start | bytes 491528 | tf_op jit(solution)/shard_map/ppermute | solution.py:409
  16.7 17.4 %copy-start.11 = (f32[5,128]{1,0:T(8,128)S(1)}, f32[5,128]{1,0:T(8,128)}, u32[]{:S(2)}) copy-start(f32[5,128]{1,0:T(8,128)} %param.23) | copy-start | bytes 7684
  16.7 17.9 %copy-start.7 = (bf16[1,16,2560]{2,1,0:T(8,128)(2,1)S(1)}, bf16[1,16,2560]{2,1,0:T(8,128)(2,1)}, u32[]{:S(2)}) copy-start(bf16[1,16,2560]{2,1,0:T(8,128)(2,1)} %o_ref.1) | copy-start | bytes 245764
  16.7 17.9 %copy-start.8 = (s32[64]{0:T(128)S(1)}, s32[64]{0:T(128)}, u32[]{:S(2)}) copy-start(s32[64]{0:T(128)} %offset_ref.1) | copy-start | bytes 772
  16.7 38.8 %all-to-all-start = ((bf16[64,32,128]{2,1,0:T(8,128)(2,1)}), bf16[64,32,128]{2,1,0:T(8,128)(2,1)S(1)}, u32[]{:S(2)}, u32[]{:S(2)}) async-start(bf16[64,32,128]{2,1,0:T(8,128)(2,1)} %broadcast_in_dim.8), calls=%async_computation | async-start | bytes 1048576 | tf_op jit(solution)/shard_map/all_to_all | solution.py:446
  34.1 0.9 copy-start.2
  34.1 2.1 %copy-start.6 = (bf16[640,128]{1,0:T(8,128)(2,1)S(1)}, bf16[640,128]{1,0:T(8,128)(2,1)}, u32[]{:S(2)}) copy-start(bf16[640,128]{1,0:T(8,128)(2,1)} %shard_map.165.a_ref) | copy-start | bytes 491524
  36.2 3.0 %copy-start.1 = (bf16[128,640]{1,0:T(8,128)(2,1)S(1)}, bf16[128,640]{1,0:T(8,128)(2,1)}, u32[]{:S(2)}) copy-start(bf16[128,640]{1,0:T(8,128)(2,1)} %rv_ref.5) | copy-start | bytes 491524
  36.8 2.4 %copy-start = (bf16[128,640]{1,0:T(8,128)(2,1)S(1)}, bf16[128,640]{1,0:T(8,128)(2,1)}, u32[]{:S(2)}) copy-start(bf16[128,640]{1,0:T(8,128)(2,1)} %rk_ref.5) | copy-start | bytes 491524
  36.8 20.2 %collective-permute-start.3 = (bf16[2,4,320,128]{3,2,1,0:T(8,128)(2,1)S(1)}, bf16[2,4,320,128]{3,2,1,0:T(8,128)(2,1)S(1)}, u32[]{:S(2)}, u32[]{:S(2)}) collective-permute-start(bf16[2,4,320,128]{3,2,1,0:T(8,128)(2,1)S(1)} %shard_map.166.rows_ref.mine_ref), channel_id=1, source_target_pairs={{0,64},{64,0},{1,65},{65,1},{2,66},{66,2},{3,67},{67,3},{4,68},{68... | collective-permute-start | bytes 1966088 | tf_op jit(solution)/shard_map/ppermute | solution.py:449
  73.0 22.0 %copy-start.9 = (bf16[4,320,128]{2,1,0:T(8,128)(2,1)}, bf16[4,320,128]{2,1,0:T(8,128)(2,1)S(1)}, u32[]{:S(2)}) copy-start(bf16[4,320,128]{2,1,0:T(8,128)(2,1)S(1)} %get-tuple-element.148) | copy-start | bytes 983044
  95.0 16.3 %copy-start.4 = (bf16[640,128]{1,0:T(8,128)(2,1)S(1)}, bf16[640,128]{1,0:T(8,128)(2,1)}, u32[]{:S(2)}) copy-start(bf16[640,128]{1,0:T(8,128)(2,1)} %vp_ref.1) | copy-start | bytes 491524
  95.0 16.3 %copy-start.5 = (bf16[128,640]{1,0:T(8,128)(2,1)S(1)}, bf16[128,640]{1,0:T(8,128)(2,1)}, u32[]{:S(2)}) copy-start(bf16[128,640]{1,0:T(8,128)(2,1)} %rq_ref.3) | copy-start | bytes 491524
  95.1 16.2 %copy-start.3 = (bf16[640,128]{1,0:T(8,128)(2,1)S(1)}, bf16[640,128]{1,0:T(8,128)(2,1)}, u32[]{:S(2)}) copy-start(bf16[640,128]{1,0:T(8,128)(2,1)} %kp_ref.1) | copy-start | bytes 491524
  112.6 5.0 %copy-start.10 = (bf16[4,320,128]{2,1,0:T(8,128)(2,1)S(1)}, bf16[4,320,128]{2,1,0:T(8,128)(2,1)}, u32[]{:S(2)}) copy-start(bf16[4,320,128]{2,1,0:T(8,128)(2,1)} %copy-done.9) | copy-start | bytes 983044
  112.6 20.7 %all-to-all-start.4 = ((bf16[32,48,128]{2,1,0:T(8,128)(2,1)}), bf16[32,48,128]{2,1,0:T(8,128)(2,1)S(1)}, u32[]{:S(2)}, u32[]{:S(2)}) async-start(bf16[32,48,128]{2,1,0:T(8,128)(2,1)} %get-tuple-element.143), calls=%async_computation.4 | async-start | bytes 786432 | tf_op jit(solution)/shard_map/all_to_all | solution.py:510
  117.6 3.5 %collective-permute-start.5 = (bf16[4,320,128]{2,1,0:T(8,128)(2,1)S(1)}, bf16[4,320,128]{2,1,0:T(8,128)(2,1)S(1)}, u32[]{:S(2)}, u32[]{:S(2)}) collective-permute-start(bf16[4,320,128]{2,1,0:T(8,128)(2,1)S(1)} %copy-done.10), channel_id=1, source_target_pairs={{0,64},{64,0},{1,65},{65,1},{2,66},{66,2},{3,67},{67,3},{4,68},{68... | collective-permute-start | bytes 983048 | tf_op jit(solution)/shard_map/ppermute | solution.py:504
  121.8 23.3 %collective-permute-start.6 = (bf16[2,320,128]{2,1,0:T(8,128)(2,1)S(1)}, bf16[2,320,128]{2,1,0:T(8,128)(2,1)S(1)}, u32[]{:S(2)}, u32[]{:S(2)}) collective-permute-start(bf16[2,320,128]{2,1,0:T(8,128)(2,1)S(1)} %get-tuple-element.150), channel_id=1, source_target_pairs={{0,256},{128,384},{256,0},{384,128},{1,257},{129,385},{257,1},{385... | collective-permute-start | bytes 491528 | tf_op jit(solution)/shard_map/ppermute | solution.py:509
  134.0 9.6 %collective-permute-start.4 = (f32[48,128]{1,0:T(8,128)S(1)}, f32[48,128]{1,0:T(8,128)S(1)}, u32[]{:S(2)}, u32[]{:S(2)}) collective-permute-start(f32[48,128]{1,0:T(8,128)S(1)} %shard_map.173), channel_id=1, source_target_pairs={{0,32},{32,0},{1,33},{33,1},{2,34},{34,2},{3,35},{35,3},{4,36},{36... | collective-permute-start | bytes 73736 | tf_op jit(solution)/shard_map/ppermute | solution.py:522
  145.1 17.5 %all-to-all-start.5 = ((bf16[32,40,128]{2,1,0:T(8,128)(2,1)}), bf16[32,40,128]{2,1,0:T(8,128)(2,1)S(1)}, u32[]{:S(2)}, u32[]{:S(2)}) async-start(bf16[32,40,128]{2,1,0:T(8,128)(2,1)} %shard_map.174), calls=%async_computation.5 | async-start | bytes 655360 | tf_op jit(solution)/shard_map/all_to_all | solution.py:533
  150.9 6.3 %collective-permute-start.7 = (bf16[320,128]{1,0:T(8,128)(2,1)S(1)}, bf16[320,128]{1,0:T(8,128)(2,1)S(1)}, u32[]{:S(2)}, u32[]{:S(2)}) collective-permute-start(bf16[320,128]{1,0:T(8,128)(2,1)S(1)} %get-tuple-element.155), channel_id=1, source_target_pairs={{0,128},{128,0},{256,384},{384,256},{1,129},{129,1},{257,385},{385... | collective-permute-start | bytes 245768 | tf_op jit(solution)/shard_map/ppermute | solution.py:532
